TPU v7x, 32 devices: a whole 2x2x4 slice. The times are simulated.
32 devices in a mesh: row: 4 (over x, core), col: 8 (over z, y).
Axes of the slice: x: 2, y: 2, z: 4, core: 2. Of those that a mesh axis runs over, the one named last changes fastest.
Arguments:
- valence: bfloat16 [2, 16, 32768], replicated, may hold values from -6 to 6
- conduction: bfloat16 [2, 128, 32768], replicated, may hold values from -6 to 6
- valence_energy: float32 [16], replicated, may hold values from -8 to -1
- conduction_energy: float32 [128], replicated, may hold values from 0.5 to 6
- band_pairs: int32 [1024, 2], P(('row', 'col')), may hold values from 0 to 127, as said below
- grid_index: int32 [16384], replicated, may hold values from 0 to 32767, as said below
Outputs:
- response: float32 [2, 16384, 16384], P(None, 'row', 'col')
Inputs may be any that keep to these rules, and one draw needn't show every extreme that they name: `band_pairs`: the rows are distinct combinations of a valence band below 16 and a conduction band below 128, half of all combinations. `grid_index`: the 16384 entries are distinct.
All inputs are finite; a program needn't handle non-finite values.
Results may differ from a plain program's by a relative error of at most 0.0039.
Values may be sent and summed in bfloat16 or wider, within the bound.
No kernel may reach another device: no remote copies, remote signals or barrier semaphores. Data moves between devices by JAX's collectives and lax.ppermute only.
A program may use at most 256 MiB of HBM per device.

v0:
```python
import math

import jax
import jax.numpy as jnp
from jax import lax
from jax.sharding import PartitionSpec as P

N1 = 32
N2 = 32
N3 = 32
NVB = 16
NCB = 128


def tables(length):
    position = jnp.arange(length, dtype=jnp.int32)
    phase_angle = (position[:, None] * position[None, :] % length).astype(jnp.float32) * (
        2.0 * math.pi / length
    )
    return (jnp.cos(phase_angle), jnp.sin(phase_angle))


def plane_table():
    plane_size = N2 * N3
    position = jnp.arange(plane_size, dtype=jnp.int32)
    second = position // N3
    third = position % N3
    phase_index = (
        second[:, None] * second[None, :] % N2 * N3 + third[:, None] * third[None, :] % N3 * N2
    )
    phase_angle = (phase_index % plane_size).astype(jnp.float32) * (2.0 * math.pi / plane_size)
    cosine = jnp.cos(phase_angle)
    sine_table = jnp.sin(phase_angle)
    upper = jnp.concatenate([cosine, -sine_table], axis=1)
    lower = jnp.concatenate([sine_table, cosine], axis=1)
    return jnp.concatenate([upper, lower], axis=0)


def transform(rho_real, rho_imag):
    pair_count = rho_real.shape[0]
    plane_size = N2 * N3
    stacked = jnp.concatenate(
        [
            rho_real.reshape(pair_count, N1, plane_size),
            rho_imag.reshape(pair_count, N1, plane_size),
        ],
        axis=2,
    )
    plane = jnp.dot(
        stacked.reshape(pair_count * N1, 2 * plane_size),
        plane_table(),
        precision=lax.Precision.HIGHEST,
    )
    plane = plane.reshape(pair_count, N1, 2 * plane_size)
    cosine, sine_table = tables(N1)
    cos_part = jnp.einsum("kr,prx->pkx", cosine, plane, precision=lax.Precision.HIGHEST)
    sin_part = jnp.einsum("kr,prx->pkx", sine_table, plane, precision=lax.Precision.HIGHEST)
    out_real = cos_part[:, :, :plane_size] + sin_part[:, :, plane_size:]
    out_imag = cos_part[:, :, plane_size:] - sin_part[:, :, :plane_size]
    return (out_real.reshape(pair_count, -1), out_imag.reshape(pair_count, -1))


def pair_spectrum(valence, conduction, valence_energy, conduction_energy, band_pairs):
    valence_rows = jnp.take(valence, band_pairs[:, 0], axis=1).astype(jnp.float32)
    conduction_rows = jnp.take(conduction, band_pairs[:, 1], axis=1).astype(jnp.float32)
    rho_real = valence_rows[0] * conduction_rows[0] + valence_rows[1] * conduction_rows[1]
    rho_imag = valence_rows[0] * conduction_rows[1] - valence_rows[1] * conduction_rows[0]
    out_real, out_imag = transform(rho_real, rho_imag)
    normalize = 1.0 / math.sqrt(N1 * N2 * N3)
    spectrum = jnp.stack([out_real, out_imag]) * normalize
    valence_hot = (
        band_pairs[:, 0][:, None] == jnp.arange(valence_energy.shape[0], dtype=jnp.int32)[None, :]
    )
    conduction_hot = (
        band_pairs[:, 1][:, None]
        == jnp.arange(conduction_energy.shape[0], dtype=jnp.int32)[None, :]
    )
    energy_gap = jnp.sum(jnp.where(valence_hot, valence_energy[None, :], 0.0), axis=1) - jnp.sum(
        jnp.where(conduction_hot, conduction_energy[None, :], 0.0), axis=1
    )
    weights = 2.0 / (math.sqrt(NVB * NCB // 2) * energy_gap)
    return (spectrum, weights)


def contract(weighted_part, operand, left_dims, right_dims):
    full_left = (0,) + tuple((d + 1 for d in left_dims))
    full_right = (0,) + tuple((d + 1 for d in right_dims))
    real_part = lax.dot_general(
        weighted_part,
        operand,
        ((full_left, full_right), ((), ())),
        preferred_element_type=jnp.float32,
    )
    pair_dims = ((left_dims, right_dims), ((), ()))
    imag_part = lax.dot_general(
        weighted_part[0], operand[1], pair_dims, preferred_element_type=jnp.float32
    ) - lax.dot_general(weighted_part[1], operand[0], pair_dims, preferred_element_type=jnp.float32)
    return jnp.stack([real_part, imag_part])


def body(valence, conduction, valence_energy, conduction_energy, band_pairs, grid_index):
    spectrum, weights = pair_spectrum(
        valence, conduction, valence_energy, conduction_energy, band_pairs
    )
    row_count = lax.axis_size("row")
    column_count = lax.axis_size("col")
    selected = jnp.take(spectrum, grid_index, axis=2)
    weighted = (weights[None, :, None] * selected).astype(jnp.bfloat16)
    density = selected.astype(jnp.bfloat16)
    weighted_block = lax.all_to_all(weighted, "row", split_axis=2, concat_axis=1, tiled=True)
    density_block = lax.all_to_all(density, "col", split_axis=2, concat_axis=1, tiled=True)
    weighted_all = lax.all_gather(weighted_block, "col", axis=1, tiled=True)
    density_all = lax.all_gather(density_block, "row", axis=1, tiled=True)
    pair_count = density_all.shape[1]
    per_device = pair_count // (row_count * column_count)
    weighted_split = weighted_all.reshape(
        2, column_count, row_count, per_device, weighted_all.shape[2]
    )
    density_split = density_all.reshape(
        2, row_count, column_count, per_device, density_all.shape[2]
    )
    return contract(weighted_split, density_split, (0, 1, 2), (1, 0, 2))


def solution(mesh):
    return jax.shard_map(
        body,
        mesh=mesh,
        in_specs=(P(), P(), P(), P(), P(("row", "col"), None), P()),
        out_specs=P(None, "row", "col"),
        check_vma=False,
    )
```

profile of v0, /device:TPU:0, one launch (start us, length us, event | category | flops | bytes accessed | tf_op | source)
XLA Modules:
  0.0 1176.3 jit_solution(9382225613152862224)
XLA Ops:
  9.9 12.2 %gather_fusion.1 = bf16[32,2,32768]{2,0,1:T(8,128)(2,1)} fusion(bf16[2,128,32768]{2,1,0:T(8,128)(2,1)} %param.7, s32[1024]{0:T(1024)S(1)} %get-tuple-element.22), kind=kCustom, calls=%fused_computation.1 | custom fusion | bytes 8388736 | tf_op jit(solution)/shard_map/jit(_take)/gather | solution.py:65
  28.3 14.9 %gather_fusion = bf16[32,2,32768]{2,0,1:T(8,128)(2,1)} fusion(bf16[2,16,32768]{2,1,0:T(8,128)(2,1)S(1)} %copy-done, s32[1024]{0:T(1024)S(1)} %get-tuple-element.23), kind=kCustom, calls=%fused_computation | custom fusion | bytes 8388736 | tf_op jit(solution)/shard_map/jit(_take)/gather | solution.py:64
  57.5 23.3 %fusion.25 = (f32[1024,1024]{1,0:T(8,128)}, f32[1024,1024]{1,0:T(8,128)}, f32[1024,1024]{1,0:T(8,128)}) fusion(s32[1024]{0:T(1024)S(1)} %get-tuple-element.24, s32[1024]{0:T(1024)S(1)} %get-tuple-element.25), kind=kLoop, calls=%fused_computation.57 | loop fusion | flops 41943040 | bytes 12591104 | tf_op jit(solution)/shard_map/neg | solution.py:34
  80.8 65.8 %fusion.1 = f32[32,32,2048]{2,1,0:T(8,128)} fusion(f32[1024,1024]{1,0:T(8,128)} %get-tuple-element.15, f32[1024,1024]{1,0:T(8,128)} %get-tuple-element.14, f32[1024,1024]{1,0:T(8,128)} %get-tuple-element.13, f32[32,32,1024]{2,1,0:T(8,128)} %bitcast.100, f32[32,32,1024]{2,1,0:T(8,128)} %bitcast.99), kind=kOutput, calls=%fused_computation.8 | convolution fusion | flops 51554287616 | bytes 29360128 | tf_op jit(solution)/shard_map/dot_general | solution.py:49
  146.6 15.6 %convolution_bitcast_fusion.1 = f32[32,32,2048]{2,1,0:T(8,128)} fusion(f32[32,32,2048]{2,1,0:T(8,128)} %fusion.1), kind=kOutput, calls=%fused_computation.39 | convolution fusion | flops 805320704 | bytes 16777216 | tf_op jit(solution)/shard_map/kr,prx->pkx/dot_general | solution.py:57
  162.2 13.6 %convolution_bitcast_fusion.2 = f32[32,32,2048]{2,1,0:T(8,128)} fusion(f32[32,32,2048]{2,1,0:T(8,128)S(1)} %copy-done.3), kind=kOutput, calls=%fused_computation.40 | convolution fusion | flops 805320704 | bytes 16777216 | tf_op jit(solution)/shard_map/kr,prx->pkx/dot_general | solution.py:56
  175.8 12.1 %slice_add_fusion = (f32[32,32,1024]{2,1,0:T(8,128)}, f32[32,32,1024]{2,1,0:T(8,128)}) fusion(f32[32,32,2048]{2,1,0:T(8,128)} %convolution_bitcast_fusion.1, f32[32,32,2048]{2,1,0:T(8,128)} %convolution_bitcast_fusion.2), kind=kLoop, calls=%fused_computation.49 | loop fusion | flops 2097152 | bytes 25165824 | tf_op jit(solution)/shard_map/add | solution.py:58
  205.2 37.2 %copy.29 = f32[2,32,32768]{1,0,2:T(2,128)} copy(f32[2,32,32768]{2,1,0:T(8,128)} %maximum_multiply_fusion) | data formatting | bytes 16777216 | tf_op jit(solution)/shard_map/mul | solution.py:70
  242.4 265.9 %gather_fusion.2 = f32[16384,2,32]{2,1,0:T(2,128)} fusion(f32[2,32,32768]{1,0,2:T(2,128)} %copy.29, s32[16384]{0:T(1024)S(1)} %fusion.26), kind=kCustom, calls=%fused_computation.2 | custom fusion | bytes 8454144 | tf_op jit(solution)/shard_map/jit(_take)/gather | solution.py:107
  508.3 59.1 %fusion.59 = bf16[16384,2,32]{2,1,0:T(2,128)(2,1)} fusion(f32[16384,2,32]{2,1,0:T(2,128)} %gather_fusion.2, pred[16384]{0:T(1024)(128)(4,1)S(1)} %compare_and_fusion), kind=kLoop, calls=%fused_computation.111 | loop fusion | flops 1048576 | bytes 6307840
  567.4 10.1 reshape.154
  577.6 55.6 %all_to_all.36 = bf16[8,2,65536]{2,1,0:T(2,128)(2,1)} all-to-all(bf16[8,2,65536]{2,1,0:T(2,128)(2,1)S(1)} %reshape.154), channel_id=1, replica_groups=mesh['row'=4,'col'=8] {'col'}, dimensions={0} | all-to-all | bytes 4194304 | tf_op jit(solution)/shard_map/all_to_all | solution.py:111
  633.2 8.6 reshape.155
  641.8 19.7 %copy.31 = bf16[2,32,8,2048]{3,1,2,0:T(8,128)(2,1)} copy(bf16[2,32,8,2048]{1,0,3,2:T(2,128)(2,1)} %bitcast.89) | data formatting | bytes 4194304 | tf_op jit(solution)/shard_map/all_to_all | solution.py:111
  661.8 59.5 %fusion.60 = bf16[16384,2,32]{2,1,0:T(2,128)(2,1)} fusion(f32[16384,2,32]{2,1,0:T(2,128)} %gather_fusion.2, pred[16384]{0:T(1024)(128)(4,1)S(1)} %compare_and_fusion, f32[32]{0:T(128)S(1)} %multiply_divide_fusion), kind=kLoop, calls=%fused_computation.112 | loop fusion | flops 3145728 | bytes 6307968
  721.4 9.7 reshape.152
  731.1 28.9 %all_to_all.37 = bf16[4,2,131072]{2,1,0:T(2,128)(2,1)} all-to-all(bf16[4,2,131072]{2,1,0:T(2,128)(2,1)S(1)} %reshape.152), channel_id=1, replica_groups=mesh['row'=4,'col'=8] {'row'}, dimensions={0} | all-to-all | bytes 4194304 | tf_op jit(solution)/shard_map/all_to_all | solution.py:110
  767.4 18.0 %copy.30 = bf16[2,4,32,4096]{3,2,1,0:T(8,128)(2,1)} copy(bf16[2,4,32,4096]{2,0,3,1:T(2,128)(2,1)} %bitcast.90) | data formatting | bytes 4194304 | tf_op jit(solution)/shard_map/all_to_all | solution.py:110
  791.7 219.6 %all-gather.3.cloned.1.call-done = bf16[2,1024,4096]{2,1,0:T(8,128)(2,1)} async-done(((bf16[2,128,4096]{2,1,0:T(8,128)(2,1)}), bf16[2,1024,4096]{2,1,0:T(8,128)(2,1)}) %all-gather.3.cloned.1.call-update) | async-done | bytes 16777232 | tf_op jit(solution)/shard_map/all_gather | solution.py:112
  1011.3 11.9 %fusion.57 = (bf16[1,1024,4096]{2,1,0:T(8,128)(2,1)}, bf16[1,1024,4096]{2,1,0:T(8,128)(2,1)}) fusion(bf16[2,1024,4096]{2,1,0:T(8,128)(2,1)} %all-gather.3.cloned.1.call-done), kind=kLoop, calls=%fused_computation.109 | loop fusion | bytes 33554432 | tf_op jit(solution)/shard_map/slice | solution.py:97
  1023.2 24.9 %fusion.21 = f32[4096,2048,1,1]{1,0,3,2:T(8,128)} fusion(bf16[8,4,32,4096]{3,2,1,0:T(8,128)(2,1)} %bitcast.98, bf16[4,8,32,2048]{3,2,1,0:T(8,128)(2,1)S(1)} %bitcast.102), kind=kOutput, calls=%fused_computation.51 | convolution fusion | flops 17179869184 | bytes 46137344 | tf_op jit(solution)/shard_map/dot_general | solution.py:95
  1048.1 41.4 %convolution_bitcast_fusion = f32[1,4096,2048]{2,1,0:T(8,128)} fusion(bf16[2,8,4,32,4096]{4,3,2,1,0:T(8,128)(2,1)} %bitcast.91, bf16[2,4,8,32,2048]{4,3,2,1,0:T(8,128)(2,1)S(1)} %bitcast.96), kind=kOutput, calls=%fused_computation.6 | convolution fusion | flops 34359738368 | bytes 58720256 | tf_op jit(solution)/shard_map/dot_general | solution.py:88
  1089.5 35.9 %fusion = f32[1,4096,2048]{2,1,0:T(8,128)} fusion(f32[4096,2048,1,1]{1,0,3,2:T(8,128)} %fusion.21, bf16[8,4,32,4096]{3,2,1,0:T(8,128)(2,1)} %bitcast.97, bf16[4,8,32,2048]{3,2,1,0:T(8,128)(2,1)} %bitcast.101), kind=kOutput, calls=%fused_computation.5 | convolution fusion | flops 17188257792 | bytes 79691776 | tf_op jit(solution)/shard_map/dot_general | solution.py:97
  1125.4 43.8 %pad_maximum_fusion = f32[2,4096,2048]{2,1,0:T(8,128)} fusion(f32[1,4096,2048]{2,1,0:T(8,128)} %fusion, f32[1,4096,2048]{2,1,0:T(8,128)} %convolution_bitcast_fusion), kind=kLoop, calls=%fused_computation.3 | loop fusion | flops 16777216 | bytes 134217728 | tf_op jit(solution)/shard_map/stack | solution.py:98
  (40 shorter events, 55.1 us)
Async XLA Ops:
  6.5 21.7 %copy-start = (bf16[2,16,32768]{2,1,0:T(8,128)(2,1)S(1)}, bf16[2,16,32768]{2,1,0:T(8,128)(2,1)}, u32[]{:S(2)}) copy-start(bf16[2,16,32768]{2,1,0:T(8,128)(2,1)} %param.6) | copy-start | bytes 6291460
  6.5 778.9 %all-gather.5.cloned.1.call-start = ((), (), s32[]{:S(2)}) async-start(), calls=%async_computation.3 | async-start | bytes 10485760 | tf_op jit(solution)/shard_map/all_gather | solution.py:113
  43.2 4.6 copy-start.2
  146.6 15.6 %copy-start.3 = (f32[32,32,2048]{2,1,0:T(8,128)S(1)}, f32[32,32,2048]{2,1,0:T(8,128)}, u32[]{:S(2)}) copy-start(f32[32,32,2048]{2,1,0:T(8,128)} %fusion.1) | copy-start | bytes 25165828
  641.8 19.8 %copy-start.6 = (f32[128]{0:T(128)S(1)}, f32[128]{0:T(128)}, u32[]{:S(2)}) copy-start(f32[128]{0:T(128)} %param.9) | copy-start | bytes 1540
  641.8 19.9 %copy-start.7 = (f32[16]{0:T(128)S(1)}, f32[16]{0:T(128)}, u32[]{:S(2)}) copy-start(f32[16]{0:T(128)} %param.8) | copy-start | bytes 196
  661.5 349.8 %all-gather.3.cloned.1.call-start = ((), (), s32[]{:S(2)}) async-start(), calls=%async_computation.2 | async-start | bytes 18874368 | tf_op jit(solution)/shard_map/all_gather | solution.py:112
  1011.3 11.9 %copy-start.5 = (bf16[1,1024,2048]{2,1,0:T(8,128)(2,1)S(1)}, bf16[1,1024,2048]{2,1,0:T(8,128)(2,1)}, u32[]{:S(2)}) copy-start(bf16[1,1024,2048]{2,1,0:T(8,128)(2,1)} %get-tuple-element.12) | copy-start | bytes 12582916
  1023.2 24.9 %copy-start.4 = (bf16[2,1024,2048]{2,1,0:T(8,128)(2,1)S(1)}, bf16[2,1024,2048]{2,1,0:T(8,128)(2,1)}, u32[]{:S(2)}) copy-start(bf16[2,1024,2048]{2,1,0:T(8,128)(2,1)} %all-gather.5.cloned.1.call-done) | copy-start | bytes 25165828
  1125.4 43.8 %copy-start.1 = (bf16[2,16,32768]{2,1,0:T(8,128)(2,1)S(1)}, bf16[2,16,32768]{2,1,0:T(8,128)(2,1)}, u32[]{:S(2)}) copy-start(bf16[2,16,32768]{2,1,0:T(8,128)(2,1)} %param.6) | copy-start | bytes 6291460
Sparse Core Ops, SparseCore 0:
  661.6 57.1 all-gather.4
  785.6 225.7 all-gather.2
where the time goes:
time: 1200 us; the launch traced here: 1180 us
  local copies, waits for them, and re-layouts  442 us (37%)
  waiting for transfers between devices  220 us (18%)
  other arithmetic  219 us (18%)
  matrix products  197 us (16%)
  blocking collectives  84.5 us (7%)
  between operations  13.7 us (1%)
    gather x1, local copies, waits for them, and re-layouts, body(): selected = jnp.take(spectrum, grid_index, axis=2)  266 us
    all_gather x1, waiting for transfers between devices, body(): weighted_all = lax.all_gather(weighted_block, 'col', axis=1, tiled=True)  220 us
    unnamed x2, other arithmetic  119 us
    dot_general x1, matrix products, transform(): jnp.dot(stacked.reshape(pair_count * N1, 2 * plane_size), plane_table(),...  65.8 us
    all_to_all x1, blocking collectives, body(): lax.all_to_all(density, 'col', split_axis=2, concat_axis=1, tiled=True)  55.6 us
    unnamed x22, local copies, waits for them, and re-layouts  46.3 us
    another operation x1, other arithmetic, contract(): return jnp.stack([real_part, imag_part])  43.8 us
    dot_general x1, matrix products, contract(): lax.dot_general(weighted_part, operand, ((full_left, full_right), ((), ()...  41.4 us
  transfers between devices with their start and end apart: 2, of which 1 were waited for; matrix products, arithmetic and copies ran while one was open for 9% of the time, Pallas kernels for 0%

commit v1 on v0

v1 whole, which is shorter than its diff:
```python
import math

import jax
import jax.numpy as jnp
import ml_dtypes
import numpy as np
from jax import lax
from jax.experimental import pallas as pl
from jax.experimental.pallas import tpu as pltpu
from jax.sharding import PartitionSpec as P

N1 = 32
N2 = 32
N3 = 32
NR = N1 * N2 * N3
LANES = 128
HI = N2 * N3 // LANES
LO = N2 // HI
ROWS = N1 * HI
VMEM_LIMIT = 58 * 1024 * 1024
CHUNKS = (2, 2, 2, 1, 1)


def split_bf16(values):
    high = values.astype(ml_dtypes.bfloat16)
    low = (values - high.astype(np.float64)).astype(ml_dtypes.bfloat16)
    return high, low


def dft_tables():
    row = np.arange(ROWS)
    left = np.exp(
        -2j
        * np.pi
        * (
            (row[:, None] // HI) * (row[None, :] // HI) / N1
            + (row[:, None] % HI) * (row[None, :] % HI) / HI
        )
    )
    lane = np.arange(LANES)
    right = np.exp(
        -2j
        * np.pi
        * (
            (lane[:, None] // N3) * (lane[None, :] // N3) / LO
            + (lane[:, None] % N3) * (lane[None, :] % N3) / N3
        )
    )
    twiddle = np.exp(-2j * np.pi * (row[:, None] % HI) * (lane[None, :] // N3) / N2)
    twiddle = twiddle / math.sqrt(NR)
    left_high, left_low = split_bf16(np.concatenate([left.real, left.imag], axis=0))
    right_full = np.concatenate(
        [
            np.concatenate([right.real, right.imag], axis=1),
            np.concatenate([-right.imag, right.real], axis=1),
        ],
        axis=0,
    )
    right_high, right_low = split_bf16(right_full)
    return (
        np.concatenate([left_high, left_low], axis=0),
        right_high,
        right_low,
        np.stack([twiddle.real, twiddle.imag]).astype(np.float32),
    )


def table_position(grid_index):
    first = grid_index // (N2 * N3)
    second = grid_index // N3 % N2
    third = grid_index % N3
    return (first * HI + second % HI) * LANES + second // HI * N3 + third


def halves(value):
    high = value.astype(jnp.bfloat16)
    low = (value - high.astype(jnp.float32)).astype(jnp.bfloat16)
    return high, low


def dot(a, b):
    return jnp.dot(a, b, preferred_element_type=jnp.float32)


def transform_kernel(
    pairs,
    load_steps,
    step_rows,
    out_rows,
    hot_c_ref,
    hot_v_ref,
    cond_ref,
    val_ref,
    left_ref,
    right_high_ref,
    right_low_ref,
    twiddle_ref,
    out_ref,
    rho_r,
    rho_i,
    spec,
):
    step = pl.program_id(0)
    features = 2 * pairs

    @pl.when(step < load_steps)
    def _():
        cond = dot(hot_c_ref[...], cond_ref[...])
        val = dot(hot_v_ref[...], val_ref[...])
        cr, ci = cond[:pairs], cond[pairs:]
        vr, vi = val[:pairs], val[pairs:]
        real = vr * cr + vi * ci
        imag = vr * ci - vi * cr
        for a in range(step_rows):
            row = pl.multiple_of((step * step_rows + a) * pairs, pairs)
            rho_r[pl.ds(row, pairs), :] = real[:, a * LANES : (a + 1) * LANES]
            rho_i[pl.ds(row, pairs), :] = imag[:, a * LANES : (a + 1) * LANES]

    @pl.when(step == load_steps)
    def _():
        def one_pair(p, carry):
            data = jnp.concatenate(
                [
                    rho_r[pl.ds(p, ROWS, stride=pairs), :],
                    rho_i[pl.ds(p, ROWS, stride=pairs), :],
                ],
                axis=1,
            )
            high, low = halves(data)
            by_high = dot(left_ref[...], high)
            by_low = dot(left_ref[0 : 2 * ROWS, :], low)
            mixed = by_high[: 2 * ROWS] + (by_high[2 * ROWS :] + by_low)
            mid_r = mixed[:ROWS, :LANES] - mixed[ROWS:, LANES:]
            mid_i = mixed[:ROWS, LANES:] + mixed[ROWS:, :LANES]
            tr, ti = twiddle_ref[0], twiddle_ref[1]
            turned = jnp.concatenate([mid_r * tr - mid_i * ti, mid_r * ti + mid_i * tr], axis=1)
            high, low = halves(turned)
            out = dot(high, right_high_ref[...]) + (
                dot(low, right_high_ref[...]) + dot(high, right_low_ref[...])
            )
            spec[pl.ds(p, ROWS, stride=features), :] = out[:, :LANES]
            spec[pl.ds(pairs + p, ROWS, stride=features), :] = out[:, LANES:]
            return carry

        lax.fori_loop(0, pairs, one_pair, 0, unroll=2)

    @pl.when(step >= load_steps)
    def _():
        block = step - load_steps

        def one_row(k, carry):
            start = pl.multiple_of((block * out_rows + k) * features, features)
            tile = spec[pl.ds(start, features), :]
            tile = jnp.concatenate([tile] * (LANES // features), axis=0)
            out_ref[pl.ds(pl.multiple_of(k * LANES, LANES), LANES), :] = tile.T
            return carry

        lax.fori_loop(0, out_rows, one_row, 0, unroll=4)


def transform(valence, conduction, band_pairs):
    pairs = band_pairs.shape[0]
    nvb, ncb = valence.shape[1], conduction.shape[1]
    load_steps, out_steps = 8, 8
    step_rows = ROWS // load_steps
    out_rows = ROWS // out_steps
    chunk = step_rows * LANES

    def hot(band, count):
        one = (band[:, None] == jnp.arange(count, dtype=jnp.int32)[None, :]).astype(jnp.bfloat16)
        return jnp.kron(jnp.eye(2, dtype=jnp.bfloat16), one)

    left, right_high, right_low, twiddle = dft_tables()
    whole = lambda shape: pl.BlockSpec(shape, lambda i: (0,) * len(shape))
    loaded = lambda i: (0, jnp.minimum(i, load_steps - 1))
    flops = 2 * pairs * (6 * ROWS * ROWS * 2 * LANES + 3 * ROWS * 4 * LANES * LANES)
    return pl.pallas_call(
        lambda *refs: transform_kernel(pairs, load_steps, step_rows, out_rows, *refs),
        grid=(load_steps + out_steps,),
        in_specs=[
            whole((2 * pairs, 2 * ncb)),
            whole((2 * pairs, 2 * nvb)),
            pl.BlockSpec((2 * ncb, chunk), loaded),
            pl.BlockSpec((2 * nvb, chunk), loaded),
            whole(left.shape),
            whole(right_high.shape),
            whole(right_low.shape),
            whole(twiddle.shape),
        ],
        out_specs=pl.BlockSpec(
            (out_rows * LANES, LANES), lambda i: (jnp.maximum(i - load_steps, 0), 0)
        ),
        out_shape=jax.ShapeDtypeStruct((NR, LANES), jnp.float32),
        scratch_shapes=[
            pltpu.VMEM((ROWS * pairs, LANES), jnp.float32),
            pltpu.VMEM((ROWS * pairs, LANES), jnp.float32),
            pltpu.VMEM((ROWS * 2 * pairs, LANES), jnp.float32),
        ],
        compiler_params=pltpu.CompilerParams(vmem_limit_bytes=VMEM_LIMIT),
        cost_estimate=pl.CostEstimate(flops=flops, bytes_accessed=40_000_000, transcendentals=0),
        name="transform",
    )(
        hot(band_pairs[:, 1], ncb),
        hot(band_pairs[:, 0], nvb),
        conduction.reshape(2 * ncb, NR),
        valence.reshape(2 * nvb, NR),
        jnp.asarray(left),
        jnp.asarray(right_high),
        jnp.asarray(right_low),
        jnp.asarray(twiddle),
    )


def select_kernel(row_count, features, count, position_ref, me_ref, table_ref, *rest):
    outs, rows = rest[:row_count], rest[row_count]
    pack = LANES // features
    part = count // pack
    lane = lax.broadcasted_iota(jnp.int32, (part, LANES), 1)
    unroll = 32
    for s in range(row_count):
        base = (me_ref[0] ^ s) * count

        def some_rows(step, carry):
            start = step * unroll
            for j in range(unroll):
                index = position_ref[base + start + j]
                rows[pl.ds(start + j, 1), :] = table_ref[pl.ds(index, 1), :]
            return carry

        lax.fori_loop(0, count // unroll, some_rows, 0)
        packed = rows[0:part, :]
        for k in range(1, pack):
            packed = jnp.where(lane >= k * features, rows[k * part : (k + 1) * part, :], packed)
        outs[s][...] = packed.astype(jnp.bfloat16)


def select(table, position, me, row_count, features):
    count = position.shape[0] // row_count
    pack = LANES // features
    shape = (count // pack, LANES)
    return pl.pallas_call(
        lambda *refs: select_kernel(row_count, features, count, *refs),
        grid_spec=pltpu.PrefetchScalarGridSpec(
            num_scalar_prefetch=2,
            grid=(),
            in_specs=[pl.BlockSpec(memory_space=pltpu.VMEM)],
            out_specs=[pl.BlockSpec(memory_space=pltpu.VMEM)] * row_count,
            scratch_shapes=[pltpu.VMEM((count, LANES), jnp.float32)],
        ),
        out_shape=[jax.ShapeDtypeStruct(shape, jnp.bfloat16)] * row_count,
        compiler_params=pltpu.CompilerParams(vmem_limit_bytes=VMEM_LIMIT),
        cost_estimate=pl.CostEstimate(flops=0, bytes_accessed=20_000_000, transcendentals=0),
        name="select",
    )(position, me, table)


def assemble_kernel(row_count, features, me_ref, *rest):
    parts, out_ref, held = rest[:row_count], rest[row_count], rest[row_count + 1]
    pack = LANES // features
    part = parts[0].shape[0]
    lane = lax.broadcasted_iota(jnp.int32, (part, LANES), 1)
    for s in range(row_count):
        held[s] = parts[s][...].astype(jnp.float32)
    for b in range(row_count // pack):
        for k in range(pack):
            block = None
            for q in range(pack):
                piece = held[(b * pack + q) ^ me_ref[0]]
                if q != k:
                    piece = pltpu.roll(piece, (q - k) * features % LANES, 1)
                block = piece if block is None else jnp.where(lane >= q * features, piece, block)
            out_ref[k * part : (k + 1) * part, b * LANES : (b + 1) * LANES] = block.astype(
                jnp.bfloat16
            )


def assemble(parts, me, features):
    row_count = len(parts)
    pack = LANES // features
    part = parts[0].shape[0]
    return pl.pallas_call(
        lambda *refs: assemble_kernel(row_count, features, *refs),
        grid_spec=pltpu.PrefetchScalarGridSpec(
            num_scalar_prefetch=1,
            grid=(),
            in_specs=[pl.BlockSpec(memory_space=pltpu.VMEM)] * row_count,
            out_specs=pl.BlockSpec(memory_space=pltpu.VMEM),
            scratch_shapes=[pltpu.VMEM((row_count, part, LANES), jnp.float32)],
        ),
        out_shape=jax.ShapeDtypeStruct((part * pack, row_count * features), jnp.bfloat16),
        compiler_params=pltpu.CompilerParams(vmem_limit_bytes=VMEM_LIMIT),
        cost_estimate=pl.CostEstimate(flops=0, bytes_accessed=2_000_000, transcendentals=0),
        name="assemble",
    )(me, *parts)


def flip_kernel(slot_count, part_ref, *rest):
    slots, out_ref = rest[:slot_count], rest[slot_count]
    width = slots[0].shape[1]
    for s in range(slot_count):
        out_ref[s * width : (s + 1) * width, :] = (
            slots[s][...].astype(jnp.float32).T.astype(jnp.bfloat16)
        )


def flip(slots, part, depth):
    slot_count = len(slots)
    width = slots[0].shape[1]
    tile = min(256, depth)
    steps = depth // tile
    pick = lambda t, part_ref: (part_ref[0] * steps + t, 0)
    return pl.pallas_call(
        lambda *refs: flip_kernel(slot_count, *refs),
        grid_spec=pltpu.PrefetchScalarGridSpec(
            num_scalar_prefetch=1,
            grid=(steps,),
            in_specs=[pl.BlockSpec((tile, width), pick)] * slot_count,
            out_specs=pl.BlockSpec((slot_count * width, tile), lambda t, part_ref: (0, t)),
        ),
        out_shape=jax.ShapeDtypeStruct((slot_count * width, depth), jnp.bfloat16),
        compiler_params=pltpu.CompilerParams(vmem_limit_bytes=VMEM_LIMIT),
        cost_estimate=pl.CostEstimate(
            flops=0, bytes_accessed=8 * slot_count * width * depth, transcendentals=0
        ),
        name="flip",
    )(part, *slots)


def contract_kernel(slot_count, pairs, aliased, *refs):
    slots = refs[:slot_count]
    weight_ref, column_ref = refs[slot_count : slot_count + 2]
    out_ref, weighted, crossed = refs[slot_count + 2 + aliased :]
    width = slots[0].shape[1]

    @pl.when(pl.program_id(0) == 0)
    def _():
        for s in range(slot_count):
            rows = slice(s * width, (s + 1) * width)
            values = column_ref[rows, :].astype(jnp.float32)
            values = values.reshape(width // (2 * pairs), 2, pairs, values.shape[1])
            turned = jnp.stack([values[:, 1], -values[:, 0]], axis=1)
            crossed[rows, :] = turned.reshape(width, values.shape[3]).astype(jnp.bfloat16)

    for s in range(slot_count):
        weighted[:, s * width : (s + 1) * width] = (
            slots[s][...].astype(jnp.float32) * weight_ref[s : s + 1, :]
        ).astype(jnp.bfloat16)
    out_ref[0, 0] = dot(weighted[...], column_ref[...])
    out_ref[1, 0] = dot(weighted[...], crossed[...])


def contract(result, slots, weights, column, pairs, parts, block, row_start, column_start):
    slot_count = len(slots)
    width = slots[0].shape[1]
    depth = slots[0].shape[0] // parts
    across = column.shape[1]
    shape = (2, parts, block, block)
    aliased = 0 if result is None else 1
    place = (row_start // depth, column_start // across)
    whole = lambda shape: pl.BlockSpec(shape, lambda h: (0, 0))
    return pl.pallas_call(
        lambda *refs: contract_kernel(slot_count, pairs, aliased, *refs),
        grid=(parts,),
        in_specs=[pl.BlockSpec((depth, width), lambda h: (h, 0))] * slot_count
        + [whole(weights.shape), whole(column.shape)]
        + [pl.BlockSpec(memory_space=pl.ANY)] * aliased,
        out_specs=pl.BlockSpec((2, 1, depth, across), lambda h: (0, h) + place),
        out_shape=jax.ShapeDtypeStruct(shape, jnp.float32),
        scratch_shapes=[
            pltpu.VMEM((depth, slot_count * width), jnp.bfloat16),
            pltpu.VMEM(column.shape, jnp.bfloat16),
        ],
        input_output_aliases={slot_count + 2: 0} if aliased else {},
        compiler_params=pltpu.CompilerParams(vmem_limit_bytes=VMEM_LIMIT),
        cost_estimate=pl.CostEstimate(
            flops=4 * parts * depth * across * slot_count * width,
            bytes_accessed=8 * parts * depth * across + 2 * parts * depth * slot_count * width,
            transcendentals=0,
        ),
        name="contract",
    )(*slots, weights, column, *([result] if aliased else []))


def pair_weights(valence_energy, conduction_energy, band_pairs):
    valence_hot = (
        band_pairs[:, 0][:, None] == jnp.arange(valence_energy.shape[0], dtype=jnp.int32)[None, :]
    )
    conduction_hot = (
        band_pairs[:, 1][:, None]
        == jnp.arange(conduction_energy.shape[0], dtype=jnp.int32)[None, :]
    )
    energy_gap = jnp.sum(jnp.where(valence_hot, valence_energy[None, :], 0.0), axis=1) - jnp.sum(
        jnp.where(conduction_hot, conduction_energy[None, :], 0.0), axis=1
    )
    return energy_gap


def body(valence, conduction, valence_energy, conduction_energy, band_pairs, grid_index):
    rows, cols = lax.axis_size("row"), lax.axis_size("col")
    row, col = lax.axis_index("row"), lax.axis_index("col")
    pairs = band_pairs.shape[0]
    features = 2 * pairs
    total = grid_index.shape[0]
    block = total // cols
    parts = cols // rows
    me = row.astype(jnp.int32).reshape(1)
    my_part = (col % parts).astype(jnp.int32).reshape(1)
    owner = col // parts

    order = list(range(0, cols, 2)) + list(range(1, cols, 2))[::-1]
    ring_up = [(order[q], order[(q + 1) % cols]) for q in range(cols)]
    ring_down = [(b, a) for a, b in ring_up]
    place = np.argsort(np.array(order))
    my_place = jnp.asarray(place, jnp.int32)[col]
    half = cols // 2
    offsets = [0]
    for t in range(1, half):
        offsets += [-t, t]
    offsets.append(half)
    sources = jnp.asarray(np.array(order), jnp.int32)[
        (my_place + jnp.asarray(np.array(offsets), jnp.int32)) % cols
    ]

    gap = pair_weights(valence_energy, conduction_energy, band_pairs)
    weight = 2.0 / (math.sqrt(pairs * rows * cols) * gap)
    weights = lax.all_gather(weight, ("row", "col"), axis=0, tiled=True)
    weights = jnp.take(weights.reshape(rows, cols, pairs).transpose(1, 0, 2), sources, axis=0)
    weights = jnp.broadcast_to(weights[:, :, None, :], (cols, rows, 2, pairs))
    weights = weights.reshape(cols, rows * features)

    position = table_position(grid_index).reshape(rows, parts, block)
    table = transform(valence, conduction, band_pairs)

    unit = block // sum(CHUNKS)
    starts = [sum(CHUNKS[:i]) * unit for i in range(len(CHUNKS))]
    chunks, columns = [], []
    result = None
    for start, share in zip(starts, CHUNKS):
        depth = share * unit
        wanted = position[:, :, start : start + depth].reshape(-1)
        sent = select(table, wanted, me, rows, features)
        got = [sent[0]] + [
            lax.ppermute(sent[s], "row", [(r, r ^ s) for r in range(rows)])
            for s in range(1, rows)
        ]
        own = assemble(got, me, features)
        slots = [own]
        up = down = own
        for _ in range(1, half):
            up = lax.ppermute(up, "col", ring_up)
            down = lax.ppermute(down, "col", ring_down)
            slots += [up, down]
        cut = own.shape[0] // 2
        slots.append(
            jnp.concatenate(
                [
                    lax.ppermute(up[:cut], "col", ring_up),
                    lax.ppermute(down[cut:], "col", ring_down),
                ],
                axis=0,
            )
        )
        column = flip(slots, my_part, depth)
        holders = [0]
        step = rows // 2
        while step:
            perm = [
                ((c // parts ^ h) * cols + c, (c // parts ^ h ^ step) * cols + c)
                for c in range(cols)
                for h in holders
            ]
            arrived = lax.ppermute(column, ("row", "col"), perm)
            column = jnp.where((row ^ owner) & step != 0, arrived, column)
            holders += [h ^ step for h in holders]
            step //= 2
        i = len(chunks)
        chunks.append(slots)
        columns.append(column)
        tiles = [(i, j) for j in range(i)] + [(j, i) for j in range(i + 1)]
        for a, b in tiles:
            result = contract(
                result, chunks[a], weights, columns[b], pairs, parts, block, starts[a], starts[b]
            )
    return result.reshape(2, parts * block, block)


def solution(mesh):
    return jax.shard_map(
        body,
        mesh=mesh,
        in_specs=(P(), P(), P(), P(), P(("row", "col"), None), P()),
        out_specs=P(None, "row", "col"),
        check_vma=False,
    )
```

time: 1200 us -> 610 us (0.51); the launches traced: 1180 us -> 600 us
  local copies, waits for them, and re-layouts: 442 us -> 20.6 us
  Pallas kernels: 0 us -> 300 us
  other arithmetic: 219 us -> 10.7 us
  matrix products: 197 us -> 0 us
  starting transfers between devices: 0.04 us -> 93.2 us
  waiting for transfers between devices: 220 us -> 128 us
  blocking collectives: 84.5 us -> 47.3 us
  between operations: 13.7 us -> 0.86 us
    pallas_call x0 -> x41, Pallas kernels: none -> 300 us  [the longest x25 165 us: contract(): pl.pallas_call(lambda *refs: contract_kernel(slot_count, pairs, aliased,...]
    gather x3 -> x2, local copies, waits for them, and re-layouts: 293 us -> 1.81 us  [the longest x1 1.17 us: body(): jnp.take(weights.reshape(rows, cols, pairs).transpose(1, 0, 2), sources,...]
    all_gather x2 -> x0, waiting for transfers between devices: 220 us -> none  [the longest x1 220 us: body(): weighted_all = lax.all_gather(weighted_block, 'col', axis=1, tiled=True)]
    dot_general x6 -> x0, matrix products: 197 us -> none  [the longest x1 65.8 us: transform(): jnp.dot(stacked.reshape(pair_count * N1, 2 * plane_size), plane_table(),...]
    ppermute x0 -> x65, waiting for transfers between devices: none -> 128 us  [the longest x15 41.1 us: body(): up = lax.ppermute(up, 'col', ring_up)]
    unnamed x2 -> x1, other arithmetic: 119 us -> 0.09 us
    ppermute x0 -> x65, starting transfers between devices: none -> 93.2 us  [the longest x10 33.6 us: body(): arrived = lax.ppermute(column, ('row', 'col'), perm)]
    all_to_all x2 -> x0, blocking collectives: 84.5 us -> none  [the longest x1 55.6 us: body(): lax.all_to_all(density, 'col', split_axis=2, concat_axis=1, tiled=True)]
  transfers between devices with their start and end apart: 2 -> 65, of which waited for: 1 -> 23; matrix products, arithmetic and copies ran while one was open for 9% -> 4% of each run, Pallas kernels for 0% -> 11%
where the time goes in v1:
time: 610 us; the launch traced here: 600 us
  Pallas kernels  300 us (49%)
  waiting for transfers between devices  128 us (21%)
  starting transfers between devices  93.2 us (15%)
  blocking collectives  47.3 us (8%)
  local copies, waits for them, and re-layouts  20.6 us (3%)
  other arithmetic  10.7 us (2%)
    pallas_call x25, Pallas kernels, contract(): pl.pallas_call(lambda *refs: contract_kernel(slot_count, pairs, aliased,...  165 us
    pallas_call x1, Pallas kernels, transform(): pl.pallas_call(lambda *refs: transform_kernel(pairs, load_steps, step_row...  56.8 us
    pallas_call x5, Pallas kernels, select(): pl.pallas_call(lambda *refs: select_kernel(row_count, features, count, *r...  52.7 us
    unnamed x1, blocking collectives  47.3 us
    ppermute x15, waiting for transfers between devices, body(): up = lax.ppermute(up, 'col', ring_up)  41.1 us
    ppermute x10, waiting for transfers between devices, body(): arrived = lax.ppermute(column, ('row', 'col'), perm)  35.4 us
    ppermute x10, starting transfers between devices, body(): arrived = lax.ppermute(column, ('row', 'col'), perm)  33.6 us
    ppermute x15, waiting for transfers between devices, body(): down = lax.ppermute(down, 'col', ring_down)  28.6 us
  transfers between devices with their start and end apart: 65, of which 23 were waited for; matrix products, arithmetic and copies ran while one was open for 4% of the time, Pallas kernels for 11%

profile of v1, /device:TPU:0, one launch (start us, length us, event | category | flops | bytes accessed | tf_op | source)
XLA Modules:
  0.0 599.9 jit_solution(15526355269277403320)
XLA Ops:
  4.2 56.8 %transform.1.refs_2_ = f32[32768,128]{1,0:T(8,128)} custom-call(bf16[64,256]{1,0:T(8,128)(2,1)} %bitcast.41, bf16[64,32]{1,0:T(8,128)(2,1)} %copy.41.refs_1_, bf16[256,32768]{1,0:T(8,128)(2,1)} %bitcast.39, bf16[32,32768]{1,0:T(8,128)(2,1)} %bitcast.40, bf16[1024,256]{1,0:T(8,128)(2,1)} %constant.145.clone.refs_4_, ...), custom_call_target="tpu_custom_call" | custom-call | flops 9663676416 | bytes 40000000 | tf_op jit(solution)/shard_map/transform/pallas_call | solution.py:177
  61.0 9.2 %select.32 = (bf16[256,128]{1,0:T(8,128)(2,1)}, bf16[256,128]{1,0:T(8,128)(2,1)}, bf16[256,128]{1,0:T(8,128)(2,1)}, bf16[256,128]{1,0:T(8,128)(2,1)}) custom-call(s32[2048]{0:T(1024)} %bitcast.47, s32[1]{0:T(128)} %bitcast.refs_1_.refs_0_, f32[32768,128]{1,0:T(8,128)} %transform.1.refs_2_), custom_call_target="tpu_custom_call" | custom-call | bytes 20000000 | tf_op jit(solution)/shard_map/select/pallas_call | solution.py:241
  73.9 9.2 %select.31 = (bf16[256,128]{1,0:T(8,128)(2,1)}, bf16[256,128]{1,0:T(8,128)(2,1)}, bf16[256,128]{1,0:T(8,128)(2,1)}, bf16[256,128]{1,0:T(8,128)(2,1)}) custom-call(s32[2048]{0:T(1024)} %bitcast.48, s32[1]{0:T(128)} %bitcast.refs_1_.refs_0_, f32[32768,128]{1,0:T(8,128)} %transform.1.refs_2_), custom_call_target="tpu_custom_call" | custom-call | bytes 20000000 | tf_op jit(solution)/shard_map/select/pallas_call | solution.py:241
  85.7 11.3 %select.35 = (bf16[512,128]{1,0:T(8,128)(2,1)}, bf16[512,128]{1,0:T(8,128)(2,1)}, bf16[512,128]{1,0:T(8,128)(2,1)}, bf16[512,128]{1,0:T(8,128)(2,1)}) custom-call(s32[4096]{0:T(1024)} %bitcast.45, s32[1]{0:T(128)} %bitcast.refs_1_.refs_0_, f32[32768,128]{1,0:T(8,128)} %transform.1.refs_2_), custom_call_target="tpu_custom_call" | custom-call | bytes 20000000 | tf_op jit(solution)/shard_map/select/pallas_call | solution.py:241
  99.6 11.5 %select.34 = (bf16[512,128]{1,0:T(8,128)(2,1)}, bf16[512,128]{1,0:T(8,128)(2,1)}, bf16[512,128]{1,0:T(8,128)(2,1)}, bf16[512,128]{1,0:T(8,128)(2,1)}) custom-call(s32[4096]{0:T(1024)} %bitcast.46, s32[1]{0:T(128)} %bitcast.refs_1_.refs_0_, f32[32768,128]{1,0:T(8,128)} %transform.1.refs_2_), custom_call_target="tpu_custom_call" | custom-call | bytes 20000000 | tf_op jit(solution)/shard_map/select/pallas_call | solution.py:241
  116.3 11.5 %select.33 = (bf16[512,128]{1,0:T(8,128)(2,1)}, bf16[512,128]{1,0:T(8,128)(2,1)}, bf16[512,128]{1,0:T(8,128)(2,1)}, bf16[512,128]{1,0:T(8,128)(2,1)}) custom-call(s32[4096]{0:T(1024)} %bitcast.44, s32[1]{0:T(128)} %bitcast.refs_1_.refs_0_, f32[32768,128]{1,0:T(8,128)} %transform.1.refs_2_), custom_call_target="tpu_custom_call" | custom-call | bytes 20000000 | tf_op jit(solution)/shard_map/select/pallas_call | solution.py:241
  151.8 13.3 %collective-permute-done.6.refs_5_.refs_4_ = bf16[512,256]{1,0:T(8,128)(2,1)S(1)} collective-permute-done((bf16[512,256]{1,0:T(8,128)(2,1)S(1)}, bf16[512,256]{1,0:T(8,128)(2,1)S(1)}, u32[]{:S(2)}, u32[]{:S(2)}) %collective-permute-start.6) | collective-permute-done | bytes 262176 | tf_op jit(solution)/shard_map/ppermute | solution.py:451
  195.6 7.1 %collective-permute-done.49.refs_2_.refs_1_ = bf16[1024,256]{1,0:T(8,128)(2,1)} collective-permute-done((bf16[1024,256]{1,0:T(8,128)(2,1)}, bf16[1024,256]{1,0:T(8,128)(2,1)}, u32[]{:S(2)}, u32[]{:S(2)}) %collective-permute-start.49) | collective-permute-done | bytes 524320 | tf_op jit(solution)/shard_map/ppermute | solution.py:450
  205.5 14.1 %collective-permute-done.7.refs_6_.refs_5_ = bf16[512,256]{1,0:T(8,128)(2,1)} collective-permute-done((bf16[512,256]{1,0:T(8,128)(2,1)}, bf16[512,256]{1,0:T(8,128)(2,1)}, u32[]{:S(2)}, u32[]{:S(2)}) %collective-permute-start.7) | collective-permute-done | bytes 262176 | tf_op jit(solution)/shard_map/ppermute | solution.py:450
  230.0 9.3 %collective-permute-done.9 = bf16[256,256]{1,0:T(8,128)(2,1)} collective-permute-done((bf16[256,256]{1,0:T(8,128)(2,1)S(1)}, bf16[256,256]{1,0:T(8,128)(2,1)}, u32[]{:S(2)}, u32[]{:S(2)}) %collective-permute-start.9) | collective-permute-done | bytes 131104 | tf_op jit(solution)/shard_map/ppermute | solution.py:457
  292.5 15.9 %collective-permute-start.59 = (bf16[2048,512]{1,0:T(8,128)(2,1)}, bf16[2048,512]{1,0:T(8,128)(2,1)}, u32[]{:S(2)}, u32[]{:S(2)}) collective-permute-start(bf16[2048,512]{1,0:T(8,128)(2,1)} %flip.7), channel_id=1, source_target_pairs={{0,16},{1,17},{10,26},{11,27},{20,4},{21,5},{30,14},{31,15}} | collective-permute-start | bytes 6291464 | tf_op jit(solution)/shard_map/ppermute | solution.py:472
  308.4 47.3 %all-reduce = f32[1024]{0:T(1024)S(1)} all-reduce(f32[1024]{0:T(1024)S(1)} %divide_dynamic-update-slice_fusion), channel_id=1, replica_groups=mesh['row'=4,'col'=8] {'row','col'}, use_global_device_ids=true, to_apply=%add | all-reduce | flops 1024 | bytes 8192
  388.7 14.6 %collective-permute-done.61 = bf16[2048,512]{1,0:T(8,128)(2,1)S(1)} collective-permute-done((bf16[2048,512]{1,0:T(8,128)(2,1)}, bf16[2048,512]{1,0:T(8,128)(2,1)S(1)}, u32[]{:S(2)}, u32[]{:S(2)}) %collective-permute-start.61) | collective-permute-done | bytes 2097184 | tf_op jit(solution)/shard_map/ppermute | solution.py:472
  405.0 20.8 %collective-permute-done.63 = bf16[2048,512]{1,0:T(8,128)(2,1)S(1)} collective-permute-done((bf16[2048,512]{1,0:T(8,128)(2,1)}, bf16[2048,512]{1,0:T(8,128)(2,1)S(1)}, u32[]{:S(2)}, u32[]{:S(2)}) %collective-permute-start.63) | collective-permute-done | bytes 2097184 | tf_op jit(solution)/shard_map/ppermute | solution.py:472
  434.3 8.7 %contract.25.refs_10_ = f32[2,2,2048,2048]{3,2,1,0:T(8,128)} custom-call(bf16[1024,256]{1,0:T(8,128)(2,1)} %assemble.9.refs_1_.refs_0_, bf16[1024,256]{1,0:T(8,128)(2,1)} %collective-permute-done.49.refs_2_.refs_1_, bf16[1024,256]{1,0:T(8,128)(2,1)} %copy-done.15, bf16[1024,256]{1,0:T(8,128)(2,1)} %collective-permute-done.51.refs_4_.refs_3_, ...), custom_call_target="tpu_custom_call" | custom-call | flops 4294967296 | bytes 8388608 | tf_op jit(solution)/shard_map/contract/pallas_call | solution.py:361
  443.0 8.7 %contract.26.refs_10_ = f32[2,2,2048,2048]{3,2,1,0:T(8,128)} custom-call(bf16[1024,256]{1,0:T(8,128)(2,1)} %assemble.8.refs_1_.refs_0_, bf16[1024,256]{1,0:T(8,128)(2,1)} %copy-done.13, bf16[1024,256]{1,0:T(8,128)(2,1)} %copy-done.12, bf16[1024,256]{1,0:T(8,128)(2,1)} %collective-permute-done.40.refs_4_.refs_3_, ...), custom_call_target="tpu_custom_call", output_to_operand_aliasing={{}: (10, {})} | custom-call | flops 4294967296 | bytes 8388608 | tf_op jit(solution)/shard_map/contract/pallas_call | solution.py:361
  451.7 8.7 %contract.27.refs_10_ = f32[2,2,2048,2048]{3,2,1,0:T(8,128)} custom-call(bf16[1024,256]{1,0:T(8,128)(2,1)} %assemble.9.refs_1_.refs_0_, bf16[1024,256]{1,0:T(8,128)(2,1)} %collective-permute-done.49.refs_2_.refs_1_, bf16[1024,256]{1,0:T(8,128)(2,1)} %copy-done.15, ...), custom_call_target="tpu_custom_call", output_to_operand_aliasing={{}: (10, {})} | custom-call | flops 4294967296 | bytes 8388608 | tf_op jit(solution)/shard_map/contract/pallas_call | solution.py:361
  460.4 8.7 %contract.28.refs_10_ = f32[2,2,2048,2048]{3,2,1,0:T(8,128)} custom-call(bf16[1024,256]{1,0:T(8,128)(2,1)} %assemble.8.refs_1_.refs_0_, bf16[1024,256]{1,0:T(8,128)(2,1)} %copy-done.13, bf16[1024,256]{1,0:T(8,128)(2,1)} %copy-done.12, bf16[1024,256]{1,0:T(8,128)(2,1)} %collective-permute-done.40.refs_4_.refs_3_, ...), custom_call_target="tpu_custom_call", output_to_operand_aliasing={{}: (10, {})} | custom-call | flops 4294967296 | bytes 8388608 | tf_op jit(solution)/shard_map/contract/pallas_call | solution.py:361
  469.1 8.7 %contract.29.refs_10_ = f32[2,2,2048,2048]{3,2,1,0:T(8,128)} custom-call(bf16[1024,256]{1,0:T(8,128)(2,1)} %assemble.7.refs_1_.refs_0_, bf16[1024,256]{1,0:T(8,128)(2,1)} %copy-done.11, bf16[1024,256]{1,0:T(8,128)(2,1)} %copy-done.10, bf16[1024,256]{1,0:T(8,128)(2,1)} %copy-done.14, ...), custom_call_target="tpu_custom_call", output_to_operand_aliasing={{}: (10, {})} | custom-call | flops 4294967296 | bytes 8388608 | tf_op jit(solution)/shard_map/contract/pallas_call | solution.py:361
  477.9 8.7 %contract.30.refs_10_ = f32[2,2,2048,2048]{3,2,1,0:T(8,128)} custom-call(bf16[1024,256]{1,0:T(8,128)(2,1)} %assemble.7.refs_1_.refs_0_, bf16[1024,256]{1,0:T(8,128)(2,1)} %copy-done.11, bf16[1024,256]{1,0:T(8,128)(2,1)} %copy-done.10, bf16[1024,256]{1,0:T(8,128)(2,1)} %copy-done.14, ...), custom_call_target="tpu_custom_call", output_to_operand_aliasing={{}: (10, {})} | custom-call | flops 4294967296 | bytes 8388608 | tf_op jit(solution)/shard_map/contract/pallas_call | solution.py:361
  486.6 9.1 %contract.31.refs_10_ = f32[2,2,2048,2048]{3,2,1,0:T(8,128)} custom-call(bf16[1024,256]{1,0:T(8,128)(2,1)} %assemble.9.refs_1_.refs_0_, bf16[1024,256]{1,0:T(8,128)(2,1)} %collective-permute-done.49.refs_2_.refs_1_, bf16[1024,256]{1,0:T(8,128)(2,1)} %copy-done.15, ...), custom_call_target="tpu_custom_call", output_to_operand_aliasing={{}: (10, {})} | custom-call | flops 4294967296 | bytes 8388608 | tf_op jit(solution)/shard_map/contract/pallas_call | solution.py:361
  495.7 8.7 %contract.32.refs_10_ = f32[2,2,2048,2048]{3,2,1,0:T(8,128)} custom-call(bf16[1024,256]{1,0:T(8,128)(2,1)} %assemble.8.refs_1_.refs_0_, bf16[1024,256]{1,0:T(8,128)(2,1)} %copy-done.13, bf16[1024,256]{1,0:T(8,128)(2,1)} %copy-done.12, bf16[1024,256]{1,0:T(8,128)(2,1)} %collective-permute-done.40.refs_4_.refs_3_, ...), custom_call_target="tpu_custom_call", output_to_operand_aliasing={{}: (10, {})} | custom-call | flops 4294967296 | bytes 8388608 | tf_op jit(solution)/shard_map/contract/pallas_call | solution.py:361
  504.4 8.7 %contract.33.refs_10_ = f32[2,2,2048,2048]{3,2,1,0:T(8,128)} custom-call(bf16[1024,256]{1,0:T(8,128)(2,1)} %assemble.7.refs_1_.refs_0_, bf16[1024,256]{1,0:T(8,128)(2,1)} %copy-done.11, bf16[1024,256]{1,0:T(8,128)(2,1)} %copy-done.10, bf16[1024,256]{1,0:T(8,128)(2,1)} %copy-done.14, ...), custom_call_target="tpu_custom_call", output_to_operand_aliasing={{}: (10, {})} | custom-call | flops 4294967296 | bytes 8388608 | tf_op jit(solution)/shard_map/contract/pallas_call | solution.py:361
  542.2 5.9 contract.39.refs_10_
  (318 shorter events, 262.4 us)
Async XLA Ops:
  70.2 26.8 %collective-permute-start.13 = (bf16[256,128]{1,0:T(8,128)(2,1)}, bf16[256,128]{1,0:T(8,128)(2,1)S(1)}, u32[]{:S(2)}, u32[]{:S(2)}) collective-permute-start(bf16[256,128]{1,0:T(8,128)(2,1)} %get-tuple-element.30), channel_id=1, source_target_pairs={{0,8},{8,0},{16,24},{24,16},{1,9},{9,1},{17,25},{25,17},{2,10},{10... | collective-permute-start | bytes 196616 | tf_op jit(solution)/shard_map/ppermute | solution.py:443
  83.1 28.0 %collective-permute-start = (bf16[256,128]{1,0:T(8,128)(2,1)}, bf16[256,128]{1,0:T(8,128)(2,1)S(1)}, u32[]{:S(2)}, u32[]{:S(2)}) collective-permute-start(bf16[256,128]{1,0:T(8,128)(2,1)} %get-tuple-element.26), channel_id=1, source_target_pairs={{0,8},{8,0},{16,24},{24,16},{1,9},{9,1},{17,25},{25,17},{2,10},{10... | collective-permute-start | bytes 196616 | tf_op jit(solution)/shard_map/ppermute | solution.py:443
  83.2 28.3 %collective-permute-start.1 = (bf16[256,128]{1,0:T(8,128)(2,1)}, bf16[256,128]{1,0:T(8,128)(2,1)S(1)}, u32[]{:S(2)}, u32[]{:S(2)}) collective-permute-start(bf16[256,128]{1,0:T(8,128)(2,1)} %get-tuple-element.27), channel_id=1, source_target_pairs={{0,16},{8,24},{16,0},{24,8},{1,17},{9,25},{17,1},{25,9},{2,18},{10... | collective-permute-start | bytes 196616 | tf_op jit(solution)/shard_map/ppermute | solution.py:443
  97.0 30.8 %collective-permute-start.46 = (bf16[512,128]{1,0:T(8,128)(2,1)}, bf16[512,128]{1,0:T(8,128)(2,1)S(1)}, u32[]{:S(2)}, u32[]{:S(2)}) collective-permute-start(bf16[512,128]{1,0:T(8,128)(2,1)} %get-tuple-element.42), channel_id=1, source_target_pairs={{0,8},{8,0},{16,24},{24,16},{1,9},{9,1},{17,25},{25,17},{2,10},{10... | collective-permute-start | bytes 393224 | tf_op jit(solution)/shard_map/ppermute | solution.py:443
  97.1 32.8 %collective-permute-start.47 = (bf16[512,128]{1,0:T(8,128)(2,1)}, bf16[512,128]{1,0:T(8,128)(2,1)S(1)}, u32[]{:S(2)}, u32[]{:S(2)}) collective-permute-start(bf16[512,128]{1,0:T(8,128)(2,1)} %get-tuple-element.43), channel_id=1, source_target_pairs={{0,16},{8,24},{16,0},{24,8},{1,17},{9,25},{17,1},{25,9},{2,18},{10... | collective-permute-start | bytes 393224 | tf_op jit(solution)/shard_map/ppermute | solution.py:443
  97.4 34.4 %collective-permute-start.48 = (bf16[512,128]{1,0:T(8,128)(2,1)}, bf16[512,128]{1,0:T(8,128)(2,1)S(1)}, u32[]{:S(2)}, u32[]{:S(2)}) collective-permute-start(bf16[512,128]{1,0:T(8,128)(2,1)} %get-tuple-element.44), channel_id=1, source_target_pairs={{0,24},{8,16},{16,8},{24,0},{1,25},{9,17},{17,9},{25,1},{2,26},{10... | collective-permute-start | bytes 393224 | tf_op jit(solution)/shard_map/ppermute | solution.py:443
  144.6 30.2 %collective-permute-start.28 = (bf16[1024,256]{1,0:T(8,128)(2,1)}, bf16[1024,256]{1,0:T(8,128)(2,1)S(1)}, u32[]{:S(2)}, u32[]{:S(2)}) collective-permute-start(bf16[1024,256]{1,0:T(8,128)(2,1)} %assemble.7.refs_1_.refs_0_), channel_id=1, source_target_pairs={{2,0},{4,2},{6,4},{7,6},{5,7},{3,5},{1,3},{0,1},{10,8},{12,10},{14... | collective-permute-start | bytes 1572872 | tf_op jit(solution)/shard_map/ppermute | solution.py:451
  174.8 28.0 %collective-permute-start.49 = (bf16[1024,256]{1,0:T(8,128)(2,1)}, bf16[1024,256]{1,0:T(8,128)(2,1)}, u32[]{:S(2)}, u32[]{:S(2)}) collective-permute-start(bf16[1024,256]{1,0:T(8,128)(2,1)} %assemble.9.refs_1_.refs_0_), channel_id=1, source_target_pairs={{0,2},{2,4},{4,6},{6,7},{7,5},{5,3},{3,1},{1,0},{8,10},{10,12},{12... | collective-permute-start | bytes 1572872 | tf_op jit(solution)/shard_map/ppermute | solution.py:450
  184.0 42.8 %collective-permute-start.29 = (bf16[1024,256]{1,0:T(8,128)(2,1)S(1)}, bf16[1024,256]{1,0:T(8,128)(2,1)S(1)}, u32[]{:S(2)}, u32[]{:S(2)}) collective-permute-start(bf16[1024,256]{1,0:T(8,128)(2,1)S(1)} %collective-permute-done.27.refs_2_.refs_1_), channel_id=1, source_target_pairs={{0,2},{2,4},{4,6},{6,7},{7,5},{5,3},{3,1},{1,0},{8,10},{10,12},{12... | collective-permute-start | bytes 1572872 | tf_op jit(solution)/shard_map/ppermute | solution.py:450
  191.4 28.2 %collective-permute-start.7 = (bf16[512,256]{1,0:T(8,128)(2,1)}, bf16[512,256]{1,0:T(8,128)(2,1)}, u32[]{:S(2)}, u32[]{:S(2)}) collective-permute-start(bf16[512,256]{1,0:T(8,128)(2,1)} %collective-permute-done.5.refs_4_.refs_3_), channel_id=1, source_target_pairs={{0,2},{2,4},{4,6},{6,7},{7,5},{5,3},{3,1},{1,0},{8,10},{10,12},{12... | collective-permute-start | bytes 786440 | tf_op jit(solution)/shard_map/ppermute | solution.py:450
  195.2 44.7 %collective-permute-start.30 = (bf16[1024,256]{1,0:T(8,128)(2,1)S(1)}, bf16[1024,256]{1,0:T(8,128)(2,1)}, u32[]{:S(2)}, u32[]{:S(2)}) collective-permute-start(bf16[1024,256]{1,0:T(8,128)(2,1)S(1)} %collective-permute-done.28.refs_3_.refs_2_), channel_id=1, source_target_pairs={{2,0},{4,2},{6,4},{7,6},{5,7},{3,5},{1,3},{0,1},{10,8},{12,10},{14... | collective-permute-start | bytes 1572872 | tf_op jit(solution)/shard_map/ppermute | solution.py:451
  219.6 26.8 %collective-permute-start.40 = (bf16[1024,256]{1,0:T(8,128)(2,1)S(1)}, bf16[1024,256]{1,0:T(8,128)(2,1)}, u32[]{:S(2)}, u32[]{:S(2)}) collective-permute-start(bf16[1024,256]{1,0:T(8,128)(2,1)S(1)} %collective-permute-done.38.refs_2_.refs_1_), channel_id=1, source_target_pairs={{0,2},{2,4},{4,6},{6,7},{7,5},{5,3},{3,1},{1,0},{8,10},{10,12},{12... | collective-permute-start | bytes 1572872 | tf_op jit(solution)/shard_map/ppermute | solution.py:450
  252.7 39.8 %collective-permute-start.43 = (bf16[1024,256]{1,0:T(8,128)(2,1)}, bf16[1024,256]{1,0:T(8,128)(2,1)S(1)}, u32[]{:S(2)}, u32[]{:S(2)}) collective-permute-start(bf16[1024,256]{1,0:T(8,128)(2,1)} %collective-permute-done.41.refs_5_.refs_4_), channel_id=1, source_target_pairs={{2,0},{4,2},{6,4},{7,6},{5,7},{3,5},{1,3},{0,1},{10,8},{12,10},{14... | collective-permute-start | bytes 1572872 | tf_op jit(solution)/shard_map/ppermute | solution.py:451
  261.7 95.2 %collective-permute-start.53 = (bf16[1024,256]{1,0:T(8,128)(2,1)}, bf16[1024,256]{1,0:T(8,128)(2,1)S(1)}, u32[]{:S(2)}, u32[]{:S(2)}) collective-permute-start(bf16[1024,256]{1,0:T(8,128)(2,1)} %collective-permute-done.51.refs_4_.refs_3_), channel_id=1, source_target_pairs={{0,2},{2,4},{4,6},{6,7},{7,5},{5,3},{3,1},{1,0},{8,10},{10,12},{12... | collective-permute-start | bytes 1572872 | tf_op jit(solution)/shard_map/ppermute | solution.py:450
  272.9 86.4 %collective-permute-start.54 = (bf16[1024,256]{1,0:T(8,128)(2,1)}, bf16[1024,256]{1,0:T(8,128)(2,1)S(1)}, u32[]{:S(2)}, u32[]{:S(2)}) collective-permute-start(bf16[1024,256]{1,0:T(8,128)(2,1)} %collective-permute-done.52.refs_5_.refs_4_), channel_id=1, source_target_pairs={{2,0},{4,2},{6,4},{7,6},{5,7},{3,5},{1,3},{0,1},{10,8},{12,10},{14... | collective-permute-start | bytes 1572872 | tf_op jit(solution)/shard_map/ppermute | solution.py:451
  285.0 98.6 %collective-permute-start.11 = (bf16[2048,256]{1,0:T(8,128)(2,1)}, bf16[2048,256]{1,0:T(8,128)(2,1)}, u32[]{:S(2)}, u32[]{:S(2)}) collective-permute-start(bf16[2048,256]{1,0:T(8,128)(2,1)} %flip.5), channel_id=1, source_target_pairs={{0,16},{1,17},{10,26},{11,27},{20,4},{21,5},{30,14},{31,15}} | collective-permute-start | bytes 3145736 | tf_op jit(solution)/shard_map/ppermute | solution.py:472
  291.1 72.9 %collective-permute-start.44 = (bf16[512,256]{1,0:T(8,128)(2,1)S(1)}, bf16[512,256]{1,0:T(8,128)(2,1)S(1)}, u32[]{:S(2)}, u32[]{:S(2)}) collective-permute-start(bf16[512,256]{1,0:T(8,128)(2,1)S(1)} %slice.84), channel_id=1, source_target_pairs={{0,2},{2,4},{4,6},{6,7},{7,5},{5,3},{3,1},{1,0},{8,10},{10,12},{12... | collective-permute-start | bytes 786440 | tf_op jit(solution)/shard_map/ppermute | solution.py:457
  292.5 94.4 %collective-permute-start.59 = (bf16[2048,512]{1,0:T(8,128)(2,1)}, bf16[2048,512]{1,0:T(8,128)(2,1)}, u32[]{:S(2)}, u32[]{:S(2)}) collective-permute-start(bf16[2048,512]{1,0:T(8,128)(2,1)} %flip.7), channel_id=1, source_target_pairs={{0,16},{1,17},{10,26},{11,27},{20,4},{21,5},{30,14},{31,15}} | collective-permute-start | bytes 6291464 | tf_op jit(solution)/shard_map/ppermute | solution.py:472
  374.8 28.6 %collective-permute-start.61 = (bf16[2048,512]{1,0:T(8,128)(2,1)}, bf16[2048,512]{1,0:T(8,128)(2,1)S(1)}, u32[]{:S(2)}, u32[]{:S(2)}) collective-permute-start(bf16[2048,512]{1,0:T(8,128)(2,1)} %flip.8), channel_id=1, source_target_pairs={{0,16},{1,17},{10,26},{11,27},{20,4},{21,5},{30,14},{31,15}} | collective-permute-start | bytes 6291464 | tf_op jit(solution)/shard_map/ppermute | solution.py:472
  382.0 43.8 %collective-permute-start.63 = (bf16[2048,512]{1,0:T(8,128)(2,1)}, bf16[2048,512]{1,0:T(8,128)(2,1)S(1)}, u32[]{:S(2)}, u32[]{:S(2)}) collective-permute-start(bf16[2048,512]{1,0:T(8,128)(2,1)} %flip.9), channel_id=1, source_target_pairs={{0,16},{1,17},{10,26},{11,27},{20,4},{21,5},{30,14},{31,15}} | collective-permute-start | bytes 6291464 | tf_op jit(solution)/shard_map/ppermute | solution.py:472
  383.7 43.7 %collective-permute-start.12 = (bf16[2048,256]{1,0:T(8,128)(2,1)S(1)}, bf16[2048,256]{1,0:T(8,128)(2,1)S(1)}, u32[]{:S(2)}, u32[]{:S(2)}) collective-permute-start(bf16[2048,256]{1,0:T(8,128)(2,1)S(1)} %broadcast_select_fusion.7), channel_id=1, source_target_pairs={{0,8},{16,24},{1,9},{17,25},{10,2},{26,18},{11,3},{27,19},{20,28},... | collective-permute-start | bytes 3145736 | tf_op jit(solution)/shard_map/ppermute | solution.py:472
  385.4 43.2 %collective-permute-start.58 = (bf16[2048,256]{1,0:T(8,128)(2,1)S(1)}, bf16[2048,256]{1,0:T(8,128)(2,1)S(1)}, u32[]{:S(2)}, u32[]{:S(2)}) collective-permute-start(bf16[2048,256]{1,0:T(8,128)(2,1)S(1)} %broadcast_select_fusion.6), channel_id=1, source_target_pairs={{0,8},{16,24},{1,9},{17,25},{10,2},{26,18},{11,3},{27,19},{20,28},... | collective-permute-start | bytes 3145736 | tf_op jit(solution)/shard_map/ppermute | solution.py:472
  387.2 42.5 %collective-permute-start.60 = (bf16[2048,512]{1,0:T(8,128)(2,1)S(1)}, bf16[2048,512]{1,0:T(8,128)(2,1)S(1)}, u32[]{:S(2)}, u32[]{:S(2)}) collective-permute-start(bf16[2048,512]{1,0:T(8,128)(2,1)S(1)} %broadcast_select_fusion.2), channel_id=1, source_target_pairs={{0,8},{16,24},{1,9},{17,25},{10,2},{26,18},{11,3},{27,19},{20,28},... | collective-permute-start | bytes 6291464 | tf_op jit(solution)/shard_map/ppermute | solution.py:472
  403.5 27.7 %collective-permute-start.62 = (bf16[2048,512]{1,0:T(8,128)(2,1)S(1)}, bf16[2048,512]{1,0:T(8,128)(2,1)S(1)}, u32[]{:S(2)}, u32[]{:S(2)}) collective-permute-start(bf16[2048,512]{1,0:T(8,128)(2,1)S(1)} %broadcast_select_fusion.1), channel_id=1, source_target_pairs={{0,8},{16,24},{1,9},{17,25},{10,2},{26,18},{11,3},{27,19},{20,28},... | collective-permute-start | bytes 6291464 | tf_op jit(solution)/shard_map/ppermute | solution.py:472
  (93 other events, 2301.3 us)

commit v2 on v1

v2 whole, which is shorter than its diff:
```python
import math

import jax
import jax.numpy as jnp
import ml_dtypes
import numpy as np
from jax import lax
from jax.experimental import pallas as pl
from jax.experimental.pallas import tpu as pltpu
from jax.sharding import PartitionSpec as P

N1 = 32
N2 = 32
N3 = 32
NR = N1 * N2 * N3
LANES = 128
HI = N2 * N3 // LANES
LO = N2 // HI
ROWS = N1 * HI
VMEM_LIMIT = 58 * 1024 * 1024
CHUNKS = ((3, 1), (4, 4), (0, 3))
EIGHTHS = 8


def split_bf16(values):
    high = values.astype(ml_dtypes.bfloat16)
    low = (values - high.astype(np.float64)).astype(ml_dtypes.bfloat16)
    return high, low


def dft_tables():
    row = np.arange(ROWS)
    left = np.exp(
        -2j
        * np.pi
        * (
            (row[:, None] // HI) * (row[None, :] // HI) / N1
            + (row[:, None] % HI) * (row[None, :] % HI) / HI
        )
    )
    lane = np.arange(LANES)
    right = np.exp(
        -2j
        * np.pi
        * (
            (lane[:, None] // N3) * (lane[None, :] // N3) / LO
            + (lane[:, None] % N3) * (lane[None, :] % N3) / N3
        )
    )
    twiddle = np.exp(-2j * np.pi * (row[:, None] % HI) * (lane[None, :] // N3) / N2)
    twiddle = twiddle / math.sqrt(NR)
    left_full = np.block([[left.real, -left.imag], [left.imag, left.real]])
    right_full = np.block([[right.real, right.imag], [-right.imag, right.real]])
    left_high, left_low = split_bf16(left_full)
    right_high, right_low = split_bf16(right_full)
    twiddle = np.concatenate([twiddle, twiddle], axis=1)
    return (
        np.concatenate([left_high, left_low, left_high], axis=1),
        np.concatenate([right_high, right_high, right_low], axis=0),
        np.stack([twiddle.real, twiddle.imag]).astype(np.float32),
    )


def table_position(grid_index):
    first = grid_index // (N2 * N3)
    second = grid_index // N3 % N2
    third = grid_index % N3
    return (first * HI + second % HI) * LANES + second // HI * N3 + third


def halves(value):
    high = value.astype(jnp.bfloat16)
    low = (value - high.astype(jnp.float32)).astype(jnp.bfloat16)
    return high, low


def dot(a, b):
    return jnp.dot(a, b, preferred_element_type=jnp.float32)


def select_rows(shapes, row_count, features, position_ref, me_ref, table, rows, outs):
    pack = LANES // features
    unroll = 32
    start = 0
    for i, count in enumerate(shapes):
        part = count // pack
        lane = lax.broadcasted_iota(jnp.int32, (part, LANES), 1)
        for s in range(row_count):
            base = start + (me_ref[0] ^ s) * count

            def some_rows(step, carry):
                first = step * unroll
                for j in range(unroll):
                    index = position_ref[base + first + j]
                    rows[pl.ds(first + j, 1), :] = table[pl.ds(index, 1), :]
                return carry

            lax.fori_loop(0, count // unroll, some_rows, 0)
            packed = rows[0:part, :]
            for k in range(1, pack):
                packed = jnp.where(lane >= k * features, rows[k * part : (k + 1) * part, :], packed)
            outs[i * row_count + s][...] = packed.astype(jnp.bfloat16)
        start += row_count * count


def transform_kernel(pairs, load_steps, step_rows, shapes, row_count, *refs):
    position_ref, me_ref, hot_c_ref, hot_v_ref, cond_ref, val_ref = refs[:6]
    left_ref, right_ref, twiddle_ref = refs[6:9]
    outs = refs[9 : 9 + len(shapes) * row_count]
    rho_r, rho_i, spec, table, middle, rows = refs[9 + len(shapes) * row_count :]
    step = pl.program_id(0)
    features = 2 * pairs

    cond = dot(hot_c_ref[...], cond_ref[...])
    val = dot(hot_v_ref[...], val_ref[...])
    cr, ci = cond[:pairs], cond[pairs:]
    vr, vi = val[:pairs], val[pairs:]
    real = vr * cr + vi * ci
    imag = vr * ci - vi * cr
    for a in range(step_rows):
        row = pl.multiple_of((step * step_rows + a) * pairs, pairs)
        rho_r[pl.ds(row, pairs), :] = real[:, a * LANES : (a + 1) * LANES]
        rho_i[pl.ds(row, pairs), :] = imag[:, a * LANES : (a + 1) * LANES]

    def left_half(group, slot):
        one, two = 2 * group, 2 * group + 1
        data = jnp.concatenate(
            [
                jnp.concatenate([ref[pl.ds(p, ROWS, stride=pairs), :] for p in (one, two)], axis=1)
                for ref in (rho_r, rho_i)
            ],
            axis=0,
        )
        high, low = halves(data)
        mixed = dot(left_ref[...], jnp.concatenate([high, high, low], axis=0))
        mid_r, mid_i = mixed[:ROWS], mixed[ROWS:]
        tr, ti = twiddle_ref[0], twiddle_ref[1]
        turn_r = mid_r * tr - mid_i * ti
        turn_i = mid_r * ti + mid_i * tr
        turned = jnp.concatenate(
            [
                jnp.concatenate([turn_r[:, :LANES], turn_i[:, :LANES]], axis=1),
                jnp.concatenate([turn_r[:, LANES:], turn_i[:, LANES:]], axis=1),
            ],
            axis=0,
        )
        high, low = halves(turned)
        middle[slot, :, : 2 * LANES] = high
        middle[slot, :, 2 * LANES :] = low

    def right_half(group, slot):
        high = middle[slot, :, : 2 * LANES]
        low = middle[slot, :, 2 * LANES :]
        out = dot(jnp.concatenate([high, low, high], axis=1), right_ref[...])
        for k in range(2):
            p = 2 * group + k
            part = out[k * ROWS : (k + 1) * ROWS]
            spec[pl.ds(p, ROWS, stride=features), :] = part[:, :LANES]
            spec[pl.ds(pairs + p, ROWS, stride=features), :] = part[:, LANES:]

    @pl.when(step == load_steps - 1)
    def _():
        groups = pairs // 2
        left_half(0, 0)

        def two_groups(k, carry):
            right_half(2 * k, 0)
            left_half(2 * k + 1, 1)
            right_half(2 * k + 1, 1)
            left_half(jnp.minimum(2 * k + 2, groups - 1), 0)
            return carry

        lax.fori_loop(0, groups // 2, two_groups, 0)

        def one_row(k, carry):
            start = pl.multiple_of(k * features, features)
            tile = spec[pl.ds(start, features), :].astype(jnp.bfloat16)
            tile = jnp.concatenate([tile] * (LANES // features), axis=0)
            table[pl.ds(pl.multiple_of(k * LANES, LANES), LANES), :] = tile.T.astype(jnp.float32)
            return carry

        lax.fori_loop(0, ROWS, one_row, 0, unroll=8)
        select_rows(shapes, row_count, features, position_ref, me_ref, table, rows, outs)


def transform(valence, conduction, band_pairs, position, me, shapes, row_count):
    pairs = band_pairs.shape[0]
    features = 2 * pairs
    pack = LANES // features
    nvb, ncb = valence.shape[1], conduction.shape[1]
    load_steps = 8
    step_rows = ROWS // load_steps
    chunk = step_rows * LANES

    def hot(band, count):
        one = (band[:, None] == jnp.arange(count, dtype=jnp.int32)[None, :]).astype(jnp.bfloat16)
        none = jnp.zeros_like(one)
        return jnp.concatenate(
            [jnp.concatenate([one, none], axis=1), jnp.concatenate([none, one], axis=1)], axis=0
        )

    left, right, twiddle = dft_tables()
    whole = lambda shape: pl.BlockSpec(shape, lambda i, *_: (0,) * len(shape))
    loaded = lambda i, *_: (0, i)
    flops = 2 * pairs * (6 * ROWS * ROWS * 2 * LANES + 3 * ROWS * 4 * LANES * LANES)
    out_shapes = [(count // pack, LANES) for count in shapes for _ in range(row_count)]
    outs = pl.pallas_call(
        lambda *refs: transform_kernel(pairs, load_steps, step_rows, shapes, row_count, *refs),
        grid_spec=pltpu.PrefetchScalarGridSpec(
            num_scalar_prefetch=2,
            grid=(load_steps,),
            in_specs=[
                whole((2 * pairs, 2 * ncb)),
                whole((2 * pairs, 2 * nvb)),
                pl.BlockSpec((2 * ncb, chunk), loaded),
                pl.BlockSpec((2 * nvb, chunk), loaded),
                whole(left.shape),
                whole(right.shape),
                whole(twiddle.shape),
            ],
            out_specs=[whole(shape) for shape in out_shapes],
            scratch_shapes=[
                pltpu.VMEM((ROWS * pairs, LANES), jnp.float32),
                pltpu.VMEM((ROWS * pairs, LANES), jnp.float32),
                pltpu.VMEM((ROWS * features, LANES), jnp.float32),
                pltpu.VMEM((NR, LANES), jnp.float32),
                pltpu.VMEM((2, 2 * ROWS, 4 * LANES), jnp.bfloat16),
                pltpu.VMEM((max(shapes), LANES), jnp.float32),
            ],
        ),
        out_shape=[jax.ShapeDtypeStruct(shape, jnp.bfloat16) for shape in out_shapes],
        compiler_params=pltpu.CompilerParams(vmem_limit_bytes=VMEM_LIMIT),
        cost_estimate=pl.CostEstimate(flops=flops, bytes_accessed=40_000_000, transcendentals=0),
        name="transform",
    )(
        position,
        me,
        hot(band_pairs[:, 1], ncb),
        hot(band_pairs[:, 0], nvb),
        conduction.reshape(2 * ncb, NR),
        valence.reshape(2 * nvb, NR),
        jnp.asarray(left),
        jnp.asarray(right),
        jnp.asarray(twiddle),
    )
    return [outs[i * row_count : (i + 1) * row_count] for i in range(len(shapes))]


def assemble_kernel(row_count, features, me_ref, *rest):
    parts, out_ref, held = rest[:row_count], rest[row_count], rest[row_count + 1]
    pack = LANES // features
    part = parts[0].shape[0]
    lane = lax.broadcasted_iota(jnp.int32, (part, LANES), 1)
    for s in range(row_count):
        held[s] = parts[s][...].astype(jnp.float32)
    for b in range(row_count // pack):
        for k in range(pack):
            block = None
            for q in range(pack):
                piece = held[(b * pack + q) ^ me_ref[0]]
                if q != k:
                    piece = pltpu.roll(piece, (q - k) * features % LANES, 1)
                block = piece if block is None else jnp.where(lane >= q * features, piece, block)
            out_ref[k * part : (k + 1) * part, b * LANES : (b + 1) * LANES] = block.astype(
                jnp.bfloat16
            )


def assemble(parts, me, features):
    row_count = len(parts)
    pack = LANES // features
    part = parts[0].shape[0]
    return pl.pallas_call(
        lambda *refs: assemble_kernel(row_count, features, *refs),
        grid_spec=pltpu.PrefetchScalarGridSpec(
            num_scalar_prefetch=1,
            grid=(),
            in_specs=[pl.BlockSpec(memory_space=pltpu.VMEM)] * row_count,
            out_specs=pl.BlockSpec(memory_space=pltpu.VMEM),
            scratch_shapes=[pltpu.VMEM((row_count, part, LANES), jnp.float32)],
        ),
        out_shape=jax.ShapeDtypeStruct((part * pack, row_count * features), jnp.bfloat16),
        compiler_params=pltpu.CompilerParams(vmem_limit_bytes=VMEM_LIMIT),
        cost_estimate=pl.CostEstimate(flops=0, bytes_accessed=2_000_000, transcendentals=0),
        name="assemble",
    )(me, *parts)


def flip_kernel(slot_count, part_ref, *rest):
    slots, out_ref = rest[:slot_count], rest[slot_count]
    width = slots[0].shape[1]
    for s in range(slot_count):
        out_ref[s * width : (s + 1) * width, :] = (
            slots[s][...].astype(jnp.float32).T.astype(jnp.bfloat16)
        )


def flip(slots, part, depth):
    slot_count = len(slots)
    width = slots[0].shape[1]
    tile = min(256, depth)
    steps = depth // tile
    pick = lambda t, part_ref: (part_ref[0] * steps + t, 0)
    return pl.pallas_call(
        lambda *refs: flip_kernel(slot_count, *refs),
        grid_spec=pltpu.PrefetchScalarGridSpec(
            num_scalar_prefetch=1,
            grid=(steps,),
            in_specs=[pl.BlockSpec((tile, width), pick)] * slot_count,
            out_specs=pl.BlockSpec((slot_count * width, tile), lambda t, part_ref: (0, t)),
        ),
        out_shape=jax.ShapeDtypeStruct((slot_count * width, depth), jnp.bfloat16),
        compiler_params=pltpu.CompilerParams(vmem_limit_bytes=VMEM_LIMIT),
        cost_estimate=pl.CostEstimate(
            flops=0, bytes_accessed=8 * slot_count * width * depth, transcendentals=0
        ),
        name="flip",
    )(part, *slots)


def settle_kernel(pairs, aliased, *refs):
    take_ref, kept_ref, arrived_ref = refs[:3]
    out_ref = refs[3 + aliased]
    kept = jnp.where(take_ref[0] != 0, arrived_ref[...], kept_ref[...])
    out_ref[0] = kept
    values = kept.astype(jnp.float32)
    rows, across = values.shape
    values = values.reshape(rows // (2 * pairs), 2, pairs, across)
    turned = jnp.stack([values[:, 1], -values[:, 0]], axis=1)
    out_ref[1] = turned.reshape(rows, across).astype(jnp.bfloat16)


def settle(held, take, kept, arrived, first_row, depth, pairs):
    rows, across = kept.shape
    tile = math.gcd(math.gcd(rows, first_row), 512)
    aliased = 0 if held is None else 1
    place = first_row // tile
    return pl.pallas_call(
        lambda *refs: settle_kernel(pairs, aliased, *refs),
        grid_spec=pltpu.PrefetchScalarGridSpec(
            num_scalar_prefetch=1,
            grid=(rows // tile,),
            in_specs=[pl.BlockSpec((tile, across), lambda t, _: (t, 0))] * 2
            + [pl.BlockSpec(memory_space=pl.ANY)] * aliased,
            out_specs=pl.BlockSpec((2, tile, across), lambda t, _: (0, place + t, 0)),
        ),
        out_shape=jax.ShapeDtypeStruct((2, depth, across), jnp.bfloat16),
        input_output_aliases={3: 0} if aliased else {},
        compiler_params=pltpu.CompilerParams(vmem_limit_bytes=VMEM_LIMIT),
        cost_estimate=pl.CostEstimate(
            flops=0, bytes_accessed=8 * rows * across, transcendentals=0
        ),
        name="settle",
    )(take, kept, arrived, *([held] if aliased else []))


def weigh_kernel(slot_count, *refs):
    slots, weight_ref, out_ref = refs[:slot_count], refs[slot_count], refs[slot_count + 1]
    width = slots[0].shape[1]
    for s in range(slot_count):
        out_ref[:, s * width : (s + 1) * width] = (
            slots[s][...].astype(jnp.float32) * weight_ref[s : s + 1, :]
        ).astype(jnp.bfloat16)


def weigh(slots, weights):
    slot_count = len(slots)
    count, width = slots[0].shape
    tile = math.gcd(count, 256)
    return pl.pallas_call(
        lambda *refs: weigh_kernel(slot_count, *refs),
        grid=(count // tile,),
        in_specs=[pl.BlockSpec((tile, width), lambda t: (t, 0))] * slot_count
        + [pl.BlockSpec(weights.shape, lambda t: (0, 0))],
        out_specs=pl.BlockSpec((tile, slot_count * width), lambda t: (t, 0)),
        out_shape=jax.ShapeDtypeStruct((count, slot_count * width), jnp.bfloat16),
        compiler_params=pltpu.CompilerParams(vmem_limit_bytes=VMEM_LIMIT),
        cost_estimate=pl.CostEstimate(
            flops=0, bytes_accessed=4 * count * slot_count * width, transcendentals=0
        ),
        name="weigh",
    )(*slots, weights)


def contract_kernel(left_spans, right_spans, aliased, *refs):
    lefts = refs[: len(left_spans)]
    rights = refs[len(left_spans) : len(left_spans) + len(right_spans)]
    out_ref = refs[len(left_spans) + len(right_spans) + aliased]
    column, row = pl.program_id(0), pl.program_id(1)

    def block(left_ref, right_ref):
        parts, unit, depth = left_ref.shape
        left = left_ref[...].reshape(parts * unit, depth)
        for z in range(2):
            out_ref[z] = dot(left, right_ref[z]).reshape(out_ref.shape[1:])

    for (left_start, left_count), left_ref in zip(left_spans, lefts):
        for (right_start, right_count), right_ref in zip(right_spans, rights):
            inside = (row >= left_start) & (row < left_start + left_count)
            inside &= (column >= right_start) & (column < right_start + right_count)
            pl.when(inside)(lambda left_ref=left_ref, right_ref=right_ref: block(left_ref, right_ref))


def contract(result, lefts, rights, unit, eighths):
    parts, _, depth = lefts[0][2].shape
    one = len(rights) == 1
    wide = 1
    if one:
        wide = 2 if rights[0][1] % 2 == 0 else rights[0][1]

    def spans(chunks, step):
        found, start = [], 0
        for _, count, _ in chunks:
            found.append((start, count // step))
            start += count // step
        return found, start

    left_spans, left_steps = spans(lefts, 1)
    right_spans, right_steps = spans(rights, wide)

    def inner(span):
        return lambda i: jnp.clip(i - span[0], 0, span[1] - 1)

    def outer(chunks, found, step):
        def place(i):
            answer = chunks[0][0] // step + i
            for (first, _, _), (start, _) in list(zip(chunks, found))[1:]:
                answer = jnp.where(i >= start, first // step + i - start, answer)
            return answer

        return place

    left_in = [inner(span) for span in left_spans]
    right_in = [inner(span) for span in right_spans]
    row_out, column_out = outer(lefts, left_spans, 1), outer(rights, right_spans, wide)
    aliased = 0 if result is None else 1
    flops = 8 * parts * left_steps * unit * right_steps * wide * unit * depth
    return pl.pallas_call(
        lambda *refs: contract_kernel(left_spans, right_spans, aliased, *refs),
        grid=(right_steps, left_steps),
        in_specs=[
            pl.BlockSpec((parts, unit, depth), lambda c, r, f=f: (0, f(r), 0)) for f in left_in
        ]
        + [
            pl.BlockSpec((2, depth, wide * unit), lambda c, r, f=f: (0, 0, f(c))) for f in right_in
        ]
        + [pl.BlockSpec(memory_space=pl.ANY)] * aliased,
        out_specs=pl.BlockSpec(
            (2, parts, unit, wide * unit), lambda c, r: (0, 0, row_out(r), column_out(c))
        ),
        out_shape=jax.ShapeDtypeStruct((2, parts, eighths * unit, eighths * unit), jnp.float32),
        input_output_aliases={len(lefts) + len(rights): 0} if aliased else {},
        compiler_params=pltpu.CompilerParams(vmem_limit_bytes=VMEM_LIMIT),
        cost_estimate=pl.CostEstimate(
            flops=flops, bytes_accessed=flops // depth + 4_000_000, transcendentals=0
        ),
        name="contract",
    )(*[a for _, _, a in lefts], *[a for _, _, a in rights], *([result] if aliased else []))


def energy_gaps(valence_energy, conduction_energy, band_pairs):
    valence_hot = (
        band_pairs[:, 0][:, None] == jnp.arange(valence_energy.shape[0], dtype=jnp.int32)[None, :]
    )
    conduction_hot = (
        band_pairs[:, 1][:, None]
        == jnp.arange(conduction_energy.shape[0], dtype=jnp.int32)[None, :]
    )
    return jnp.sum(jnp.where(valence_hot, valence_energy[None, :], 0.0), axis=1) - jnp.sum(
        jnp.where(conduction_hot, conduction_energy[None, :], 0.0), axis=1
    )


def after(value, *others):
    return lax.optimization_barrier((value,) + others)[0]


def body(valence, conduction, valence_energy, conduction_energy, band_pairs, grid_index):
    rows, cols = lax.axis_size("row"), lax.axis_size("col")
    row, col = lax.axis_index("row"), lax.axis_index("col")
    pairs = band_pairs.shape[0]
    features = 2 * pairs
    width = rows * features
    block = grid_index.shape[0] // cols
    parts = cols // rows
    unit = block // EIGHTHS
    me = row.astype(jnp.int32).reshape(1)
    my_part = (col % parts).astype(jnp.int32).reshape(1)
    owner = col // parts

    order = list(range(0, cols, 2)) + list(range(1, cols, 2))[::-1]
    ring_up = [(order[q], order[(q + 1) % cols]) for q in range(cols)]
    ring_down = [(b, a) for a, b in ring_up]
    my_place = jnp.asarray(np.argsort(np.array(order)), jnp.int32)[col]
    half = cols // 2
    offsets = [0]
    for t in range(1, half):
        offsets += [-t, t]
    offsets.append(half)
    sources = jnp.asarray(np.array(order), jnp.int32)[
        (my_place + jnp.asarray(np.array(offsets), jnp.int32)) % cols
    ]

    gap = energy_gaps(valence_energy, conduction_energy, band_pairs)
    weight = 2.0 / (math.sqrt(pairs * rows * cols) * gap)
    weight = jnp.broadcast_to(jnp.pad(weight, (0, LANES - pairs))[None, :], (8, LANES))
    weights = lax.all_gather(weight, ("row", "col"), axis=0, tiled=True)
    weights = weights.reshape(rows, cols, 8, LANES)[:, :, 0, :pairs].transpose(1, 0, 2)
    weights = jnp.take(weights, sources, axis=0)
    weights = jnp.broadcast_to(weights[:, :, None, :], (cols, rows, 2, pairs))
    weights = weights.reshape(cols, width)

    position = table_position(grid_index).reshape(rows, parts, EIGHTHS, unit)
    position = jnp.concatenate(
        [position[:, :, first : first + share].reshape(-1) for first, share in CHUNKS]
    )
    counts = [parts * share * unit for _, share in CHUNKS]
    sent = transform(valence, conduction, band_pairs, after(position, weight), me, counts, rows)
    me = after(me, weights)

    owns, moved = [], None
    for i in range(len(CHUNKS)):
        parcels = [sent[i][s] if moved is None else after(sent[i][s], moved) for s in range(rows)]
        got = parcels[:1] + [
            lax.ppermute(parcels[s], "row", [(r, r ^ s) for r in range(rows)])
            for s in range(1, rows)
        ]
        moved = got[-1]
        owns.append(assemble(got, me, features))

    def send_column(held, kept, first_row):
        holders, step = [0], rows // 2
        while step:
            perm = [
                ((c // parts ^ h) * cols + c, (c // parts ^ h ^ step) * cols + c)
                for c in range(cols)
                for h in holders
            ]
            arrived = lax.ppermute(kept, ("row", "col"), perm)
            take = (row ^ owner) & step != 0
            if step > 1:
                kept = jnp.where(take, arrived, kept)
            holders += [h ^ step for h in holders]
            step //= 2
        take = take.astype(jnp.int32).reshape(1)
        return settle(held, take, kept, arrived, first_row, cols * width, pairs)

    result, lefts, rights = None, [], []
    second = None
    for (first, share), own in zip(CHUNKS, owns):
        if second is not None:
            own = after(own, *second)
        groups = [[own]]
        up = down = own
        for t in range(1, half):
            up = lax.ppermute(up, "col", ring_up)
            down = lax.ppermute(down, "col", ring_down)
            if t == min(2, half - 1):
                second = (up, down)
            if t > 1 and share > 1:
                groups.append([])
            groups[-1] += [up, down]
        cut = own.shape[0] // 2
        groups[-1].append(
            jnp.concatenate(
                [
                    lax.ppermute(up[:cut], "col", ring_up),
                    lax.ppermute(down[cut:], "col", ring_down),
                ],
                axis=0,
            )
        )
        if share == 3:
            groups = [sum(groups[:-1], []), groups[-1]]
        held, first_row = None, 0
        for group in groups:
            if result is not None and group is groups[-1]:
                group = [after(group[0], result)] + group[1:]
            held = send_column(held, flip(group, my_part, share * unit), first_row)
            first_row += len(group) * width
        left = weigh(sum(groups, []), weights).reshape(parts, share * unit, cols * width)
        lefts.append((first, share, left))
        if rights:
            result = contract(result, lefts[-1:], rights, unit, EIGHTHS)
        rights.append((first, share, held))
        result = contract(result, lefts, rights[-1:], unit, EIGHTHS)
    return result.reshape(2, parts * block, block)


def solution(mesh):
    return jax.shard_map(
        body,
        mesh=mesh,
        in_specs=(P(), P(), P(), P(), P(("row", "col"), None), P()),
        out_specs=P(None, "row", "col"),
        check_vma=False,
    )
```

time: 610 us -> 505 us (0.83); the launches traced: 600 us -> 502 us
  Pallas kernels: 300 us -> 246 us
  starting transfers between devices: 93.2 us -> 63.1 us
  waiting for transfers between devices: 128 us -> 98.1 us
  blocking collectives: 47.3 us -> 69.7 us
    all_gather x0 -> x1, blocking collectives: none -> 69.7 us  [body(): weights = lax.all_gather(weight, ('row', 'col'), axis=0, tiled=True)]
    pallas_call x30 -> x14, Pallas kernels: 218 us -> 152 us  [the longest x5 108 us: contract(): pl.pallas_call(lambda *refs: contract_kernel(left_spans, right_spans, ali...]
    unnamed x1 -> x0, blocking collectives: 47.3 us -> none
    ppermute x15 -> x9, waiting for transfers between devices: 28.6 us -> 0.02 us  [body(): down = lax.ppermute(down, 'col', ring_down)]
    ppermute x15 -> x9, waiting for transfers between devices: 41.1 us -> 68.9 us  [body(): up = lax.ppermute(up, 'col', ring_up)]
    ppermute x15 -> x9, starting transfers between devices: 21 us -> 2.9 us  [body(): up = lax.ppermute(up, 'col', ring_up)]
    ppermute x25 -> x21, waiting for transfers between devices: 41 us -> 25.6 us  [the longest x9 15.1 us: body(): lax.ppermute(parcels[s], 'row', [(r, r ^ s) for r in range(rows)])]
    pallas_call x1, Pallas kernels: 56.8 us -> 64.7 us  [transform(): pl.pallas_call(lambda *refs: transform_kernel(pairs, load_steps, step_row...]
  transfers between devices with their start and end apart: 65 -> 45, of which waited for: 23 -> 13; matrix products, arithmetic and copies ran while one was open for 4% -> 3% of each run, Pallas kernels for 11% -> 28%
where the time goes in v2:
time: 505 us; the launch traced here: 502 us
  Pallas kernels  246 us (49%)
  waiting for transfers between devices  98.1 us (19%)
  blocking collectives  69.7 us (14%)
  starting transfers between devices  63.1 us (12%)
  local copies, waits for them, and re-layouts  16.2 us (3%)
  other arithmetic  7.77 us (2%)
    pallas_call x5, Pallas kernels, contract(): pl.pallas_call(lambda *refs: contract_kernel(left_spans, right_spans, ali...  108 us
    all_gather x1, blocking collectives, body(): weights = lax.all_gather(weight, ('row', 'col'), axis=0, tiled=True)  69.7 us
    ppermute x9, waiting for transfers between devices, body(): up = lax.ppermute(up, 'col', ring_up)  68.9 us
    pallas_call x1, Pallas kernels, transform(): pl.pallas_call(lambda *refs: transform_kernel(pairs, load_steps, step_row...  64.7 us
    ppermute x12, starting transfers between devices, send_column(): arrived = lax.ppermute(kept, ('row', 'col'), perm)  32.9 us
    pallas_call x6, Pallas kernels, settle(): pl.pallas_call(lambda *refs: settle_kernel(pairs, aliased, *refs), grid_s...  25.2 us
    pallas_call x6, Pallas kernels, flip(): pl.pallas_call(lambda *refs: flip_kernel(slot_count, *refs), grid_spec=pl...  22.1 us
    pallas_call x3, Pallas kernels, weigh(): pl.pallas_call(lambda *refs: weigh_kernel(slot_count, *refs), grid=(count...  19.3 us
  transfers between devices with their start and end apart: 45, of which 13 were waited for; matrix products, arithmetic and copies ran while one was open for 3% of the time, Pallas kernels for 28%

profile of v2, /device:TPU:0, one launch (start us, length us, event | category | flops | bytes accessed | tf_op | source)
XLA Modules:
  0.0 501.7 jit_solution(13765166019367435959)
XLA Ops:
  5.7 64.7 %transform.1 = (bf16[256,128]{1,0:T(8,128)(2,1)}, bf16[256,128]{1,0:T(8,128)(2,1)}, bf16[256,128]{1,0:T(8,128)(2,1)}, bf16[256,128]{1,0:T(8,128)(2,1)}, bf16[102...) custom-call(s32[16384]{0:T(1024)} %pad_add_fusion.refs_0_, ...), custom_call_target="tpu_custom_call" | custom-call | flops 9663676416 | bytes 40000000 | tf_op jit(solution)/shard_map/transform/pallas_call | solution.py:207
  73.5 69.7 %all_gather.3 = f32[256,128]{1,0:T(8,128)S(1)} all-gather(f32[8,128]{1,0:T(8,128)S(1)} %broadcast_in_dim.63), channel_id=1, replica_groups=mesh['row'=4,'col'=8] {'row','col'}, dimensions={0}, use_global_device_ids=true | all-gather | bytes 135168 | tf_op jit(solution)/shard_map/all_gather | solution.py:507
  160.6 4.8 collective-permute-done.13.refs_4_
  172.9 27.0 %collective-permute-done.7.refs_5_.refs_6_ = bf16[512,256]{1,0:T(8,128)(2,1)S(1)} collective-permute-done((bf16[512,256]{1,0:T(8,128)(2,1)S(1)}, bf16[512,256]{1,0:T(8,128)(2,1)S(1)}, u32[]{:S(2)}, u32[]{:S(2)}) %collective-permute-start.7) | collective-permute-done | bytes 262176 | tf_op jit(solution)/shard_map/ppermute | solution.py:556
  216.1 15.5 %collective-permute-done.16.refs_3_.refs_1_ = bf16[2048,256]{1,0:T(8,128)(2,1)} collective-permute-done((bf16[2048,256]{1,0:T(8,128)(2,1)S(1)}, bf16[2048,256]{1,0:T(8,128)(2,1)}, u32[]{:S(2)}, u32[]{:S(2)}) %collective-permute-start.16) | collective-permute-done | bytes 1048608 | tf_op jit(solution)/shard_map/ppermute | solution.py:556
  237.3 17.1 %collective-permute-done.18.refs_5_.refs_1_ = bf16[2048,256]{1,0:T(8,128)(2,1)S(1)} collective-permute-done((bf16[2048,256]{1,0:T(8,128)(2,1)}, bf16[2048,256]{1,0:T(8,128)(2,1)S(1)}, u32[]{:S(2)}, u32[]{:S(2)}) %collective-permute-start.18) | collective-permute-done | bytes 1048608 | tf_op jit(solution)/shard_map/ppermute | solution.py:556
  262.2 4.3 collective-permute-done.24.refs_4_
  271.8 4.1 flip.9
  285.4 4.4 contract.5.refs_2_
  293.0 4.0 flip.7
  310.0 6.5 %collective-permute-done.27.refs_3_.refs_4_ = bf16[1536,256]{1,0:T(8,128)(2,1)} collective-permute-done((bf16[1536,256]{1,0:T(8,128)(2,1)S(1)}, bf16[1536,256]{1,0:T(8,128)(2,1)}, u32[]{:S(2)}, u32[]{:S(2)}) %collective-permute-start.27) | collective-permute-done | bytes 786464 | tf_op jit(solution)/shard_map/ppermute | solution.py:556
  321.5 6.4 %collective-permute-done.37 = bf16[512,1024]{1,0:T(8,128)(2,1)S(1)} collective-permute-done((bf16[512,1024]{1,0:T(8,128)(2,1)}, bf16[512,1024]{1,0:T(8,128)(2,1)S(1)}, u32[]{:S(2)}, u32[]{:S(2)}) %collective-permute-start.37) | collective-permute-done | bytes 1048608 | tf_op jit(solution)/shard_map/ppermute | solution.py:539
  330.3 9.3 %weigh.4 = bf16[2048,2048]{1,0:T(8,128)(2,1)} custom-call(bf16[2048,256]{1,0:T(8,128)(2,1)} %assemble.4.refs_0_.refs_1_, bf16[2048,256]{1,0:T(8,128)(2,1)} %copy-done.18, bf16[2048,256]{1,0:T(8,128)(2,1)} %copy-done.19, bf16[2048,256]{1,0:T(8,128)(2,1)} %collective-permute-done.16.refs_3_.refs_1_, bf16[2048,256]{1,0:T(8,128)(2,1)} %collective-permute-done.17.refs_4_.refs_2_, ...), custom_call_target="tpu_custom_call" | custom-call | bytes 16777216 | tf_op jit(solution)/shard_map/weigh/pallas_call | solution.py:370
  343.4 9.1 %contract.6.refs_3_ = f32[2,2,2048,2048]{3,2,1,0:T(8,128)} custom-call(bf16[2,1024,2048]{2,1,0:T(8,128)(2,1)} %bitcast.27, bf16[2,2048,256]{2,1,0:T(8,128)(2,1)} %settle.6.refs_1_, f32[2,2,2048,2048]{3,2,1,0:T(8,128)} %contract.5.refs_2_), custom_call_target="tpu_custom_call", output_to_operand_aliasing={{}: (2, {})} | custom-call | flops 8589934592 | bytes 8194304 | tf_op jit(solution)/shard_map/contract/pallas_call | solution.py:438
  352.5 4.2 flip.11
  356.7 5.5 %collective-permute-start.43 = (bf16[1280,768]{1,0:T(8,128)(2,1)}, bf16[1280,768]{1,0:T(8,128)(2,1)}, u32[]{:S(2)}, u32[]{:S(2)}) collective-permute-start(bf16[1280,768]{1,0:T(8,128)(2,1)} %flip.11), channel_id=1, source_target_pairs={{0,16},{1,17},{10,26},{11,27},{20,4},{21,5},{30,14},{31,15}} | collective-permute-start | bytes 5898248 | tf_op jit(solution)/shard_map/ppermute | solution.py:539
  362.2 4.4 settle.7.refs_3_
  370.3 4.7 settle.9.refs_2_
  375.1 30.4 %contract.7.refs_3_ = f32[2,2,2048,2048]{3,2,1,0:T(8,128)} custom-call(bf16[2,256,2048]{2,1,0:T(8,128)(2,1)} %bitcast.33, bf16[2,1024,2048]{2,1,0:T(8,128)(2,1)} %bitcast.28, bf16[2,2048,1024]{2,1,0:T(8,128)(2,1)} %settle.9.refs_2_, f32[2,2,2048,2048]{3,2,1,0:T(8,128)} %contract.6.refs_3_), custom_call_target="tpu_custom_call", output_to_operand_aliasing={{}: (3, {})} | custom-call | flops 42949672960 | bytes 24971520 | tf_op jit(solution)/shard_map/contract/pallas_call | solution.py:438
  411.4 7.1 %weigh.5 = bf16[1536,2048]{1,0:T(8,128)(2,1)} custom-call(bf16[1536,256]{1,0:T(8,128)(2,1)} %assemble.5.refs_0_.refs_1_, bf16[1536,256]{1,0:T(8,128)(2,1)} %copy-done.21, bf16[1536,256]{1,0:T(8,128)(2,1)} %collective-permute-done.26.refs_2_.refs_3_, bf16[1536,256]{1,0:T(8,128)(2,1)} %collective-permute-done.27.refs_3_.refs_4_, ...), custom_call_target="tpu_custom_call" | custom-call | bytes 12582912 | tf_op jit(solution)/shard_map/weigh/pallas_call | solution.py:370
  420.3 4.0 collective-permute-done.41
  426.9 29.7 %contract.8.refs_4_ = f32[2,2,2048,2048]{3,2,1,0:T(8,128)} custom-call(bf16[2,768,2048]{2,1,0:T(8,128)(2,1)} %bitcast.30, bf16[2,2048,256]{2,1,0:T(8,128)(2,1)} %settle.6.refs_1_, bf16[2,2048,1024]{2,1,0:T(8,128)(2,1)} %settle.9.refs_2_, f32[2,2,2048,2048]{3,2,1,0:T(8,128)} %contract.7.refs_3_), custom_call_target="tpu_custom_call", output_to_operand_aliasing={{}: (3, {})} | custom-call | flops 32212254720 | bytes 19728640 | tf_op jit(solution)/shard_map/contract/pallas_call | solution.py:438
  457.9 5.7 %settle.10.refs_3_ = bf16[2,2048,768]{2,1,0:T(8,128)(2,1)} custom-call(s32[1]{0:T(128)} %bitcast.15.refs_0_, bf16[1280,768]{1,0:T(8,128)(2,1)} %copy-done.1, bf16[1280,768]{1,0:T(8,128)(2,1)} %copy-done.22), custom_call_target="tpu_custom_call" | custom-call | bytes 7864320 | tf_op jit(solution)/shard_map/settle/pallas_call | solution.py:338
  467.5 34.2 %contract.9 = f32[2,2,2048,2048]{3,2,1,0:T(8,128)} custom-call(bf16[2,256,2048]{2,1,0:T(8,128)(2,1)} %bitcast.34, bf16[2,1024,2048]{2,1,0:T(8,128)(2,1)} %bitcast.29, bf16[2,768,2048]{2,1,0:T(8,128)(2,1)} %bitcast.31, bf16[2,2048,768]{2,1,0:T(8,128)(2,1)} %settle.11.refs_3_, f32[2,2,2048,2048]{3,2,1,0:T(8,128)} %contract.8.refs_4_), custom_call_target="tpu_custom_call", output_to_operand_aliasing={{}: (4, {})} | custom-call | flops 51539607552 | bytes 29165824 | tf_op jit(solution)/shard_map/contract/pallas_call | solution.py:438
  (220 shorter events, 123.9 us)
Async XLA Ops:
  70.4 76.3 %collective-permute-start = (bf16[256,128]{1,0:T(8,128)(2,1)}, bf16[256,128]{1,0:T(8,128)(2,1)S(1)}, u32[]{:S(2)}, u32[]{:S(2)}) collective-permute-start(bf16[256,128]{1,0:T(8,128)(2,1)} %get-tuple-element.34), channel_id=1, source_target_pairs={{0,8},{8,0},{16,24},{24,16},{1,9},{9,1},{17,25},{25,17},{2,10},{10... | collective-permute-start | bytes 196616 | tf_op jit(solution)/shard_map/ppermute | solution.py:525
  70.9 75.8 %collective-permute-start.1 = (bf16[256,128]{1,0:T(8,128)(2,1)}, bf16[256,128]{1,0:T(8,128)(2,1)S(1)}, u32[]{:S(2)}, u32[]{:S(2)}) collective-permute-start(bf16[256,128]{1,0:T(8,128)(2,1)} %get-tuple-element.35), channel_id=1, source_target_pairs={{0,16},{8,24},{16,0},{24,8},{1,17},{9,25},{17,1},{25,9},{2,18},{10... | collective-permute-start | bytes 196616 | tf_op jit(solution)/shard_map/ppermute | solution.py:525
  73.5 73.3 %collective-permute-start.2 = (bf16[256,128]{1,0:T(8,128)(2,1)}, bf16[256,128]{1,0:T(8,128)(2,1)S(1)}, u32[]{:S(2)}, u32[]{:S(2)}) collective-permute-start(bf16[256,128]{1,0:T(8,128)(2,1)} %get-tuple-element.36), channel_id=1, source_target_pairs={{0,24},{8,16},{16,8},{24,0},{1,25},{9,17},{17,9},{25,1},{2,26},{10... | collective-permute-start | bytes 196616 | tf_op jit(solution)/shard_map/ppermute | solution.py:525
  168.8 39.1 %collective-permute-start.14 = (bf16[2048,256]{1,0:T(8,128)(2,1)}, bf16[2048,256]{1,0:T(8,128)(2,1)S(1)}, u32[]{:S(2)}, u32[]{:S(2)}) collective-permute-start(bf16[2048,256]{1,0:T(8,128)(2,1)} %assemble.4.refs_0_.refs_1_), channel_id=1, source_target_pairs={{0,2},{2,4},{4,6},{6,7},{7,5},{5,3},{3,1},{1,0},{8,10},{10,12},{12... | collective-permute-start | bytes 3145736 | tf_op jit(solution)/shard_map/ppermute | solution.py:556
  168.9 39.3 %collective-permute-start.15 = (bf16[2048,256]{1,0:T(8,128)(2,1)}, bf16[2048,256]{1,0:T(8,128)(2,1)S(1)}, u32[]{:S(2)}, u32[]{:S(2)}) collective-permute-start(bf16[2048,256]{1,0:T(8,128)(2,1)} %assemble.4.refs_0_.refs_1_), channel_id=1, source_target_pairs={{2,0},{4,2},{6,4},{7,6},{5,7},{3,5},{1,3},{0,1},{10,8},{12,10},{14... | collective-permute-start | bytes 3145736 | tf_op jit(solution)/shard_map/ppermute | solution.py:557
  170.9 29.1 %collective-permute-start.7 = (bf16[512,256]{1,0:T(8,128)(2,1)S(1)}, bf16[512,256]{1,0:T(8,128)(2,1)S(1)}, u32[]{:S(2)}, u32[]{:S(2)}) collective-permute-start(bf16[512,256]{1,0:T(8,128)(2,1)S(1)} %collective-permute-done.5.refs_3_.refs_4_), channel_id=1, source_target_pairs={{0,2},{2,4},{4,6},{6,7},{7,5},{5,3},{3,1},{1,0},{8,10},{10,12},{12... | collective-permute-start | bytes 786440 | tf_op jit(solution)/shard_map/ppermute | solution.py:556
  171.0 30.0 %collective-permute-start.8 = (bf16[512,256]{1,0:T(8,128)(2,1)S(1)}, bf16[512,256]{1,0:T(8,128)(2,1)S(1)}, u32[]{:S(2)}, u32[]{:S(2)}) collective-permute-start(bf16[512,256]{1,0:T(8,128)(2,1)S(1)} %collective-permute-done.6.refs_4_.refs_5_), channel_id=1, source_target_pairs={{2,0},{4,2},{6,4},{7,6},{5,7},{3,5},{1,3},{0,1},{10,8},{12,10},{14... | collective-permute-start | bytes 786440 | tf_op jit(solution)/shard_map/ppermute | solution.py:557
  207.9 23.7 %collective-permute-start.16 = (bf16[2048,256]{1,0:T(8,128)(2,1)S(1)}, bf16[2048,256]{1,0:T(8,128)(2,1)}, u32[]{:S(2)}, u32[]{:S(2)}) collective-permute-start(bf16[2048,256]{1,0:T(8,128)(2,1)S(1)} %collective-permute-done.14.refs_1_.refs_2_), channel_id=1, source_target_pairs={{0,2},{2,4},{4,6},{6,7},{7,5},{5,3},{3,1},{1,0},{8,10},{10,12},{12... | collective-permute-start | bytes 3145736 | tf_op jit(solution)/shard_map/ppermute | solution.py:556
  208.2 24.0 %collective-permute-start.17 = (bf16[2048,256]{1,0:T(8,128)(2,1)S(1)}, bf16[2048,256]{1,0:T(8,128)(2,1)}, u32[]{:S(2)}, u32[]{:S(2)}) collective-permute-start(bf16[2048,256]{1,0:T(8,128)(2,1)S(1)} %collective-permute-done.15.refs_2_.refs_3_), channel_id=1, source_target_pairs={{2,0},{4,2},{6,4},{7,6},{5,7},{3,5},{1,3},{0,1},{10,8},{12,10},{14... | collective-permute-start | bytes 3145736 | tf_op jit(solution)/shard_map/ppermute | solution.py:557
  231.6 22.8 %collective-permute-start.18 = (bf16[2048,256]{1,0:T(8,128)(2,1)}, bf16[2048,256]{1,0:T(8,128)(2,1)S(1)}, u32[]{:S(2)}, u32[]{:S(2)}) collective-permute-start(bf16[2048,256]{1,0:T(8,128)(2,1)} %collective-permute-done.16.refs_3_.refs_1_), channel_id=1, source_target_pairs={{0,2},{2,4},{4,6},{6,7},{7,5},{5,3},{3,1},{1,0},{8,10},{10,12},{12... | collective-permute-start | bytes 3145736 | tf_op jit(solution)/shard_map/ppermute | solution.py:556
  232.1 24.6 %collective-permute-start.19 = (bf16[2048,256]{1,0:T(8,128)(2,1)}, bf16[2048,256]{1,0:T(8,128)(2,1)S(1)}, u32[]{:S(2)}, u32[]{:S(2)}) collective-permute-start(bf16[2048,256]{1,0:T(8,128)(2,1)} %collective-permute-done.17.refs_4_.refs_2_), channel_id=1, source_target_pairs={{2,0},{4,2},{6,4},{7,6},{5,7},{3,5},{1,3},{0,1},{10,8},{12,10},{14... | collective-permute-start | bytes 3145736 | tf_op jit(solution)/shard_map/ppermute | solution.py:557
  235.0 44.6 %collective-permute-start.34 = (bf16[2048,256]{1,0:T(8,128)(2,1)S(1)}, bf16[2048,256]{1,0:T(8,128)(2,1)}, u32[]{:S(2)}, u32[]{:S(2)}) collective-permute-start(bf16[2048,256]{1,0:T(8,128)(2,1)S(1)} %broadcast_select_fusion.5.refs_1_), channel_id=1, source_target_pairs={{0,8},{16,24},{1,9},{17,25},{10,2},{26,18},{11,3},{27,19},{20,28},... | collective-permute-start | bytes 3145736 | tf_op jit(solution)/shard_map/ppermute | solution.py:539
  255.4 34.5 %collective-permute-start.20 = (bf16[1024,256]{1,0:T(8,128)(2,1)}, bf16[1024,256]{1,0:T(8,128)(2,1)}, u32[]{:S(2)}, u32[]{:S(2)}) collective-permute-start(bf16[1024,256]{1,0:T(8,128)(2,1)} %slice.60), channel_id=1, source_target_pairs={{0,2},{2,4},{4,6},{6,7},{7,5},{5,3},{3,1},{1,0},{8,10},{10,12},{12... | collective-permute-start | bytes 1572872 | tf_op jit(solution)/shard_map/ppermute | solution.py:567
  257.7 33.3 %collective-permute-start.21 = (bf16[1024,256]{1,0:T(8,128)(2,1)}, bf16[1024,256]{1,0:T(8,128)(2,1)}, u32[]{:S(2)}, u32[]{:S(2)}) collective-permute-start(bf16[1024,256]{1,0:T(8,128)(2,1)} %slice.61), channel_id=1, source_target_pairs={{2,0},{4,2},{6,4},{7,6},{5,7},{3,5},{1,3},{0,1},{10,8},{12,10},{14... | collective-permute-start | bytes 1572872 | tf_op jit(solution)/shard_map/ppermute | solution.py:568
  276.0 31.1 %collective-permute-start.39 = (bf16[768,1024]{1,0:T(8,128)(2,1)}, bf16[768,1024]{1,0:T(8,128)(2,1)}, u32[]{:S(2)}, u32[]{:S(2)}) collective-permute-start(bf16[768,1024]{1,0:T(8,128)(2,1)} %flip.9), channel_id=1, source_target_pairs={{0,16},{1,17},{10,26},{11,27},{20,4},{21,5},{30,14},{31,15}} | collective-permute-start | bytes 4718600 | tf_op jit(solution)/shard_map/ppermute | solution.py:539
  307.3 49.4 %collective-permute-start.40 = (bf16[768,1024]{1,0:T(8,128)(2,1)S(1)}, bf16[768,1024]{1,0:T(8,128)(2,1)}, u32[]{:S(2)}, u32[]{:S(2)}) collective-permute-start(bf16[768,1024]{1,0:T(8,128)(2,1)S(1)} %broadcast_select_fusion.1.refs_1_), channel_id=1, source_target_pairs={{0,8},{16,24},{1,9},{17,25},{10,2},{26,18},{11,3},{27,19},{20,28},... | collective-permute-start | bytes 4718600 | tf_op jit(solution)/shard_map/ppermute | solution.py:539
  316.5 23.1 %collective-permute-start.29 = (bf16[1536,256]{1,0:T(8,128)(2,1)}, bf16[1536,256]{1,0:T(8,128)(2,1)S(1)}, u32[]{:S(2)}, u32[]{:S(2)}) collective-permute-start(bf16[1536,256]{1,0:T(8,128)(2,1)} %collective-permute-done.27.refs_3_.refs_4_), channel_id=1, source_target_pairs={{0,2},{2,4},{4,6},{6,7},{7,5},{5,3},{3,1},{1,0},{8,10},{10,12},{12... | collective-permute-start | bytes 2359304 | tf_op jit(solution)/shard_map/ppermute | solution.py:556
  319.0 51.3 %collective-permute-start.36 = (bf16[768,1024]{1,0:T(8,128)(2,1)S(1)}, bf16[768,1024]{1,0:T(8,128)(2,1)}, u32[]{:S(2)}, u32[]{:S(2)}) collective-permute-start(bf16[768,1024]{1,0:T(8,128)(2,1)S(1)} %broadcast_select_fusion.2.refs_1_), channel_id=1, source_target_pairs={{0,8},{16,24},{1,9},{17,25},{10,2},{26,18},{11,3},{27,19},{20,28},... | collective-permute-start | bytes 4718600 | tf_op jit(solution)/shard_map/ppermute | solution.py:539
  328.1 38.6 %collective-permute-start.38 = (bf16[512,1024]{1,0:T(8,128)(2,1)S(1)}, bf16[512,1024]{1,0:T(8,128)(2,1)}, u32[]{:S(2)}, u32[]{:S(2)}) collective-permute-start(bf16[512,1024]{1,0:T(8,128)(2,1)S(1)} %broadcast_select_fusion.4.refs_1_), channel_id=1, source_target_pairs={{0,8},{16,24},{1,9},{17,25},{10,2},{26,18},{11,3},{27,19},{20,28},... | collective-permute-start | bytes 3145736 | tf_op jit(solution)/shard_map/ppermute | solution.py:539
  340.5 28.7 %collective-permute-start.31 = (bf16[768,256]{1,0:T(8,128)(2,1)}, bf16[768,256]{1,0:T(8,128)(2,1)S(1)}, u32[]{:S(2)}, u32[]{:S(2)}) collective-permute-start(bf16[768,256]{1,0:T(8,128)(2,1)} %slice.62), channel_id=1, source_target_pairs={{0,2},{2,4},{4,6},{6,7},{7,5},{5,3},{3,1},{1,0},{8,10},{10,12},{12... | collective-permute-start | bytes 1179656 | tf_op jit(solution)/shard_map/ppermute | solution.py:567
  341.3 27.9 %collective-permute-start.32 = (bf16[768,256]{1,0:T(8,128)(2,1)}, bf16[768,256]{1,0:T(8,128)(2,1)}, u32[]{:S(2)}, u32[]{:S(2)}) collective-permute-start(bf16[768,256]{1,0:T(8,128)(2,1)} %slice.63), channel_id=1, source_target_pairs={{2,0},{4,2},{6,4},{7,6},{5,7},{3,5},{1,3},{0,1},{10,8},{12,10},{14... | collective-permute-start | bytes 1179656 | tf_op jit(solution)/shard_map/ppermute | solution.py:568
  356.7 61.9 %collective-permute-start.43 = (bf16[1280,768]{1,0:T(8,128)(2,1)}, bf16[1280,768]{1,0:T(8,128)(2,1)}, u32[]{:S(2)}, u32[]{:S(2)}) collective-permute-start(bf16[1280,768]{1,0:T(8,128)(2,1)} %flip.11), channel_id=1, source_target_pairs={{0,16},{1,17},{10,26},{11,27},{20,4},{21,5},{30,14},{31,15}} | collective-permute-start | bytes 5898248 | tf_op jit(solution)/shard_map/ppermute | solution.py:539
  418.8 37.8 %collective-permute-start.44 = (bf16[1280,768]{1,0:T(8,128)(2,1)S(1)}, bf16[1280,768]{1,0:T(8,128)(2,1)S(1)}, u32[]{:S(2)}, u32[]{:S(2)}) collective-permute-start(bf16[1280,768]{1,0:T(8,128)(2,1)S(1)} %broadcast_select_fusion.refs_1_), channel_id=1, source_target_pairs={{0,8},{16,24},{1,9},{17,25},{10,2},{26,18},{11,3},{27,19},{20,28},... | collective-permute-start | bytes 5898248 | tf_op jit(solution)/shard_map/ppermute | solution.py:539
  424.6 39.0 %collective-permute-start.42 = (bf16[768,768]{1,0:T(8,128)(2,1)S(1)}, bf16[768,768]{1,0:T(8,128)(2,1)}, u32[]{:S(2)}, u32[]{:S(2)}) collective-permute-start(bf16[768,768]{1,0:T(8,128)(2,1)S(1)} %broadcast_select_fusion.3.refs_1_), channel_id=1, source_target_pairs={{0,8},{16,24},{1,9},{17,25},{10,2},{26,18},{11,3},{27,19},{20,28},... | collective-permute-start | bytes 3538952 | tf_op jit(solution)/shard_map/ppermute | solution.py:539
  (61 other events, 1253.6 us)

commit v3 on v2

v3 whole, which is shorter than its diff:
```python
import math

import jax
import jax.numpy as jnp
import ml_dtypes
import numpy as np
from jax import lax
from jax.experimental import pallas as pl
from jax.experimental.pallas import tpu as pltpu
from jax.sharding import PartitionSpec as P

N1 = 32
N2 = 32
N3 = 32
NR = N1 * N2 * N3
LANES = 128
HI = N2 * N3 // LANES
LO = N2 // HI
ROWS = N1 * HI
VMEM_LIMIT = 58 * 1024 * 1024
CHUNKS = ((0, 2), (2, 6))
EIGHTHS = 8
GROUP = 4


def split_bf16(values):
    high = values.astype(ml_dtypes.bfloat16)
    low = (values - high.astype(np.float64)).astype(ml_dtypes.bfloat16)
    return high, low


def dft_tables():
    row = np.arange(ROWS)
    left = np.exp(
        -2j
        * np.pi
        * (
            (row[:, None] // HI) * (row[None, :] // HI) / N1
            + (row[:, None] % HI) * (row[None, :] % HI) / HI
        )
    )
    lane = np.arange(LANES)
    right = np.exp(
        -2j
        * np.pi
        * (
            (lane[:, None] // N3) * (lane[None, :] // N3) / LO
            + (lane[:, None] % N3) * (lane[None, :] % N3) / N3
        )
    )
    twiddle = np.exp(-2j * np.pi * (row[:, None] % HI) * (lane[None, :] // N3) / N2)
    twiddle = twiddle / math.sqrt(NR)
    left_full = np.block([[left.real, -left.imag], [left.imag, left.real]])
    right_full = np.block([[right.real, right.imag], [-right.imag, right.real]])
    left_high, left_low = split_bf16(left_full)
    right_high, right_low = split_bf16(right_full)
    twiddle = np.concatenate([twiddle] * GROUP, axis=1)
    return (
        np.concatenate([left_high, left_low, left_high], axis=1),
        np.concatenate([right_high, right_low], axis=1),
        np.stack([twiddle.real, twiddle.imag]).astype(np.float32),
    )


def table_position(grid_index):
    first = grid_index // (N2 * N3)
    second = grid_index // N3 % N2
    third = grid_index % N3
    return (first * HI + second % HI) * LANES + second // HI * N3 + third


def halves(value):
    high = value.astype(jnp.bfloat16)
    low = (value - high.astype(jnp.float32)).astype(jnp.bfloat16)
    return high, low


def dot(a, b):
    return jnp.dot(a, b, preferred_element_type=jnp.float32)


def select_rows(shapes, row_count, features, position_ref, me_ref, table, rows, outs):
    pack = LANES // features
    unroll = 32
    start = 0
    for i, count in enumerate(shapes):
        part = count // pack
        lane = lax.broadcasted_iota(jnp.int32, (part, LANES), 1)
        for s in range(row_count):
            base = start + (me_ref[0] ^ s) * count

            def some_rows(step, carry):
                first = step * unroll
                for j in range(unroll):
                    index = position_ref[base + first + j]
                    rows[pl.ds(first + j, 1), :] = table[pl.ds(index, 1), :]
                return carry

            lax.fori_loop(0, count // unroll, some_rows, 0)
            packed = rows[0:part, :]
            for k in range(1, pack):
                packed = jnp.where(lane >= k * features, rows[k * part : (k + 1) * part, :], packed)
            outs[i * row_count + s][...] = packed.astype(jnp.bfloat16)
        start += row_count * count


def transform_kernel(pairs, load_steps, step_rows, shapes, row_count, *refs):
    position_ref, me_ref, hot_c_ref, hot_v_ref, scale_ref, cond_ref, val_ref = refs[:7]
    left_ref, right_ref, twiddle_ref = refs[7:10]
    outs = refs[10 : 10 + len(shapes) * row_count]
    rho_r, rho_i, spec, table, middle, rows = refs[10 + len(shapes) * row_count :]
    step = pl.program_id(0)
    features = 2 * pairs

    cond = dot(hot_c_ref[...], cond_ref[...])
    val = dot(hot_v_ref[...], val_ref[...]) * scale_ref[...]
    cr, ci = cond[:pairs], cond[pairs:]
    vr, vi = val[:pairs], val[pairs:]
    real = vr * cr + vi * ci
    imag = vr * ci - vi * cr
    for a in range(step_rows):
        row = pl.multiple_of((step * step_rows + a) * pairs, pairs)
        rho_r[pl.ds(row, pairs), :] = real[:, a * LANES : (a + 1) * LANES]
        rho_i[pl.ds(row, pairs), :] = imag[:, a * LANES : (a + 1) * LANES]

    def left_half(group, slot):
        members = [GROUP * group + k for k in range(GROUP)]
        data = jnp.concatenate(
            [
                jnp.concatenate([ref[pl.ds(p, ROWS, stride=pairs), :] for p in members], axis=1)
                for ref in (rho_r, rho_i)
            ],
            axis=0,
        )
        high, low = halves(data)
        mixed = dot(left_ref[...], jnp.concatenate([high, high, low], axis=0))
        mid_r, mid_i = mixed[:ROWS], mixed[ROWS:]
        tr, ti = twiddle_ref[0], twiddle_ref[1]
        turn_r = mid_r * tr - mid_i * ti
        turn_i = mid_r * ti + mid_i * tr
        for k in range(GROUP):
            lanes = slice(k * LANES, (k + 1) * LANES)
            rows_k = slice(k * ROWS, (k + 1) * ROWS)
            for z, turned in enumerate((turn_r, turn_i)):
                high, low = halves(turned[:, lanes])
                middle[slot, rows_k, z * LANES : (z + 1) * LANES] = high
                middle[slot, rows_k, (2 + z) * LANES : (3 + z) * LANES] = low

    def right_half(group, slot):
        high = middle[slot, :, : 2 * LANES]
        low = middle[slot, :, 2 * LANES :]
        by_high = dot(high, right_ref[...])
        by_low = dot(low, right_ref[:, : 2 * LANES])
        out = by_high[:, : 2 * LANES] + (by_high[:, 2 * LANES :] + by_low)
        for k in range(GROUP):
            p = GROUP * group + k
            part = out[k * ROWS : (k + 1) * ROWS]
            spec[pl.ds(p, ROWS, stride=features), :] = part[:, :LANES]
            spec[pl.ds(pairs + p, ROWS, stride=features), :] = part[:, LANES:]

    @pl.when(step == load_steps - 1)
    def _():
        groups = pairs // GROUP
        left_half(0, 0)

        def two_groups(k, carry):
            right_half(2 * k, 0)
            left_half(2 * k + 1, 1)
            right_half(2 * k + 1, 1)
            left_half(jnp.minimum(2 * k + 2, groups - 1), 0)
            return carry

        lax.fori_loop(0, groups // 2, two_groups, 0)

        def one_row(k, carry):
            start = pl.multiple_of(k * features, features)
            tile = spec[pl.ds(start, features), :].astype(jnp.bfloat16)
            tile = jnp.concatenate([tile] * (LANES // features), axis=0)
            table[pl.ds(pl.multiple_of(k * LANES, LANES), LANES), :] = tile.T.astype(jnp.float32)
            return carry

        lax.fori_loop(0, ROWS, one_row, 0, unroll=8)
        select_rows(shapes, row_count, features, position_ref, me_ref, table, rows, outs)


def transform(valence, conduction, band_pairs, scale, position, me, shapes, row_count):
    pairs = band_pairs.shape[0]
    features = 2 * pairs
    pack = LANES // features
    nvb, ncb = valence.shape[1], conduction.shape[1]
    load_steps = 8
    step_rows = ROWS // load_steps
    chunk = step_rows * LANES

    def hot(band, count):
        one = (band[:, None] == jnp.arange(count, dtype=jnp.int32)[None, :]).astype(jnp.bfloat16)
        none = jnp.zeros_like(one)
        return jnp.concatenate(
            [jnp.concatenate([one, none], axis=1), jnp.concatenate([none, one], axis=1)], axis=0
        )

    left, right, twiddle = dft_tables()
    whole = lambda shape: pl.BlockSpec(shape, lambda i, *_: (0,) * len(shape))
    loaded = lambda i, *_: (0, i)
    flops = 2 * pairs * (6 * ROWS * ROWS * 2 * LANES + 3 * ROWS * 4 * LANES * LANES)
    out_shapes = [(count // pack, LANES) for count in shapes for _ in range(row_count)]
    outs = pl.pallas_call(
        lambda *refs: transform_kernel(pairs, load_steps, step_rows, shapes, row_count, *refs),
        grid_spec=pltpu.PrefetchScalarGridSpec(
            num_scalar_prefetch=2,
            grid=(load_steps,),
            in_specs=[
                whole((2 * pairs, 2 * ncb)),
                whole((2 * pairs, 2 * nvb)),
                whole((2 * pairs, 1)),
                pl.BlockSpec((2 * ncb, chunk), loaded),
                pl.BlockSpec((2 * nvb, chunk), loaded),
                whole(left.shape),
                whole(right.shape),
                whole(twiddle.shape),
            ],
            out_specs=[whole(shape) for shape in out_shapes],
            scratch_shapes=[
                pltpu.VMEM((ROWS * pairs, LANES), jnp.float32),
                pltpu.VMEM((ROWS * pairs, LANES), jnp.float32),
                pltpu.VMEM((ROWS * features, LANES), jnp.float32),
                pltpu.VMEM((NR, LANES), jnp.float32),
                pltpu.VMEM((2, GROUP * ROWS, 4 * LANES), jnp.bfloat16),
                pltpu.VMEM((max(shapes), LANES), jnp.float32),
            ],
        ),
        out_shape=[jax.ShapeDtypeStruct(shape, jnp.bfloat16) for shape in out_shapes],
        compiler_params=pltpu.CompilerParams(vmem_limit_bytes=VMEM_LIMIT),
        cost_estimate=pl.CostEstimate(flops=flops, bytes_accessed=40_000_000, transcendentals=0),
        name="transform",
    )(
        position,
        me,
        hot(band_pairs[:, 1], ncb),
        hot(band_pairs[:, 0], nvb),
        jnp.concatenate([scale, scale])[:, None],
        conduction.reshape(2 * ncb, NR),
        valence.reshape(2 * nvb, NR),
        jnp.asarray(left),
        jnp.asarray(right),
        jnp.asarray(twiddle),
    )
    return [outs[i * row_count : (i + 1) * row_count] for i in range(len(shapes))]


def assemble_kernel(row_count, features, me_ref, *rest):
    parts, out_ref, held = rest[:row_count], rest[row_count], rest[row_count + 1]
    pack = LANES // features
    part = parts[0].shape[0]
    lane = lax.broadcasted_iota(jnp.int32, (part, LANES), 1)
    for s in range(row_count):
        held[s] = parts[s][...].astype(jnp.float32)
    for b in range(row_count // pack):
        for k in range(pack):
            block = None
            for q in range(pack):
                piece = held[(b * pack + q) ^ me_ref[0]]
                if q != k:
                    piece = pltpu.roll(piece, (q - k) * features % LANES, 1)
                block = piece if block is None else jnp.where(lane >= q * features, piece, block)
            out_ref[k * part : (k + 1) * part, b * LANES : (b + 1) * LANES] = block.astype(
                jnp.bfloat16
            )


def assemble(parts, me, features):
    row_count = len(parts)
    pack = LANES // features
    part = parts[0].shape[0]
    return pl.pallas_call(
        lambda *refs: assemble_kernel(row_count, features, *refs),
        grid_spec=pltpu.PrefetchScalarGridSpec(
            num_scalar_prefetch=1,
            grid=(),
            in_specs=[pl.BlockSpec(memory_space=pltpu.VMEM)] * row_count,
            out_specs=pl.BlockSpec(memory_space=pltpu.VMEM),
            scratch_shapes=[pltpu.VMEM((row_count, part, LANES), jnp.float32)],
        ),
        out_shape=jax.ShapeDtypeStruct((part * pack, row_count * features), jnp.bfloat16),
        compiler_params=pltpu.CompilerParams(vmem_limit_bytes=VMEM_LIMIT),
        cost_estimate=pl.CostEstimate(flops=0, bytes_accessed=2_000_000, transcendentals=0),
        name="assemble",
    )(me, *parts)


def spans(shares, step):
    found, start = [], 0
    for share in shares:
        found.append((start, share // step))
        start += share // step
    return found


def clipped(span, offset=0):
    return lambda i: offset + jnp.clip(i - span[0], 0, span[1] - 1)


def flip_kernel(slot_count, found, part_ref, *refs):
    out_ref = refs[-1]
    tile = pl.program_id(0)
    for k, (start, count) in enumerate(found):

        @pl.when((tile >= start) & (tile < start + count))
        def _():
            for s in range(slot_count):
                values = refs[k * slot_count + s][...]
                width = values.shape[1]
                out_ref[s * width : (s + 1) * width, :] = (
                    values.astype(jnp.float32).T.astype(jnp.bfloat16)
                )


def flip(chunks, shares, part, unit):
    slot_count = len(chunks[0])
    width = chunks[0][0].shape[1]
    found = spans(shares, 1)
    steps = sum(shares)

    def pick(span, share):
        place = clipped(span)
        return lambda t, part_ref: (part_ref[0] * share + place(t), 0)

    return pl.pallas_call(
        lambda *refs: flip_kernel(slot_count, found, *refs),
        grid_spec=pltpu.PrefetchScalarGridSpec(
            num_scalar_prefetch=1,
            grid=(steps,),
            in_specs=[
                pl.BlockSpec((unit, width), pick(span, share))
                for span, share in zip(found, shares)
                for _ in range(slot_count)
            ],
            out_specs=pl.BlockSpec((slot_count * width, unit), lambda t, part_ref: (0, t)),
        ),
        out_shape=jax.ShapeDtypeStruct((slot_count * width, steps * unit), jnp.bfloat16),
        compiler_params=pltpu.CompilerParams(vmem_limit_bytes=VMEM_LIMIT),
        cost_estimate=pl.CostEstimate(
            flops=0, bytes_accessed=8 * slot_count * width * steps * unit, transcendentals=0
        ),
        name="flip",
    )(part, *[slot for chunk in chunks for slot in chunk])


def settle_kernel(pairs, take_ref, kept_ref, arrived_ref, out_ref):
    values = jnp.where(take_ref[0] != 0, arrived_ref[...], kept_ref[...]).astype(jnp.float32)
    rows, across = values.shape
    out_ref[0] = (-values).astype(jnp.bfloat16)
    values = values.reshape(rows // (2 * pairs), 2, pairs, across)
    turned = jnp.stack([-values[:, 1], values[:, 0]], axis=1)
    out_ref[1] = turned.reshape(rows, across).astype(jnp.bfloat16)


def settle(take, kept, arrived, pairs):
    rows, across = kept.shape
    tile = math.gcd(rows, 256)
    return pl.pallas_call(
        lambda *refs: settle_kernel(pairs, *refs),
        grid_spec=pltpu.PrefetchScalarGridSpec(
            num_scalar_prefetch=1,
            grid=(rows // tile,),
            in_specs=[pl.BlockSpec((tile, across), lambda t, _: (t, 0))] * 2,
            out_specs=pl.BlockSpec((2, tile, across), lambda t, _: (0, t, 0)),
        ),
        out_shape=jax.ShapeDtypeStruct((2, rows, across), jnp.bfloat16),
        compiler_params=pltpu.CompilerParams(vmem_limit_bytes=VMEM_LIMIT),
        cost_estimate=pl.CostEstimate(
            flops=0, bytes_accessed=8 * rows * across, transcendentals=0
        ),
        name="settle",
    )(take, kept, arrived)


def contract_kernel(slot_count, found, right_count, alias, add, *refs):
    chunks = len(found)
    rights = refs[chunks * slot_count : chunks * slot_count + right_count]
    out_ref = refs[-1]
    row = pl.program_id(1)
    for k, (start, count) in enumerate(found):

        @pl.when((row >= start) & (row < start + count))
        def _():
            slots = refs[k * slot_count : (k + 1) * slot_count]
            parts, depth, width = slots[0].shape
            left = jnp.concatenate(
                [slot[...].reshape(parts * depth, width) for slot in slots], axis=1
            )
            for z in range(2):
                right = jnp.concatenate([ref[z] for ref in rights], axis=0)
                total = dot(left, right).reshape(out_ref.shape[1:])
                out_ref[z] = total + refs[-2][z] if add else total


def contract(result, lefts, shares, rights, unit, row_units, column_units, first, steps, add):
    parts, _, width = lefts[0][0].shape
    slot_count = len(lefts[0])
    found = spans(shares, row_units)
    row_steps = sum(shares) // row_units
    depth, side = slot_count * width, sum(shares) * unit
    rows, columns = row_units * unit, column_units * unit
    alias = 0 if result is None else 1
    block = pl.BlockSpec((2, parts, rows, columns), lambda c, r: (0, 0, r, first + c))
    flops = 8 * parts * side * steps * columns * depth
    in_specs = [
        pl.BlockSpec((parts, rows, width), lambda c, r, f=clipped(span): (0, f(r), 0))
        for span in found
        for _ in range(slot_count)
    ]
    in_specs += [
        pl.BlockSpec((2, right.shape[1], columns), lambda c, r: (0, 0, first + c))
        for right in rights
    ]
    if alias:
        in_specs.append(block if add else pl.BlockSpec(memory_space=pl.ANY))
    arrays = [slot for chunk in lefts for slot in chunk] + list(rights)
    return pl.pallas_call(
        lambda *refs: contract_kernel(slot_count, found, len(rights), alias, add, *refs),
        grid=(steps, row_steps),
        in_specs=in_specs,
        out_specs=block,
        out_shape=jax.ShapeDtypeStruct((2, parts, side, side), jnp.float32),
        input_output_aliases={len(arrays): 0} if alias else {},
        compiler_params=pltpu.CompilerParams(vmem_limit_bytes=VMEM_LIMIT),
        cost_estimate=pl.CostEstimate(
            flops=flops, bytes_accessed=flops // depth * (2 if add else 1), transcendentals=0
        ),
        name="contract",
    )(*arrays, *([result] if alias else []))


def energy_gaps(valence_energy, conduction_energy, band_pairs):
    valence_hot = (
        band_pairs[:, 0][:, None] == jnp.arange(valence_energy.shape[0], dtype=jnp.int32)[None, :]
    )
    conduction_hot = (
        band_pairs[:, 1][:, None]
        == jnp.arange(conduction_energy.shape[0], dtype=jnp.int32)[None, :]
    )
    return jnp.sum(jnp.where(valence_hot, valence_energy[None, :], 0.0), axis=1) - jnp.sum(
        jnp.where(conduction_hot, conduction_energy[None, :], 0.0), axis=1
    )


def after(value, *others):
    return lax.optimization_barrier((value,) + others)[0]


def body(valence, conduction, valence_energy, conduction_energy, band_pairs, grid_index):
    rows, cols = lax.axis_size("row"), lax.axis_size("col")
    row, col = lax.axis_index("row"), lax.axis_index("col")
    pairs = band_pairs.shape[0]
    features = 2 * pairs
    width = rows * features
    block = grid_index.shape[0] // cols
    parts = cols // rows
    unit = block // EIGHTHS
    me = row.astype(jnp.int32).reshape(1)
    my_part = (col % parts).astype(jnp.int32).reshape(1)
    owner = col // parts

    order = list(range(0, cols, 2)) + list(range(1, cols, 2))[::-1]
    ring_up = [(order[q], order[(q + 1) % cols]) for q in range(cols)]
    ring_down = [(b, a) for a, b in ring_up]
    my_place = jnp.asarray(np.argsort(np.array(order)), jnp.int32)[col]
    half = cols // 2
    offsets = [0]
    for t in range(1, half):
        offsets += [-t, t]
    offsets.append(half)
    sources = jnp.asarray(np.array(order), jnp.int32)[
        (my_place + jnp.asarray(np.array(offsets), jnp.int32)) % cols
    ]

    gap = energy_gaps(valence_energy, conduction_energy, band_pairs)
    scale = jnp.sqrt(-2.0 / (math.sqrt(pairs * rows * cols) * gap))

    shares = [share for _, share in CHUNKS]
    position = table_position(grid_index).reshape(rows, parts, EIGHTHS, unit)
    position = jnp.concatenate(
        [position[:, :, first : first + share].reshape(-1) for first, share in CHUNKS]
    )
    counts = [parts * share * unit for share in shares]
    sent = transform(valence, conduction, band_pairs, scale, position, me, counts, rows)

    def go_round(below, above):
        return [lax.ppermute(below, "col", ring_up), lax.ppermute(above, "col", ring_down)]

    slots = [[] for _ in range(half)]
    ahead = []
    for i in range(len(CHUNKS)):
        parcels = [after(sent[i][s], *ahead) if ahead else sent[i][s] for s in range(rows)]
        got = parcels[:1] + [
            lax.ppermute(parcels[s], "row", [(r, r ^ s) for r in range(rows)])
            for s in range(1, rows)
        ]
        own = assemble(got, me, features)
        slots[0].append([own])
        if i:
            own = after(own, *slots[1][i - 1])
            slots[1][i - 1] = [after(block, *got) for block in slots[1][i - 1]]
        slots[1].append(go_round(own, own))
        ahead = [own]
    for t in range(2, half):
        for i in range(len(CHUNKS)):
            slots[t].append(go_round(*slots[t - 1][i]))

    def send_column(kept):
        holders, step = [0], rows // 2
        while step:
            perm = [
                ((c // parts ^ h) * cols + c, (c // parts ^ h ^ step) * cols + c)
                for c in range(cols)
                for h in holders
            ]
            arrived = lax.ppermute(kept, ("row", "col"), perm)
            take = (row ^ owner) & step != 0
            if step > 1:
                kept = jnp.where(take, arrived, kept)
            holders += [h ^ step for h in holders]
            step //= 2
        return settle(take.astype(jnp.int32).reshape(1), kept, arrived, pairs)

    def gathered(times):
        return [sum([slots[t][k] for t in times], []) for k in range(len(CHUNKS))]

    def column(times, *before):
        group = gathered(times)
        if before:
            group[0] = [after(group[0][0], *before)] + group[0][1:]
        return send_column(flip(group, shares, my_part, unit))

    def contract_times(result, times, rights, row_units, column_units, first, steps, add):
        lefts = [
            [slot.reshape(parts, share * unit, width) for slot in chunk]
            for chunk, share in zip(gathered(times), shares)
        ]
        return contract(
            result, lefts, shares, rights, unit, row_units, column_units, first, steps, add
        )

    early, late = list(range(half // 2 + 1)), list(range(half // 2 + 1, half + 1))
    rights = [column([0, 1], *slots[half - 1][0])] + [column([t]) for t in early[2:]]
    results = [None]
    for first in range(4):
        results.append(contract_times(results[-1], early, rights, 2, 2, first, 1, False))

    slots.append([])
    for k in range(len(CHUNKS)):
        up, down = slots[half - 1][k][0], slots[half - 1][k][-1]
        if k == len(CHUNKS) - 1:
            up, down = after(up, results[1]), after(down, results[1])
        cut = up.shape[0] // 2
        slots[half].append([jnp.concatenate(go_round(up[:cut], down[cut:]), axis=0)])

    rights = [column([t], results[1 + i]) for i, t in enumerate(late)]
    result = contract_times(results[-1], late, rights, 1, 4, 0, 2, True)
    return result.reshape(2, parts * block, block)


def solution(mesh):
    return jax.shard_map(
        body,
        mesh=mesh,
        in_specs=(P(), P(), P(), P(), P(("row", "col"), None), P()),
        out_specs=P(None, "row", "col"),
        check_vma=False,
    )
```

time: 505 us -> 458 us (0.907)
  blocking collectives: 69.7 us -> 0 us
  waiting for transfers between devices: 98.1 us -> 150 us
  starting transfers between devices: 63.1 us -> 43.4 us
  Pallas kernels: 246 us -> 237 us
    all_gather x1 -> x0, blocking collectives: 69.7 us -> none  [body(): weights = lax.all_gather(weight, ('row', 'col'), axis=0, tiled=True)]
    ppermute x24 -> x16, waiting for transfers between devices: 72.5 us -> 105 us  [the longest x8 70.2 us: go_round(): lax.ppermute(above, 'col', ring_down)]
    ppermute x12 -> x8, starting transfers between devices: 32.9 us -> 21.8 us  [send_column(): arrived = lax.ppermute(kept, ('row', 'col'), perm)]
    ppermute x12 -> x8, waiting for transfers between devices: 10.5 us -> 20.6 us  [send_column(): arrived = lax.ppermute(kept, ('row', 'col'), perm)]
    ppermute x9 -> x6, waiting for transfers between devices: 15.1 us -> 25 us  [body(): lax.ppermute(parcels[s], 'row', [(r, r ^ s) for r in range(rows)])]
    ppermute x24 -> x16, starting transfers between devices: 24.6 us -> 16.7 us  [the longest x8 9.9 us: go_round(): lax.ppermute(below, 'col', ring_up)]
    pallas_call x1, Pallas kernels: 64.7 us -> 59.6 us  [transform(): pl.pallas_call(lambda *refs: transform_kernel(pairs, load_steps, step_row...]
    pallas_call x20 -> x13, Pallas kernels: 174 us -> 172 us  [the longest x5 129 us: contract(): pl.pallas_call(lambda *refs: contract_kernel(slot_count, found, len(right...]
  transfers between devices with their start and end apart: 45 -> 30, of which waited for: 13 -> 14; matrix products, arithmetic and copies ran while one was open for 3% -> 3% of each run, Pallas kernels for 28% -> 23%
where the time goes in v3:
time: 458 us; the launch traced here: 456 us
  Pallas kernels  237 us (52%)
  waiting for transfers between devices  150 us (33%)
  starting transfers between devices  43.4 us (9%)
  local copies, waits for them, and re-layouts  14.8 us (3%)
  other arithmetic  10.8 us (2%)
    pallas_call x5, Pallas kernels, contract(): pl.pallas_call(lambda *refs: contract_kernel(slot_count, found, len(right...  129 us
    ppermute x8, waiting for transfers between devices, go_round(): lax.ppermute(above, 'col', ring_down)  70.2 us
    pallas_call x1, Pallas kernels, transform(): pl.pallas_call(lambda *refs: transform_kernel(pairs, load_steps, step_row...  59.6 us
    ppermute x8, waiting for transfers between devices, go_round(): lax.ppermute(below, 'col', ring_up)  34.4 us
    pallas_call x4, Pallas kernels, flip(): pl.pallas_call(lambda *refs: flip_kernel(slot_count, found, *refs), grid_...  25 us
    ppermute x6, waiting for transfers between devices, body(): lax.ppermute(parcels[s], 'row', [(r, r ^ s) for r in range(rows)])  25 us
    ppermute x8, starting transfers between devices, send_column(): arrived = lax.ppermute(kept, ('row', 'col'), perm)  21.8 us
    ppermute x8, waiting for transfers between devices, send_column(): arrived = lax.ppermute(kept, ('row', 'col'), perm)  20.6 us
  transfers between devices with their start and end apart: 30, of which 14 were waited for; matrix products, arithmetic and copies ran while one was open for 3% of the time, Pallas kernels for 23%

profile of v3, /device:TPU:0, one launch (start us, length us, event | category | flops | bytes accessed | tf_op | source)
XLA Modules:
  0.0 455.9 jit_solution(12217723081748729702)
XLA Ops:
  6.4 59.6 %transform.1 = (bf16[512,128]{1,0:T(8,128)(2,1)}, bf16[512,128]{1,0:T(8,128)(2,1)}, bf16[512,128]{1,0:T(8,128)(2,1)}, bf16[512,128]{1,0:T(8,128)(2,1)}, bf16[153...) custom-call(s32[16384]{0:T(1024)} %pad_add_fusion.refs_0_, ...), custom_call_target="tpu_custom_call" | custom-call | flops 9663676416 | bytes 40000000 | tf_op jit(solution)/shard_map/transform/pallas_call | solution.py:207
  69.1 4.5 collective-permute-done.1.refs_3_
  82.6 9.7 %collective-permute-done.6.refs_4_ = bf16[1536,128]{1,0:T(8,128)(2,1)S(1)} collective-permute-done((bf16[1536,128]{1,0:T(8,128)(2,1)}, bf16[1536,128]{1,0:T(8,128)(2,1)S(1)}, u32[]{:S(2)}, u32[]{:S(2)}) %collective-permute-start.6) | collective-permute-done | bytes 393248 | tf_op jit(solution)/shard_map/ppermute | solution.py:497
  92.3 8.5 %collective-permute-done.5.refs_3_ = bf16[1536,128]{1,0:T(8,128)(2,1)S(1)} collective-permute-done((bf16[1536,128]{1,0:T(8,128)(2,1)}, bf16[1536,128]{1,0:T(8,128)(2,1)S(1)}, u32[]{:S(2)}, u32[]{:S(2)}) %collective-permute-start.5) | collective-permute-done | bytes 393248 | tf_op jit(solution)/shard_map/ppermute | solution.py:497
  109.6 45.3 %collective-permute-done.10.refs_2_ = bf16[1024,256]{1,0:T(8,128)(2,1)} collective-permute-done((bf16[1024,256]{1,0:T(8,128)(2,1)S(1)}, bf16[1024,256]{1,0:T(8,128)(2,1)}, u32[]{:S(2)}, u32[]{:S(2)}) %collective-permute-start.10) | collective-permute-done | bytes 524320 | tf_op jit(solution)/shard_map/ppermute | solution.py:490
  156.9 11.1 %collective-permute-done.11.refs_2_ = bf16[1024,256]{1,0:T(8,128)(2,1)} collective-permute-done((bf16[1024,256]{1,0:T(8,128)(2,1)}, bf16[1024,256]{1,0:T(8,128)(2,1)}, u32[]{:S(2)}, u32[]{:S(2)}) %collective-permute-start.11) | collective-permute-done | bytes 524320 | tf_op jit(solution)/shard_map/ppermute | solution.py:490
  169.7 6.8 %flip.4 = bf16[768,2048]{1,0:T(8,128)(2,1)} custom-call(s32[1]{0:T(128)} %bitcast.22.refs_0_, bf16[1024,256]{1,0:T(8,128)(2,1)} %assemble.2.refs_1_, bf16[1024,256]{1,0:T(8,128)(2,1)} %copy-done.6, bf16[1024,256]{1,0:T(8,128)(2,1)} %copy-done.7, bf16[3072,256]{1,0:T(8,128)(2,1)} %assemble.3.refs_4_, bf16[3072,256]{1,0:T(8,128)(2,1)} %copy-done, ...), custom_call_target="tpu_custom_call" | custom-call | bytes 12582912 | tf_op jit(solution)/shard_map/flip/pallas_call | solution.py:328
  176.5 4.9 %collective-permute-start.20 = (bf16[768,2048]{1,0:T(8,128)(2,1)}, bf16[768,2048]{1,0:T(8,128)(2,1)}, u32[]{:S(2)}, u32[]{:S(2)}) collective-permute-start(bf16[768,2048]{1,0:T(8,128)(2,1)} %flip.4), channel_id=1, source_target_pairs={{0,16},{1,17},{10,26},{11,27},{20,4},{21,5},{30,14},{31,15}} | collective-permute-start | bytes 9437192 | tf_op jit(solution)/shard_map/ppermute | solution.py:519
  183.5 31.3 %collective-permute-done.15.refs_3_ = bf16[3072,256]{1,0:T(8,128)(2,1)S(1)} collective-permute-done((bf16[3072,256]{1,0:T(8,128)(2,1)}, bf16[3072,256]{1,0:T(8,128)(2,1)S(1)}, u32[]{:S(2)}, u32[]{:S(2)}) %collective-permute-start.15) | collective-permute-done | bytes 1572896 | tf_op jit(solution)/shard_map/ppermute | solution.py:490
  218.1 6.4 %flip.5 = bf16[512,2048]{1,0:T(8,128)(2,1)} custom-call(s32[1]{0:T(128)} %bitcast.22.refs_0_, bf16[1024,256]{1,0:T(8,128)(2,1)} %collective-permute-done.7.refs_1_, bf16[1024,256]{1,0:T(8,128)(2,1)} %collective-permute-done.10.refs_2_, bf16[3072,256]{1,0:T(8,128)(2,1)} %copy-done.2, bf16[3072,256]{1,0:T(8,128)(2,1)} %copy-done.4), custom_call_target="tpu_custom_call" | custom-call | bytes 8388608 | tf_op jit(solution)/shard_map/flip/pallas_call | solution.py:328
  227.1 4.0 broadcast_select_fusion.refs_1_
  234.1 15.4 %collective-permute-done.22 = bf16[512,2048]{1,0:T(8,128)(2,1)} collective-permute-done((bf16[512,2048]{1,0:T(8,128)(2,1)}, bf16[512,2048]{1,0:T(8,128)(2,1)}, u32[]{:S(2)}, u32[]{:S(2)}) %collective-permute-start.22) | collective-permute-done | bytes 2097184 | tf_op jit(solution)/shard_map/ppermute | solution.py:519
  263.2 7.5 %collective-permute-done.13 = bf16[512,256]{1,0:T(8,128)(2,1)S(1)} collective-permute-done((bf16[512,256]{1,0:T(8,128)(2,1)}, bf16[512,256]{1,0:T(8,128)(2,1)S(1)}, u32[]{:S(2)}, u32[]{:S(2)}) %collective-permute-start.13) | collective-permute-done | bytes 262176 | tf_op jit(solution)/shard_map/ppermute | solution.py:490
  272.8 3.8 settle.5.refs_11_
  276.6 6.5 %settle.4.refs_10_ = bf16[2,768,2048]{2,1,0:T(8,128)(2,1)} custom-call(s32[1]{0:T(128)} %bitcast.21.refs_0_, bf16[768,2048]{1,0:T(8,128)(2,1)} %broadcast_select_fusion.refs_1_, bf16[768,2048]{1,0:T(8,128)(2,1)} %collective-permute-done.21.refs_2_), custom_call_target="tpu_custom_call" | custom-call | bytes 12582912 | tf_op jit(solution)/shard_map/settle/pallas_call | solution.py:361
  283.1 17.3 %contract.5.refs_12_ = f32[2,2,2048,2048]{3,2,1,0:T(8,128)} custom-call(bf16[2,512,256]{2,1,0:T(8,128)(2,1)} %bitcast.50, bf16[2,512,256]{2,1,0:T(8,128)(2,1)} %bitcast.54, bf16[2,512,256]{2,1,0:T(8,128)(2,1)} %bitcast.58, bf16[2,512,256]{2,1,0:T(8,128)(2,1)} %bitcast.14.refs_3_, bf16[2,512,256]{2,1,0:T(8,128)(2,1)} %bitcast.15.refs_4_, ...), custom_call_target="tpu_custom_call" | custom-call | flops 21474836480 | bytes 16777216 | tf_op jit(solution)/shard_map/contract/pallas_call | solution.py:420
  300.4 4.3 collective-permute-done.19.refs_4_
  308.8 17.3 %contract.6.refs_12_ = f32[2,2,2048,2048]{3,2,1,0:T(8,128)} custom-call(bf16[2,512,256]{2,1,0:T(8,128)(2,1)} %bitcast.51, bf16[2,512,256]{2,1,0:T(8,128)(2,1)} %bitcast.55, bf16[2,512,256]{2,1,0:T(8,128)(2,1)} %bitcast.59, bf16[2,512,256]{2,1,0:T(8,128)(2,1)} %bitcast.14.refs_3_, ...), custom_call_target="tpu_custom_call", output_to_operand_aliasing={{}: (12, {})} | custom-call | flops 21474836480 | bytes 16777216 | tf_op jit(solution)/shard_map/contract/pallas_call | solution.py:420
  326.1 6.3 %flip.6 = bf16[512,2048]{1,0:T(8,128)(2,1)} custom-call(s32[1]{0:T(128)} %bitcast.22.refs_0_, bf16[1024,256]{1,0:T(8,128)(2,1)} %collective-permute-done.8.refs_1_, bf16[1024,256]{1,0:T(8,128)(2,1)} %collective-permute-done.11.refs_2_, bf16[3072,256]{1,0:T(8,128)(2,1)} %collective-permute-done.16.refs_3_, bf16[3072,256]{1,0:T(8,128)(2,1)} %copy-done.13), custom_call_target="tpu_custom_call" | custom-call | bytes 8388608 | tf_op jit(solution)/shard_map/flip/pallas_call | solution.py:328
  336.3 5.6 %flip.7 = bf16[256,2048]{1,0:T(8,128)(2,1)} custom-call(s32[1]{0:T(128)} %bitcast.22.refs_0_, bf16[1024,256]{1,0:T(8,128)(2,1)} %copy-done.15, bf16[3072,256]{1,0:T(8,128)(2,1)} %copy-done.14), custom_call_target="tpu_custom_call" | custom-call | bytes 4194304 | tf_op jit(solution)/shard_map/flip/pallas_call | solution.py:328
  343.4 17.3 %contract.7.refs_12_ = f32[2,2,2048,2048]{3,2,1,0:T(8,128)} custom-call(bf16[2,512,256]{2,1,0:T(8,128)(2,1)} %bitcast.52, bf16[2,512,256]{2,1,0:T(8,128)(2,1)} %bitcast.56, bf16[2,512,256]{2,1,0:T(8,128)(2,1)} %bitcast.60, bf16[2,512,256]{2,1,0:T(8,128)(2,1)} %bitcast.14.refs_3_, ...), custom_call_target="tpu_custom_call", output_to_operand_aliasing={{}: (12, {})} | custom-call | flops 21474836480 | bytes 16777216 | tf_op jit(solution)/shard_map/contract/pallas_call | solution.py:420
  363.7 5.1 %collective-permute-done.28 = bf16[256,2048]{1,0:T(8,128)(2,1)S(1)} collective-permute-done((bf16[256,2048]{1,0:T(8,128)(2,1)}, bf16[256,2048]{1,0:T(8,128)(2,1)S(1)}, u32[]{:S(2)}, u32[]{:S(2)}) %collective-permute-start.28) | collective-permute-done | bytes 1048608 | tf_op jit(solution)/shard_map/ppermute | solution.py:519
  370.5 17.3 %contract.8.refs_8_ = f32[2,2,2048,2048]{3,2,1,0:T(8,128)} custom-call(bf16[2,512,256]{2,1,0:T(8,128)(2,1)} %bitcast.53, bf16[2,512,256]{2,1,0:T(8,128)(2,1)} %bitcast.57, bf16[2,512,256]{2,1,0:T(8,128)(2,1)} %bitcast.61, bf16[2,512,256]{2,1,0:T(8,128)(2,1)} %bitcast.14.refs_3_, ...), custom_call_target="tpu_custom_call", output_to_operand_aliasing={{}: (12, {})} | custom-call | flops 21474836480 | bytes 16777216 | tf_op jit(solution)/shard_map/contract/pallas_call | solution.py:420
  395.7 60.3 %contract.9 = f32[2,2,2048,2048]{3,2,1,0:T(8,128)} custom-call(bf16[2,512,256]{2,1,0:T(8,128)(2,1)} %bitcast.6.refs_0_, bf16[2,512,256]{2,1,0:T(8,128)(2,1)} %bitcast.7.refs_1_, bf16[2,512,256]{2,1,0:T(8,128)(2,1)} %bitcast.64, bf16[2,1536,256]{2,1,0:T(8,128)(2,1)} %bitcast.9.refs_3_, ...), custom_call_target="tpu_custom_call", output_to_operand_aliasing={{}: (8, {})} | custom-call | flops 51539607552 | bytes 134217728 | tf_op jit(solution)/shard_map/contract/pallas_call | solution.py:420
  (127 shorter events, 79.7 us)
Async XLA Ops:
  78.7 26.8 %collective-permute-start.3 = (bf16[1024,256]{1,0:T(8,128)(2,1)}, bf16[1024,256]{1,0:T(8,128)(2,1)S(1)}, u32[]{:S(2)}, u32[]{:S(2)}) collective-permute-start(bf16[1024,256]{1,0:T(8,128)(2,1)} %assemble.2.refs_1_), channel_id=1, source_target_pairs={{0,2},{2,4},{4,6},{6,7},{7,5},{5,3},{3,1},{1,0},{8,10},{10,12},{12... | collective-permute-start | bytes 1572872 | tf_op jit(solution)/shard_map/ppermute | solution.py:490
  80.4 25.1 %collective-permute-start.9 = (bf16[1024,256]{1,0:T(8,128)(2,1)}, bf16[1024,256]{1,0:T(8,128)(2,1)S(1)}, u32[]{:S(2)}, u32[]{:S(2)}) collective-permute-start(bf16[1024,256]{1,0:T(8,128)(2,1)} %assemble.2.refs_1_), channel_id=1, source_target_pairs={{2,0},{4,2},{6,4},{7,6},{5,7},{3,5},{1,3},{0,1},{10,8},{12,10},{14... | collective-permute-start | bytes 1572872 | tf_op jit(solution)/shard_map/ppermute | solution.py:490
  81.6 19.2 %collective-permute-start.5 = (bf16[1536,128]{1,0:T(8,128)(2,1)}, bf16[1536,128]{1,0:T(8,128)(2,1)S(1)}, u32[]{:S(2)}, u32[]{:S(2)}) collective-permute-start(bf16[1536,128]{1,0:T(8,128)(2,1)} %get-tuple-element.34), channel_id=1, source_target_pairs={{0,16},{8,24},{16,0},{24,8},{1,17},{9,25},{17,1},{25,9},{2,18},{10... | collective-permute-start | bytes 1179656 | tf_op jit(solution)/shard_map/ppermute | solution.py:497
  82.3 18.5 %collective-permute-start.4 = (bf16[1536,128]{1,0:T(8,128)(2,1)}, bf16[1536,128]{1,0:T(8,128)(2,1)S(1)}, u32[]{:S(2)}, u32[]{:S(2)}) collective-permute-start(bf16[1536,128]{1,0:T(8,128)(2,1)} %get-tuple-element.32), channel_id=1, source_target_pairs={{0,8},{8,0},{16,24},{24,16},{1,9},{9,1},{17,25},{25,17},{2,10},{10... | collective-permute-start | bytes 1179656 | tf_op jit(solution)/shard_map/ppermute | solution.py:497
  105.5 62.5 %collective-permute-start.14 = (bf16[3072,256]{1,0:T(8,128)(2,1)}, bf16[3072,256]{1,0:T(8,128)(2,1)S(1)}, u32[]{:S(2)}, u32[]{:S(2)}) collective-permute-start(bf16[3072,256]{1,0:T(8,128)(2,1)} %assemble.3.refs_4_), channel_id=1, source_target_pairs={{0,2},{2,4},{4,6},{6,7},{7,5},{5,3},{3,1},{1,0},{8,10},{10,12},{12... | collective-permute-start | bytes 4718600 | tf_op jit(solution)/shard_map/ppermute | solution.py:490
  107.2 60.8 %collective-permute-start.17 = (bf16[3072,256]{1,0:T(8,128)(2,1)}, bf16[3072,256]{1,0:T(8,128)(2,1)S(1)}, u32[]{:S(2)}, u32[]{:S(2)}) collective-permute-start(bf16[3072,256]{1,0:T(8,128)(2,1)} %assemble.3.refs_4_), channel_id=1, source_target_pairs={{2,0},{4,2},{6,4},{7,6},{5,7},{3,5},{1,3},{0,1},{10,8},{12,10},{14... | collective-permute-start | bytes 4718600 | tf_op jit(solution)/shard_map/ppermute | solution.py:490
  107.6 47.3 %collective-permute-start.10 = (bf16[1024,256]{1,0:T(8,128)(2,1)S(1)}, bf16[1024,256]{1,0:T(8,128)(2,1)}, u32[]{:S(2)}, u32[]{:S(2)}) collective-permute-start(bf16[1024,256]{1,0:T(8,128)(2,1)S(1)} %collective-permute-done.9.refs_3_), channel_id=1, source_target_pairs={{2,0},{4,2},{6,4},{7,6},{5,7},{3,5},{1,3},{0,1},{10,8},{12,10},{14... | collective-permute-start | bytes 1572872 | tf_op jit(solution)/shard_map/ppermute | solution.py:490
  109.1 46.1 %collective-permute-start.7 = (bf16[1024,256]{1,0:T(8,128)(2,1)S(1)}, bf16[1024,256]{1,0:T(8,128)(2,1)}, u32[]{:S(2)}, u32[]{:S(2)}) collective-permute-start(bf16[1024,256]{1,0:T(8,128)(2,1)S(1)} %collective-permute-done.3.refs_2_), channel_id=1, source_target_pairs={{0,2},{2,4},{4,6},{6,7},{7,5},{5,3},{3,1},{1,0},{8,10},{10,12},{12... | collective-permute-start | bytes 1572872 | tf_op jit(solution)/shard_map/ppermute | solution.py:490
  154.9 13.1 %collective-permute-start.11 = (bf16[1024,256]{1,0:T(8,128)(2,1)}, bf16[1024,256]{1,0:T(8,128)(2,1)}, u32[]{:S(2)}, u32[]{:S(2)}) collective-permute-start(bf16[1024,256]{1,0:T(8,128)(2,1)} %collective-permute-done.10.refs_2_), channel_id=1, source_target_pairs={{2,0},{4,2},{6,4},{7,6},{5,7},{3,5},{1,3},{0,1},{10,8},{12,10},{14... | collective-permute-start | bytes 1572872 | tf_op jit(solution)/shard_map/ppermute | solution.py:490
  176.5 50.6 %collective-permute-start.20 = (bf16[768,2048]{1,0:T(8,128)(2,1)}, bf16[768,2048]{1,0:T(8,128)(2,1)}, u32[]{:S(2)}, u32[]{:S(2)}) collective-permute-start(bf16[768,2048]{1,0:T(8,128)(2,1)} %flip.4), channel_id=1, source_target_pairs={{0,16},{1,17},{10,26},{11,27},{20,4},{21,5},{30,14},{31,15}} | collective-permute-start | bytes 9437192 | tf_op jit(solution)/shard_map/ppermute | solution.py:519
  181.4 33.3 %collective-permute-start.15 = (bf16[3072,256]{1,0:T(8,128)(2,1)}, bf16[3072,256]{1,0:T(8,128)(2,1)S(1)}, u32[]{:S(2)}, u32[]{:S(2)}) collective-permute-start(bf16[3072,256]{1,0:T(8,128)(2,1)} %copy-done), channel_id=1, source_target_pairs={{0,2},{2,4},{4,6},{6,7},{7,5},{5,3},{3,1},{1,0},{8,10},{10,12},{12... | collective-permute-start | bytes 4718600 | tf_op jit(solution)/shard_map/ppermute | solution.py:490
  181.4 35.4 %collective-permute-start.18 = (bf16[3072,256]{1,0:T(8,128)(2,1)}, bf16[3072,256]{1,0:T(8,128)(2,1)S(1)}, u32[]{:S(2)}, u32[]{:S(2)}) collective-permute-start(bf16[3072,256]{1,0:T(8,128)(2,1)} %copy-done.1), channel_id=1, source_target_pairs={{2,0},{4,2},{6,4},{7,6},{5,7},{3,5},{1,3},{0,1},{10,8},{12,10},{14... | collective-permute-start | bytes 4718600 | tf_op jit(solution)/shard_map/ppermute | solution.py:490
  224.4 25.1 %collective-permute-start.22 = (bf16[512,2048]{1,0:T(8,128)(2,1)}, bf16[512,2048]{1,0:T(8,128)(2,1)}, u32[]{:S(2)}, u32[]{:S(2)}) collective-permute-start(bf16[512,2048]{1,0:T(8,128)(2,1)} %flip.5), channel_id=1, source_target_pairs={{0,16},{1,17},{10,26},{11,27},{20,4},{21,5},{30,14},{31,15}} | collective-permute-start | bytes 6291464 | tf_op jit(solution)/shard_map/ppermute | solution.py:519
  231.1 45.5 %collective-permute-start.21 = (bf16[768,2048]{1,0:T(8,128)(2,1)}, bf16[768,2048]{1,0:T(8,128)(2,1)}, u32[]{:S(2)}, u32[]{:S(2)}) collective-permute-start(bf16[768,2048]{1,0:T(8,128)(2,1)} %broadcast_select_fusion.refs_1_), channel_id=1, source_target_pairs={{0,8},{16,24},{1,9},{17,25},{10,2},{26,18},{11,3},{27,19},{20,28},... | collective-permute-start | bytes 9437192 | tf_op jit(solution)/shard_map/ppermute | solution.py:519
  251.2 21.7 %collective-permute-start.23 = (bf16[512,2048]{1,0:T(8,128)(2,1)}, bf16[512,2048]{1,0:T(8,128)(2,1)}, u32[]{:S(2)}, u32[]{:S(2)}) collective-permute-start(bf16[512,2048]{1,0:T(8,128)(2,1)} %broadcast_select_fusion.2.refs_1_), channel_id=1, source_target_pairs={{0,8},{16,24},{1,9},{17,25},{10,2},{26,18},{11,3},{27,19},{20,28},... | collective-permute-start | bytes 6291464 | tf_op jit(solution)/shard_map/ppermute | solution.py:519
  257.3 13.4 %collective-permute-start.13 = (bf16[512,256]{1,0:T(8,128)(2,1)}, bf16[512,256]{1,0:T(8,128)(2,1)S(1)}, u32[]{:S(2)}, u32[]{:S(2)}) collective-permute-start(bf16[512,256]{1,0:T(8,128)(2,1)} %slice.37), channel_id=1, source_target_pairs={{2,0},{4,2},{6,4},{7,6},{5,7},{3,5},{1,3},{0,1},{10,8},{12,10},{14... | collective-permute-start | bytes 786440 | tf_op jit(solution)/shard_map/ppermute | solution.py:490
  270.7 34.0 %collective-permute-start.19 = (bf16[3072,256]{1,0:T(8,128)(2,1)S(1)}, bf16[3072,256]{1,0:T(8,128)(2,1)S(1)}, u32[]{:S(2)}, u32[]{:S(2)}) collective-permute-start(bf16[3072,256]{1,0:T(8,128)(2,1)S(1)} %copy-done.5), channel_id=1, source_target_pairs={{2,0},{4,2},{6,4},{7,6},{5,7},{3,5},{1,3},{0,1},{10,8},{12,10},{14... | collective-permute-start | bytes 4718600 | tf_op jit(solution)/shard_map/ppermute | solution.py:490
  270.8 33.9 %collective-permute-start.16 = (bf16[3072,256]{1,0:T(8,128)(2,1)S(1)}, bf16[3072,256]{1,0:T(8,128)(2,1)}, u32[]{:S(2)}, u32[]{:S(2)}) collective-permute-start(bf16[3072,256]{1,0:T(8,128)(2,1)S(1)} %copy-done.3), channel_id=1, source_target_pairs={{0,2},{2,4},{4,6},{6,7},{7,5},{5,3},{3,1},{1,0},{8,10},{10,12},{12... | collective-permute-start | bytes 4718600 | tf_op jit(solution)/shard_map/ppermute | solution.py:490
  304.8 30.3 %collective-permute-start.25 = (bf16[1536,256]{1,0:T(8,128)(2,1)S(1)}, bf16[1536,256]{1,0:T(8,128)(2,1)S(1)}, u32[]{:S(2)}, u32[]{:S(2)}) collective-permute-start(bf16[1536,256]{1,0:T(8,128)(2,1)S(1)} %slice.33), channel_id=1, source_target_pairs={{2,0},{4,2},{6,4},{7,6},{5,7},{3,5},{1,3},{0,1},{10,8},{12,10},{14... | collective-permute-start | bytes 2359304 | tf_op jit(solution)/shard_map/ppermute | solution.py:490
  306.5 28.6 %collective-permute-start.24 = (bf16[1536,256]{1,0:T(8,128)(2,1)S(1)}, bf16[1536,256]{1,0:T(8,128)(2,1)S(1)}, u32[]{:S(2)}, u32[]{:S(2)}) collective-permute-start(bf16[1536,256]{1,0:T(8,128)(2,1)S(1)} %slice.32), channel_id=1, source_target_pairs={{0,2},{2,4},{4,6},{6,7},{7,5},{5,3},{3,1},{1,0},{8,10},{10,12},{12... | collective-permute-start | bytes 2359304 | tf_op jit(solution)/shard_map/ppermute | solution.py:490
  332.4 28.2 %collective-permute-start.26 = (bf16[512,2048]{1,0:T(8,128)(2,1)}, bf16[512,2048]{1,0:T(8,128)(2,1)}, u32[]{:S(2)}, u32[]{:S(2)}) collective-permute-start(bf16[512,2048]{1,0:T(8,128)(2,1)} %flip.6), channel_id=1, source_target_pairs={{0,16},{1,17},{10,26},{11,27},{20,4},{21,5},{30,14},{31,15}} | collective-permute-start | bytes 6291464 | tf_op jit(solution)/shard_map/ppermute | solution.py:519
  341.9 26.9 %collective-permute-start.28 = (bf16[256,2048]{1,0:T(8,128)(2,1)}, bf16[256,2048]{1,0:T(8,128)(2,1)S(1)}, u32[]{:S(2)}, u32[]{:S(2)}) collective-permute-start(bf16[256,2048]{1,0:T(8,128)(2,1)} %flip.7), channel_id=1, source_target_pairs={{0,16},{1,17},{10,26},{11,27},{20,4},{21,5},{30,14},{31,15}} | collective-permute-start | bytes 3145736 | tf_op jit(solution)/shard_map/ppermute | solution.py:519
  360.9 31.0 %collective-permute-start.27 = (bf16[512,2048]{1,0:T(8,128)(2,1)S(1)}, bf16[512,2048]{1,0:T(8,128)(2,1)}, u32[]{:S(2)}, u32[]{:S(2)}) collective-permute-start(bf16[512,2048]{1,0:T(8,128)(2,1)S(1)} %broadcast_select_fusion.1.refs_1_), channel_id=1, source_target_pairs={{0,8},{16,24},{1,9},{17,25},{10,2},{26,18},{11,3},{27,19},{20,28},... | collective-permute-start | bytes 6291464 | tf_op jit(solution)/shard_map/ppermute | solution.py:519
  368.9 18.9 %collective-permute-start.29 = (bf16[256,2048]{1,0:T(8,128)(2,1)S(1)}, bf16[256,2048]{1,0:T(8,128)(2,1)S(1)}, u32[]{:S(2)}, u32[]{:S(2)}) collective-permute-start(bf16[256,2048]{1,0:T(8,128)(2,1)S(1)} %broadcast_select_fusion.3.refs_1_), channel_id=1, source_target_pairs={{0,8},{16,24},{1,9},{17,25},{10,2},{26,18},{11,3},{27,19},{20,28},... | collective-permute-start | bytes 3145736 | tf_op jit(solution)/shard_map/ppermute | solution.py:519
  (29 other events, 292.9 us)

commit v4 on v3

--- a/solution.py
+++ b/solution.py
@@ -18,7 +18,7 @@
 LO = N2 // HI
 ROWS = N1 * HI
 VMEM_LIMIT = 58 * 1024 * 1024
-CHUNKS = ((0, 2), (2, 6))
+CHUNKS = ((0, 4), (4, 4))
 EIGHTHS = 8
 GROUP = 4
 
@@ -79,36 +79,58 @@
     return jnp.dot(a, b, preferred_element_type=jnp.float32)
 
 
-def select_rows(shapes, row_count, features, position_ref, me_ref, table, rows, outs):
+def select_rows(count, row_count, features, position_ref, me_ref, table, rows, outs):
     pack = LANES // features
+    part = count // pack
     unroll = 32
-    start = 0
-    for i, count in enumerate(shapes):
-        part = count // pack
-        lane = lax.broadcasted_iota(jnp.int32, (part, LANES), 1)
-        for s in range(row_count):
-            base = start + (me_ref[0] ^ s) * count
-
-            def some_rows(step, carry):
-                first = step * unroll
-                for j in range(unroll):
-                    index = position_ref[base + first + j]
-                    rows[pl.ds(first + j, 1), :] = table[pl.ds(index, 1), :]
-                return carry
-
-            lax.fori_loop(0, count // unroll, some_rows, 0)
-            packed = rows[0:part, :]
-            for k in range(1, pack):
-                packed = jnp.where(lane >= k * features, rows[k * part : (k + 1) * part, :], packed)
-            outs[i * row_count + s][...] = packed.astype(jnp.bfloat16)
-        start += row_count * count
-
-
-def transform_kernel(pairs, load_steps, step_rows, shapes, row_count, *refs):
+    lane = lax.broadcasted_iota(jnp.int32, (part, LANES), 1)
+    for s in range(row_count):
+        base = (me_ref[0] ^ s) * count
+
+        def some_rows(step, carry):
+            first = step * unroll
+            for j in range(unroll):
+                index = position_ref[base + first + j]
+                rows[pl.ds(first + j, 1), :] = table[pl.ds(index, 1), :]
+            return carry
+
+        lax.fori_loop(0, count // unroll, some_rows, 0)
+        packed = rows[0:part, :]
+        for k in range(1, pack):
+            packed = jnp.where(lane >= k * features, rows[k * part : (k + 1) * part, :], packed)
+        outs[s][...] = packed.astype(jnp.bfloat16)
+
+
+def select_kernel(row_count, features, count, position_ref, me_ref, table_ref, *rest):
+    select_rows(
+        count, row_count, features, position_ref, me_ref, table_ref, rest[-1], rest[:row_count]
+    )
+
+
+def select(table, position, me, row_count, features):
+    count = position.shape[0] // row_count
+    shape = (count * features // LANES, LANES)
+    return pl.pallas_call(
+        lambda *refs: select_kernel(row_count, features, count, *refs),
+        grid_spec=pltpu.PrefetchScalarGridSpec(
+            num_scalar_prefetch=2,
+            grid=(),
+            in_specs=[pl.BlockSpec(memory_space=pltpu.VMEM)],
+            out_specs=[pl.BlockSpec(memory_space=pltpu.VMEM)] * row_count,
+            scratch_shapes=[pltpu.VMEM((count, LANES), jnp.float32)],
+        ),
+        out_shape=[jax.ShapeDtypeStruct(shape, jnp.bfloat16)] * row_count,
+        compiler_params=pltpu.CompilerParams(vmem_limit_bytes=VMEM_LIMIT),
+        cost_estimate=pl.CostEstimate(flops=0, bytes_accessed=50_000_000, transcendentals=0),
+        name="select",
+    )(position, me, table)
+
+
+def transform_kernel(pairs, load_steps, step_rows, count, row_count, *refs):
     position_ref, me_ref, hot_c_ref, hot_v_ref, scale_ref, cond_ref, val_ref = refs[:7]
     left_ref, right_ref, twiddle_ref = refs[7:10]
-    outs = refs[10 : 10 + len(shapes) * row_count]
-    rho_r, rho_i, spec, table, middle, rows = refs[10 + len(shapes) * row_count :]
+    outs = refs[10 : 10 + row_count]
+    table_ref, rho_r, rho_i, spec, table, middle, rows, sem = refs[10 + row_count :]
     step = pl.program_id(0)
     features = 2 * pairs
 
@@ -180,10 +202,14 @@
             return carry
 
         lax.fori_loop(0, ROWS, one_row, 0, unroll=8)
-        select_rows(shapes, row_count, features, position_ref, me_ref, table, rows, outs)
-
-
-def transform(valence, conduction, band_pairs, scale, position, me, shapes, row_count):
+        keep = pltpu.make_async_copy(table, table_ref, sem)
+        keep.start()
+        select_rows(count, row_count, features, position_ref, me_ref, table, rows, outs)
+        keep.wait()
+
+
+def transform(valence, conduction, band_pairs, scale, position, me, row_count):
+    count = position.shape[0] // row_count
     pairs = band_pairs.shape[0]
     features = 2 * pairs
     pack = LANES // features
@@ -203,9 +229,9 @@
     whole = lambda shape: pl.BlockSpec(shape, lambda i, *_: (0,) * len(shape))
     loaded = lambda i, *_: (0, i)
     flops = 2 * pairs * (6 * ROWS * ROWS * 2 * LANES + 3 * ROWS * 4 * LANES * LANES)
-    out_shapes = [(count // pack, LANES) for count in shapes for _ in range(row_count)]
+    out_shapes = [(count // pack, LANES)] * row_count
     outs = pl.pallas_call(
-        lambda *refs: transform_kernel(pairs, load_steps, step_rows, shapes, row_count, *refs),
+        lambda *refs: transform_kernel(pairs, load_steps, step_rows, count, row_count, *refs),
         grid_spec=pltpu.PrefetchScalarGridSpec(
             num_scalar_prefetch=2,
             grid=(load_steps,),
@@ -219,17 +245,19 @@
                 whole(right.shape),
                 whole(twiddle.shape),
             ],
-            out_specs=[whole(shape) for shape in out_shapes],
+            out_specs=[whole(shape) for shape in out_shapes] + [pl.BlockSpec(memory_space=pl.ANY)],
             scratch_shapes=[
                 pltpu.VMEM((ROWS * pairs, LANES), jnp.float32),
                 pltpu.VMEM((ROWS * pairs, LANES), jnp.float32),
                 pltpu.VMEM((ROWS * features, LANES), jnp.float32),
                 pltpu.VMEM((NR, LANES), jnp.float32),
                 pltpu.VMEM((2, GROUP * ROWS, 4 * LANES), jnp.bfloat16),
-                pltpu.VMEM((max(shapes), LANES), jnp.float32),
+                pltpu.VMEM((count, LANES), jnp.float32),
+                pltpu.SemaphoreType.DMA,
             ],
         ),
-        out_shape=[jax.ShapeDtypeStruct(shape, jnp.bfloat16) for shape in out_shapes],
+        out_shape=[jax.ShapeDtypeStruct(shape, jnp.bfloat16) for shape in out_shapes]
+        + [jax.ShapeDtypeStruct((NR, LANES), jnp.float32)],
         compiler_params=pltpu.CompilerParams(vmem_limit_bytes=VMEM_LIMIT),
         cost_estimate=pl.CostEstimate(flops=flops, bytes_accessed=40_000_000, transcendentals=0),
         name="transform",
@@ -245,7 +273,7 @@
         jnp.asarray(right),
         jnp.asarray(twiddle),
     )
-    return [outs[i * row_count : (i + 1) * row_count] for i in range(len(shapes))]
+    return outs[:row_count], outs[row_count]
 
 
 def assemble_kernel(row_count, features, me_ref, *rest):
@@ -288,82 +316,66 @@
     )(me, *parts)
 
 
-def spans(shares, step):
-    found, start = [], 0
-    for share in shares:
-        found.append((start, share // step))
-        start += share // step
-    return found
-
-
-def clipped(span, offset=0):
-    return lambda i: offset + jnp.clip(i - span[0], 0, span[1] - 1)
-
-
-def flip_kernel(slot_count, found, part_ref, *refs):
-    out_ref = refs[-1]
-    tile = pl.program_id(0)
-    for k, (start, count) in enumerate(found):
-
-        @pl.when((tile >= start) & (tile < start + count))
-        def _():
-            for s in range(slot_count):
-                values = refs[k * slot_count + s][...]
-                width = values.shape[1]
-                out_ref[s * width : (s + 1) * width, :] = (
-                    values.astype(jnp.float32).T.astype(jnp.bfloat16)
-                )
-
-
-def flip(chunks, shares, part, unit):
-    slot_count = len(chunks[0])
-    width = chunks[0][0].shape[1]
-    found = spans(shares, 1)
-    steps = sum(shares)
-
-    def pick(span, share):
-        place = clipped(span)
-        return lambda t, part_ref: (part_ref[0] * share + place(t), 0)
-
+def flip_kernel(slot_count, part_ref, *refs):
+    out_ref = refs[slot_count]
+    for s in range(slot_count):
+        width = refs[s].shape[1]
+        out_ref[s * width : (s + 1) * width, :] = refs[s][...].T
+
+
+def flip(slots, part, parts, unit):
+    slot_count = len(slots)
+    width = slots[0].shape[1]
+    depth = slots[0].shape[0] // parts
+    steps = depth // unit
     return pl.pallas_call(
-        lambda *refs: flip_kernel(slot_count, found, *refs),
+        lambda *refs: flip_kernel(slot_count, *refs),
         grid_spec=pltpu.PrefetchScalarGridSpec(
             num_scalar_prefetch=1,
             grid=(steps,),
             in_specs=[
-                pl.BlockSpec((unit, width), pick(span, share))
-                for span, share in zip(found, shares)
-                for _ in range(slot_count)
-            ],
+                pl.BlockSpec((unit, width), lambda t, part_ref: (part_ref[0] * steps + t, 0))
+            ]
+            * slot_count,
             out_specs=pl.BlockSpec((slot_count * width, unit), lambda t, part_ref: (0, t)),
         ),
-        out_shape=jax.ShapeDtypeStruct((slot_count * width, steps * unit), jnp.bfloat16),
+        out_shape=jax.ShapeDtypeStruct((slot_count * width, depth), jnp.bfloat16),
         compiler_params=pltpu.CompilerParams(vmem_limit_bytes=VMEM_LIMIT),
         cost_estimate=pl.CostEstimate(
-            flops=0, bytes_accessed=8 * slot_count * width * steps * unit, transcendentals=0
+            flops=0, bytes_accessed=8 * slot_count * width * depth, transcendentals=0
         ),
         name="flip",
-    )(part, *[slot for chunk in chunks for slot in chunk])
-
-
-def settle_kernel(pairs, take_ref, kept_ref, arrived_ref, out_ref):
-    values = jnp.where(take_ref[0] != 0, arrived_ref[...], kept_ref[...]).astype(jnp.float32)
-    rows, across = values.shape
-    out_ref[0] = (-values).astype(jnp.bfloat16)
-    values = values.reshape(rows // (2 * pairs), 2, pairs, across)
-    turned = jnp.stack([-values[:, 1], values[:, 0]], axis=1)
-    out_ref[1] = turned.reshape(rows, across).astype(jnp.bfloat16)
-
-
-def settle(take, kept, arrived, pairs):
-    rows, across = kept.shape
+    )(part, *slots)
+
+
+def settle_kernel(pairs, row_count, which_ref, *refs):
+    out_ref = refs[row_count]
+    for k in range(row_count):
+
+        @pl.when(which_ref[0] == k)
+        def _():
+            values = refs[k][...].astype(jnp.float32)
+            rows, across = values.shape
+            out_ref[0] = (-values).astype(jnp.bfloat16)
+            values = values.reshape(rows // (2 * pairs), 2, pairs, across)
+            turned = jnp.stack([-values[:, 1], values[:, 0]], axis=1)
+            out_ref[1] = turned.reshape(rows, across).astype(jnp.bfloat16)
+
+
+def settle(which, copies, pairs):
+    rows, across = copies[0].shape
     tile = math.gcd(rows, 256)
+    row_count = len(copies)
+
+    def pick(k):
+        return lambda t, which_ref: (jnp.where(which_ref[0] == k, t, 0), 0)
+
     return pl.pallas_call(
-        lambda *refs: settle_kernel(pairs, *refs),
+        lambda *refs: settle_kernel(pairs, row_count, *refs),
         grid_spec=pltpu.PrefetchScalarGridSpec(
             num_scalar_prefetch=1,
             grid=(rows // tile,),
-            in_specs=[pl.BlockSpec((tile, across), lambda t, _: (t, 0))] * 2,
+            in_specs=[pl.BlockSpec((tile, across), pick(k)) for k in range(row_count)],
             out_specs=pl.BlockSpec((2, tile, across), lambda t, _: (0, t, 0)),
         ),
         out_shape=jax.ShapeDtypeStruct((2, rows, across), jnp.bfloat16),
@@ -372,17 +384,17 @@
             flops=0, bytes_accessed=8 * rows * across, transcendentals=0
         ),
         name="settle",
-    )(take, kept, arrived)
-
-
-def contract_kernel(slot_count, found, right_count, alias, add, *refs):
-    chunks = len(found)
-    rights = refs[chunks * slot_count : chunks * slot_count + right_count]
+    )(which, *copies)
+
+
+def contract_kernel(slot_count, shares, right_count, *refs):
+    rights = refs[len(shares) * slot_count : len(shares) * slot_count + right_count]
     out_ref = refs[-1]
     row = pl.program_id(1)
-    for k, (start, count) in enumerate(found):
-
-        @pl.when((row >= start) & (row < start + count))
+    for k, share in enumerate(shares):
+        start = sum(shares[:k])
+
+        @pl.when((row >= start) & (row < start + share))
         def _():
             slots = refs[k * slot_count : (k + 1) * slot_count]
             parts, depth, width = slots[0].shape
@@ -391,42 +403,45 @@
             )
             for z in range(2):
                 right = jnp.concatenate([ref[z] for ref in rights], axis=0)
-                total = dot(left, right).reshape(out_ref.shape[1:])
-                out_ref[z] = total + refs[-2][z] if add else total
-
-
-def contract(result, lefts, shares, rights, unit, row_units, column_units, first, steps, add):
+                out_ref[z] = dot(left, right).reshape(out_ref.shape[1:])
+
+
+def contract(result, lefts, rights, unit, row_first, wide, tile_first, steps, out_first):
     parts, _, width = lefts[0][0].shape
     slot_count = len(lefts[0])
-    found = spans(shares, row_units)
-    row_steps = sum(shares) // row_units
-    depth, side = slot_count * width, sum(shares) * unit
-    rows, columns = row_units * unit, column_units * unit
+    shares = [chunk[0].shape[1] // unit for chunk in lefts]
+    depth = slot_count * width
+    columns, side = wide * unit, EIGHTHS * unit
     alias = 0 if result is None else 1
-    block = pl.BlockSpec((2, parts, rows, columns), lambda c, r: (0, 0, r, first + c))
-    flops = 8 * parts * side * steps * columns * depth
+    flops = 8 * parts * sum(shares) * unit * steps * columns * depth
+
+    def place(start, share):
+        return lambda c, r: (0, jnp.clip(r - start, 0, share - 1), 0)
+
     in_specs = [
-        pl.BlockSpec((parts, rows, width), lambda c, r, f=clipped(span): (0, f(r), 0))
-        for span in found
+        pl.BlockSpec((parts, unit, width), place(sum(shares[:k]), share))
+        for k, share in enumerate(shares)
         for _ in range(slot_count)
     ]
     in_specs += [
-        pl.BlockSpec((2, right.shape[1], columns), lambda c, r: (0, 0, first + c))
+        pl.BlockSpec((2, right.shape[1], columns), lambda c, r: (0, 0, tile_first + c))
         for right in rights
     ]
     if alias:
-        in_specs.append(block if add else pl.BlockSpec(memory_space=pl.ANY))
+        in_specs.append(pl.BlockSpec(memory_space=pl.ANY))
     arrays = [slot for chunk in lefts for slot in chunk] + list(rights)
     return pl.pallas_call(
-        lambda *refs: contract_kernel(slot_count, found, len(rights), alias, add, *refs),
-        grid=(steps, row_steps),
+        lambda *refs: contract_kernel(slot_count, shares, len(rights), *refs),
+        grid=(steps, sum(shares)),
         in_specs=in_specs,
-        out_specs=block,
+        out_specs=pl.BlockSpec(
+            (2, parts, unit, columns), lambda c, r: (0, 0, row_first + r, out_first + c)
+        ),
         out_shape=jax.ShapeDtypeStruct((2, parts, side, side), jnp.float32),
         input_output_aliases={len(arrays): 0} if alias else {},
         compiler_params=pltpu.CompilerParams(vmem_limit_bytes=VMEM_LIMIT),
         cost_estimate=pl.CostEstimate(
-            flops=flops, bytes_accessed=flops // depth * (2 if add else 1), transcendentals=0
+            flops=flops, bytes_accessed=flops // depth, transcendentals=0
         ),
         name="contract",
     )(*arrays, *([result] if alias else []))
@@ -478,86 +493,73 @@
     gap = energy_gaps(valence_energy, conduction_energy, band_pairs)
     scale = jnp.sqrt(-2.0 / (math.sqrt(pairs * rows * cols) * gap))
 
-    shares = [share for _, share in CHUNKS]
     position = table_position(grid_index).reshape(rows, parts, EIGHTHS, unit)
-    position = jnp.concatenate(
-        [position[:, :, first : first + share].reshape(-1) for first, share in CHUNKS]
-    )
-    counts = [parts * share * unit for share in shares]
-    sent = transform(valence, conduction, band_pairs, scale, position, me, counts, rows)
-
-    def go_round(below, above):
-        return [lax.ppermute(below, "col", ring_up), lax.ppermute(above, "col", ring_down)]
-
-    slots = [[] for _ in range(half)]
-    ahead = []
-    for i in range(len(CHUNKS)):
-        parcels = [after(sent[i][s], *ahead) if ahead else sent[i][s] for s in range(rows)]
-        got = parcels[:1] + [
+    positions = [
+        position[:, :, first : first + share].reshape(-1) for first, share in CHUNKS
+    ]
+    sent, table = transform(valence, conduction, band_pairs, scale, positions[0], me, rows)
+
+    def across_rows(parcels):
+        return [parcels[0]] + [
             lax.ppermute(parcels[s], "row", [(r, r ^ s) for r in range(rows)])
             for s in range(1, rows)
         ]
-        own = assemble(got, me, features)
-        slots[0].append([own])
-        if i:
-            own = after(own, *slots[1][i - 1])
-            slots[1][i - 1] = [after(block, *got) for block in slots[1][i - 1]]
-        slots[1].append(go_round(own, own))
-        ahead = [own]
+
+    def go_round(below, above):
+        return [lax.ppermute(below, "col", ring_up), lax.ppermute(above, "col", ring_down)]
+
+    def last_round(below, above):
+        cut = below.shape[0] // 2
+        return [jnp.concatenate(go_round(below[:cut], above[cut:]), axis=0)]
+
+    def column(slots, *before):
+        slots = [after(slots[0], *before)] + slots[1:] if before else slots
+        copies = [flip(slots, my_part, parts, unit)]
+        for relation in range(1, rows):
+            source = relation & (relation - 1)
+            perm = [
+                ((c // parts ^ source) * cols + c, (c // parts ^ relation) * cols + c)
+                for c in range(cols)
+            ]
+            copies.append(lax.ppermute(copies[source], ("row", "col"), perm))
+        return copies
+
+    which = (row ^ owner).astype(jnp.int32).reshape(1)
+
+    own = assemble(across_rows(sent), me, features)
+    one = [[own], go_round(own, own)]
+    sent = select(after(table, own), positions[1], me, rows, features)
+    one[1] = [after(block, *sent) for block in one[1]]
+    own = assemble(across_rows(sent), me, features)
     for t in range(2, half):
-        for i in range(len(CHUNKS)):
-            slots[t].append(go_round(*slots[t - 1][i]))
-
-    def send_column(kept):
-        holders, step = [0], rows // 2
-        while step:
-            perm = [
-                ((c // parts ^ h) * cols + c, (c // parts ^ h ^ step) * cols + c)
-                for c in range(cols)
-                for h in holders
-            ]
-            arrived = lax.ppermute(kept, ("row", "col"), perm)
-            take = (row ^ owner) & step != 0
-            if step > 1:
-                kept = jnp.where(take, arrived, kept)
-            holders += [h ^ step for h in holders]
-            step //= 2
-        return settle(take.astype(jnp.int32).reshape(1), kept, arrived, pairs)
-
-    def gathered(times):
-        return [sum([slots[t][k] for t in times], []) for k in range(len(CHUNKS))]
-
-    def column(times, *before):
-        group = gathered(times)
-        if before:
-            group[0] = [after(group[0][0], *before)] + group[0][1:]
-        return send_column(flip(group, shares, my_part, unit))
-
-    def contract_times(result, times, rights, row_units, column_units, first, steps, add):
-        lefts = [
-            [slot.reshape(parts, share * unit, width) for slot in chunk]
-            for chunk, share in zip(gathered(times), shares)
-        ]
-        return contract(
-            result, lefts, shares, rights, unit, row_units, column_units, first, steps, add
-        )
-
-    early, late = list(range(half // 2 + 1)), list(range(half // 2 + 1, half + 1))
-    rights = [column([0, 1], *slots[half - 1][0])] + [column([t]) for t in early[2:]]
-    results = [None]
-    for first in range(4):
-        results.append(contract_times(results[-1], early, rights, 2, 2, first, 1, False))
-
-    slots.append([])
-    for k in range(len(CHUNKS)):
-        up, down = slots[half - 1][k][0], slots[half - 1][k][-1]
-        if k == len(CHUNKS) - 1:
-            up, down = after(up, results[1]), after(down, results[1])
-        cut = up.shape[0] // 2
-        slots[half].append([jnp.concatenate(go_round(up[:cut], down[cut:]), axis=0)])
-
-    rights = [column([t], results[1 + i]) for i, t in enumerate(late)]
-    result = contract_times(results[-1], late, rights, 1, 4, 0, 2, True)
+        one.append(go_round(*one[t - 1]))
+    one.append(last_round(*one[half - 1]))
+    copies = [column(sum(one[:2], [])), column(sum(one[2:half], [])), column(one[half])]
+    rights = [settle(which, copies[0], pairs)]
+
+    two = [[own], go_round(*[after(own, rights[0], *one[half - 1])] * 2)]
+    two.append(go_round(*[after(block, copies[1][0]) for block in two[1]]))
+    rights += [settle(which, some, pairs) for some in copies[1:]]
+
+    def as_lefts(slots):
+        return [slot.reshape(parts, -1, width) for slot in sum(slots, [])]
+
+    lefts = as_lefts(one)
+    wide = CHUNKS[0][1] // 2
+    first = contract(None, [lefts], rights, unit, 0, wide, 0, 1, 0)
+    two.append(go_round(*[after(block, first) for block in two[2]]))
+    second = contract(first, [lefts], rights, unit, 0, wide, 1, 1, 1)
+    for t in range(4, half):
+        two.append(go_round(*two[t - 1]))
+    middle = half // 2 + 1
+    copies = [column(sum(two[:middle], []))]
+    two.append(last_round(*[after(block, second, copies[0][0]) for block in two[half - 1]]))
+    copies.append(column(sum(two[middle:], [])))
+    share = CHUNKS[0][1]
+    both = [lefts, as_lefts(two)]
+    result = contract(second, both[1:], rights, unit, share, share, 0, 1, 0)
+    rights = [settle(which, some, pairs) for some in copies]
+    result = contract(result, both, rights, unit, 0, share, 0, 1, 1)
     return result.reshape(2, parts * block, block)
 
 

time: 458 us -> 439 us (0.959)
  Pallas kernels: 237 us -> 210 us
  starting transfers between devices: 43.4 us -> 58.7 us
  other arithmetic: 10.8 us -> 4.22 us
    pallas_call x13 -> x15, Pallas kernels: 172 us -> 153 us  [the longest x4 95.6 us: contract(): pl.pallas_call(lambda *refs: contract_kernel(slot_count, shares, len(righ...]
    ppermute x14 -> x21, starting transfers between devices: 26.7 us -> 41.6 us  [the longest x15 38.4 us: column(): copies.append(lax.ppermute(copies[source], ('row', 'col'), perm))]
    ppermute x8, waiting for transfers between devices: 34.4 us -> 23.7 us  [go_round(): lax.ppermute(below, 'col', ring_up)]
    pallas_call x1, Pallas kernels: 59.6 us -> 51 us  [transform(): pl.pallas_call(lambda *refs: transform_kernel(pairs, load_steps, step_row...]
    ppermute x8, starting transfers between devices: 6.79 us -> 13.1 us  [go_round(): lax.ppermute(above, 'col', ring_down)]
    ppermute x8, starting transfers between devices: 9.9 us -> 3.89 us  [go_round(): lax.ppermute(below, 'col', ring_up)]
    select_n x4 -> x0, other arithmetic: 5.98 us -> none  [send_column(): kept = jnp.where(take, arrived, kept)]
    ppermute x14 -> x21, waiting for transfers between devices: 45.5 us -> 50.9 us  [the longest x6 39.9 us: across_rows(): lax.ppermute(parcels[s], 'row', [(r, r ^ s) for r in range(rows)])]
  transfers between devices with their start and end apart: 30 -> 37, of which waited for: 14 -> 14; matrix products, arithmetic and copies ran while one was open for 3% -> 1% of each run, Pallas kernels for 23% -> 25%
where the time goes in v4:
time: 439 us; the launch traced here: 435 us
  Pallas kernels  210 us (48%)
  waiting for transfers between devices  146 us (33%)
  starting transfers between devices  58.7 us (13%)
  local copies, waits for them, and re-layouts  15.9 us (4%)
    pallas_call x4, Pallas kernels, contract(): pl.pallas_call(lambda *refs: contract_kernel(slot_count, shares, len(righ...  95.6 us
    ppermute x8, waiting for transfers between devices, go_round(): lax.ppermute(above, 'col', ring_down)  71.4 us
    pallas_call x1, Pallas kernels, transform(): pl.pallas_call(lambda *refs: transform_kernel(pairs, load_steps, step_row...  51 us
    ppermute x6, waiting for transfers between devices, across_rows(): lax.ppermute(parcels[s], 'row', [(r, r ^ s) for r in range(rows)])  39.9 us
    ppermute x15, starting transfers between devices, column(): copies.append(lax.ppermute(copies[source], ('row', 'col'), perm))  38.4 us
    ppermute x8, waiting for transfers between devices, go_round(): lax.ppermute(below, 'col', ring_up)  23.7 us
    pallas_call x5, Pallas kernels, settle(): pl.pallas_call(lambda *refs: settle_kernel(pairs, row_count, *refs), grid...  22 us
    pallas_call x5, Pallas kernels, flip(): pl.pallas_call(lambda *refs: flip_kernel(slot_count, *refs), grid_spec=pl...  20.2 us
  transfers between devices with their start and end apart: 37, of which 14 were waited for; matrix products, arithmetic and copies ran while one was open for 1% of the time, Pallas kernels for 25%

profile of v4, /device:TPU:0, one launch (start us, length us, event | category | flops | bytes accessed | tf_op | source)
XLA Modules:
  0.0 435.1 jit_solution(12217362602760943908)
XLA Ops:
  6.4 51.0 %transform.1 = (bf16[1024,128]{1,0:T(8,128)(2,1)}, bf16[1024,128]{1,0:T(8,128)(2,1)}, bf16[1024,128]{1,0:T(8,128)(2,1)}, bf16[1024,128]{1,0:T(8,128)(2,1)}, f32[32768,128]{1,0:T(8,128)}) custom-call(s32[8192]{0:T(1024)} %bitcast.70, s32[1]{0:T(128)} %bitcast.refs_1_.refs_0_, bf16[64,256]{1,0:T(8,128)(2,1)} %fusion.16.refs_2_, ...), custom_call_target="tpu_custom_call" | custom-call | flops 9663676416 | bytes 40000000 | tf_op jit(solution)/shard_map/transform/pallas_call | solution.py:233
  60.6 7.3 %collective-permute-done.1.refs_3_ = bf16[1024,128]{1,0:T(8,128)(2,1)S(1)} collective-permute-done((bf16[1024,128]{1,0:T(8,128)(2,1)}, bf16[1024,128]{1,0:T(8,128)(2,1)S(1)}, u32[]{:S(2)}, u32[]{:S(2)}) %collective-permute-start.1) | collective-permute-done | bytes 262176 | tf_op jit(solution)/shard_map/ppermute | solution.py:504
  67.9 5.1 %collective-permute-done.2.refs_4_ = bf16[1024,128]{1,0:T(8,128)(2,1)S(1)} collective-permute-done((bf16[1024,128]{1,0:T(8,128)(2,1)}, bf16[1024,128]{1,0:T(8,128)(2,1)S(1)}, u32[]{:S(2)}, u32[]{:S(2)}) %collective-permute-start.2) | collective-permute-done | bytes 262176 | tf_op jit(solution)/shard_map/ppermute | solution.py:504
  79.1 15.7 %select.45 = (bf16[1024,128]{1,0:T(8,128)(2,1)}, bf16[1024,128]{1,0:T(8,128)(2,1)}, bf16[1024,128]{1,0:T(8,128)(2,1)}, bf16[1024,128]{1,0:T(8,128)(2,1)}) custom-call(s32[8192]{0:T(1024)} %bitcast.67, s32[1]{0:T(128)} %bitcast.refs_1_.refs_0_, f32[32768,128]{1,0:T(8,128)} %get-tuple-element.29.refs_2_), custom_call_target="tpu_custom_call" | custom-call | bytes 50000000 | tf_op jit(solution)/shard_map/select/pallas_call | solution.py:113
  94.7 7.2 %collective-permute-done.4.refs_3_ = bf16[2048,256]{1,0:T(8,128)(2,1)S(1)} collective-permute-done((bf16[2048,256]{1,0:T(8,128)(2,1)}, bf16[2048,256]{1,0:T(8,128)(2,1)S(1)}, u32[]{:S(2)}, u32[]{:S(2)}) %collective-permute-start.4) | collective-permute-done | bytes 1048608 | tf_op jit(solution)/shard_map/ppermute | solution.py:509
  108.6 4.7 %collective-permute-start.15 = (bf16[768,1024]{1,0:T(8,128)(2,1)}, bf16[768,1024]{1,0:T(8,128)(2,1)}, u32[]{:S(2)}, u32[]{:S(2)}) collective-permute-start(bf16[768,1024]{1,0:T(8,128)(2,1)} %flip.5.refs_1_), channel_id=1, source_target_pairs={{0,16},{1,17},{10,26},{11,27},{20,4},{21,5},{30,14},{31,15}} | collective-permute-start | bytes 4718600 | tf_op jit(solution)/shard_map/ppermute | solution.py:524
  113.3 13.2 %collective-permute-done.6.refs_2_ = bf16[2048,256]{1,0:T(8,128)(2,1)S(1)} collective-permute-done((bf16[2048,256]{1,0:T(8,128)(2,1)S(1)}, bf16[2048,256]{1,0:T(8,128)(2,1)S(1)}, u32[]{:S(2)}, u32[]{:S(2)}) %collective-permute-start.6) | collective-permute-done | bytes 1048608 | tf_op jit(solution)/shard_map/ppermute | solution.py:509
  128.5 21.7 %collective-permute-done.8.refs_4_ = bf16[2048,256]{1,0:T(8,128)(2,1)S(1)} collective-permute-done((bf16[2048,256]{1,0:T(8,128)(2,1)S(1)}, bf16[2048,256]{1,0:T(8,128)(2,1)S(1)}, u32[]{:S(2)}, u32[]{:S(2)}) %collective-permute-start.8) | collective-permute-done | bytes 1048608 | tf_op jit(solution)/shard_map/ppermute | solution.py:509
  156.9 4.7 %collective-permute-start.22 = (bf16[1024,1024]{1,0:T(8,128)(2,1)}, bf16[1024,1024]{1,0:T(8,128)(2,1)}, u32[]{:S(2)}, u32[]{:S(2)}) collective-permute-start(bf16[1024,1024]{1,0:T(8,128)(2,1)} %flip.6.refs_1_), channel_id=1, source_target_pairs={{0,16},{1,17},{10,26},{11,27},{20,4},{21,5},{30,14},{31,15}} | collective-permute-start | bytes 6291464 | tf_op jit(solution)/shard_map/ppermute | solution.py:524
  167.7 21.9 %collective-permute-done.12.refs_3_ = bf16[1024,128]{1,0:T(8,128)(2,1)S(1)} collective-permute-done((bf16[1024,128]{1,0:T(8,128)(2,1)S(1)}, bf16[1024,128]{1,0:T(8,128)(2,1)S(1)}, u32[]{:S(2)}, u32[]{:S(2)}) %collective-permute-start.12) | collective-permute-done | bytes 262176 | tf_op jit(solution)/shard_map/ppermute | solution.py:504
  191.6 5.6 %collective-permute-done.13.refs_4_ = bf16[1024,128]{1,0:T(8,128)(2,1)S(1)} collective-permute-done((bf16[1024,128]{1,0:T(8,128)(2,1)S(1)}, bf16[1024,128]{1,0:T(8,128)(2,1)S(1)}, u32[]{:S(2)}, u32[]{:S(2)}) %collective-permute-start.13) | collective-permute-done | bytes 262176 | tf_op jit(solution)/shard_map/ppermute | solution.py:504
  202.6 4.4 %settle.5.refs_8_ = bf16[2,768,1024]{2,1,0:T(8,128)(2,1)} custom-call(s32[1]{0:T(128)} %bitcast.15.refs_0_, bf16[768,1024]{1,0:T(8,128)(2,1)} %flip.5.refs_1_, bf16[768,1024]{1,0:T(8,128)(2,1)} %copy-done.18, bf16[768,1024]{1,0:T(8,128)(2,1)} %collective-permute-done.15.refs_3_, bf16[768,1024]{1,0:T(8,128)(2,1)} %collective-permute-done.16.refs_4_), custom_call_target="tpu_custom_call" | custom-call | bytes 6291456 | tf_op jit(solution)/shard_map/settle/pallas_call | solution.py:373
  222.8 11.8 %collective-permute-done.18.refs_3_ = bf16[2048,256]{1,0:T(8,128)(2,1)S(1)} collective-permute-done((bf16[2048,256]{1,0:T(8,128)(2,1)S(1)}, bf16[2048,256]{1,0:T(8,128)(2,1)S(1)}, u32[]{:S(2)}, u32[]{:S(2)}) %collective-permute-start.18) | collective-permute-done | bytes 1048608 | tf_op jit(solution)/shard_map/ppermute | solution.py:509
  243.4 17.6 %collective-permute-done.20.refs_5_ = bf16[2048,256]{1,0:T(8,128)(2,1)S(1)} collective-permute-done((bf16[2048,256]{1,0:T(8,128)(2,1)S(1)}, bf16[2048,256]{1,0:T(8,128)(2,1)S(1)}, u32[]{:S(2)}, u32[]{:S(2)}) %collective-permute-start.20) | collective-permute-done | bytes 1048608 | tf_op jit(solution)/shard_map/ppermute | solution.py:509
  263.8 4.6 %flip.8.refs_1_ = bf16[1280,1024]{1,0:T(8,128)(2,1)} custom-call(s32[1]{0:T(128)} %bitcast.16.refs_0_, bf16[2048,256]{1,0:T(8,128)(2,1)} %assemble.3.refs_1_, bf16[2048,256]{1,0:T(8,128)(2,1)} %collective-permute-done.17.refs_2_, bf16[2048,256]{1,0:T(8,128)(2,1)} %copy-done.12, bf16[2048,256]{1,0:T(8,128)(2,1)} %copy-done.15, bf16[2048,256]{1,0:T(8,128)(2,1)} %copy-done.13), custom_call_target="tpu_custom_call" | custom-call | bytes 10485760 | tf_op jit(solution)/shard_map/flip/pallas_call | solution.py:331
  271.2 4.9 %settle.6.refs_9_ = bf16[2,1024,1024]{2,1,0:T(8,128)(2,1)} custom-call(s32[1]{0:T(128)} %bitcast.15.refs_0_, bf16[1024,1024]{1,0:T(8,128)(2,1)} %flip.6.refs_1_, bf16[1024,1024]{1,0:T(8,128)(2,1)} %collective-permute-done.21.refs_2_, bf16[1024,1024]{1,0:T(8,128)(2,1)} %collective-permute-done.22.refs_3_, bf16[1024,1024]{1,0:T(8,128)(2,1)} %collective-permute-done.23.refs_4_), custom_call_target="tpu_custom_call" | custom-call | bytes 8388608 | tf_op jit(solution)/shard_map/settle/pallas_call | solution.py:373
  276.1 13.8 %contract.4.refs_11_ = f32[2,2,2048,2048]{3,2,1,0:T(8,128)} custom-call(bf16[2,1024,256]{2,1,0:T(8,128)(2,1)} %bitcast.32, bf16[2,1024,256]{2,1,0:T(8,128)(2,1)} %bitcast.47, bf16[2,1024,256]{2,1,0:T(8,128)(2,1)} %bitcast.44, bf16[2,1024,256]{2,1,0:T(8,128)(2,1)} %bitcast.9.refs_3_, bf16[2,1024,256]{2,1,0:T(8,128)(2,1)} %bitcast.50, ...), custom_call_target="tpu_custom_call" | custom-call | flops 17179869184 | bytes 8388608 | tf_op jit(solution)/shard_map/contract/pallas_call | solution.py:433
  292.3 13.7 %contract.5.refs_11_ = f32[2,2,2048,2048]{3,2,1,0:T(8,128)} custom-call(bf16[2,1024,256]{2,1,0:T(8,128)(2,1)} %bitcast.33, bf16[2,1024,256]{2,1,0:T(8,128)(2,1)} %bitcast.48, bf16[2,1024,256]{2,1,0:T(8,128)(2,1)} %bitcast.45, bf16[2,1024,256]{2,1,0:T(8,128)(2,1)} %bitcast.9.refs_3_, bf16[2,1024,256]{2,1,0:T(8,128)(2,1)} %bitcast.51, ...), custom_call_target="tpu_custom_call", output_to_operand_aliasing={{}: (11, {})} | custom-call | flops 17179869184 | bytes 8388608 | tf_op jit(solution)/shard_map/contract/pallas_call | solution.py:433
  306.0 9.6 %collective-permute-done.27.refs_1_ = bf16[2048,256]{1,0:T(8,128)(2,1)S(1)} collective-permute-done((bf16[2048,256]{1,0:T(8,128)(2,1)S(1)}, bf16[2048,256]{1,0:T(8,128)(2,1)S(1)}, u32[]{:S(2)}, u32[]{:S(2)}) %collective-permute-start.27) | collective-permute-done | bytes 1048608 | tf_op jit(solution)/shard_map/ppermute | solution.py:509
  317.9 10.8 %collective-permute-done.29 = bf16[1024,256]{1,0:T(8,128)(2,1)S(1)} collective-permute-done((bf16[1024,256]{1,0:T(8,128)(2,1)S(1)}, bf16[1024,256]{1,0:T(8,128)(2,1)S(1)}, u32[]{:S(2)}, u32[]{:S(2)}) %collective-permute-start.29) | collective-permute-done | bytes 524320 | tf_op jit(solution)/shard_map/ppermute | solution.py:509
  342.5 11.0 %collective-permute-done.35.refs_3_ = bf16[768,1024]{1,0:T(8,128)(2,1)} collective-permute-done((bf16[768,1024]{1,0:T(8,128)(2,1)}, bf16[768,1024]{1,0:T(8,128)(2,1)}, u32[]{:S(2)}, u32[]{:S(2)}) %collective-permute-start.35) | collective-permute-done | bytes 1572896 | tf_op jit(solution)/shard_map/ppermute | solution.py:524
  355.2 24.2 %contract.6.refs_18_ = f32[2,2,2048,2048]{3,2,1,0:T(8,128)} custom-call(bf16[2,1024,256]{2,1,0:T(8,128)(2,1)} %bitcast.53, bf16[2,1024,256]{2,1,0:T(8,128)(2,1)} %bitcast.17.refs_1_.refs_9_, bf16[2,1024,256]{2,1,0:T(8,128)(2,1)} %bitcast.61, bf16[2,1024,256]{2,1,0:T(8,128)(2,1)} %bitcast.65, ...), custom_call_target="tpu_custom_call", output_to_operand_aliasing={{}: (11, {})} | custom-call | flops 34359738368 | bytes 16777216 | tf_op jit(solution)/shard_map/contract/pallas_call | solution.py:433
  381.0 5.8 %settle.8.refs_16_ = bf16[2,1280,1024]{2,1,0:T(8,128)(2,1)} custom-call(s32[1]{0:T(128)} %bitcast.15.refs_0_, bf16[1280,1024]{1,0:T(8,128)(2,1)} %flip.8.refs_1_, bf16[1280,1024]{1,0:T(8,128)(2,1)} %copy-done.17, bf16[1280,1024]{1,0:T(8,128)(2,1)} %collective-permute-done.32.refs_3_, bf16[1280,1024]{1,0:T(8,128)(2,1)} %collective-permute-done.33.refs_4_), custom_call_target="tpu_custom_call" | custom-call | bytes 10485760 | tf_op jit(solution)/shard_map/settle/pallas_call | solution.py:373
  391.1 43.9 %contract.7 = f32[2,2,2048,2048]{3,2,1,0:T(8,128)} custom-call(bf16[2,1024,256]{2,1,0:T(8,128)(2,1)} %bitcast.34, bf16[2,1024,256]{2,1,0:T(8,128)(2,1)} %bitcast.49, bf16[2,1024,256]{2,1,0:T(8,128)(2,1)} %bitcast.46, bf16[2,1024,256]{2,1,0:T(8,128)(2,1)} %bitcast.9.refs_3_, bf16[2,1024,256]{2,1,0:T(8,128)(2,1)} %bitcast.52, ...), custom_call_target="tpu_custom_call", output_to_operand_aliasing={{}: (18, {})} | custom-call | flops 68719476736 | bytes 33554432 | tf_op jit(solution)/shard_map/contract/pallas_call | solution.py:433
  (149 shorter events, 100.6 us)
Async XLA Ops:
  76.4 25.5 %collective-permute-start.4 = (bf16[2048,256]{1,0:T(8,128)(2,1)}, bf16[2048,256]{1,0:T(8,128)(2,1)S(1)}, u32[]{:S(2)}, u32[]{:S(2)}) collective-permute-start(bf16[2048,256]{1,0:T(8,128)(2,1)} %assemble.2.refs_1_), channel_id=1, source_target_pairs={{2,0},{4,2},{6,4},{7,6},{5,7},{3,5},{1,3},{0,1},{10,8},{12,10},{14... | collective-permute-start | bytes 3145736 | tf_op jit(solution)/shard_map/ppermute | solution.py:509
  78.0 25.6 %collective-permute-start.3 = (bf16[2048,256]{1,0:T(8,128)(2,1)}, bf16[2048,256]{1,0:T(8,128)(2,1)S(1)}, u32[]{:S(2)}, u32[]{:S(2)}) collective-permute-start(bf16[2048,256]{1,0:T(8,128)(2,1)} %assemble.2.refs_1_), channel_id=1, source_target_pairs={{0,2},{2,4},{4,6},{6,7},{7,5},{5,3},{3,1},{1,0},{8,10},{10,12},{12... | collective-permute-start | bytes 3145736 | tf_op jit(solution)/shard_map/ppermute | solution.py:509
  101.9 24.5 %collective-permute-start.6 = (bf16[2048,256]{1,0:T(8,128)(2,1)S(1)}, bf16[2048,256]{1,0:T(8,128)(2,1)S(1)}, u32[]{:S(2)}, u32[]{:S(2)}) collective-permute-start(bf16[2048,256]{1,0:T(8,128)(2,1)S(1)} %collective-permute-done.4.refs_3_), channel_id=1, source_target_pairs={{2,0},{4,2},{6,4},{7,6},{5,7},{3,5},{1,3},{0,1},{10,8},{12,10},{14... | collective-permute-start | bytes 3145736 | tf_op jit(solution)/shard_map/ppermute | solution.py:509
  103.6 24.5 %collective-permute-start.5 = (bf16[2048,256]{1,0:T(8,128)(2,1)S(1)}, bf16[2048,256]{1,0:T(8,128)(2,1)}, u32[]{:S(2)}, u32[]{:S(2)}) collective-permute-start(bf16[2048,256]{1,0:T(8,128)(2,1)S(1)} %collective-permute-done.3.refs_2_), channel_id=1, source_target_pairs={{0,2},{2,4},{4,6},{6,7},{7,5},{5,3},{3,1},{1,0},{8,10},{10,12},{12... | collective-permute-start | bytes 3145736 | tf_op jit(solution)/shard_map/ppermute | solution.py:509
  108.6 54.4 %collective-permute-start.15 = (bf16[768,1024]{1,0:T(8,128)(2,1)}, bf16[768,1024]{1,0:T(8,128)(2,1)}, u32[]{:S(2)}, u32[]{:S(2)}) collective-permute-start(bf16[768,1024]{1,0:T(8,128)(2,1)} %flip.5.refs_1_), channel_id=1, source_target_pairs={{0,16},{1,17},{10,26},{11,27},{20,4},{21,5},{30,14},{31,15}} | collective-permute-start | bytes 4718600 | tf_op jit(solution)/shard_map/ppermute | solution.py:524
  126.4 23.7 %collective-permute-start.8 = (bf16[2048,256]{1,0:T(8,128)(2,1)S(1)}, bf16[2048,256]{1,0:T(8,128)(2,1)S(1)}, u32[]{:S(2)}, u32[]{:S(2)}) collective-permute-start(bf16[2048,256]{1,0:T(8,128)(2,1)S(1)} %collective-permute-done.6.refs_2_), channel_id=1, source_target_pairs={{2,0},{4,2},{6,4},{7,6},{5,7},{3,5},{1,3},{0,1},{10,8},{12,10},{14... | collective-permute-start | bytes 3145736 | tf_op jit(solution)/shard_map/ppermute | solution.py:509
  128.1 23.6 %collective-permute-start.7 = (bf16[2048,256]{1,0:T(8,128)(2,1)}, bf16[2048,256]{1,0:T(8,128)(2,1)S(1)}, u32[]{:S(2)}, u32[]{:S(2)}) collective-permute-start(bf16[2048,256]{1,0:T(8,128)(2,1)} %collective-permute-done.5.refs_1_), channel_id=1, source_target_pairs={{0,2},{2,4},{4,6},{6,7},{7,5},{5,3},{3,1},{1,0},{8,10},{10,12},{12... | collective-permute-start | bytes 3145736 | tf_op jit(solution)/shard_map/ppermute | solution.py:509
  156.9 55.4 %collective-permute-start.22 = (bf16[1024,1024]{1,0:T(8,128)(2,1)}, bf16[1024,1024]{1,0:T(8,128)(2,1)}, u32[]{:S(2)}, u32[]{:S(2)}) collective-permute-start(bf16[1024,1024]{1,0:T(8,128)(2,1)} %flip.6.refs_1_), channel_id=1, source_target_pairs={{0,16},{1,17},{10,26},{11,27},{20,4},{21,5},{30,14},{31,15}} | collective-permute-start | bytes 6291464 | tf_op jit(solution)/shard_map/ppermute | solution.py:524
  161.6 39.8 %collective-permute-start.14 = (bf16[768,1024]{1,0:T(8,128)(2,1)}, bf16[768,1024]{1,0:T(8,128)(2,1)S(1)}, u32[]{:S(2)}, u32[]{:S(2)}) collective-permute-start(bf16[768,1024]{1,0:T(8,128)(2,1)} %flip.5.refs_1_), channel_id=1, source_target_pairs={{0,8},{1,9},{10,2},{11,3},{20,28},{21,29},{30,22},{31,23}} | collective-permute-start | bytes 4718600 | tf_op jit(solution)/shard_map/ppermute | solution.py:524
  163.0 38.5 %collective-permute-start.16 = (bf16[768,1024]{1,0:T(8,128)(2,1)}, bf16[768,1024]{1,0:T(8,128)(2,1)}, u32[]{:S(2)}, u32[]{:S(2)}) collective-permute-start(bf16[768,1024]{1,0:T(8,128)(2,1)} %collective-permute-done.15.refs_3_), channel_id=1, source_target_pairs={{16,24},{17,25},{26,18},{27,19},{4,12},{5,13},{14,6},{15,7}} | collective-permute-start | bytes 4718600 | tf_op jit(solution)/shard_map/ppermute | solution.py:524
  164.9 24.8 %collective-permute-start.12 = (bf16[1024,128]{1,0:T(8,128)(2,1)S(1)}, bf16[1024,128]{1,0:T(8,128)(2,1)S(1)}, u32[]{:S(2)}, u32[]{:S(2)}) collective-permute-start(bf16[1024,128]{1,0:T(8,128)(2,1)S(1)} %copy-done.27), channel_id=1, source_target_pairs={{0,16},{8,24},{16,0},{24,8},{1,17},{9,25},{17,1},{25,9},{2,18},{10... | collective-permute-start | bytes 786440 | tf_op jit(solution)/shard_map/ppermute | solution.py:504
  166.8 42.2 %collective-permute-start.9 = (bf16[1024,256]{1,0:T(8,128)(2,1)}, bf16[1024,256]{1,0:T(8,128)(2,1)S(1)}, u32[]{:S(2)}, u32[]{:S(2)}) collective-permute-start(bf16[1024,256]{1,0:T(8,128)(2,1)} %slice.36), channel_id=1, source_target_pairs={{0,2},{2,4},{4,6},{6,7},{7,5},{5,3},{3,1},{1,0},{8,10},{10,12},{12... | collective-permute-start | bytes 1572872 | tf_op jit(solution)/shard_map/ppermute | solution.py:509
  207.0 27.6 %collective-permute-start.18 = (bf16[2048,256]{1,0:T(8,128)(2,1)S(1)}, bf16[2048,256]{1,0:T(8,128)(2,1)S(1)}, u32[]{:S(2)}, u32[]{:S(2)}) collective-permute-start(bf16[2048,256]{1,0:T(8,128)(2,1)S(1)} %copy-done.7), channel_id=1, source_target_pairs={{2,0},{4,2},{6,4},{7,6},{5,7},{3,5},{1,3},{0,1},{10,8},{12,10},{14... | collective-permute-start | bytes 3145736 | tf_op jit(solution)/shard_map/ppermute | solution.py:509
  207.7 29.6 %collective-permute-start.17 = (bf16[2048,256]{1,0:T(8,128)(2,1)S(1)}, bf16[2048,256]{1,0:T(8,128)(2,1)}, u32[]{:S(2)}, u32[]{:S(2)}) collective-permute-start(bf16[2048,256]{1,0:T(8,128)(2,1)S(1)} %copy-done.7), channel_id=1, source_target_pairs={{0,2},{2,4},{4,6},{6,7},{7,5},{5,3},{3,1},{1,0},{8,10},{10,12},{12... | collective-permute-start | bytes 3145736 | tf_op jit(solution)/shard_map/ppermute | solution.py:509
  209.0 62.2 %collective-permute-start.21 = (bf16[1024,1024]{1,0:T(8,128)(2,1)S(1)}, bf16[1024,1024]{1,0:T(8,128)(2,1)}, u32[]{:S(2)}, u32[]{:S(2)}) collective-permute-start(bf16[1024,1024]{1,0:T(8,128)(2,1)S(1)} %copy-done.8), channel_id=1, source_target_pairs={{0,8},{1,9},{10,2},{11,3},{20,28},{21,29},{30,22},{31,23}} | collective-permute-start | bytes 6291464 | tf_op jit(solution)/shard_map/ppermute | solution.py:524
  212.2 59.0 %collective-permute-start.23 = (bf16[1024,1024]{1,0:T(8,128)(2,1)}, bf16[1024,1024]{1,0:T(8,128)(2,1)}, u32[]{:S(2)}, u32[]{:S(2)}) collective-permute-start(bf16[1024,1024]{1,0:T(8,128)(2,1)} %collective-permute-done.22.refs_3_), channel_id=1, source_target_pairs={{16,24},{17,25},{26,18},{27,19},{4,12},{5,13},{14,6},{15,7}} | collective-permute-start | bytes 6291464 | tf_op jit(solution)/shard_map/ppermute | solution.py:524
  237.3 23.7 %collective-permute-start.20 = (bf16[2048,256]{1,0:T(8,128)(2,1)S(1)}, bf16[2048,256]{1,0:T(8,128)(2,1)S(1)}, u32[]{:S(2)}, u32[]{:S(2)}) collective-permute-start(bf16[2048,256]{1,0:T(8,128)(2,1)S(1)} %collective-permute-done.18.refs_3_), channel_id=1, source_target_pairs={{2,0},{4,2},{6,4},{7,6},{5,7},{3,5},{1,3},{0,1},{10,8},{12,10},{14... | collective-permute-start | bytes 3145736 | tf_op jit(solution)/shard_map/ppermute | solution.py:509
  238.9 23.9 %collective-permute-start.19 = (bf16[2048,256]{1,0:T(8,128)(2,1)}, bf16[2048,256]{1,0:T(8,128)(2,1)S(1)}, u32[]{:S(2)}, u32[]{:S(2)}) collective-permute-start(bf16[2048,256]{1,0:T(8,128)(2,1)} %collective-permute-done.17.refs_2_), channel_id=1, source_target_pairs={{0,2},{2,4},{4,6},{6,7},{7,5},{5,3},{3,1},{1,0},{8,10},{10,12},{12... | collective-permute-start | bytes 3145736 | tf_op jit(solution)/shard_map/ppermute | solution.py:509
  268.3 69.5 %collective-permute-start.32 = (bf16[1280,1024]{1,0:T(8,128)(2,1)}, bf16[1280,1024]{1,0:T(8,128)(2,1)}, u32[]{:S(2)}, u32[]{:S(2)}) collective-permute-start(bf16[1280,1024]{1,0:T(8,128)(2,1)} %flip.8.refs_1_), channel_id=1, source_target_pairs={{0,16},{1,17},{10,26},{11,27},{20,4},{21,5},{30,14},{31,15}} | collective-permute-start | bytes 7864328 | tf_op jit(solution)/shard_map/ppermute | solution.py:524
  289.9 25.8 %collective-permute-start.28 = (bf16[2048,256]{1,0:T(8,128)(2,1)S(1)}, bf16[2048,256]{1,0:T(8,128)(2,1)S(1)}, u32[]{:S(2)}, u32[]{:S(2)}) collective-permute-start(bf16[2048,256]{1,0:T(8,128)(2,1)S(1)} %copy-done.14), channel_id=1, source_target_pairs={{2,0},{4,2},{6,4},{7,6},{5,7},{3,5},{1,3},{0,1},{10,8},{12,10},{14... | collective-permute-start | bytes 3145736 | tf_op jit(solution)/shard_map/ppermute | solution.py:509
  336.4 43.1 %collective-permute-start.31 = (bf16[1280,1024]{1,0:T(8,128)(2,1)S(1)}, bf16[1280,1024]{1,0:T(8,128)(2,1)S(1)}, u32[]{:S(2)}, u32[]{:S(2)}) collective-permute-start(bf16[1280,1024]{1,0:T(8,128)(2,1)S(1)} %copy-done.3), channel_id=1, source_target_pairs={{0,8},{1,9},{10,2},{11,3},{20,28},{21,29},{30,22},{31,23}} | collective-permute-start | bytes 7864328 | tf_op jit(solution)/shard_map/ppermute | solution.py:524
  337.8 41.6 %collective-permute-start.33 = (bf16[1280,1024]{1,0:T(8,128)(2,1)}, bf16[1280,1024]{1,0:T(8,128)(2,1)}, u32[]{:S(2)}, u32[]{:S(2)}) collective-permute-start(bf16[1280,1024]{1,0:T(8,128)(2,1)} %collective-permute-done.32.refs_3_), channel_id=1, source_target_pairs={{16,24},{17,25},{26,18},{27,19},{4,12},{5,13},{14,6},{15,7}} | collective-permute-start | bytes 7864328 | tf_op jit(solution)/shard_map/ppermute | solution.py:524
  340.0 46.8 %collective-permute-start.34 = (bf16[768,1024]{1,0:T(8,128)(2,1)}, bf16[768,1024]{1,0:T(8,128)(2,1)}, u32[]{:S(2)}, u32[]{:S(2)}) collective-permute-start(bf16[768,1024]{1,0:T(8,128)(2,1)} %flip.9.refs_1_), channel_id=1, source_target_pairs={{0,8},{1,9},{10,2},{11,3},{20,28},{21,29},{30,22},{31,23}} | collective-permute-start | bytes 4718600 | tf_op jit(solution)/shard_map/ppermute | solution.py:524
  353.4 33.4 %collective-permute-start.36 = (bf16[768,1024]{1,0:T(8,128)(2,1)}, bf16[768,1024]{1,0:T(8,128)(2,1)}, u32[]{:S(2)}, u32[]{:S(2)}) collective-permute-start(bf16[768,1024]{1,0:T(8,128)(2,1)} %collective-permute-done.35.refs_3_), channel_id=1, source_target_pairs={{16,24},{17,25},{26,18},{27,19},{4,12},{5,13},{14,6},{15,7}} | collective-permute-start | bytes 4718600 | tf_op jit(solution)/shard_map/ppermute | solution.py:524
  (42 other events, 542.7 us)

commit v5 on v4

--- a/solution.py
+++ b/solution.py
@@ -512,16 +512,23 @@
         cut = below.shape[0] // 2
         return [jnp.concatenate(go_round(below[:cut], above[cut:]), axis=0)]
 
-    def column(slots, *before):
+    def column(slots, before=(), behind=()):
         slots = [after(slots[0], *before)] + slots[1:] if before else slots
         copies = [flip(slots, my_part, parts, unit)]
         for relation in range(1, rows):
             source = relation & (relation - 1)
+            hop = relation ^ source
+            held = copies[source]
+            if source and behind:
+                held = after(held, *behind)
+            if hop == 1:
+                copies.append(lax.ppermute(held, "row", [(r, r ^ 1) for r in range(rows)]))
+                continue
             perm = [
                 ((c // parts ^ source) * cols + c, (c // parts ^ relation) * cols + c)
                 for c in range(cols)
             ]
-            copies.append(lax.ppermute(copies[source], ("row", "col"), perm))
+            copies.append(lax.ppermute(held, ("row", "col"), perm))
         return copies
 
     which = (row ^ owner).astype(jnp.int32).reshape(1)
@@ -531,15 +538,20 @@
     sent = select(after(table, own), positions[1], me, rows, features)
     one[1] = [after(block, *sent) for block in one[1]]
     own = assemble(across_rows(sent), me, features)
-    for t in range(2, half):
+    one.append(go_round(*one[1]))
+    copies = [column(sum(one[:2], []))]
+    one[2] = [after(block, own, copies[0][0]) for block in one[2]]
+    for t in range(3, half):
         one.append(go_round(*one[t - 1]))
-    one.append(last_round(*one[half - 1]))
-    copies = [column(sum(one[:2], [])), column(sum(one[2:half], [])), column(one[half])]
-    rights = [settle(which, copies[0], pairs)]
-
-    two = [[own], go_round(*[after(own, rights[0], *one[half - 1])] * 2)]
-    two.append(go_round(*[after(block, copies[1][0]) for block in two[1]]))
-    rights += [settle(which, some, pairs) for some in copies[1:]]
+    copies.append(column(sum(one[2 : half - 1], [])))
+    below, above = [after(block, copies[1][0]) for block in one[half - 1]]
+    one.append(last_round(below, above))
+    two = [[own], go_round(*[after(own, below)] * 2)]
+    two.append(go_round(*two[1]))
+    copies.append(column(sum(one[half - 1 :], []), two[1], two[2]))
+    rights = [settle(which, some, pairs) for some in copies]
+    for t in range(3, half):
+        two.append(go_round(*two[t - 1]))
 
     def as_lefts(slots):
         return [slot.reshape(parts, -1, width) for slot in sum(slots, [])]
@@ -547,17 +559,14 @@
     lefts = as_lefts(one)
     wide = CHUNKS[0][1] // 2
     first = contract(None, [lefts], rights, unit, 0, wide, 0, 1, 0)
-    two.append(go_round(*[after(block, first) for block in two[2]]))
     second = contract(first, [lefts], rights, unit, 0, wide, 1, 1, 1)
-    for t in range(4, half):
-        two.append(go_round(*two[t - 1]))
     middle = half // 2 + 1
-    copies = [column(sum(two[:middle], []))]
-    two.append(last_round(*[after(block, second, copies[0][0]) for block in two[half - 1]]))
-    copies.append(column(sum(two[middle:], [])))
+    copies = [column(sum(two[:middle], []), two[half - 1] + [first])]
+    two.append(last_round(*[after(block, *rights) for block in two[half - 1]]))
     share = CHUNKS[0][1]
     both = [lefts, as_lefts(two)]
     result = contract(second, both[1:], rights, unit, share, share, 0, 1, 0)
+    copies.append(column(sum(two[middle:], []), (), (result,)))
     rights = [settle(which, some, pairs) for some in copies]
     result = contract(result, both, rights, unit, 0, share, 0, 1, 1)
     return result.reshape(2, parts * block, block)

time: 439 us -> 389 us (0.89)
  waiting for transfers between devices: 146 us -> 121 us
  starting transfers between devices: 58.7 us -> 40.8 us
  local copies, waits for them, and re-layouts: 15.9 us -> 10.9 us
    ppermute x8, waiting for transfers between devices: 71.4 us -> 5.88 us  [go_round(): lax.ppermute(above, 'col', ring_down)]
    ppermute x8, waiting for transfers between devices: 23.7 us -> 75.3 us  [go_round(): lax.ppermute(below, 'col', ring_up)]
    ppermute x15, starting transfers between devices: 38.4 us -> 19.3 us  [the longest x5 18.2 us: column(): copies.append(lax.ppermute(held, ('row', 'col'), perm))]
    ppermute x6, waiting for transfers between devices: 39.9 us -> 24.7 us  [across_rows(): lax.ppermute(parcels[s], 'row', [(r, r ^ s) for r in range(rows)])]
    ppermute x8, starting transfers between devices: 13.1 us -> 6.73 us  [go_round(): lax.ppermute(above, 'col', ring_down)]
    ppermute x8, starting transfers between devices: 3.89 us -> 9.68 us  [go_round(): lax.ppermute(below, 'col', ring_up)]
    unnamed x62 -> x54, local copies, waits for them, and re-layouts: 9.32 us -> 9.2 us
  transfers between devices with their start and end apart: 37 -> 37, of which waited for: 14 -> 17; matrix products, arithmetic and copies ran while one was open for 1% -> 0% of each run, Pallas kernels for 25% -> 26%
where the time goes in v5:
time: 389 us; the launch traced here: 388 us
  Pallas kernels  210 us (54%)
  waiting for transfers between devices  121 us (31%)
  starting transfers between devices  40.8 us (10%)
  local copies, waits for them, and re-layouts  10.9 us (3%)
  other arithmetic  4.23 us (1%)
    pallas_call x4, Pallas kernels, contract(): pl.pallas_call(lambda *refs: contract_kernel(slot_count, shares, len(righ...  95.8 us
    ppermute x8, waiting for transfers between devices, go_round(): lax.ppermute(below, 'col', ring_up)  75.3 us
    pallas_call x1, Pallas kernels, transform(): pl.pallas_call(lambda *refs: transform_kernel(pairs, load_steps, step_row...  51 us
    ppermute x6, waiting for transfers between devices, across_rows(): lax.ppermute(parcels[s], 'row', [(r, r ^ s) for r in range(rows)])  24.7 us
    pallas_call x5, Pallas kernels, settle(): pl.pallas_call(lambda *refs: settle_kernel(pairs, row_count, *refs), grid...  21.7 us
    pallas_call x5, Pallas kernels, flip(): pl.pallas_call(lambda *refs: flip_kernel(slot_count, *refs), grid_spec=pl...  20.9 us
    ppermute x5, starting transfers between devices, column(): copies.append(lax.ppermute(held, ('row', 'col'), perm))  18.2 us
    pallas_call x1, Pallas kernels, select(): pl.pallas_call(lambda *refs: select_kernel(row_count, features, count, *r...  15.6 us
  transfers between devices with their start and end apart: 37, of which 17 were waited for; matrix products, arithmetic and copies ran while one was open for 0% of the time, Pallas kernels for 26%

profile of v5, /device:TPU:0, one launch (start us, length us, event | category | flops | bytes accessed | tf_op | source)
XLA Modules:
  0.0 387.7 jit_solution(16129697188800229446)
XLA Ops:
  6.4 51.0 %transform.1 = (bf16[1024,128]{1,0:T(8,128)(2,1)}, bf16[1024,128]{1,0:T(8,128)(2,1)}, bf16[1024,128]{1,0:T(8,128)(2,1)}, bf16[1024,128]{1,0:T(8,128)(2,1)}, f32[32768,128]{1,0:T(8,128)}) custom-call(s32[8192]{0:T(1024)} %bitcast.67, s32[1]{0:T(128)} %bitcast.refs_1_.refs_0_, bf16[64,256]{1,0:T(8,128)(2,1)} %fusion.16.refs_2_, ...), custom_call_target="tpu_custom_call" | custom-call | flops 9663676416 | bytes 40000000 | tf_op jit(solution)/shard_map/transform/pallas_call | solution.py:233
  60.6 7.3 %collective-permute-done.1.refs_3_ = bf16[1024,128]{1,0:T(8,128)(2,1)S(1)} collective-permute-done((bf16[1024,128]{1,0:T(8,128)(2,1)}, bf16[1024,128]{1,0:T(8,128)(2,1)S(1)}, u32[]{:S(2)}, u32[]{:S(2)}) %collective-permute-start.1) | collective-permute-done | bytes 262176 | tf_op jit(solution)/shard_map/ppermute | solution.py:504
  67.9 5.1 %collective-permute-done.2.refs_4_ = bf16[1024,128]{1,0:T(8,128)(2,1)S(1)} collective-permute-done((bf16[1024,128]{1,0:T(8,128)(2,1)}, bf16[1024,128]{1,0:T(8,128)(2,1)S(1)}, u32[]{:S(2)}, u32[]{:S(2)}) %collective-permute-start.2) | collective-permute-done | bytes 262176 | tf_op jit(solution)/shard_map/ppermute | solution.py:504
  79.0 15.6 %select.45 = (bf16[1024,128]{1,0:T(8,128)(2,1)}, bf16[1024,128]{1,0:T(8,128)(2,1)}, bf16[1024,128]{1,0:T(8,128)(2,1)}, bf16[1024,128]{1,0:T(8,128)(2,1)}) custom-call(s32[8192]{0:T(1024)} %bitcast.64, s32[1]{0:T(128)} %bitcast.refs_1_.refs_0_, f32[32768,128]{1,0:T(8,128)} %get-tuple-element.33.refs_2_), custom_call_target="tpu_custom_call" | custom-call | bytes 50000000 | tf_op jit(solution)/shard_map/select/pallas_call | solution.py:113
  94.7 7.1 %collective-permute-done.3.refs_2_ = bf16[2048,256]{1,0:T(8,128)(2,1)S(1)} collective-permute-done((bf16[2048,256]{1,0:T(8,128)(2,1)}, bf16[2048,256]{1,0:T(8,128)(2,1)S(1)}, u32[]{:S(2)}, u32[]{:S(2)}) %collective-permute-start.3) | collective-permute-done | bytes 1048608 | tf_op jit(solution)/shard_map/ppermute | solution.py:509
  105.7 7.4 %collective-permute-done.7.refs_3_ = bf16[1024,128]{1,0:T(8,128)(2,1)S(1)} collective-permute-done((bf16[1024,128]{1,0:T(8,128)(2,1)}, bf16[1024,128]{1,0:T(8,128)(2,1)S(1)}, u32[]{:S(2)}, u32[]{:S(2)}) %collective-permute-start.7) | collective-permute-done | bytes 262176 | tf_op jit(solution)/shard_map/ppermute | solution.py:504
  113.1 4.8 %collective-permute-done.8.refs_4_ = bf16[1024,128]{1,0:T(8,128)(2,1)S(1)} collective-permute-done((bf16[1024,128]{1,0:T(8,128)(2,1)}, bf16[1024,128]{1,0:T(8,128)(2,1)S(1)}, u32[]{:S(2)}, u32[]{:S(2)}) %collective-permute-start.8) | collective-permute-done | bytes 262176 | tf_op jit(solution)/shard_map/ppermute | solution.py:504
  132.1 19.0 %collective-permute-done.10.refs_1_ = bf16[2048,256]{1,0:T(8,128)(2,1)S(1)} collective-permute-done((bf16[2048,256]{1,0:T(8,128)(2,1)}, bf16[2048,256]{1,0:T(8,128)(2,1)S(1)}, u32[]{:S(2)}, u32[]{:S(2)}) %collective-permute-start.10) | collective-permute-done | bytes 1048608 | tf_op jit(solution)/shard_map/ppermute | solution.py:509
  155.4 4.8 %collective-permute-start.21 = (bf16[768,1024]{1,0:T(8,128)(2,1)}, bf16[768,1024]{1,0:T(8,128)(2,1)}, u32[]{:S(2)}, u32[]{:S(2)}) collective-permute-start(bf16[768,1024]{1,0:T(8,128)(2,1)} %flip.5.refs_1_), channel_id=1, source_target_pairs={{0,16},{1,17},{10,26},{11,27},{20,4},{21,5},{30,14},{31,15}} | collective-permute-start | bytes 4718600 | tf_op jit(solution)/shard_map/ppermute | solution.py:531
  160.2 26.0 %collective-permute-done.12 = bf16[1024,256]{1,0:T(8,128)(2,1)S(1)} collective-permute-done((bf16[1024,256]{1,0:T(8,128)(2,1)S(1)}, bf16[1024,256]{1,0:T(8,128)(2,1)S(1)}, u32[]{:S(2)}, u32[]{:S(2)}) %collective-permute-start.12) | collective-permute-done | bytes 524320 | tf_op jit(solution)/shard_map/ppermute | solution.py:509
  188.7 4.5 %flip.7.refs_1_ = bf16[768,1024]{1,0:T(8,128)(2,1)} custom-call(s32[1]{0:T(128)} %bitcast.9.refs_0_, bf16[2048,256]{1,0:T(8,128)(2,1)} %copy-done, bf16[2048,256]{1,0:T(8,128)(2,1)} %copy-done.1, bf16[2048,256]{1,0:T(8,128)(2,1)} %copy-done.2), custom_call_target="tpu_custom_call" | custom-call | bytes 6291456 | tf_op jit(solution)/shard_map/flip/pallas_call | solution.py:331
  193.2 4.5 %collective-permute-start.27 = (bf16[768,1024]{1,0:T(8,128)(2,1)}, bf16[768,1024]{1,0:T(8,128)(2,1)}, u32[]{:S(2)}, u32[]{:S(2)}) collective-permute-start(bf16[768,1024]{1,0:T(8,128)(2,1)} %flip.7.refs_1_), channel_id=1, source_target_pairs={{0,16},{1,17},{10,26},{11,27},{20,4},{21,5},{30,14},{31,15}} | collective-permute-start | bytes 4718600 | tf_op jit(solution)/shard_map/ppermute | solution.py:531
  202.0 16.9 %collective-permute-done.16.refs_4_ = bf16[2048,256]{1,0:T(8,128)(2,1)S(1)} collective-permute-done((bf16[2048,256]{1,0:T(8,128)(2,1)S(1)}, bf16[2048,256]{1,0:T(8,128)(2,1)S(1)}, u32[]{:S(2)}, u32[]{:S(2)}) %collective-permute-start.16) | collective-permute-done | bytes 1048608 | tf_op jit(solution)/shard_map/ppermute | solution.py:509
  235.0 4.4 %settle.5.refs_8_ = bf16[2,768,1024]{2,1,0:T(8,128)(2,1)} custom-call(s32[1]{0:T(128)} %bitcast.22.refs_0_, bf16[768,1024]{1,0:T(8,128)(2,1)} %flip.5.refs_1_, bf16[768,1024]{1,0:T(8,128)(2,1)} %collective-permute-done.20.refs_2_, bf16[768,1024]{1,0:T(8,128)(2,1)} %collective-permute-done.21.refs_3_, bf16[768,1024]{1,0:T(8,128)(2,1)} %collective-permute-done.22.refs_4_), custom_call_target="tpu_custom_call" | custom-call | bytes 6291456 | tf_op jit(solution)/shard_map/settle/pallas_call | solution.py:373
  241.4 4.2 %settle.7.refs_10_ = bf16[2,768,1024]{2,1,0:T(8,128)(2,1)} custom-call(s32[1]{0:T(128)} %bitcast.22.refs_0_, bf16[768,1024]{1,0:T(8,128)(2,1)} %flip.7.refs_1_, bf16[768,1024]{1,0:T(8,128)(2,1)} %collective-permute-done.26.refs_2_, bf16[768,1024]{1,0:T(8,128)(2,1)} %collective-permute-done.27.refs_3_, bf16[768,1024]{1,0:T(8,128)(2,1)} %collective-permute-done.28.refs_4_), custom_call_target="tpu_custom_call" | custom-call | bytes 6291456 | tf_op jit(solution)/shard_map/settle/pallas_call | solution.py:373
  245.7 13.8 %contract.4.refs_11_ = f32[2,2,2048,2048]{3,2,1,0:T(8,128)} custom-call(bf16[2,1024,256]{2,1,0:T(8,128)(2,1)} %bitcast.32, bf16[2,1024,256]{2,1,0:T(8,128)(2,1)} %bitcast.44, bf16[2,1024,256]{2,1,0:T(8,128)(2,1)} %bitcast.47, bf16[2,1024,256]{2,1,0:T(8,128)(2,1)} %bitcast.10.refs_3_, bf16[2,1024,256]{2,1,0:T(8,128)(2,1)} %bitcast.11.refs_4_, ...), custom_call_target="tpu_custom_call" | custom-call | flops 17179869184 | bytes 8388608 | tf_op jit(solution)/shard_map/contract/pallas_call | solution.py:433
  259.5 5.1 %collective-permute-done.18.refs_1_ = bf16[2048,256]{1,0:T(8,128)(2,1)S(1)} collective-permute-done((bf16[2048,256]{1,0:T(8,128)(2,1)S(1)}, bf16[2048,256]{1,0:T(8,128)(2,1)S(1)}, u32[]{:S(2)}, u32[]{:S(2)}) %collective-permute-start.18) | collective-permute-done | bytes 1048608 | tf_op jit(solution)/shard_map/ppermute | solution.py:509
  266.8 4.9 %flip.8.refs_1_ = bf16[1280,1024]{1,0:T(8,128)(2,1)} custom-call(s32[1]{0:T(128)} %bitcast.9.refs_0_, bf16[2048,256]{1,0:T(8,128)(2,1)} %assemble.3.refs_1_, bf16[2048,256]{1,0:T(8,128)(2,1)} %copy-done.9, bf16[2048,256]{1,0:T(8,128)(2,1)} %copy-done.10, bf16[2048,256]{1,0:T(8,128)(2,1)} %copy-done.11, bf16[2048,256]{1,0:T(8,128)(2,1)} %copy-done.13), custom_call_target="tpu_custom_call" | custom-call | bytes 10485760 | tf_op jit(solution)/shard_map/flip/pallas_call | solution.py:331
  278.0 13.8 %contract.5.refs_11_ = f32[2,2,2048,2048]{3,2,1,0:T(8,128)} custom-call(bf16[2,1024,256]{2,1,0:T(8,128)(2,1)} %bitcast.33, bf16[2,1024,256]{2,1,0:T(8,128)(2,1)} %bitcast.45, bf16[2,1024,256]{2,1,0:T(8,128)(2,1)} %bitcast.48, bf16[2,1024,256]{2,1,0:T(8,128)(2,1)} %bitcast.10.refs_3_, ...), custom_call_target="tpu_custom_call", output_to_operand_aliasing={{}: (11, {})} | custom-call | flops 17179869184 | bytes 8388608 | tf_op jit(solution)/shard_map/contract/pallas_call | solution.py:433
  299.4 4.4 %collective-permute-done.32.refs_3_ = bf16[1280,1024]{1,0:T(8,128)(2,1)} collective-permute-done((bf16[1280,1024]{1,0:T(8,128)(2,1)}, bf16[1280,1024]{1,0:T(8,128)(2,1)}, u32[]{:S(2)}, u32[]{:S(2)}) %collective-permute-start.32) | collective-permute-done | bytes 2621472 | tf_op jit(solution)/shard_map/ppermute | solution.py:531
  303.8 24.4 %contract.6.refs_18_ = f32[2,2,2048,2048]{3,2,1,0:T(8,128)} custom-call(bf16[2,1024,256]{2,1,0:T(8,128)(2,1)} %bitcast.15.refs_0_.refs_8_, bf16[2,1024,256]{2,1,0:T(8,128)(2,1)} %bitcast.56, bf16[2,1024,256]{2,1,0:T(8,128)(2,1)} %bitcast.58, bf16[2,1024,256]{2,1,0:T(8,128)(2,1)} %bitcast.60, ...), custom_call_target="tpu_custom_call", output_to_operand_aliasing={{}: (11, {})} | custom-call | flops 34359738368 | bytes 16777216 | tf_op jit(solution)/shard_map/contract/pallas_call | solution.py:433
  332.1 4.3 %settle.9.refs_17_ = bf16[2,768,1024]{2,1,0:T(8,128)(2,1)} custom-call(s32[1]{0:T(128)} %bitcast.22.refs_0_, bf16[768,1024]{1,0:T(8,128)(2,1)} %flip.9.refs_1_, bf16[768,1024]{1,0:T(8,128)(2,1)} %collective-permute-done.34.refs_2_, bf16[768,1024]{1,0:T(8,128)(2,1)} %collective-permute-done.35.refs_3_, bf16[768,1024]{1,0:T(8,128)(2,1)} %collective-permute-done.36.refs_4_), custom_call_target="tpu_custom_call" | custom-call | bytes 6291456 | tf_op jit(solution)/shard_map/settle/pallas_call | solution.py:373
  337.9 5.8 %settle.8.refs_16_ = bf16[2,1280,1024]{2,1,0:T(8,128)(2,1)} custom-call(s32[1]{0:T(128)} %bitcast.22.refs_0_, bf16[1280,1024]{1,0:T(8,128)(2,1)} %flip.8.refs_1_, bf16[1280,1024]{1,0:T(8,128)(2,1)} %collective-permute-done.31.refs_2_, bf16[1280,1024]{1,0:T(8,128)(2,1)} %collective-permute-done.32.refs_3_, bf16[1280,1024]{1,0:T(8,128)(2,1)} %copy-done.16), custom_call_target="tpu_custom_call" | custom-call | bytes 10485760 | tf_op jit(solution)/shard_map/settle/pallas_call | solution.py:373
  343.7 43.9 %contract.7 = f32[2,2,2048,2048]{3,2,1,0:T(8,128)} custom-call(bf16[2,1024,256]{2,1,0:T(8,128)(2,1)} %bitcast.34, bf16[2,1024,256]{2,1,0:T(8,128)(2,1)} %bitcast.46, bf16[2,1024,256]{2,1,0:T(8,128)(2,1)} %bitcast.49, bf16[2,1024,256]{2,1,0:T(8,128)(2,1)} %bitcast.10.refs_3_, bf16[2,1024,256]{2,1,0:T(8,128)(2,1)} %bitcast.11.refs_4_, ...), custom_call_target="tpu_custom_call", output_to_operand_aliasing={{}: (18, {})} | custom-call | flops 68719476736 | bytes 33554432 | tf_op jit(solution)/shard_map/contract/pallas_call | solution.py:433
  (141 shorter events, 84.3 us)
Async XLA Ops:
  76.4 25.4 %collective-permute-start.3 = (bf16[2048,256]{1,0:T(8,128)(2,1)}, bf16[2048,256]{1,0:T(8,128)(2,1)S(1)}, u32[]{:S(2)}, u32[]{:S(2)}) collective-permute-start(bf16[2048,256]{1,0:T(8,128)(2,1)} %assemble.2.refs_1_), channel_id=1, source_target_pairs={{0,2},{2,4},{4,6},{6,7},{7,5},{5,3},{3,1},{1,0},{8,10},{10,12},{12... | collective-permute-start | bytes 3145736 | tf_op jit(solution)/shard_map/ppermute | solution.py:509
  78.0 25.6 %collective-permute-start.4 = (bf16[2048,256]{1,0:T(8,128)(2,1)}, bf16[2048,256]{1,0:T(8,128)(2,1)S(1)}, u32[]{:S(2)}, u32[]{:S(2)}) collective-permute-start(bf16[2048,256]{1,0:T(8,128)(2,1)} %assemble.2.refs_1_), channel_id=1, source_target_pairs={{2,0},{4,2},{6,4},{7,6},{5,7},{3,5},{1,3},{0,1},{10,8},{12,10},{14... | collective-permute-start | bytes 3145736 | tf_op jit(solution)/shard_map/ppermute | solution.py:509
  101.8 24.6 %collective-permute-start.5 = (bf16[2048,256]{1,0:T(8,128)(2,1)S(1)}, bf16[2048,256]{1,0:T(8,128)(2,1)}, u32[]{:S(2)}, u32[]{:S(2)}) collective-permute-start(bf16[2048,256]{1,0:T(8,128)(2,1)S(1)} %collective-permute-done.3.refs_2_), channel_id=1, source_target_pairs={{0,2},{2,4},{4,6},{6,7},{7,5},{5,3},{3,1},{1,0},{8,10},{10,12},{12... | collective-permute-start | bytes 3145736 | tf_op jit(solution)/shard_map/ppermute | solution.py:509
  103.6 24.6 %collective-permute-start.9 = (bf16[2048,256]{1,0:T(8,128)(2,1)S(1)}, bf16[2048,256]{1,0:T(8,128)(2,1)}, u32[]{:S(2)}, u32[]{:S(2)}) collective-permute-start(bf16[2048,256]{1,0:T(8,128)(2,1)S(1)} %collective-permute-done.4.refs_3_), channel_id=1, source_target_pairs={{2,0},{4,2},{6,4},{7,6},{5,7},{3,5},{1,3},{0,1},{10,8},{12,10},{14... | collective-permute-start | bytes 3145736 | tf_op jit(solution)/shard_map/ppermute | solution.py:509
  126.4 24.7 %collective-permute-start.10 = (bf16[2048,256]{1,0:T(8,128)(2,1)}, bf16[2048,256]{1,0:T(8,128)(2,1)S(1)}, u32[]{:S(2)}, u32[]{:S(2)}) collective-permute-start(bf16[2048,256]{1,0:T(8,128)(2,1)} %collective-permute-done.5.refs_1_), channel_id=1, source_target_pairs={{0,2},{2,4},{4,6},{6,7},{7,5},{5,3},{3,1},{1,0},{8,10},{10,12},{12... | collective-permute-start | bytes 3145736 | tf_op jit(solution)/shard_map/ppermute | solution.py:509
  128.2 26.8 %collective-permute-start.11 = (bf16[2048,256]{1,0:T(8,128)(2,1)}, bf16[2048,256]{1,0:T(8,128)(2,1)S(1)}, u32[]{:S(2)}, u32[]{:S(2)}) collective-permute-start(bf16[2048,256]{1,0:T(8,128)(2,1)} %collective-permute-done.9.refs_2_), channel_id=1, source_target_pairs={{2,0},{4,2},{6,4},{7,6},{5,7},{3,5},{1,3},{0,1},{10,8},{12,10},{14... | collective-permute-start | bytes 3145736 | tf_op jit(solution)/shard_map/ppermute | solution.py:509
  151.1 36.6 %collective-permute-start.14 = (bf16[2048,256]{1,0:T(8,128)(2,1)}, bf16[2048,256]{1,0:T(8,128)(2,1)S(1)}, u32[]{:S(2)}, u32[]{:S(2)}) collective-permute-start(bf16[2048,256]{1,0:T(8,128)(2,1)} %assemble.3.refs_1_), channel_id=1, source_target_pairs={{0,2},{2,4},{4,6},{6,7},{7,5},{5,3},{3,1},{1,0},{8,10},{10,12},{12... | collective-permute-start | bytes 3145736 | tf_op jit(solution)/shard_map/ppermute | solution.py:509
  152.9 34.8 %collective-permute-start.15 = (bf16[2048,256]{1,0:T(8,128)(2,1)}, bf16[2048,256]{1,0:T(8,128)(2,1)S(1)}, u32[]{:S(2)}, u32[]{:S(2)}) collective-permute-start(bf16[2048,256]{1,0:T(8,128)(2,1)} %assemble.3.refs_1_), channel_id=1, source_target_pairs={{2,0},{4,2},{6,4},{7,6},{5,7},{3,5},{1,3},{0,1},{10,8},{12,10},{14... | collective-permute-start | bytes 3145736 | tf_op jit(solution)/shard_map/ppermute | solution.py:509
  153.2 33.0 %collective-permute-start.12 = (bf16[1024,256]{1,0:T(8,128)(2,1)S(1)}, bf16[1024,256]{1,0:T(8,128)(2,1)S(1)}, u32[]{:S(2)}, u32[]{:S(2)}) collective-permute-start(bf16[1024,256]{1,0:T(8,128)(2,1)S(1)} %slice.30), channel_id=1, source_target_pairs={{0,2},{2,4},{4,6},{6,7},{7,5},{5,3},{3,1},{1,0},{8,10},{10,12},{12... | collective-permute-start | bytes 1572872 | tf_op jit(solution)/shard_map/ppermute | solution.py:509
  155.1 32.6 %collective-permute-start.13 = (bf16[1024,256]{1,0:T(8,128)(2,1)S(1)}, bf16[1024,256]{1,0:T(8,128)(2,1)S(1)}, u32[]{:S(2)}, u32[]{:S(2)}) collective-permute-start(bf16[1024,256]{1,0:T(8,128)(2,1)S(1)} %slice.31), channel_id=1, source_target_pairs={{2,0},{4,2},{6,4},{7,6},{5,7},{3,5},{1,3},{0,1},{10,8},{12,10},{14... | collective-permute-start | bytes 1572872 | tf_op jit(solution)/shard_map/ppermute | solution.py:509
  155.4 46.6 %collective-permute-start.21 = (bf16[768,1024]{1,0:T(8,128)(2,1)}, bf16[768,1024]{1,0:T(8,128)(2,1)}, u32[]{:S(2)}, u32[]{:S(2)}) collective-permute-start(bf16[768,1024]{1,0:T(8,128)(2,1)} %flip.5.refs_1_), channel_id=1, source_target_pairs={{0,16},{1,17},{10,26},{11,27},{20,4},{21,5},{30,14},{31,15}} | collective-permute-start | bytes 4718600 | tf_op jit(solution)/shard_map/ppermute | solution.py:531
  193.2 28.9 %collective-permute-start.27 = (bf16[768,1024]{1,0:T(8,128)(2,1)}, bf16[768,1024]{1,0:T(8,128)(2,1)}, u32[]{:S(2)}, u32[]{:S(2)}) collective-permute-start(bf16[768,1024]{1,0:T(8,128)(2,1)} %flip.7.refs_1_), channel_id=1, source_target_pairs={{0,16},{1,17},{10,26},{11,27},{20,4},{21,5},{30,14},{31,15}} | collective-permute-start | bytes 4718600 | tf_op jit(solution)/shard_map/ppermute | solution.py:531
  197.7 21.2 %collective-permute-start.16 = (bf16[2048,256]{1,0:T(8,128)(2,1)S(1)}, bf16[2048,256]{1,0:T(8,128)(2,1)S(1)}, u32[]{:S(2)}, u32[]{:S(2)}) collective-permute-start(bf16[2048,256]{1,0:T(8,128)(2,1)S(1)} %collective-permute-done.14.refs_2_), channel_id=1, source_target_pairs={{0,2},{2,4},{4,6},{6,7},{7,5},{5,3},{3,1},{1,0},{8,10},{10,12},{12... | collective-permute-start | bytes 3145736 | tf_op jit(solution)/shard_map/ppermute | solution.py:509
  197.7 23.4 %collective-permute-start.17 = (bf16[2048,256]{1,0:T(8,128)(2,1)S(1)}, bf16[2048,256]{1,0:T(8,128)(2,1)S(1)}, u32[]{:S(2)}, u32[]{:S(2)}) collective-permute-start(bf16[2048,256]{1,0:T(8,128)(2,1)S(1)} %collective-permute-done.15.refs_3_), channel_id=1, source_target_pairs={{2,0},{4,2},{6,4},{7,6},{5,7},{3,5},{1,3},{0,1},{10,8},{12,10},{14... | collective-permute-start | bytes 3145736 | tf_op jit(solution)/shard_map/ppermute | solution.py:509
  199.7 26.2 %collective-permute-start.24 = (bf16[512,1024]{1,0:T(8,128)(2,1)S(1)}, bf16[512,1024]{1,0:T(8,128)(2,1)}, u32[]{:S(2)}, u32[]{:S(2)}) collective-permute-start(bf16[512,1024]{1,0:T(8,128)(2,1)S(1)} %copy-done.15), channel_id=1, source_target_pairs={{0,16},{1,17},{10,26},{11,27},{20,4},{21,5},{30,14},{31,15}} | collective-permute-start | bytes 3145736 | tf_op jit(solution)/shard_map/ppermute | solution.py:531
  202.0 23.9 %collective-permute-start.23 = (bf16[512,1024]{1,0:T(8,128)(2,1)S(1)}, bf16[512,1024]{1,0:T(8,128)(2,1)S(1)}, u32[]{:S(2)}, u32[]{:S(2)}) collective-permute-start(bf16[512,1024]{1,0:T(8,128)(2,1)S(1)} %copy-done.15), channel_id=1, source_target_pairs={{0,8},{8,0},{16,24},{24,16},{1,9},{9,1},{17,25},{25,17},{2,10},{10... | collective-permute-start | bytes 3145736 | tf_op jit(solution)/shard_map/ppermute | solution.py:525
  222.1 19.4 %collective-permute-start.26 = (bf16[768,1024]{1,0:T(8,128)(2,1)}, bf16[768,1024]{1,0:T(8,128)(2,1)}, u32[]{:S(2)}, u32[]{:S(2)}) collective-permute-start(bf16[768,1024]{1,0:T(8,128)(2,1)} %flip.7.refs_1_), channel_id=1, source_target_pairs={{0,8},{8,0},{16,24},{24,16},{1,9},{9,1},{17,25},{25,17},{2,10},{10... | collective-permute-start | bytes 4718600 | tf_op jit(solution)/shard_map/ppermute | solution.py:525
  239.4 25.2 %collective-permute-start.18 = (bf16[2048,256]{1,0:T(8,128)(2,1)S(1)}, bf16[2048,256]{1,0:T(8,128)(2,1)S(1)}, u32[]{:S(2)}, u32[]{:S(2)}) collective-permute-start(bf16[2048,256]{1,0:T(8,128)(2,1)S(1)} %copy-done.12), channel_id=1, source_target_pairs={{0,2},{2,4},{4,6},{6,7},{7,5},{5,3},{3,1},{1,0},{8,10},{10,12},{12... | collective-permute-start | bytes 3145736 | tf_op jit(solution)/shard_map/ppermute | solution.py:509
  239.4 27.4 %collective-permute-start.19 = (bf16[2048,256]{1,0:T(8,128)(2,1)S(1)}, bf16[2048,256]{1,0:T(8,128)(2,1)S(1)}, u32[]{:S(2)}, u32[]{:S(2)}) collective-permute-start(bf16[2048,256]{1,0:T(8,128)(2,1)S(1)} %copy-done.14), channel_id=1, source_target_pairs={{2,0},{4,2},{6,4},{7,6},{5,7},{3,5},{1,3},{0,1},{10,8},{12,10},{14... | collective-permute-start | bytes 3145736 | tf_op jit(solution)/shard_map/ppermute | solution.py:509
  271.7 32.1 %collective-permute-start.32 = (bf16[1280,1024]{1,0:T(8,128)(2,1)}, bf16[1280,1024]{1,0:T(8,128)(2,1)}, u32[]{:S(2)}, u32[]{:S(2)}) collective-permute-start(bf16[1280,1024]{1,0:T(8,128)(2,1)} %flip.8.refs_1_), channel_id=1, source_target_pairs={{0,16},{1,17},{10,26},{11,27},{20,4},{21,5},{30,14},{31,15}} | collective-permute-start | bytes 7864328 | tf_op jit(solution)/shard_map/ppermute | solution.py:531
  291.8 44.5 %collective-permute-start.31 = (bf16[1280,1024]{1,0:T(8,128)(2,1)S(1)}, bf16[1280,1024]{1,0:T(8,128)(2,1)}, u32[]{:S(2)}, u32[]{:S(2)}) collective-permute-start(bf16[1280,1024]{1,0:T(8,128)(2,1)S(1)} %copy-done.3), channel_id=1, source_target_pairs={{0,8},{8,0},{16,24},{24,16},{1,9},{9,1},{17,25},{25,17},{2,10},{10... | collective-permute-start | bytes 7864328 | tf_op jit(solution)/shard_map/ppermute | solution.py:525
  296.9 31.2 %collective-permute-start.35 = (bf16[768,1024]{1,0:T(8,128)(2,1)}, bf16[768,1024]{1,0:T(8,128)(2,1)}, u32[]{:S(2)}, u32[]{:S(2)}) collective-permute-start(bf16[768,1024]{1,0:T(8,128)(2,1)} %flip.9.refs_1_), channel_id=1, source_target_pairs={{0,16},{1,17},{10,26},{11,27},{20,4},{21,5},{30,14},{31,15}} | collective-permute-start | bytes 4718600 | tf_op jit(solution)/shard_map/ppermute | solution.py:531
  299.4 29.3 %collective-permute-start.34 = (bf16[768,1024]{1,0:T(8,128)(2,1)}, bf16[768,1024]{1,0:T(8,128)(2,1)}, u32[]{:S(2)}, u32[]{:S(2)}) collective-permute-start(bf16[768,1024]{1,0:T(8,128)(2,1)} %flip.9.refs_1_), channel_id=1, source_target_pairs={{0,8},{8,0},{16,24},{24,16},{1,9},{9,1},{17,25},{25,17},{2,10},{10... | collective-permute-start | bytes 4718600 | tf_op jit(solution)/shard_map/ppermute | solution.py:525
  303.8 32.5 %collective-permute-start.33 = (bf16[1280,1024]{1,0:T(8,128)(2,1)}, bf16[1280,1024]{1,0:T(8,128)(2,1)S(1)}, u32[]{:S(2)}, u32[]{:S(2)}) collective-permute-start(bf16[1280,1024]{1,0:T(8,128)(2,1)} %collective-permute-done.32.refs_3_), channel_id=1, source_target_pairs={{0,8},{8,0},{16,24},{24,16},{1,9},{9,1},{17,25},{25,17},{2,10},{10... | collective-permute-start | bytes 7864328 | tf_op jit(solution)/shard_map/ppermute | solution.py:525
  (38 other events, 360.9 us)

commit v6 on v5

--- a/solution.py
+++ b/solution.py
@@ -350,15 +350,16 @@
 
 def settle_kernel(pairs, row_count, which_ref, *refs):
     out_ref = refs[row_count]
+    kind = jnp.float32 if pairs % 16 else jnp.bfloat16
     for k in range(row_count):
 
         @pl.when(which_ref[0] == k)
         def _():
-            values = refs[k][...].astype(jnp.float32)
+            values = -refs[k][...].astype(kind)
             rows, across = values.shape
-            out_ref[0] = (-values).astype(jnp.bfloat16)
+            out_ref[0] = values.astype(jnp.bfloat16)
             values = values.reshape(rows // (2 * pairs), 2, pairs, across)
-            turned = jnp.stack([-values[:, 1], values[:, 0]], axis=1)
+            turned = jnp.stack([values[:, 1], -values[:, 0]], axis=1)
             out_ref[1] = turned.reshape(rows, across).astype(jnp.bfloat16)
 
 
@@ -537,21 +538,20 @@
     one = [[own], go_round(own, own)]
     sent = select(after(table, own), positions[1], me, rows, features)
     one[1] = [after(block, *sent) for block in one[1]]
-    own = assemble(across_rows(sent), me, features)
+    own = assemble(across_rows([after(part, *one[1]) for part in sent]), me, features)
     one.append(go_round(*one[1]))
-    copies = [column(sum(one[:2], []))]
+    copies = [column(sum(one[:2], []), (own,))]
     one[2] = [after(block, own, copies[0][0]) for block in one[2]]
     for t in range(3, half):
         one.append(go_round(*one[t - 1]))
     copies.append(column(sum(one[2 : half - 1], [])))
     below, above = [after(block, copies[1][0]) for block in one[half - 1]]
+    copies.append(column(one[half - 1]))
     one.append(last_round(below, above))
-    two = [[own], go_round(*[after(own, below)] * 2)]
-    two.append(go_round(*two[1]))
-    copies.append(column(sum(one[half - 1 :], []), two[1], two[2]))
+    two = [[own], go_round(*[after(own, *one[half])] * 2)]
+    copies.append(column(one[half], (), two[1]))
     rights = [settle(which, some, pairs) for some in copies]
-    for t in range(3, half):
-        two.append(go_round(*two[t - 1]))
+    two.append(go_round(*[after(block, *rights[:2]) for block in two[1]]))
 
     def as_lefts(slots):
         return [slot.reshape(parts, -1, width) for slot in sum(slots, [])]
@@ -560,13 +560,16 @@
     wide = CHUNKS[0][1] // 2
     first = contract(None, [lefts], rights, unit, 0, wide, 0, 1, 0)
     second = contract(first, [lefts], rights, unit, 0, wide, 1, 1, 1)
-    middle = half // 2 + 1
-    copies = [column(sum(two[:middle], []), two[half - 1] + [first])]
-    two.append(last_round(*[after(block, *rights) for block in two[half - 1]]))
+    copies = [column(sum(two[:2], []), two[2])]
+    two.append(go_round(*[after(block, first) for block in two[2]]))
+    for t in range(4, half):
+        two.append(go_round(*two[t - 1]))
+    copies.append(column(sum(two[2:half], []), two[half - 1]))
+    two.append(last_round(*[after(block, second, copies[0][0]) for block in two[half - 1]]))
     share = CHUNKS[0][1]
     both = [lefts, as_lefts(two)]
     result = contract(second, both[1:], rights, unit, share, share, 0, 1, 0)
-    copies.append(column(sum(two[middle:], []), (), (result,)))
+    copies.append(column(two[half], (), (result,)))
     rights = [settle(which, some, pairs) for some in copies]
     result = contract(result, both, rights, unit, 0, share, 0, 1, 1)
     return result.reshape(2, parts * block, block)

time: 389 us -> 394 us (1.013)
  waiting for transfers between devices: 121 us -> 112 us
  Pallas kernels: 210 us -> 218 us
  starting transfers between devices: 40.8 us -> 47.4 us
    ppermute x8, waiting for transfers between devices: 75.3 us -> 39.2 us  [go_round(): lax.ppermute(below, 'col', ring_up)]
    ppermute x8, waiting for transfers between devices: 5.88 us -> 29.4 us  [go_round(): lax.ppermute(above, 'col', ring_down)]
    ppermute x5 -> x7, waiting for transfers between devices: 8.21 us -> 17 us  [column(): copies.append(lax.ppermute(held, ('row', 'col'), perm))]
    ppermute x5 -> x7, starting transfers between devices: 18.2 us -> 23.6 us  [column(): copies.append(lax.ppermute(held, ('row', 'col'), perm))]
    pallas_call x5 -> x7, Pallas kernels: 20.9 us -> 26.2 us  [flip(): pl.pallas_call(lambda *refs: flip_kernel(slot_count, *refs), grid_spec=pl...]
    ppermute x10 -> x14, waiting for transfers between devices: 7.02 us -> 1.88 us  [column(): copies.append(lax.ppermute(held, 'row', [(r, r ^ 1) for r in range(rows)]))]
    pallas_call x5 -> x7, Pallas kernels: 21.7 us -> 24.7 us  [settle(): pl.pallas_call(lambda *refs: settle_kernel(pairs, row_count, *refs), grid...]
    unnamed x54 -> x56, local copies, waits for them, and re-layouts: 9.2 us -> 7.23 us
  transfers between devices with their start and end apart: 37 -> 43, of which waited for: 17 -> 19; matrix products, arithmetic and copies ran while one was open for 0% -> 0% of each run, Pallas kernels for 26% -> 30%
where the time goes in v6:
time: 394 us; the launch traced here: 392 us
  Pallas kernels  218 us (55%)
  waiting for transfers between devices  112 us (28%)
  starting transfers between devices  47.4 us (12%)
  local copies, waits for them, and re-layouts  8.94 us (2%)
  other arithmetic  4.21 us (1%)
    pallas_call x4, Pallas kernels, contract(): pl.pallas_call(lambda *refs: contract_kernel(slot_count, shares, len(righ...  95.5 us
    pallas_call x1, Pallas kernels, transform(): pl.pallas_call(lambda *refs: transform_kernel(pairs, load_steps, step_row...  51 us
    ppermute x8, waiting for transfers between devices, go_round(): lax.ppermute(below, 'col', ring_up)  39.2 us
    ppermute x8, waiting for transfers between devices, go_round(): lax.ppermute(above, 'col', ring_down)  29.4 us
    pallas_call x7, Pallas kernels, flip(): pl.pallas_call(lambda *refs: flip_kernel(slot_count, *refs), grid_spec=pl...  26.2 us
    ppermute x6, waiting for transfers between devices, across_rows(): lax.ppermute(parcels[s], 'row', [(r, r ^ s) for r in range(rows)])  25 us
    pallas_call x7, Pallas kernels, settle(): pl.pallas_call(lambda *refs: settle_kernel(pairs, row_count, *refs), grid...  24.7 us
    ppermute x7, starting transfers between devices, column(): copies.append(lax.ppermute(held, ('row', 'col'), perm))  23.6 us
  transfers between devices with their start and end apart: 43, of which 19 were waited for; matrix products, arithmetic and copies ran while one was open for 0% of the time, Pallas kernels for 30%

profile of v6, /device:TPU:0, one launch (start us, length us, event | category | flops | bytes accessed | tf_op | source)
XLA Modules:
  0.0 391.9 jit_solution(15844423882558488534)
XLA Ops:
  6.4 51.0 %transform.1 = (bf16[1024,128]{1,0:T(8,128)(2,1)}, bf16[1024,128]{1,0:T(8,128)(2,1)}, bf16[1024,128]{1,0:T(8,128)(2,1)}, bf16[1024,128]{1,0:T(8,128)(2,1)}, f32[32768,128]{1,0:T(8,128)}) custom-call(s32[8192]{0:T(1024)} %bitcast.65, s32[1]{0:T(128)} %bitcast.refs_1_.refs_0_, bf16[64,256]{1,0:T(8,128)(2,1)} %fusion.16.refs_2_, ...), custom_call_target="tpu_custom_call" | custom-call | flops 9663676416 | bytes 40000000 | tf_op jit(solution)/shard_map/transform/pallas_call | solution.py:233
  60.5 7.3 %collective-permute-done.1.refs_3_ = bf16[1024,128]{1,0:T(8,128)(2,1)S(1)} collective-permute-done((bf16[1024,128]{1,0:T(8,128)(2,1)}, bf16[1024,128]{1,0:T(8,128)(2,1)S(1)}, u32[]{:S(2)}, u32[]{:S(2)}) %collective-permute-start.1) | collective-permute-done | bytes 262176 | tf_op jit(solution)/shard_map/ppermute | solution.py:505
  67.8 5.1 %collective-permute-done.2.refs_4_ = bf16[1024,128]{1,0:T(8,128)(2,1)S(1)} collective-permute-done((bf16[1024,128]{1,0:T(8,128)(2,1)}, bf16[1024,128]{1,0:T(8,128)(2,1)S(1)}, u32[]{:S(2)}, u32[]{:S(2)}) %collective-permute-start.2) | collective-permute-done | bytes 262176 | tf_op jit(solution)/shard_map/ppermute | solution.py:505
  78.9 15.6 %select.45 = (bf16[1024,128]{1,0:T(8,128)(2,1)}, bf16[1024,128]{1,0:T(8,128)(2,1)}, bf16[1024,128]{1,0:T(8,128)(2,1)}, bf16[1024,128]{1,0:T(8,128)(2,1)}) custom-call(s32[8192]{0:T(1024)} %bitcast.62, s32[1]{0:T(128)} %bitcast.refs_1_.refs_0_, f32[32768,128]{1,0:T(8,128)} %get-tuple-element.42.refs_2_), custom_call_target="tpu_custom_call" | custom-call | bytes 50000000 | tf_op jit(solution)/shard_map/select/pallas_call | solution.py:113
  94.6 7.1 %collective-permute-done.3.refs_2_ = bf16[2048,256]{1,0:T(8,128)(2,1)S(1)} collective-permute-done((bf16[2048,256]{1,0:T(8,128)(2,1)}, bf16[2048,256]{1,0:T(8,128)(2,1)S(1)}, u32[]{:S(2)}, u32[]{:S(2)}) %collective-permute-start.3) | collective-permute-done | bytes 1048608 | tf_op jit(solution)/shard_map/ppermute | solution.py:510
  105.6 6.7 %collective-permute-done.8.refs_4_ = bf16[1024,128]{1,0:T(8,128)(2,1)S(1)} collective-permute-done((bf16[1024,128]{1,0:T(8,128)(2,1)}, bf16[1024,128]{1,0:T(8,128)(2,1)S(1)}, u32[]{:S(2)}, u32[]{:S(2)}) %collective-permute-start.8) | collective-permute-done | bytes 262176 | tf_op jit(solution)/shard_map/ppermute | solution.py:505
  112.3 5.9 %collective-permute-done.7.refs_3_ = bf16[1024,128]{1,0:T(8,128)(2,1)S(1)} collective-permute-done((bf16[1024,128]{1,0:T(8,128)(2,1)}, bf16[1024,128]{1,0:T(8,128)(2,1)S(1)}, u32[]{:S(2)}, u32[]{:S(2)}) %collective-permute-start.7) | collective-permute-done | bytes 262176 | tf_op jit(solution)/shard_map/ppermute | solution.py:505
  135.8 15.8 %collective-permute-done.10.refs_1_ = bf16[2048,256]{1,0:T(8,128)(2,1)S(1)} collective-permute-done((bf16[2048,256]{1,0:T(8,128)(2,1)}, bf16[2048,256]{1,0:T(8,128)(2,1)S(1)}, u32[]{:S(2)}, u32[]{:S(2)}) %collective-permute-start.10) | collective-permute-done | bytes 1048608 | tf_op jit(solution)/shard_map/ppermute | solution.py:510
  175.3 10.7 %collective-permute-done.28.refs_3_ = bf16[256,1024]{1,0:T(8,128)(2,1)S(1)} collective-permute-done((bf16[256,1024]{1,0:T(8,128)(2,1)}, bf16[256,1024]{1,0:T(8,128)(2,1)S(1)}, u32[]{:S(2)}, u32[]{:S(2)}) %collective-permute-start.28) | collective-permute-done | bytes 524320 | tf_op jit(solution)/shard_map/ppermute | solution.py:532
  186.5 9.4 %collective-permute-done.15.refs_3_ = bf16[2048,256]{1,0:T(8,128)(2,1)S(1)} collective-permute-done((bf16[2048,256]{1,0:T(8,128)(2,1)S(1)}, bf16[2048,256]{1,0:T(8,128)(2,1)S(1)}, u32[]{:S(2)}, u32[]{:S(2)}) %collective-permute-start.15) | collective-permute-done | bytes 1048608 | tf_op jit(solution)/shard_map/ppermute | solution.py:510
  200.9 4.2 %settle.7.refs_8_ = bf16[2,768,1024]{2,1,0:T(8,128)(2,1)} custom-call(s32[1]{0:T(128)} %bitcast.18.refs_0_, bf16[768,1024]{1,0:T(8,128)(2,1)} %flip.7.refs_1_, bf16[768,1024]{1,0:T(8,128)(2,1)} %collective-permute-done.16.refs_2_, bf16[768,1024]{1,0:T(8,128)(2,1)} %copy-done.15, bf16[768,1024]{1,0:T(8,128)(2,1)} %collective-permute-done.18.refs_4_), custom_call_target="tpu_custom_call" | custom-call | bytes 6291456 | tf_op jit(solution)/shard_map/settle/pallas_call | solution.py:374
  212.7 13.7 %contract.4.refs_12_ = f32[2,2,2048,2048]{3,2,1,0:T(8,128)} custom-call(bf16[2,1024,256]{2,1,0:T(8,128)(2,1)} %bitcast.32, bf16[2,1024,256]{2,1,0:T(8,128)(2,1)} %bitcast.44, bf16[2,1024,256]{2,1,0:T(8,128)(2,1)} %bitcast.47, bf16[2,1024,256]{2,1,0:T(8,128)(2,1)} %bitcast.10.refs_3_, bf16[2,1024,256]{2,1,0:T(8,128)(2,1)} %bitcast.11.refs_4_, ...), custom_call_target="tpu_custom_call" | custom-call | flops 17179869184 | bytes 8388608 | tf_op jit(solution)/shard_map/contract/pallas_call | solution.py:434
  226.4 4.2 %collective-permute-done.23.refs_2_ = bf16[2048,256]{1,0:T(8,128)(2,1)} collective-permute-done((bf16[2048,256]{1,0:T(8,128)(2,1)S(1)}, bf16[2048,256]{1,0:T(8,128)(2,1)}, u32[]{:S(2)}, u32[]{:S(2)}) %collective-permute-start.23) | collective-permute-done | bytes 1048608 | tf_op jit(solution)/shard_map/ppermute | solution.py:510
  238.1 5.1 %collective-permute-start.35 = (bf16[768,1024]{1,0:T(8,128)(2,1)}, bf16[768,1024]{1,0:T(8,128)(2,1)}, u32[]{:S(2)}, u32[]{:S(2)}) collective-permute-start(bf16[768,1024]{1,0:T(8,128)(2,1)} %flip.11.refs_1_), channel_id=1, source_target_pairs={{0,16},{1,17},{10,26},{11,27},{20,4},{21,5},{30,14},{31,15}} | collective-permute-start | bytes 4718600 | tf_op jit(solution)/shard_map/ppermute | solution.py:532
  243.3 13.5 %collective-permute-done.31.refs_4_ = bf16[2048,256]{1,0:T(8,128)(2,1)S(1)} collective-permute-done((bf16[2048,256]{1,0:T(8,128)(2,1)}, bf16[2048,256]{1,0:T(8,128)(2,1)S(1)}, u32[]{:S(2)}, u32[]{:S(2)}) %collective-permute-start.31) | collective-permute-done | bytes 1048608 | tf_op jit(solution)/shard_map/ppermute | solution.py:510
  259.0 4.3 %flip.12.refs_1_ = bf16[1024,1024]{1,0:T(8,128)(2,1)} custom-call(s32[1]{0:T(128)} %bitcast.9.refs_0_, bf16[2048,256]{1,0:T(8,128)(2,1)} %collective-permute-done.22.refs_1_, bf16[2048,256]{1,0:T(8,128)(2,1)} %collective-permute-done.23.refs_2_, bf16[2048,256]{1,0:T(8,128)(2,1)} %copy-done.9, bf16[2048,256]{1,0:T(8,128)(2,1)} %copy-done.7), custom_call_target="tpu_custom_call" | custom-call | bytes 8388608 | tf_op jit(solution)/shard_map/flip/pallas_call | solution.py:331
  263.2 5.8 %collective-permute-start.38 = (bf16[1024,1024]{1,0:T(8,128)(2,1)}, bf16[1024,1024]{1,0:T(8,128)(2,1)}, u32[]{:S(2)}, u32[]{:S(2)}) collective-permute-start(bf16[1024,1024]{1,0:T(8,128)(2,1)} %flip.12.refs_1_), channel_id=1, source_target_pairs={{0,16},{1,17},{10,26},{11,27},{20,4},{21,5},{30,14},{31,15}} | collective-permute-start | bytes 6291464 | tf_op jit(solution)/shard_map/ppermute | solution.py:532
  269.0 13.7 %contract.5.refs_12_ = f32[2,2,2048,2048]{3,2,1,0:T(8,128)} custom-call(bf16[2,1024,256]{2,1,0:T(8,128)(2,1)} %bitcast.33, bf16[2,1024,256]{2,1,0:T(8,128)(2,1)} %bitcast.45, bf16[2,1024,256]{2,1,0:T(8,128)(2,1)} %bitcast.48, bf16[2,1024,256]{2,1,0:T(8,128)(2,1)} %bitcast.10.refs_3_, ...), custom_call_target="tpu_custom_call", output_to_operand_aliasing={{}: (12, {})} | custom-call | flops 17179869184 | bytes 8388608 | tf_op jit(solution)/shard_map/contract/pallas_call | solution.py:434
  284.9 8.5 %collective-permute-done.32 = bf16[1024,256]{1,0:T(8,128)(2,1)S(1)} collective-permute-done((bf16[1024,256]{1,0:T(8,128)(2,1)S(1)}, bf16[1024,256]{1,0:T(8,128)(2,1)S(1)}, u32[]{:S(2)}, u32[]{:S(2)}) %collective-permute-start.32) | collective-permute-done | bytes 524320 | tf_op jit(solution)/shard_map/ppermute | solution.py:510
  302.1 6.3 %collective-permute-done.41.refs_3_ = bf16[256,1024]{1,0:T(8,128)(2,1)S(1)} collective-permute-done((bf16[256,1024]{1,0:T(8,128)(2,1)}, bf16[256,1024]{1,0:T(8,128)(2,1)S(1)}, u32[]{:S(2)}, u32[]{:S(2)}) %collective-permute-start.41) | collective-permute-done | bytes 524320 | tf_op jit(solution)/shard_map/ppermute | solution.py:532
  308.9 24.3 %contract.6.refs_19_ = f32[2,2,2048,2048]{3,2,1,0:T(8,128)} custom-call(bf16[2,1024,256]{2,1,0:T(8,128)(2,1)} %bitcast.50, bf16[2,1024,256]{2,1,0:T(8,128)(2,1)} %bitcast.60, bf16[2,1024,256]{2,1,0:T(8,128)(2,1)} %bitcast.58, bf16[2,1024,256]{2,1,0:T(8,128)(2,1)} %bitcast.19.refs_3_.refs_11_, ...), custom_call_target="tpu_custom_call", output_to_operand_aliasing={{}: (12, {})} | custom-call | flops 34359738368 | bytes 16777216 | tf_op jit(solution)/shard_map/contract/pallas_call | solution.py:434
  338.8 4.2 %settle.11.refs_16_ = bf16[2,768,1024]{2,1,0:T(8,128)(2,1)} custom-call(s32[1]{0:T(128)} %bitcast.18.refs_0_, bf16[768,1024]{1,0:T(8,128)(2,1)} %flip.11.refs_1_, bf16[768,1024]{1,0:T(8,128)(2,1)} %collective-permute-done.34.refs_2_, bf16[768,1024]{1,0:T(8,128)(2,1)} %collective-permute-done.35.refs_3_, bf16[768,1024]{1,0:T(8,128)(2,1)} %collective-permute-done.36.refs_4_), custom_call_target="tpu_custom_call" | custom-call | bytes 6291456 | tf_op jit(solution)/shard_map/settle/pallas_call | solution.py:374
  343.0 4.9 %settle.12.refs_17_ = bf16[2,1024,1024]{2,1,0:T(8,128)(2,1)} custom-call(s32[1]{0:T(128)} %bitcast.18.refs_0_, bf16[1024,1024]{1,0:T(8,128)(2,1)} %flip.12.refs_1_, bf16[1024,1024]{1,0:T(8,128)(2,1)} %collective-permute-done.37.refs_2_, bf16[1024,1024]{1,0:T(8,128)(2,1)} %collective-permute-done.38.refs_3_, bf16[1024,1024]{1,0:T(8,128)(2,1)} %collective-permute-done.39.refs_4_), custom_call_target="tpu_custom_call" | custom-call | bytes 8388608 | tf_op jit(solution)/shard_map/settle/pallas_call | solution.py:374
  347.9 43.8 %contract.7 = f32[2,2,2048,2048]{3,2,1,0:T(8,128)} custom-call(bf16[2,1024,256]{2,1,0:T(8,128)(2,1)} %bitcast.34, bf16[2,1024,256]{2,1,0:T(8,128)(2,1)} %bitcast.46, bf16[2,1024,256]{2,1,0:T(8,128)(2,1)} %bitcast.49, bf16[2,1024,256]{2,1,0:T(8,128)(2,1)} %bitcast.10.refs_3_, bf16[2,1024,256]{2,1,0:T(8,128)(2,1)} %bitcast.11.refs_4_, ...), custom_call_target="tpu_custom_call", output_to_operand_aliasing={{}: (19, {})} | custom-call | flops 68719476736 | bytes 33554432 | tf_op jit(solution)/shard_map/contract/pallas_call | solution.py:434
  (159 shorter events, 100.2 us)
Async XLA Ops:
  76.3 25.4 %collective-permute-start.3 = (bf16[2048,256]{1,0:T(8,128)(2,1)}, bf16[2048,256]{1,0:T(8,128)(2,1)S(1)}, u32[]{:S(2)}, u32[]{:S(2)}) collective-permute-start(bf16[2048,256]{1,0:T(8,128)(2,1)} %assemble.2.refs_1_), channel_id=1, source_target_pairs={{0,2},{2,4},{4,6},{6,7},{7,5},{5,3},{3,1},{1,0},{8,10},{10,12},{12... | collective-permute-start | bytes 3145736 | tf_op jit(solution)/shard_map/ppermute | solution.py:510
  77.9 25.6 %collective-permute-start.4 = (bf16[2048,256]{1,0:T(8,128)(2,1)}, bf16[2048,256]{1,0:T(8,128)(2,1)S(1)}, u32[]{:S(2)}, u32[]{:S(2)}) collective-permute-start(bf16[2048,256]{1,0:T(8,128)(2,1)} %assemble.2.refs_1_), channel_id=1, source_target_pairs={{2,0},{4,2},{6,4},{7,6},{5,7},{3,5},{1,3},{0,1},{10,8},{12,10},{14... | collective-permute-start | bytes 3145736 | tf_op jit(solution)/shard_map/ppermute | solution.py:510
  101.7 24.6 %collective-permute-start.5 = (bf16[2048,256]{1,0:T(8,128)(2,1)S(1)}, bf16[2048,256]{1,0:T(8,128)(2,1)}, u32[]{:S(2)}, u32[]{:S(2)}) collective-permute-start(bf16[2048,256]{1,0:T(8,128)(2,1)S(1)} %collective-permute-done.3.refs_2_), channel_id=1, source_target_pairs={{0,2},{2,4},{4,6},{6,7},{7,5},{5,3},{3,1},{1,0},{8,10},{10,12},{12... | collective-permute-start | bytes 3145736 | tf_op jit(solution)/shard_map/ppermute | solution.py:510
  103.5 24.6 %collective-permute-start.9 = (bf16[2048,256]{1,0:T(8,128)(2,1)S(1)}, bf16[2048,256]{1,0:T(8,128)(2,1)}, u32[]{:S(2)}, u32[]{:S(2)}) collective-permute-start(bf16[2048,256]{1,0:T(8,128)(2,1)S(1)} %collective-permute-done.4.refs_3_), channel_id=1, source_target_pairs={{2,0},{4,2},{6,4},{7,6},{5,7},{3,5},{1,3},{0,1},{10,8},{12,10},{14... | collective-permute-start | bytes 3145736 | tf_op jit(solution)/shard_map/ppermute | solution.py:510
  126.4 25.3 %collective-permute-start.10 = (bf16[2048,256]{1,0:T(8,128)(2,1)}, bf16[2048,256]{1,0:T(8,128)(2,1)S(1)}, u32[]{:S(2)}, u32[]{:S(2)}) collective-permute-start(bf16[2048,256]{1,0:T(8,128)(2,1)} %collective-permute-done.5.refs_1_), channel_id=1, source_target_pairs={{0,2},{2,4},{4,6},{6,7},{7,5},{5,3},{3,1},{1,0},{8,10},{10,12},{12... | collective-permute-start | bytes 3145736 | tf_op jit(solution)/shard_map/ppermute | solution.py:510
  128.1 25.3 %collective-permute-start.11 = (bf16[2048,256]{1,0:T(8,128)(2,1)}, bf16[2048,256]{1,0:T(8,128)(2,1)S(1)}, u32[]{:S(2)}, u32[]{:S(2)}) collective-permute-start(bf16[2048,256]{1,0:T(8,128)(2,1)} %collective-permute-done.9.refs_2_), channel_id=1, source_target_pairs={{2,0},{4,2},{6,4},{7,6},{5,7},{3,5},{1,3},{0,1},{10,8},{12,10},{14... | collective-permute-start | bytes 3145736 | tf_op jit(solution)/shard_map/ppermute | solution.py:510
  128.4 44.8 %collective-permute-start.17 = (bf16[768,1024]{1,0:T(8,128)(2,1)}, bf16[768,1024]{1,0:T(8,128)(2,1)S(1)}, u32[]{:S(2)}, u32[]{:S(2)}) collective-permute-start(bf16[768,1024]{1,0:T(8,128)(2,1)} %flip.7.refs_1_), channel_id=1, source_target_pairs={{0,16},{1,17},{10,26},{11,27},{20,4},{21,5},{30,14},{31,15}} | collective-permute-start | bytes 4718600 | tf_op jit(solution)/shard_map/ppermute | solution.py:532
  132.1 42.8 %collective-permute-start.16 = (bf16[768,1024]{1,0:T(8,128)(2,1)}, bf16[768,1024]{1,0:T(8,128)(2,1)}, u32[]{:S(2)}, u32[]{:S(2)}) collective-permute-start(bf16[768,1024]{1,0:T(8,128)(2,1)} %flip.7.refs_1_), channel_id=1, source_target_pairs={{0,8},{8,0},{16,24},{24,16},{1,9},{9,1},{17,25},{25,17},{2,10},{10... | collective-permute-start | bytes 4718600 | tf_op jit(solution)/shard_map/ppermute | solution.py:526
  153.9 21.5 %collective-permute-start.20 = (bf16[512,1024]{1,0:T(8,128)(2,1)}, bf16[512,1024]{1,0:T(8,128)(2,1)}, u32[]{:S(2)}, u32[]{:S(2)}) collective-permute-start(bf16[512,1024]{1,0:T(8,128)(2,1)} %flip.8.refs_1_), channel_id=1, source_target_pairs={{0,16},{1,17},{10,26},{11,27},{20,4},{21,5},{30,14},{31,15}} | collective-permute-start | bytes 3145736 | tf_op jit(solution)/shard_map/ppermute | solution.py:532
  164.7 21.3 %collective-permute-start.25 = (bf16[512,1024]{1,0:T(8,128)(2,1)}, bf16[512,1024]{1,0:T(8,128)(2,1)}, u32[]{:S(2)}, u32[]{:S(2)}) collective-permute-start(bf16[512,1024]{1,0:T(8,128)(2,1)} %flip.9.refs_1_), channel_id=1, source_target_pairs={{0,16},{1,17},{10,26},{11,27},{20,4},{21,5},{30,14},{31,15}} | collective-permute-start | bytes 3145736 | tf_op jit(solution)/shard_map/ppermute | solution.py:532
  173.2 22.7 %collective-permute-start.15 = (bf16[2048,256]{1,0:T(8,128)(2,1)S(1)}, bf16[2048,256]{1,0:T(8,128)(2,1)S(1)}, u32[]{:S(2)}, u32[]{:S(2)}) collective-permute-start(bf16[2048,256]{1,0:T(8,128)(2,1)S(1)} %copy-done.5), channel_id=1, source_target_pairs={{2,0},{4,2},{6,4},{7,6},{5,7},{3,5},{1,3},{0,1},{10,8},{12,10},{14... | collective-permute-start | bytes 3145736 | tf_op jit(solution)/shard_map/ppermute | solution.py:510
  174.9 22.4 %collective-permute-start.14 = (bf16[2048,256]{1,0:T(8,128)(2,1)S(1)}, bf16[2048,256]{1,0:T(8,128)(2,1)S(1)}, u32[]{:S(2)}, u32[]{:S(2)}) collective-permute-start(bf16[2048,256]{1,0:T(8,128)(2,1)S(1)} %copy-done.5), channel_id=1, source_target_pairs={{0,2},{2,4},{4,6},{6,7},{7,5},{5,3},{3,1},{1,0},{8,10},{10,12},{12... | collective-permute-start | bytes 3145736 | tf_op jit(solution)/shard_map/ppermute | solution.py:510
  175.3 25.5 %collective-permute-start.18 = (bf16[768,1024]{1,0:T(8,128)(2,1)}, bf16[768,1024]{1,0:T(8,128)(2,1)}, u32[]{:S(2)}, u32[]{:S(2)}) collective-permute-start(bf16[768,1024]{1,0:T(8,128)(2,1)} %copy-done.15), channel_id=1, source_target_pairs={{0,8},{8,0},{16,24},{24,16},{1,9},{9,1},{17,25},{25,17},{2,10},{10... | collective-permute-start | bytes 4718600 | tf_op jit(solution)/shard_map/ppermute | solution.py:526
  205.1 25.6 %collective-permute-start.23 = (bf16[2048,256]{1,0:T(8,128)(2,1)S(1)}, bf16[2048,256]{1,0:T(8,128)(2,1)}, u32[]{:S(2)}, u32[]{:S(2)}) collective-permute-start(bf16[2048,256]{1,0:T(8,128)(2,1)S(1)} %collective-permute-done.15.refs_3_), channel_id=1, source_target_pairs={{2,0},{4,2},{6,4},{7,6},{5,7},{3,5},{1,3},{0,1},{10,8},{12,10},{14... | collective-permute-start | bytes 3145736 | tf_op jit(solution)/shard_map/ppermute | solution.py:510
  206.8 25.3 %collective-permute-start.22 = (bf16[2048,256]{1,0:T(8,128)(2,1)S(1)}, bf16[2048,256]{1,0:T(8,128)(2,1)}, u32[]{:S(2)}, u32[]{:S(2)}) collective-permute-start(bf16[2048,256]{1,0:T(8,128)(2,1)S(1)} %collective-permute-done.14.refs_2_), channel_id=1, source_target_pairs={{0,2},{2,4},{4,6},{6,7},{7,5},{5,3},{3,1},{1,0},{8,10},{10,12},{12... | collective-permute-start | bytes 3145736 | tf_op jit(solution)/shard_map/ppermute | solution.py:510
  232.1 24.6 %collective-permute-start.31 = (bf16[2048,256]{1,0:T(8,128)(2,1)}, bf16[2048,256]{1,0:T(8,128)(2,1)S(1)}, u32[]{:S(2)}, u32[]{:S(2)}) collective-permute-start(bf16[2048,256]{1,0:T(8,128)(2,1)} %collective-permute-done.23.refs_2_), channel_id=1, source_target_pairs={{2,0},{4,2},{6,4},{7,6},{5,7},{3,5},{1,3},{0,1},{10,8},{12,10},{14... | collective-permute-start | bytes 3145736 | tf_op jit(solution)/shard_map/ppermute | solution.py:510
  233.6 24.3 %collective-permute-start.30 = (bf16[2048,256]{1,0:T(8,128)(2,1)}, bf16[2048,256]{1,0:T(8,128)(2,1)S(1)}, u32[]{:S(2)}, u32[]{:S(2)}) collective-permute-start(bf16[2048,256]{1,0:T(8,128)(2,1)} %collective-permute-done.22.refs_1_), channel_id=1, source_target_pairs={{0,2},{2,4},{4,6},{6,7},{7,5},{5,3},{3,1},{1,0},{8,10},{10,12},{12... | collective-permute-start | bytes 3145736 | tf_op jit(solution)/shard_map/ppermute | solution.py:510
  238.1 63.9 %collective-permute-start.35 = (bf16[768,1024]{1,0:T(8,128)(2,1)}, bf16[768,1024]{1,0:T(8,128)(2,1)}, u32[]{:S(2)}, u32[]{:S(2)}) collective-permute-start(bf16[768,1024]{1,0:T(8,128)(2,1)} %flip.11.refs_1_), channel_id=1, source_target_pairs={{0,16},{1,17},{10,26},{11,27},{20,4},{21,5},{30,14},{31,15}} | collective-permute-start | bytes 4718600 | tf_op jit(solution)/shard_map/ppermute | solution.py:532
  263.2 45.1 %collective-permute-start.38 = (bf16[1024,1024]{1,0:T(8,128)(2,1)}, bf16[1024,1024]{1,0:T(8,128)(2,1)}, u32[]{:S(2)}, u32[]{:S(2)}) collective-permute-start(bf16[1024,1024]{1,0:T(8,128)(2,1)} %flip.12.refs_1_), channel_id=1, source_target_pairs={{0,16},{1,17},{10,26},{11,27},{20,4},{21,5},{30,14},{31,15}} | collective-permute-start | bytes 6291464 | tf_op jit(solution)/shard_map/ppermute | solution.py:532
  301.4 37.4 %collective-permute-start.34 = (bf16[768,1024]{1,0:T(8,128)(2,1)S(1)}, bf16[768,1024]{1,0:T(8,128)(2,1)}, u32[]{:S(2)}, u32[]{:S(2)}) collective-permute-start(bf16[768,1024]{1,0:T(8,128)(2,1)S(1)} %copy-done.12), channel_id=1, source_target_pairs={{0,8},{8,0},{16,24},{24,16},{1,9},{9,1},{17,25},{25,17},{2,10},{10... | collective-permute-start | bytes 4718600 | tf_op jit(solution)/shard_map/ppermute | solution.py:526
  301.5 41.5 %collective-permute-start.37 = (bf16[1024,1024]{1,0:T(8,128)(2,1)S(1)}, bf16[1024,1024]{1,0:T(8,128)(2,1)}, u32[]{:S(2)}, u32[]{:S(2)}) collective-permute-start(bf16[1024,1024]{1,0:T(8,128)(2,1)S(1)} %copy-done.6), channel_id=1, source_target_pairs={{0,8},{8,0},{16,24},{24,16},{1,9},{9,1},{17,25},{25,17},{2,10},{10... | collective-permute-start | bytes 6291464 | tf_op jit(solution)/shard_map/ppermute | solution.py:526
  302.0 31.2 %collective-permute-start.40 = (bf16[256,1024]{1,0:T(8,128)(2,1)}, bf16[256,1024]{1,0:T(8,128)(2,1)S(1)}, u32[]{:S(2)}, u32[]{:S(2)}) collective-permute-start(bf16[256,1024]{1,0:T(8,128)(2,1)} %flip.13.refs_1_), channel_id=1, source_target_pairs={{0,8},{8,0},{16,24},{24,16},{1,9},{9,1},{17,25},{25,17},{2,10},{10... | collective-permute-start | bytes 1572872 | tf_op jit(solution)/shard_map/ppermute | solution.py:526
  308.4 30.4 %collective-permute-start.36 = (bf16[768,1024]{1,0:T(8,128)(2,1)}, bf16[768,1024]{1,0:T(8,128)(2,1)}, u32[]{:S(2)}, u32[]{:S(2)}) collective-permute-start(bf16[768,1024]{1,0:T(8,128)(2,1)} %collective-permute-done.35.refs_3_), channel_id=1, source_target_pairs={{0,8},{8,0},{16,24},{24,16},{1,9},{9,1},{17,25},{25,17},{2,10},{10... | collective-permute-start | bytes 4718600 | tf_op jit(solution)/shard_map/ppermute | solution.py:526
  308.4 34.7 %collective-permute-start.39 = (bf16[1024,1024]{1,0:T(8,128)(2,1)}, bf16[1024,1024]{1,0:T(8,128)(2,1)}, u32[]{:S(2)}, u32[]{:S(2)}) collective-permute-start(bf16[1024,1024]{1,0:T(8,128)(2,1)} %collective-permute-done.38.refs_3_), channel_id=1, source_target_pairs={{0,8},{8,0},{16,24},{24,16},{1,9},{9,1},{17,25},{25,17},{2,10},{10... | collective-permute-start | bytes 6291464 | tf_op jit(solution)/shard_map/ppermute | solution.py:526
  (45 other events, 434.0 us)

commit v7 on v6

--- a/solution.py
+++ b/solution.py
@@ -522,13 +522,11 @@
             held = copies[source]
             if source and behind:
                 held = after(held, *behind)
-            if hop == 1:
-                copies.append(lax.ppermute(held, "row", [(r, r ^ 1) for r in range(rows)]))
-                continue
-            perm = [
-                ((c // parts ^ source) * cols + c, (c // parts ^ relation) * cols + c)
-                for c in range(cols)
-            ]
+            perm = []
+            for c in range(cols):
+                for r in range(rows):
+                    moves = hop == 1 or (r ^ c // parts) in (source, relation)
+                    perm.append((r * cols + c, (r ^ hop if moves else r) * cols + c))
             copies.append(lax.ppermute(held, ("row", "col"), perm))
         return copies
 
@@ -545,13 +543,14 @@
     for t in range(3, half):
         one.append(go_round(*one[t - 1]))
     copies.append(column(sum(one[2 : half - 1], [])))
-    below, above = [after(block, copies[1][0]) for block in one[half - 1]]
+    two = [[own], go_round(*[after(own, copies[1][0])] * 2)]
+    below, above = one[half - 1]
     copies.append(column(one[half - 1]))
     one.append(last_round(below, above))
-    two = [[own], go_round(*[after(own, *one[half])] * 2)]
-    copies.append(column(one[half], (), two[1]))
-    rights = [settle(which, some, pairs) for some in copies]
-    two.append(go_round(*[after(block, *rights[:2]) for block in two[1]]))
+    rights = [settle(which, some, pairs) for some in copies[:2]]
+    copies.append(column(one[half], rights))
+    rights += [settle(which, some, pairs) for some in copies[2:]]
+    two.append(go_round(*two[1]))
 
     def as_lefts(slots):
         return [slot.reshape(parts, -1, width) for slot in sum(slots, [])]
@@ -559,13 +558,13 @@
     lefts = as_lefts(one)
     wide = CHUNKS[0][1] // 2
     first = contract(None, [lefts], rights, unit, 0, wide, 0, 1, 0)
+    for t in range(3, half):
+        two.append(go_round(*two[t - 1]))
+    copies = [column(sum(two[:2], []), two[2] + [first])]
+    lefts = [after(lefts[0], copies[0][0], *two[half - 1])] + lefts[1:]
     second = contract(first, [lefts], rights, unit, 0, wide, 1, 1, 1)
-    copies = [column(sum(two[:2], []), two[2])]
-    two.append(go_round(*[after(block, first) for block in two[2]]))
-    for t in range(4, half):
-        two.append(go_round(*two[t - 1]))
     copies.append(column(sum(two[2:half], []), two[half - 1]))
-    two.append(last_round(*[after(block, second, copies[0][0]) for block in two[half - 1]]))
+    two.append(last_round(*[after(block, first) for block in two[half - 1]]))
     share = CHUNKS[0][1]
     both = [lefts, as_lefts(two)]
     result = contract(second, both[1:], rights, unit, share, share, 0, 1, 0)

time: 394 us -> 400 us (1.015)
  waiting for transfers between devices: 112 us -> 78.6 us
  starting transfers between devices: 47.4 us -> 77.9 us
  local copies, waits for them, and re-layouts: 8.94 us -> 15 us
    ppermute x7 -> x21, starting transfers between devices: 23.6 us -> 54.2 us  [column(): copies.append(lax.ppermute(held, ('row', 'col'), perm))]
    ppermute x8, waiting for transfers between devices: 39.2 us -> 15 us  [go_round(): lax.ppermute(below, 'col', ring_up)]
    ppermute x8, starting transfers between devices: 8.25 us -> 16.1 us  [go_round(): lax.ppermute(above, 'col', ring_down)]
    ppermute x8, waiting for transfers between devices: 29.4 us -> 23.5 us  [go_round(): lax.ppermute(above, 'col', ring_down)]
    ppermute x8, starting transfers between devices: 8.2 us -> 2.7 us  [go_round(): lax.ppermute(below, 'col', ring_up)]
    ppermute x7 -> x21, waiting for transfers between devices: 17 us -> 15.1 us  [column(): copies.append(lax.ppermute(held, ('row', 'col'), perm))]
  transfers between devices with their start and end apart: 43 -> 43, of which waited for: 19 -> 17; matrix products, arithmetic and copies ran while one was open for 0% -> 2% of each run, Pallas kernels for 30% -> 30%
where the time goes in v7:
time: 400 us; the launch traced here: 396 us
  Pallas kernels  219 us (55%)
  waiting for transfers between devices  78.6 us (20%)
  starting transfers between devices  77.9 us (19%)
  local copies, waits for them, and re-layouts  15 us (4%)
  other arithmetic  4.21 us (1%)
    pallas_call x4, Pallas kernels, contract(): pl.pallas_call(lambda *refs: contract_kernel(slot_count, shares, len(righ...  96.2 us
    ppermute x21, starting transfers between devices, column(): copies.append(lax.ppermute(held, ('row', 'col'), perm))  54.2 us
    pallas_call x1, Pallas kernels, transform(): pl.pallas_call(lambda *refs: transform_kernel(pairs, load_steps, step_row...  51 us
    pallas_call x7, Pallas kernels, flip(): pl.pallas_call(lambda *refs: flip_kernel(slot_count, *refs), grid_spec=pl...  26.2 us
    ppermute x6, waiting for transfers between devices, across_rows(): lax.ppermute(parcels[s], 'row', [(r, r ^ s) for r in range(rows)])  25 us
    pallas_call x7, Pallas kernels, settle(): pl.pallas_call(lambda *refs: settle_kernel(pairs, row_count, *refs), grid...  25 us
    ppermute x8, waiting for transfers between devices, go_round(): lax.ppermute(above, 'col', ring_down)  23.5 us
    ppermute x8, starting transfers between devices, go_round(): lax.ppermute(above, 'col', ring_down)  16.1 us
  transfers between devices with their start and end apart: 43, of which 17 were waited for; matrix products, arithmetic and copies ran while one was open for 2% of the time, Pallas kernels for 30%

profile of v7, /device:TPU:0, one launch (start us, length us, event | category | flops | bytes accessed | tf_op | source)
XLA Modules:
  0.0 395.5 jit_solution(3551298807629408727)
XLA Ops:
  6.4 51.0 %transform.1 = (bf16[1024,128]{1,0:T(8,128)(2,1)}, bf16[1024,128]{1,0:T(8,128)(2,1)}, bf16[1024,128]{1,0:T(8,128)(2,1)}, bf16[1024,128]{1,0:T(8,128)(2,1)}, f32[32768,128]{1,0:T(8,128)}) custom-call(s32[8192]{0:T(1024)} %bitcast.67, s32[1]{0:T(128)} %bitcast.refs_1_.refs_0_, bf16[64,256]{1,0:T(8,128)(2,1)} %fusion.16.refs_2_, ...), custom_call_target="tpu_custom_call" | custom-call | flops 9663676416 | bytes 40000000 | tf_op jit(solution)/shard_map/transform/pallas_call | solution.py:233
  60.5 7.3 %collective-permute-done.1.refs_3_ = bf16[1024,128]{1,0:T(8,128)(2,1)S(1)} collective-permute-done((bf16[1024,128]{1,0:T(8,128)(2,1)}, bf16[1024,128]{1,0:T(8,128)(2,1)S(1)}, u32[]{:S(2)}, u32[]{:S(2)}) %collective-permute-start.1) | collective-permute-done | bytes 262176 | tf_op jit(solution)/shard_map/ppermute | solution.py:505
  67.8 5.1 %collective-permute-done.2.refs_4_ = bf16[1024,128]{1,0:T(8,128)(2,1)S(1)} collective-permute-done((bf16[1024,128]{1,0:T(8,128)(2,1)}, bf16[1024,128]{1,0:T(8,128)(2,1)S(1)}, u32[]{:S(2)}, u32[]{:S(2)}) %collective-permute-start.2) | collective-permute-done | bytes 262176 | tf_op jit(solution)/shard_map/ppermute | solution.py:505
  78.9 15.6 %select.45 = (bf16[1024,128]{1,0:T(8,128)(2,1)}, bf16[1024,128]{1,0:T(8,128)(2,1)}, bf16[1024,128]{1,0:T(8,128)(2,1)}, bf16[1024,128]{1,0:T(8,128)(2,1)}) custom-call(s32[8192]{0:T(1024)} %bitcast.64, s32[1]{0:T(128)} %bitcast.refs_1_.refs_0_, f32[32768,128]{1,0:T(8,128)} %get-tuple-element.37.refs_2_), custom_call_target="tpu_custom_call" | custom-call | bytes 50000000 | tf_op jit(solution)/shard_map/select/pallas_call | solution.py:113
  94.6 7.2 %collective-permute-done.4.refs_3_ = bf16[2048,256]{1,0:T(8,128)(2,1)S(1)} collective-permute-done((bf16[2048,256]{1,0:T(8,128)(2,1)}, bf16[2048,256]{1,0:T(8,128)(2,1)S(1)}, u32[]{:S(2)}, u32[]{:S(2)}) %collective-permute-start.4) | collective-permute-done | bytes 1048608 | tf_op jit(solution)/shard_map/ppermute | solution.py:510
  105.6 6.7 %collective-permute-done.7.refs_4_ = bf16[1024,128]{1,0:T(8,128)(2,1)S(1)} collective-permute-done((bf16[1024,128]{1,0:T(8,128)(2,1)}, bf16[1024,128]{1,0:T(8,128)(2,1)S(1)}, u32[]{:S(2)}, u32[]{:S(2)}) %collective-permute-start.7) | collective-permute-done | bytes 262176 | tf_op jit(solution)/shard_map/ppermute | solution.py:505
  112.3 5.8 %collective-permute-done.6.refs_3_ = bf16[1024,128]{1,0:T(8,128)(2,1)S(1)} collective-permute-done((bf16[1024,128]{1,0:T(8,128)(2,1)}, bf16[1024,128]{1,0:T(8,128)(2,1)S(1)}, u32[]{:S(2)}, u32[]{:S(2)}) %collective-permute-start.6) | collective-permute-done | bytes 262176 | tf_op jit(solution)/shard_map/ppermute | solution.py:505
  122.2 3.9 flip.7.refs_1_
  131.4 9.6 %collective-permute-start.18 = (bf16[768,1024]{1,0:T(8,128)(2,1)}, bf16[768,1024]{1,0:T(8,128)(2,1)S(1)}, u32[]{:S(2)}, u32[]{:S(2)}) collective-permute-start(bf16[768,1024]{1,0:T(8,128)(2,1)} %flip.7.refs_1_), channel_id=1, source_target_pairs={{0,8},{8,0},{16,24},{24,16},{1,9},{9,1},{17,25},{25,17},{2,10},{10... | collective-permute-start | bytes 4718600 | tf_op jit(solution)/shard_map/ppermute | solution.py:530
  155.8 10.5 %collective-permute-done.14.refs_1_ = bf16[2048,256]{1,0:T(8,128)(2,1)S(1)} collective-permute-done((bf16[2048,256]{1,0:T(8,128)(2,1)}, bf16[2048,256]{1,0:T(8,128)(2,1)S(1)}, u32[]{:S(2)}, u32[]{:S(2)}) %collective-permute-start.14) | collective-permute-done | bytes 1048608 | tf_op jit(solution)/shard_map/ppermute | solution.py:510
  175.6 5.9 %collective-permute-done.17 = bf16[1024,256]{1,0:T(8,128)(2,1)} collective-permute-done((bf16[1024,256]{1,0:T(8,128)(2,1)}, bf16[1024,256]{1,0:T(8,128)(2,1)}, u32[]{:S(2)}, u32[]{:S(2)}) %collective-permute-start.17) | collective-permute-done | bytes 524320 | tf_op jit(solution)/shard_map/ppermute | solution.py:510
  196.6 5.8 %collective-permute-done.12.refs_3_ = bf16[2048,256]{1,0:T(8,128)(2,1)S(1)} collective-permute-done((bf16[2048,256]{1,0:T(8,128)(2,1)S(1)}, bf16[2048,256]{1,0:T(8,128)(2,1)S(1)}, u32[]{:S(2)}, u32[]{:S(2)}) %collective-permute-start.12) | collective-permute-done | bytes 1048608 | tf_op jit(solution)/shard_map/ppermute | solution.py:510
  205.7 4.2 %settle.7.refs_8_ = bf16[2,768,1024]{2,1,0:T(8,128)(2,1)} custom-call(s32[1]{0:T(128)} %bitcast.15.refs_0_, bf16[768,1024]{1,0:T(8,128)(2,1)} %flip.7.refs_1_, bf16[768,1024]{1,0:T(8,128)(2,1)} %copy-done.15, bf16[768,1024]{1,0:T(8,128)(2,1)} %collective-permute-done.19.refs_3_, bf16[768,1024]{1,0:T(8,128)(2,1)} %collective-permute-done.20.refs_4_), custom_call_target="tpu_custom_call" | custom-call | bytes 6291456 | tf_op jit(solution)/shard_map/settle/pallas_call | solution.py:374
  219.1 5.6 %collective-permute-done.28.refs_3_ = bf16[256,1024]{1,0:T(8,128)(2,1)} collective-permute-done((bf16[256,1024]{1,0:T(8,128)(2,1)}, bf16[256,1024]{1,0:T(8,128)(2,1)}, u32[]{:S(2)}, u32[]{:S(2)}) %collective-permute-start.28) | collective-permute-done | bytes 524320 | tf_op jit(solution)/shard_map/ppermute | solution.py:530
  235.5 13.7 %contract.4.refs_12_ = f32[2,2,2048,2048]{3,2,1,0:T(8,128)} custom-call(bf16[2,1024,256]{2,1,0:T(8,128)(2,1)} %bitcast.32, bf16[2,1024,256]{2,1,0:T(8,128)(2,1)} %bitcast.47, bf16[2,1024,256]{2,1,0:T(8,128)(2,1)} %bitcast.44, bf16[2,1024,256]{2,1,0:T(8,128)(2,1)} %bitcast.10.refs_3_, bf16[2,1024,256]{2,1,0:T(8,128)(2,1)} %bitcast.11.refs_4_, ...), custom_call_target="tpu_custom_call" | custom-call | flops 17179869184 | bytes 8388608 | tf_op jit(solution)/shard_map/contract/pallas_call | solution.py:434
  255.2 4.3 %flip.12.refs_1_ = bf16[1024,1024]{1,0:T(8,128)(2,1)} custom-call(s32[1]{0:T(128)} %bitcast.7.refs_0_, bf16[2048,256]{1,0:T(8,128)(2,1)} %copy-done.11, bf16[2048,256]{1,0:T(8,128)(2,1)} %collective-permute-done.13.refs_2_, bf16[2048,256]{1,0:T(8,128)(2,1)} %copy-done.7, bf16[2048,256]{1,0:T(8,128)(2,1)} %copy-done.6), custom_call_target="tpu_custom_call" | custom-call | bytes 8388608 | tf_op jit(solution)/shard_map/flip/pallas_call | solution.py:331
  263.1 4.0 %flip.11.refs_1_ = bf16[768,1024]{1,0:T(8,128)(2,1)} custom-call(s32[1]{0:T(128)} %bitcast.7.refs_0_, bf16[2048,256]{1,0:T(8,128)(2,1)} %assemble.3.refs_1_, bf16[2048,256]{1,0:T(8,128)(2,1)} %copy-done.10, bf16[2048,256]{1,0:T(8,128)(2,1)} %copy-done.9), custom_call_target="tpu_custom_call" | custom-call | bytes 6291456 | tf_op jit(solution)/shard_map/flip/pallas_call | solution.py:331
  269.4 11.5 %collective-permute-start.34 = (bf16[768,1024]{1,0:T(8,128)(2,1)}, bf16[768,1024]{1,0:T(8,128)(2,1)}, u32[]{:S(2)}, u32[]{:S(2)}) collective-permute-start(bf16[768,1024]{1,0:T(8,128)(2,1)} %flip.11.refs_1_), channel_id=1, source_target_pairs={{0,8},{8,0},{16,24},{24,16},{1,9},{9,1},{17,25},{25,17},{2,10},{10... | collective-permute-start | bytes 4718600 | tf_op jit(solution)/shard_map/ppermute | solution.py:530
  288.7 13.7 %contract.5.refs_12_ = f32[2,2,2048,2048]{3,2,1,0:T(8,128)} custom-call(bf16[2,1024,256]{2,1,0:T(8,128)(2,1)} %bitcast.33, bf16[2,1024,256]{2,1,0:T(8,128)(2,1)} %bitcast.48, bf16[2,1024,256]{2,1,0:T(8,128)(2,1)} %bitcast.45, bf16[2,1024,256]{2,1,0:T(8,128)(2,1)} %bitcast.10.refs_3_, ...), custom_call_target="tpu_custom_call", output_to_operand_aliasing={{}: (12, {})} | custom-call | flops 17179869184 | bytes 8388608 | tf_op jit(solution)/shard_map/contract/pallas_call | solution.py:434
  302.5 7.6 %collective-permute-done.41.refs_3_ = bf16[256,1024]{1,0:T(8,128)(2,1)S(1)} collective-permute-done((bf16[256,1024]{1,0:T(8,128)(2,1)}, bf16[256,1024]{1,0:T(8,128)(2,1)S(1)}, u32[]{:S(2)}, u32[]{:S(2)}) %collective-permute-start.41) | collective-permute-done | bytes 524320 | tf_op jit(solution)/shard_map/ppermute | solution.py:530
  310.7 24.9 %contract.6.refs_19_ = f32[2,2,2048,2048]{3,2,1,0:T(8,128)} custom-call(bf16[2,1024,256]{2,1,0:T(8,128)(2,1)} %bitcast.50, bf16[2,1024,256]{2,1,0:T(8,128)(2,1)} %bitcast.60, bf16[2,1024,256]{2,1,0:T(8,128)(2,1)} %bitcast.58, bf16[2,1024,256]{2,1,0:T(8,128)(2,1)} %bitcast.62, ...), custom_call_target="tpu_custom_call", output_to_operand_aliasing={{}: (12, {})} | custom-call | flops 34359738368 | bytes 16777216 | tf_op jit(solution)/shard_map/contract/pallas_call | solution.py:434
  341.2 4.2 %settle.11.refs_16_ = bf16[2,768,1024]{2,1,0:T(8,128)(2,1)} custom-call(s32[1]{0:T(128)} %bitcast.15.refs_0_, bf16[768,1024]{1,0:T(8,128)(2,1)} %flip.11.refs_1_, bf16[768,1024]{1,0:T(8,128)(2,1)} %collective-permute-done.34.refs_2_, bf16[768,1024]{1,0:T(8,128)(2,1)} %collective-permute-done.35.refs_3_, bf16[768,1024]{1,0:T(8,128)(2,1)} %collective-permute-done.36.refs_4_), custom_call_target="tpu_custom_call" | custom-call | bytes 6291456 | tf_op jit(solution)/shard_map/settle/pallas_call | solution.py:374
  346.7 4.8 %settle.12.refs_17_ = bf16[2,1024,1024]{2,1,0:T(8,128)(2,1)} custom-call(s32[1]{0:T(128)} %bitcast.15.refs_0_, bf16[1024,1024]{1,0:T(8,128)(2,1)} %flip.12.refs_1_, bf16[1024,1024]{1,0:T(8,128)(2,1)} %copy-done.13, bf16[1024,1024]{1,0:T(8,128)(2,1)} %copy-done.12, bf16[1024,1024]{1,0:T(8,128)(2,1)} %collective-permute-done.39.refs_4_), custom_call_target="tpu_custom_call" | custom-call | bytes 8388608 | tf_op jit(solution)/shard_map/settle/pallas_call | solution.py:374
  351.6 43.8 %contract.7 = f32[2,2,2048,2048]{3,2,1,0:T(8,128)} custom-call(bf16[2,1024,256]{2,1,0:T(8,128)(2,1)} %bitcast.34, bf16[2,1024,256]{2,1,0:T(8,128)(2,1)} %bitcast.49, bf16[2,1024,256]{2,1,0:T(8,128)(2,1)} %bitcast.46, bf16[2,1024,256]{2,1,0:T(8,128)(2,1)} %bitcast.10.refs_3_, bf16[2,1024,256]{2,1,0:T(8,128)(2,1)} %bitcast.11.refs_4_, ...), custom_call_target="tpu_custom_call", output_to_operand_aliasing={{}: (19, {})} | custom-call | flops 68719476736 | bytes 33554432 | tf_op jit(solution)/shard_map/contract/pallas_call | solution.py:434
  (159 shorter events, 118.0 us)
Async XLA Ops:
  76.3 25.4 %collective-permute-start.4 = (bf16[2048,256]{1,0:T(8,128)(2,1)}, bf16[2048,256]{1,0:T(8,128)(2,1)S(1)}, u32[]{:S(2)}, u32[]{:S(2)}) collective-permute-start(bf16[2048,256]{1,0:T(8,128)(2,1)} %assemble.2.refs_1_), channel_id=1, source_target_pairs={{2,0},{4,2},{6,4},{7,6},{5,7},{3,5},{1,3},{0,1},{10,8},{12,10},{14... | collective-permute-start | bytes 3145736 | tf_op jit(solution)/shard_map/ppermute | solution.py:510
  77.9 25.6 %collective-permute-start.3 = (bf16[2048,256]{1,0:T(8,128)(2,1)}, bf16[2048,256]{1,0:T(8,128)(2,1)S(1)}, u32[]{:S(2)}, u32[]{:S(2)}) collective-permute-start(bf16[2048,256]{1,0:T(8,128)(2,1)} %assemble.2.refs_1_), channel_id=1, source_target_pairs={{0,2},{2,4},{4,6},{6,7},{7,5},{5,3},{3,1},{1,0},{8,10},{10,12},{12... | collective-permute-start | bytes 3145736 | tf_op jit(solution)/shard_map/ppermute | solution.py:510
  101.7 24.6 %collective-permute-start.9 = (bf16[2048,256]{1,0:T(8,128)(2,1)S(1)}, bf16[2048,256]{1,0:T(8,128)(2,1)}, u32[]{:S(2)}, u32[]{:S(2)}) collective-permute-start(bf16[2048,256]{1,0:T(8,128)(2,1)S(1)} %collective-permute-done.4.refs_3_), channel_id=1, source_target_pairs={{2,0},{4,2},{6,4},{7,6},{5,7},{3,5},{1,3},{0,1},{10,8},{12,10},{14... | collective-permute-start | bytes 3145736 | tf_op jit(solution)/shard_map/ppermute | solution.py:510
  103.5 37.6 %collective-permute-start.8 = (bf16[2048,256]{1,0:T(8,128)(2,1)S(1)}, bf16[2048,256]{1,0:T(8,128)(2,1)}, u32[]{:S(2)}, u32[]{:S(2)}) collective-permute-start(bf16[2048,256]{1,0:T(8,128)(2,1)S(1)} %collective-permute-done.3.refs_2_), channel_id=1, source_target_pairs={{0,2},{2,4},{4,6},{6,7},{7,5},{5,3},{3,1},{1,0},{8,10},{10,12},{12... | collective-permute-start | bytes 3145736 | tf_op jit(solution)/shard_map/ppermute | solution.py:510
  126.3 25.2 %collective-permute-start.15 = (bf16[2048,256]{1,0:T(8,128)(2,1)}, bf16[2048,256]{1,0:T(8,128)(2,1)S(1)}, u32[]{:S(2)}, u32[]{:S(2)}) collective-permute-start(bf16[2048,256]{1,0:T(8,128)(2,1)} %collective-permute-done.9.refs_2_), channel_id=1, source_target_pairs={{2,0},{4,2},{6,4},{7,6},{5,7},{3,5},{1,3},{0,1},{10,8},{12,10},{14... | collective-permute-start | bytes 3145736 | tf_op jit(solution)/shard_map/ppermute | solution.py:510
  128.1 41.2 %collective-permute-start.19 = (bf16[768,1024]{1,0:T(8,128)(2,1)}, bf16[768,1024]{1,0:T(8,128)(2,1)}, u32[]{:S(2)}, u32[]{:S(2)}) collective-permute-start(bf16[768,1024]{1,0:T(8,128)(2,1)} %flip.7.refs_1_), channel_id=1, source_target_pairs={{0,16},{8,8},{16,0},{24,24},{1,17},{9,9},{17,1},{25,25},{2,2},{10,... | collective-permute-start | bytes 4718600 | tf_op jit(solution)/shard_map/ppermute | solution.py:530
  131.4 37.9 %collective-permute-start.18 = (bf16[768,1024]{1,0:T(8,128)(2,1)}, bf16[768,1024]{1,0:T(8,128)(2,1)S(1)}, u32[]{:S(2)}, u32[]{:S(2)}) collective-permute-start(bf16[768,1024]{1,0:T(8,128)(2,1)} %flip.7.refs_1_), channel_id=1, source_target_pairs={{0,8},{8,0},{16,24},{24,16},{1,9},{9,1},{17,25},{25,17},{2,10},{10... | collective-permute-start | bytes 4718600 | tf_op jit(solution)/shard_map/ppermute | solution.py:530
  141.0 25.3 %collective-permute-start.14 = (bf16[2048,256]{1,0:T(8,128)(2,1)}, bf16[2048,256]{1,0:T(8,128)(2,1)S(1)}, u32[]{:S(2)}, u32[]{:S(2)}) collective-permute-start(bf16[2048,256]{1,0:T(8,128)(2,1)} %collective-permute-done.8.refs_1_), channel_id=1, source_target_pairs={{0,2},{2,4},{4,6},{6,7},{7,5},{5,3},{3,1},{1,0},{8,10},{10,12},{12... | collective-permute-start | bytes 3145736 | tf_op jit(solution)/shard_map/ppermute | solution.py:510
  145.4 24.1 %collective-permute-start.22 = (bf16[512,1024]{1,0:T(8,128)(2,1)}, bf16[512,1024]{1,0:T(8,128)(2,1)}, u32[]{:S(2)}, u32[]{:S(2)}) collective-permute-start(bf16[512,1024]{1,0:T(8,128)(2,1)} %flip.8.refs_1_), channel_id=1, source_target_pairs={{0,16},{8,8},{16,0},{24,24},{1,17},{9,9},{17,1},{25,25},{2,2},{10,... | collective-permute-start | bytes 3145736 | tf_op jit(solution)/shard_map/ppermute | solution.py:530
  169.3 36.3 %collective-permute-start.20 = (bf16[768,1024]{1,0:T(8,128)(2,1)}, bf16[768,1024]{1,0:T(8,128)(2,1)}, u32[]{:S(2)}, u32[]{:S(2)}) collective-permute-start(bf16[768,1024]{1,0:T(8,128)(2,1)} %collective-permute-done.19.refs_3_), channel_id=1, source_target_pairs={{0,8},{8,0},{16,24},{24,16},{1,9},{9,1},{17,25},{25,17},{2,10},{10... | collective-permute-start | bytes 4718600 | tf_op jit(solution)/shard_map/ppermute | solution.py:530
  173.6 28.7 %collective-permute-start.12 = (bf16[2048,256]{1,0:T(8,128)(2,1)S(1)}, bf16[2048,256]{1,0:T(8,128)(2,1)S(1)}, u32[]{:S(2)}, u32[]{:S(2)}) collective-permute-start(bf16[2048,256]{1,0:T(8,128)(2,1)S(1)} %copy-done.5), channel_id=1, source_target_pairs={{2,0},{4,2},{6,4},{7,6},{5,7},{3,5},{1,3},{0,1},{10,8},{12,10},{14... | collective-permute-start | bytes 3145736 | tf_op jit(solution)/shard_map/ppermute | solution.py:510
  181.5 23.8 %collective-permute-start.10 = (bf16[2048,256]{1,0:T(8,128)(2,1)S(1)}, bf16[2048,256]{1,0:T(8,128)(2,1)S(1)}, u32[]{:S(2)}, u32[]{:S(2)}) collective-permute-start(bf16[2048,256]{1,0:T(8,128)(2,1)S(1)} %copy-done.5), channel_id=1, source_target_pairs={{0,2},{2,4},{4,6},{6,7},{7,5},{5,3},{3,1},{1,0},{8,10},{10,12},{12... | collective-permute-start | bytes 3145736 | tf_op jit(solution)/shard_map/ppermute | solution.py:510
  187.2 29.6 %collective-permute-start.24 = (bf16[512,1024]{1,0:T(8,128)(2,1)}, bf16[512,1024]{1,0:T(8,128)(2,1)}, u32[]{:S(2)}, u32[]{:S(2)}) collective-permute-start(bf16[512,1024]{1,0:T(8,128)(2,1)} %flip.9.refs_1_), channel_id=1, source_target_pairs={{0,8},{8,0},{16,24},{24,16},{1,9},{9,1},{17,25},{25,17},{2,10},{10... | collective-permute-start | bytes 3145736 | tf_op jit(solution)/shard_map/ppermute | solution.py:530
  202.3 24.1 %collective-permute-start.13 = (bf16[2048,256]{1,0:T(8,128)(2,1)S(1)}, bf16[2048,256]{1,0:T(8,128)(2,1)}, u32[]{:S(2)}, u32[]{:S(2)}) collective-permute-start(bf16[2048,256]{1,0:T(8,128)(2,1)S(1)} %collective-permute-done.12.refs_3_), channel_id=1, source_target_pairs={{2,0},{4,2},{6,4},{7,6},{5,7},{3,5},{1,3},{0,1},{10,8},{12,10},{14... | collective-permute-start | bytes 3145736 | tf_op jit(solution)/shard_map/ppermute | solution.py:510
  226.5 25.8 %collective-permute-start.31 = (bf16[2048,256]{1,0:T(8,128)(2,1)}, bf16[2048,256]{1,0:T(8,128)(2,1)S(1)}, u32[]{:S(2)}, u32[]{:S(2)}) collective-permute-start(bf16[2048,256]{1,0:T(8,128)(2,1)} %collective-permute-done.13.refs_2_), channel_id=1, source_target_pairs={{2,0},{4,2},{6,4},{7,6},{5,7},{3,5},{1,3},{0,1},{10,8},{12,10},{14... | collective-permute-start | bytes 3145736 | tf_op jit(solution)/shard_map/ppermute | solution.py:510
  253.3 27.6 %collective-permute-start.33 = (bf16[1024,256]{1,0:T(8,128)(2,1)}, bf16[1024,256]{1,0:T(8,128)(2,1)}, u32[]{:S(2)}, u32[]{:S(2)}) collective-permute-start(bf16[1024,256]{1,0:T(8,128)(2,1)} %slice.33), channel_id=1, source_target_pairs={{2,0},{4,2},{6,4},{7,6},{5,7},{3,5},{1,3},{0,1},{10,8},{12,10},{14... | collective-permute-start | bytes 1572872 | tf_op jit(solution)/shard_map/ppermute | solution.py:510
  259.5 51.1 %collective-permute-start.38 = (bf16[1024,1024]{1,0:T(8,128)(2,1)}, bf16[1024,1024]{1,0:T(8,128)(2,1)S(1)}, u32[]{:S(2)}, u32[]{:S(2)}) collective-permute-start(bf16[1024,1024]{1,0:T(8,128)(2,1)} %flip.12.refs_1_), channel_id=1, source_target_pairs={{0,16},{8,8},{16,0},{24,24},{1,17},{9,9},{17,1},{25,25},{2,2},{10,... | collective-permute-start | bytes 6291464 | tf_op jit(solution)/shard_map/ppermute | solution.py:530
  263.0 82.4 %collective-permute-start.37 = (bf16[1024,1024]{1,0:T(8,128)(2,1)}, bf16[1024,1024]{1,0:T(8,128)(2,1)S(1)}, u32[]{:S(2)}, u32[]{:S(2)}) collective-permute-start(bf16[1024,1024]{1,0:T(8,128)(2,1)} %flip.12.refs_1_), channel_id=1, source_target_pairs={{0,8},{8,0},{16,24},{24,16},{1,9},{9,1},{17,25},{25,17},{2,10},{10... | collective-permute-start | bytes 6291464 | tf_op jit(solution)/shard_map/ppermute | solution.py:530
  267.2 42.9 %collective-permute-start.35 = (bf16[768,1024]{1,0:T(8,128)(2,1)}, bf16[768,1024]{1,0:T(8,128)(2,1)}, u32[]{:S(2)}, u32[]{:S(2)}) collective-permute-start(bf16[768,1024]{1,0:T(8,128)(2,1)} %flip.11.refs_1_), channel_id=1, source_target_pairs={{0,16},{8,8},{16,0},{24,24},{1,17},{9,9},{17,1},{25,25},{2,2},{10,... | collective-permute-start | bytes 4718600 | tf_op jit(solution)/shard_map/ppermute | solution.py:530
  269.4 71.8 %collective-permute-start.34 = (bf16[768,1024]{1,0:T(8,128)(2,1)}, bf16[768,1024]{1,0:T(8,128)(2,1)}, u32[]{:S(2)}, u32[]{:S(2)}) collective-permute-start(bf16[768,1024]{1,0:T(8,128)(2,1)} %flip.11.refs_1_), channel_id=1, source_target_pairs={{0,8},{8,0},{16,24},{24,16},{1,9},{9,1},{17,25},{25,17},{2,10},{10... | collective-permute-start | bytes 4718600 | tf_op jit(solution)/shard_map/ppermute | solution.py:530
  286.3 23.8 %collective-permute-start.41 = (bf16[256,1024]{1,0:T(8,128)(2,1)}, bf16[256,1024]{1,0:T(8,128)(2,1)S(1)}, u32[]{:S(2)}, u32[]{:S(2)}) collective-permute-start(bf16[256,1024]{1,0:T(8,128)(2,1)} %flip.13.refs_1_), channel_id=1, source_target_pairs={{0,16},{8,8},{16,0},{24,24},{1,17},{9,9},{17,1},{25,25},{2,2},{10,... | collective-permute-start | bytes 1572872 | tf_op jit(solution)/shard_map/ppermute | solution.py:530
  310.1 25.5 %collective-permute-start.40 = (bf16[256,1024]{1,0:T(8,128)(2,1)S(1)}, bf16[256,1024]{1,0:T(8,128)(2,1)S(1)}, u32[]{:S(2)}, u32[]{:S(2)}) collective-permute-start(bf16[256,1024]{1,0:T(8,128)(2,1)S(1)} %copy-done.14), channel_id=1, source_target_pairs={{0,8},{8,0},{16,24},{24,16},{1,9},{9,1},{17,25},{25,17},{2,10},{10... | collective-permute-start | bytes 1572872 | tf_op jit(solution)/shard_map/ppermute | solution.py:530
  310.1 31.1 %collective-permute-start.36 = (bf16[768,1024]{1,0:T(8,128)(2,1)}, bf16[768,1024]{1,0:T(8,128)(2,1)}, u32[]{:S(2)}, u32[]{:S(2)}) collective-permute-start(bf16[768,1024]{1,0:T(8,128)(2,1)} %collective-permute-done.35.refs_3_), channel_id=1, source_target_pairs={{0,8},{8,0},{16,24},{24,16},{1,9},{9,1},{17,25},{25,17},{2,10},{10... | collective-permute-start | bytes 4718600 | tf_op jit(solution)/shard_map/ppermute | solution.py:530
  310.6 34.8 %collective-permute-start.39 = (bf16[1024,1024]{1,0:T(8,128)(2,1)S(1)}, bf16[1024,1024]{1,0:T(8,128)(2,1)}, u32[]{:S(2)}, u32[]{:S(2)}) collective-permute-start(bf16[1024,1024]{1,0:T(8,128)(2,1)S(1)} %collective-permute-done.38.refs_3_), channel_id=1, source_target_pairs={{0,8},{8,0},{16,24},{24,16},{1,9},{9,1},{17,25},{25,17},{2,10},{10... | collective-permute-start | bytes 6291464 | tf_op jit(solution)/shard_map/ppermute | solution.py:530
  (45 other events, 501.0 us)

commit v8 on v7

--- a/solution.py
+++ b/solution.py
@@ -513,20 +513,22 @@
         cut = below.shape[0] // 2
         return [jnp.concatenate(go_round(below[:cut], above[cut:]), axis=0)]
 
-    def column(slots, before=(), behind=()):
+    def column(slots, before=(), behind=(), flipped=None):
         slots = [after(slots[0], *before)] + slots[1:] if before else slots
-        copies = [flip(slots, my_part, parts, unit)]
+        copies = [flip(slots, my_part, parts, unit) if flipped is None else flipped]
         for relation in range(1, rows):
             source = relation & (relation - 1)
             hop = relation ^ source
             held = copies[source]
             if source and behind:
                 held = after(held, *behind)
-            perm = []
-            for c in range(cols):
-                for r in range(rows):
-                    moves = hop == 1 or (r ^ c // parts) in (source, relation)
-                    perm.append((r * cols + c, (r ^ hop if moves else r) * cols + c))
+            if hop == 1:
+                copies.append(lax.ppermute(held, "row", [(r, r ^ 1) for r in range(rows)]))
+                continue
+            perm = [
+                ((c // parts ^ source) * cols + c, (c // parts ^ relation) * cols + c)
+                for c in range(cols)
+            ]
             copies.append(lax.ppermute(held, ("row", "col"), perm))
         return copies
 
@@ -538,12 +540,12 @@
     one[1] = [after(block, *sent) for block in one[1]]
     own = assemble(across_rows([after(part, *one[1]) for part in sent]), me, features)
     one.append(go_round(*one[1]))
-    copies = [column(sum(one[:2], []), (own,))]
-    one[2] = [after(block, own, copies[0][0]) for block in one[2]]
+    one[2] = [after(block, own) for block in one[2]]
     for t in range(3, half):
         one.append(go_round(*one[t - 1]))
-    copies.append(column(sum(one[2 : half - 1], [])))
-    two = [[own], go_round(*[after(own, copies[1][0])] * 2)]
+    copies = [column(sum(one[:2], []), one[half - 1])]
+    copies.append(column(sum(one[2 : half - 1], []), one[half - 1]))
+    two = [[own], go_round(*[after(own, *one[half - 2])] * 2)]
     below, above = one[half - 1]
     copies.append(column(one[half - 1]))
     one.append(last_round(below, above))
@@ -557,18 +559,20 @@
 
     lefts = as_lefts(one)
     wide = CHUNKS[0][1] // 2
+    copies = [column(sum(two[:2], []), two[2])]
+    lefts = [after(lefts[0], copies[0][0])] + lefts[1:]
     first = contract(None, [lefts], rights, unit, 0, wide, 0, 1, 0)
     for t in range(3, half):
         two.append(go_round(*two[t - 1]))
-    copies = [column(sum(two[:2], []), two[2] + [first])]
-    lefts = [after(lefts[0], copies[0][0], *two[half - 1])] + lefts[1:]
     second = contract(first, [lefts], rights, unit, 0, wide, 1, 1, 1)
-    copies.append(column(sum(two[2:half], []), two[half - 1]))
     two.append(last_round(*[after(block, first) for block in two[half - 1]]))
     share = CHUNKS[0][1]
+    flipped = flip(two[half], my_part, parts, unit)
     both = [lefts, as_lefts(two)]
+    both[1][0] = after(both[1][0], flipped)
     result = contract(second, both[1:], rights, unit, share, share, 0, 1, 0)
-    copies.append(column(two[half], (), (result,)))
+    copies.append(column(sum(two[2:half], []), two[half - 1] + [first], (result,)))
+    copies.append(column(two[half], (), (result,), flipped))
     rights = [settle(which, some, pairs) for some in copies]
     result = contract(result, both, rights, unit, 0, share, 0, 1, 1)
     return result.reshape(2, parts * block, block)

time: 400 us -> 394 us (0.985)
  starting transfers between devices: 77.9 us -> 50 us
  waiting for transfers between devices: 78.6 us -> 104 us
    ppermute x21 -> x7, starting transfers between devices: 54.2 us -> 23.7 us  [column(): copies.append(lax.ppermute(held, ('row', 'col'), perm))]
    ppermute x8, waiting for transfers between devices: 23.5 us -> 46.5 us  [go_round(): lax.ppermute(above, 'col', ring_down)]
    unnamed x56 -> x66, local copies, waits for them, and re-layouts: 8.63 us -> 10.4 us
    ppermute x21 -> x7, waiting for transfers between devices: 15.1 us -> 16 us  [column(): copies.append(lax.ppermute(held, ('row', 'col'), perm))]
  transfers between devices with their start and end apart: 43 -> 43, of which waited for: 17 -> 17; matrix products, arithmetic and copies ran while one was open for 2% -> 1% of each run, Pallas kernels for 30% -> 29%
where the time goes in v8:
time: 394 us; the launch traced here: 392 us
  Pallas kernels  219 us (56%)
  waiting for transfers between devices  104 us (26%)
  starting transfers between devices  50 us (13%)
  local copies, waits for them, and re-layouts  14 us (4%)
  other arithmetic  4.21 us (1%)
    pallas_call x4, Pallas kernels, contract(): pl.pallas_call(lambda *refs: contract_kernel(slot_count, shares, len(righ...  95.6 us
    pallas_call x1, Pallas kernels, transform(): pl.pallas_call(lambda *refs: transform_kernel(pairs, load_steps, step_row...  51 us
    ppermute x8, waiting for transfers between devices, go_round(): lax.ppermute(above, 'col', ring_down)  46.5 us
    pallas_call x7, Pallas kernels, flip(): pl.pallas_call(lambda *refs: flip_kernel(slot_count, *refs), grid_spec=pl...  27 us
    ppermute x6, waiting for transfers between devices, across_rows(): lax.ppermute(parcels[s], 'row', [(r, r ^ s) for r in range(rows)])  25 us
    pallas_call x7, Pallas kernels, settle(): pl.pallas_call(lambda *refs: settle_kernel(pairs, row_count, *refs), grid...  24.9 us
    ppermute x7, starting transfers between devices, column(): copies.append(lax.ppermute(held, ('row', 'col'), perm))  23.7 us
    ppermute x8, waiting for transfers between devices, go_round(): lax.ppermute(below, 'col', ring_up)  16.6 us
  transfers between devices with their start and end apart: 43, of which 17 were waited for; matrix products, arithmetic and copies ran while one was open for 1% of the time, Pallas kernels for 29%

profile of v8, /device:TPU:0, one launch (start us, length us, event | category | flops | bytes accessed | tf_op | source)
XLA Modules:
  0.0 392.2 jit_solution(1619236103322027159)
XLA Ops:
  6.4 51.0 %transform.1 = (bf16[1024,128]{1,0:T(8,128)(2,1)}, bf16[1024,128]{1,0:T(8,128)(2,1)}, bf16[1024,128]{1,0:T(8,128)(2,1)}, bf16[1024,128]{1,0:T(8,128)(2,1)}, f32[32768,128]{1,0:T(8,128)}) custom-call(s32[8192]{0:T(1024)} %bitcast.69, s32[1]{0:T(128)} %bitcast.refs_1_.refs_0_, bf16[64,256]{1,0:T(8,128)(2,1)} %fusion.16.refs_2_, ...), custom_call_target="tpu_custom_call" | custom-call | flops 9663676416 | bytes 40000000 | tf_op jit(solution)/shard_map/transform/pallas_call | solution.py:233
  60.5 7.3 %collective-permute-done.1.refs_3_ = bf16[1024,128]{1,0:T(8,128)(2,1)S(1)} collective-permute-done((bf16[1024,128]{1,0:T(8,128)(2,1)}, bf16[1024,128]{1,0:T(8,128)(2,1)S(1)}, u32[]{:S(2)}, u32[]{:S(2)}) %collective-permute-start.1) | collective-permute-done | bytes 262176 | tf_op jit(solution)/shard_map/ppermute | solution.py:505
  67.8 5.1 %collective-permute-done.2.refs_4_ = bf16[1024,128]{1,0:T(8,128)(2,1)S(1)} collective-permute-done((bf16[1024,128]{1,0:T(8,128)(2,1)}, bf16[1024,128]{1,0:T(8,128)(2,1)S(1)}, u32[]{:S(2)}, u32[]{:S(2)}) %collective-permute-start.2) | collective-permute-done | bytes 262176 | tf_op jit(solution)/shard_map/ppermute | solution.py:505
  79.0 15.6 %select.45 = (bf16[1024,128]{1,0:T(8,128)(2,1)}, bf16[1024,128]{1,0:T(8,128)(2,1)}, bf16[1024,128]{1,0:T(8,128)(2,1)}, bf16[1024,128]{1,0:T(8,128)(2,1)}) custom-call(s32[8192]{0:T(1024)} %bitcast.66, s32[1]{0:T(128)} %bitcast.refs_1_.refs_0_, f32[32768,128]{1,0:T(8,128)} %get-tuple-element.40.refs_2_), custom_call_target="tpu_custom_call" | custom-call | bytes 50000000 | tf_op jit(solution)/shard_map/select/pallas_call | solution.py:113
  94.6 7.2 %collective-permute-done.4.refs_3_ = bf16[2048,256]{1,0:T(8,128)(2,1)S(1)} collective-permute-done((bf16[2048,256]{1,0:T(8,128)(2,1)}, bf16[2048,256]{1,0:T(8,128)(2,1)S(1)}, u32[]{:S(2)}, u32[]{:S(2)}) %collective-permute-start.4) | collective-permute-done | bytes 1048608 | tf_op jit(solution)/shard_map/ppermute | solution.py:510
  105.7 6.7 %collective-permute-done.7.refs_4_ = bf16[1024,128]{1,0:T(8,128)(2,1)S(1)} collective-permute-done((bf16[1024,128]{1,0:T(8,128)(2,1)}, bf16[1024,128]{1,0:T(8,128)(2,1)S(1)}, u32[]{:S(2)}, u32[]{:S(2)}) %collective-permute-start.7) | collective-permute-done | bytes 262176 | tf_op jit(solution)/shard_map/ppermute | solution.py:505
  112.4 5.8 %collective-permute-done.6.refs_3_ = bf16[1024,128]{1,0:T(8,128)(2,1)S(1)} collective-permute-done((bf16[1024,128]{1,0:T(8,128)(2,1)}, bf16[1024,128]{1,0:T(8,128)(2,1)S(1)}, u32[]{:S(2)}, u32[]{:S(2)}) %collective-permute-start.6) | collective-permute-done | bytes 262176 | tf_op jit(solution)/shard_map/ppermute | solution.py:505
  128.4 21.8 %collective-permute-done.15.refs_2_ = bf16[2048,256]{1,0:T(8,128)(2,1)S(1)} collective-permute-done((bf16[2048,256]{1,0:T(8,128)(2,1)}, bf16[2048,256]{1,0:T(8,128)(2,1)S(1)}, u32[]{:S(2)}, u32[]{:S(2)}) %collective-permute-start.15) | collective-permute-done | bytes 1048608 | tf_op jit(solution)/shard_map/ppermute | solution.py:510
  151.7 4.3 %flip.8.refs_1_ = bf16[768,1024]{1,0:T(8,128)(2,1)} custom-call(s32[1]{0:T(128)} %bitcast.7.refs_0_, bf16[2048,256]{1,0:T(8,128)(2,1)} %assemble.2.refs_1_, bf16[2048,256]{1,0:T(8,128)(2,1)} %copy-done.4, bf16[2048,256]{1,0:T(8,128)(2,1)} %copy-done.3), custom_call_target="tpu_custom_call" | custom-call | bytes 6291456 | tf_op jit(solution)/shard_map/flip/pallas_call | solution.py:331
  156.0 4.5 %collective-permute-start.20 = (bf16[768,1024]{1,0:T(8,128)(2,1)}, bf16[768,1024]{1,0:T(8,128)(2,1)}, u32[]{:S(2)}, u32[]{:S(2)}) collective-permute-start(bf16[768,1024]{1,0:T(8,128)(2,1)} %flip.8.refs_1_), channel_id=1, source_target_pairs={{0,16},{1,17},{10,26},{11,27},{20,4},{21,5},{30,14},{31,15}} | collective-permute-start | bytes 4718600 | tf_op jit(solution)/shard_map/ppermute | solution.py:532
  170.2 11.1 %collective-permute-done.10.refs_2_ = bf16[2048,256]{1,0:T(8,128)(2,1)S(1)} collective-permute-done((bf16[2048,256]{1,0:T(8,128)(2,1)S(1)}, bf16[2048,256]{1,0:T(8,128)(2,1)S(1)}, u32[]{:S(2)}, u32[]{:S(2)}) %collective-permute-start.10) | collective-permute-done | bytes 1048608 | tf_op jit(solution)/shard_map/ppermute | solution.py:510
  187.1 7.3 %collective-permute-done.17 = bf16[1024,256]{1,0:T(8,128)(2,1)S(1)} collective-permute-done((bf16[1024,256]{1,0:T(8,128)(2,1)S(1)}, bf16[1024,256]{1,0:T(8,128)(2,1)S(1)}, u32[]{:S(2)}, u32[]{:S(2)}) %collective-permute-start.17) | collective-permute-done | bytes 524320 | tf_op jit(solution)/shard_map/ppermute | solution.py:510
  220.5 4.4 %collective-permute-start.29 = (bf16[256,1024]{1,0:T(8,128)(2,1)}, bf16[256,1024]{1,0:T(8,128)(2,1)S(1)}, u32[]{:S(2)}, u32[]{:S(2)}) collective-permute-start(bf16[256,1024]{1,0:T(8,128)(2,1)} %flip.11.refs_1_), channel_id=1, source_target_pairs={{0,16},{1,17},{10,26},{11,27},{20,4},{21,5},{30,14},{31,15}} | collective-permute-start | bytes 1572872 | tf_op jit(solution)/shard_map/ppermute | solution.py:532
  226.4 5.5 %collective-permute-done.29.refs_3_ = bf16[256,1024]{1,0:T(8,128)(2,1)S(1)} collective-permute-done((bf16[256,1024]{1,0:T(8,128)(2,1)}, bf16[256,1024]{1,0:T(8,128)(2,1)S(1)}, u32[]{:S(2)}, u32[]{:S(2)}) %collective-permute-start.29) | collective-permute-done | bytes 524320 | tf_op jit(solution)/shard_map/ppermute | solution.py:532
  231.9 4.4 %flip.7.refs_1_ = bf16[768,1024]{1,0:T(8,128)(2,1)} custom-call(s32[1]{0:T(128)} %bitcast.7.refs_0_, bf16[2048,256]{1,0:T(8,128)(2,1)} %assemble.3.refs_1_, bf16[2048,256]{1,0:T(8,128)(2,1)} %copy-done.9, bf16[2048,256]{1,0:T(8,128)(2,1)} %copy-done.10), custom_call_target="tpu_custom_call" | custom-call | bytes 6291456 | tf_op jit(solution)/shard_map/flip/pallas_call | solution.py:331
  236.4 5.6 %collective-permute-start.35 = (bf16[768,1024]{1,0:T(8,128)(2,1)}, bf16[768,1024]{1,0:T(8,128)(2,1)}, u32[]{:S(2)}, u32[]{:S(2)}) collective-permute-start(bf16[768,1024]{1,0:T(8,128)(2,1)} %flip.7.refs_1_), channel_id=1, source_target_pairs={{0,16},{1,17},{10,26},{11,27},{20,4},{21,5},{30,14},{31,15}} | collective-permute-start | bytes 4718600 | tf_op jit(solution)/shard_map/ppermute | solution.py:532
  251.4 13.7 %contract.4.refs_12_ = f32[2,2,2048,2048]{3,2,1,0:T(8,128)} custom-call(bf16[2,1024,256]{2,1,0:T(8,128)(2,1)} %bitcast.32, bf16[2,1024,256]{2,1,0:T(8,128)(2,1)} %bitcast.47, bf16[2,1024,256]{2,1,0:T(8,128)(2,1)} %bitcast.44, bf16[2,1024,256]{2,1,0:T(8,128)(2,1)} %bitcast.10.refs_3_, bf16[2,1024,256]{2,1,0:T(8,128)(2,1)} %bitcast.11.refs_4_, ...), custom_call_target="tpu_custom_call" | custom-call | flops 17179869184 | bytes 8388608 | tf_op jit(solution)/shard_map/contract/pallas_call | solution.py:434
  273.9 13.7 %contract.5.refs_12_ = f32[2,2,2048,2048]{3,2,1,0:T(8,128)} custom-call(bf16[2,1024,256]{2,1,0:T(8,128)(2,1)} %bitcast.33, bf16[2,1024,256]{2,1,0:T(8,128)(2,1)} %bitcast.48, bf16[2,1024,256]{2,1,0:T(8,128)(2,1)} %bitcast.45, bf16[2,1024,256]{2,1,0:T(8,128)(2,1)} %bitcast.10.refs_3_, ...), custom_call_target="tpu_custom_call", output_to_operand_aliasing={{}: (12, {})} | custom-call | flops 17179869184 | bytes 8388608 | tf_op jit(solution)/shard_map/contract/pallas_call | solution.py:434
  287.7 4.2 %flip.13.refs_1_ = bf16[1024,1024]{1,0:T(8,128)(2,1)} custom-call(s32[1]{0:T(128)} %bitcast.7.refs_0_, bf16[2048,256]{1,0:T(8,128)(2,1)} %copy-done.11, bf16[2048,256]{1,0:T(8,128)(2,1)} %copy-done.12, bf16[2048,256]{1,0:T(8,128)(2,1)} %copy-done.6, bf16[2048,256]{1,0:T(8,128)(2,1)} %copy-done.7), custom_call_target="tpu_custom_call" | custom-call | bytes 8388608 | tf_op jit(solution)/shard_map/flip/pallas_call | solution.py:331
  300.8 24.3 %contract.6.refs_19_ = f32[2,2,2048,2048]{3,2,1,0:T(8,128)} custom-call(bf16[2,1024,256]{2,1,0:T(8,128)(2,1)} %bitcast.50, bf16[2,1024,256]{2,1,0:T(8,128)(2,1)} %bitcast.58, bf16[2,1024,256]{2,1,0:T(8,128)(2,1)} %bitcast.60, bf16[2,1024,256]{2,1,0:T(8,128)(2,1)} %bitcast.62, bf16[2,1024,256]{2,1,0:T(8,128)(2,1)} %bitcast.64, ...), custom_call_target="tpu_custom_call", output_to_operand_aliasing={{}: (12, {})} | custom-call | flops 34359738368 | bytes 16777216 | tf_op jit(solution)/shard_map/contract/pallas_call | solution.py:434
  327.1 6.6 %collective-permute-done.41.refs_3_ = bf16[256,1024]{1,0:T(8,128)(2,1)S(1)} collective-permute-done((bf16[256,1024]{1,0:T(8,128)(2,1)S(1)}, bf16[256,1024]{1,0:T(8,128)(2,1)S(1)}, u32[]{:S(2)}, u32[]{:S(2)}) %collective-permute-start.41) | collective-permute-done | bytes 524320 | tf_op jit(solution)/shard_map/ppermute | solution.py:532
  334.3 4.2 %settle.11.refs_16_ = bf16[2,768,1024]{2,1,0:T(8,128)(2,1)} custom-call(s32[1]{0:T(128)} %bitcast.16.refs_0_, bf16[768,1024]{1,0:T(8,128)(2,1)} %flip.7.refs_1_, bf16[768,1024]{1,0:T(8,128)(2,1)} %collective-permute-done.34.refs_2_, bf16[768,1024]{1,0:T(8,128)(2,1)} %collective-permute-done.35.refs_3_, bf16[768,1024]{1,0:T(8,128)(2,1)} %collective-permute-done.36.refs_4_), custom_call_target="tpu_custom_call" | custom-call | bytes 6291456 | tf_op jit(solution)/shard_map/settle/pallas_call | solution.py:374
  343.4 4.8 %settle.12.refs_17_ = bf16[2,1024,1024]{2,1,0:T(8,128)(2,1)} custom-call(s32[1]{0:T(128)} %bitcast.16.refs_0_, bf16[1024,1024]{1,0:T(8,128)(2,1)} %flip.13.refs_1_, bf16[1024,1024]{1,0:T(8,128)(2,1)} %copy-done.15, bf16[1024,1024]{1,0:T(8,128)(2,1)} %copy-done.14, bf16[1024,1024]{1,0:T(8,128)(2,1)} %collective-permute-done.39.refs_4_), custom_call_target="tpu_custom_call" | custom-call | bytes 8388608 | tf_op jit(solution)/shard_map/settle/pallas_call | solution.py:374
  348.3 43.8 %contract.7 = f32[2,2,2048,2048]{3,2,1,0:T(8,128)} custom-call(bf16[2,1024,256]{2,1,0:T(8,128)(2,1)} %bitcast.34, bf16[2,1024,256]{2,1,0:T(8,128)(2,1)} %bitcast.49, bf16[2,1024,256]{2,1,0:T(8,128)(2,1)} %bitcast.46, bf16[2,1024,256]{2,1,0:T(8,128)(2,1)} %bitcast.10.refs_3_, bf16[2,1024,256]{2,1,0:T(8,128)(2,1)} %bitcast.11.refs_4_, ...), custom_call_target="tpu_custom_call", output_to_operand_aliasing={{}: (19, {})} | custom-call | flops 68719476736 | bytes 33554432 | tf_op jit(solution)/shard_map/contract/pallas_call | solution.py:434
  (169 shorter events, 108.5 us)
Async XLA Ops:
  76.3 25.4 %collective-permute-start.4 = (bf16[2048,256]{1,0:T(8,128)(2,1)}, bf16[2048,256]{1,0:T(8,128)(2,1)S(1)}, u32[]{:S(2)}, u32[]{:S(2)}) collective-permute-start(bf16[2048,256]{1,0:T(8,128)(2,1)} %assemble.2.refs_1_), channel_id=1, source_target_pairs={{2,0},{4,2},{6,4},{7,6},{5,7},{3,5},{1,3},{0,1},{10,8},{12,10},{14... | collective-permute-start | bytes 3145736 | tf_op jit(solution)/shard_map/ppermute | solution.py:510
  78.0 25.6 %collective-permute-start.3 = (bf16[2048,256]{1,0:T(8,128)(2,1)}, bf16[2048,256]{1,0:T(8,128)(2,1)S(1)}, u32[]{:S(2)}, u32[]{:S(2)}) collective-permute-start(bf16[2048,256]{1,0:T(8,128)(2,1)} %assemble.2.refs_1_), channel_id=1, source_target_pairs={{0,2},{2,4},{4,6},{6,7},{7,5},{5,3},{3,1},{1,0},{8,10},{10,12},{12... | collective-permute-start | bytes 3145736 | tf_op jit(solution)/shard_map/ppermute | solution.py:510
  101.8 24.6 %collective-permute-start.9 = (bf16[2048,256]{1,0:T(8,128)(2,1)S(1)}, bf16[2048,256]{1,0:T(8,128)(2,1)}, u32[]{:S(2)}, u32[]{:S(2)}) collective-permute-start(bf16[2048,256]{1,0:T(8,128)(2,1)S(1)} %collective-permute-done.4.refs_3_), channel_id=1, source_target_pairs={{2,0},{4,2},{6,4},{7,6},{5,7},{3,5},{1,3},{0,1},{10,8},{12,10},{14... | collective-permute-start | bytes 3145736 | tf_op jit(solution)/shard_map/ppermute | solution.py:510
  103.5 24.6 %collective-permute-start.8 = (bf16[2048,256]{1,0:T(8,128)(2,1)S(1)}, bf16[2048,256]{1,0:T(8,128)(2,1)}, u32[]{:S(2)}, u32[]{:S(2)}) collective-permute-start(bf16[2048,256]{1,0:T(8,128)(2,1)S(1)} %collective-permute-done.3.refs_2_), channel_id=1, source_target_pairs={{0,2},{2,4},{4,6},{6,7},{7,5},{5,3},{3,1},{1,0},{8,10},{10,12},{12... | collective-permute-start | bytes 3145736 | tf_op jit(solution)/shard_map/ppermute | solution.py:510
  126.4 23.8 %collective-permute-start.15 = (bf16[2048,256]{1,0:T(8,128)(2,1)}, bf16[2048,256]{1,0:T(8,128)(2,1)S(1)}, u32[]{:S(2)}, u32[]{:S(2)}) collective-permute-start(bf16[2048,256]{1,0:T(8,128)(2,1)} %collective-permute-done.9.refs_2_), channel_id=1, source_target_pairs={{2,0},{4,2},{6,4},{7,6},{5,7},{3,5},{1,3},{0,1},{10,8},{12,10},{14... | collective-permute-start | bytes 3145736 | tf_op jit(solution)/shard_map/ppermute | solution.py:510
  128.1 23.5 %collective-permute-start.14 = (bf16[2048,256]{1,0:T(8,128)(2,1)}, bf16[2048,256]{1,0:T(8,128)(2,1)S(1)}, u32[]{:S(2)}, u32[]{:S(2)}) collective-permute-start(bf16[2048,256]{1,0:T(8,128)(2,1)} %collective-permute-done.8.refs_1_), channel_id=1, source_target_pairs={{0,2},{2,4},{4,6},{6,7},{7,5},{5,3},{3,1},{1,0},{8,10},{10,12},{12... | collective-permute-start | bytes 3145736 | tf_op jit(solution)/shard_map/ppermute | solution.py:510
  156.0 30.6 %collective-permute-start.20 = (bf16[768,1024]{1,0:T(8,128)(2,1)}, bf16[768,1024]{1,0:T(8,128)(2,1)}, u32[]{:S(2)}, u32[]{:S(2)}) collective-permute-start(bf16[768,1024]{1,0:T(8,128)(2,1)} %flip.8.refs_1_), channel_id=1, source_target_pairs={{0,16},{1,17},{10,26},{11,27},{20,4},{21,5},{30,14},{31,15}} | collective-permute-start | bytes 4718600 | tf_op jit(solution)/shard_map/ppermute | solution.py:532
  160.5 26.1 %collective-permute-start.12 = (bf16[2048,256]{1,0:T(8,128)(2,1)S(1)}, bf16[2048,256]{1,0:T(8,128)(2,1)S(1)}, u32[]{:S(2)}, u32[]{:S(2)}) collective-permute-start(bf16[2048,256]{1,0:T(8,128)(2,1)S(1)} %copy-done.5), channel_id=1, source_target_pairs={{2,0},{4,2},{6,4},{7,6},{5,7},{3,5},{1,3},{0,1},{10,8},{12,10},{14... | collective-permute-start | bytes 3145736 | tf_op jit(solution)/shard_map/ppermute | solution.py:510
  166.2 28.2 %collective-permute-start.23 = (bf16[512,1024]{1,0:T(8,128)(2,1)}, bf16[512,1024]{1,0:T(8,128)(2,1)}, u32[]{:S(2)}, u32[]{:S(2)}) collective-permute-start(bf16[512,1024]{1,0:T(8,128)(2,1)} %flip.9.refs_1_), channel_id=1, source_target_pairs={{0,16},{1,17},{10,26},{11,27},{20,4},{21,5},{30,14},{31,15}} | collective-permute-start | bytes 3145736 | tf_op jit(solution)/shard_map/ppermute | solution.py:532
  168.5 25.9 %collective-permute-start.17 = (bf16[1024,256]{1,0:T(8,128)(2,1)S(1)}, bf16[1024,256]{1,0:T(8,128)(2,1)S(1)}, u32[]{:S(2)}, u32[]{:S(2)}) collective-permute-start(bf16[1024,256]{1,0:T(8,128)(2,1)S(1)} %slice.37), channel_id=1, source_target_pairs={{2,0},{4,2},{6,4},{7,6},{5,7},{3,5},{1,3},{0,1},{10,8},{12,10},{14... | collective-permute-start | bytes 1572872 | tf_op jit(solution)/shard_map/ppermute | solution.py:510
  186.6 25.9 %collective-permute-start.19 = (bf16[768,1024]{1,0:T(8,128)(2,1)}, bf16[768,1024]{1,0:T(8,128)(2,1)}, u32[]{:S(2)}, u32[]{:S(2)}) collective-permute-start(bf16[768,1024]{1,0:T(8,128)(2,1)} %flip.8.refs_1_), channel_id=1, source_target_pairs={{0,8},{8,0},{16,24},{24,16},{1,9},{9,1},{17,25},{25,17},{2,10},{10... | collective-permute-start | bytes 4718600 | tf_op jit(solution)/shard_map/ppermute | solution.py:526
  186.6 26.4 %collective-permute-start.21 = (bf16[768,1024]{1,0:T(8,128)(2,1)}, bf16[768,1024]{1,0:T(8,128)(2,1)}, u32[]{:S(2)}, u32[]{:S(2)}) collective-permute-start(bf16[768,1024]{1,0:T(8,128)(2,1)} %collective-permute-done.20.refs_3_), channel_id=1, source_target_pairs={{0,8},{8,0},{16,24},{24,16},{1,9},{9,1},{17,25},{25,17},{2,10},{10... | collective-permute-start | bytes 4718600 | tf_op jit(solution)/shard_map/ppermute | solution.py:526
  201.9 24.5 %collective-permute-start.11 = (bf16[2048,256]{1,0:T(8,128)(2,1)S(1)}, bf16[2048,256]{1,0:T(8,128)(2,1)S(1)}, u32[]{:S(2)}, u32[]{:S(2)}) collective-permute-start(bf16[2048,256]{1,0:T(8,128)(2,1)S(1)} %collective-permute-done.10.refs_2_), channel_id=1, source_target_pairs={{0,2},{2,4},{4,6},{6,7},{7,5},{5,3},{3,1},{1,0},{8,10},{10,12},{12... | collective-permute-start | bytes 3145736 | tf_op jit(solution)/shard_map/ppermute | solution.py:510
  202.0 30.0 %collective-permute-start.13 = (bf16[2048,256]{1,0:T(8,128)(2,1)}, bf16[2048,256]{1,0:T(8,128)(2,1)S(1)}, u32[]{:S(2)}, u32[]{:S(2)}) collective-permute-start(bf16[2048,256]{1,0:T(8,128)(2,1)} %copy-done.10), channel_id=1, source_target_pairs={{2,0},{4,2},{6,4},{7,6},{5,7},{3,5},{1,3},{0,1},{10,8},{12,10},{14... | collective-permute-start | bytes 3145736 | tf_op jit(solution)/shard_map/ppermute | solution.py:510
  212.5 29.4 %collective-permute-start.25 = (bf16[512,1024]{1,0:T(8,128)(2,1)S(1)}, bf16[512,1024]{1,0:T(8,128)(2,1)S(1)}, u32[]{:S(2)}, u32[]{:S(2)}) collective-permute-start(bf16[512,1024]{1,0:T(8,128)(2,1)S(1)} %copy-done.13), channel_id=1, source_target_pairs={{0,8},{8,0},{16,24},{24,16},{1,9},{9,1},{17,25},{25,17},{2,10},{10... | collective-permute-start | bytes 3145736 | tf_op jit(solution)/shard_map/ppermute | solution.py:526
  212.6 30.3 %collective-permute-start.27 = (bf16[512,1024]{1,0:T(8,128)(2,1)}, bf16[512,1024]{1,0:T(8,128)(2,1)}, u32[]{:S(2)}, u32[]{:S(2)}) collective-permute-start(bf16[512,1024]{1,0:T(8,128)(2,1)} %collective-permute-done.26.refs_3_), channel_id=1, source_target_pairs={{0,8},{8,0},{16,24},{24,16},{1,9},{9,1},{17,25},{25,17},{2,10},{10... | collective-permute-start | bytes 3145736 | tf_op jit(solution)/shard_map/ppermute | solution.py:526
  236.4 89.3 %collective-permute-start.35 = (bf16[768,1024]{1,0:T(8,128)(2,1)}, bf16[768,1024]{1,0:T(8,128)(2,1)}, u32[]{:S(2)}, u32[]{:S(2)}) collective-permute-start(bf16[768,1024]{1,0:T(8,128)(2,1)} %flip.7.refs_1_), channel_id=1, source_target_pairs={{0,16},{1,17},{10,26},{11,27},{20,4},{21,5},{30,14},{31,15}} | collective-permute-start | bytes 4718600 | tf_op jit(solution)/shard_map/ppermute | solution.py:532
  241.9 91.8 %collective-permute-start.34 = (bf16[768,1024]{1,0:T(8,128)(2,1)}, bf16[768,1024]{1,0:T(8,128)(2,1)}, u32[]{:S(2)}, u32[]{:S(2)}) collective-permute-start(bf16[768,1024]{1,0:T(8,128)(2,1)} %flip.7.refs_1_), channel_id=1, source_target_pairs={{0,8},{8,0},{16,24},{24,16},{1,9},{9,1},{17,25},{25,17},{2,10},{10... | collective-permute-start | bytes 4718600 | tf_op jit(solution)/shard_map/ppermute | solution.py:526
  242.9 24.7 %collective-permute-start.18 = (bf16[2048,256]{1,0:T(8,128)(2,1)S(1)}, bf16[2048,256]{1,0:T(8,128)(2,1)S(1)}, u32[]{:S(2)}, u32[]{:S(2)}) collective-permute-start(bf16[2048,256]{1,0:T(8,128)(2,1)S(1)} %collective-permute-done.11.refs_1_), channel_id=1, source_target_pairs={{0,2},{2,4},{4,6},{6,7},{7,5},{5,3},{3,1},{1,0},{8,10},{10,12},{12... | collective-permute-start | bytes 3145736 | tf_op jit(solution)/shard_map/ppermute | solution.py:510
  245.9 25.0 %collective-permute-start.32 = (bf16[2048,256]{1,0:T(8,128)(2,1)S(1)}, bf16[2048,256]{1,0:T(8,128)(2,1)S(1)}, u32[]{:S(2)}, u32[]{:S(2)}) collective-permute-start(bf16[2048,256]{1,0:T(8,128)(2,1)S(1)} %collective-permute-done.13.refs_2_), channel_id=1, source_target_pairs={{2,0},{4,2},{6,4},{7,6},{5,7},{3,5},{1,3},{0,1},{10,8},{12,10},{14... | collective-permute-start | bytes 3145736 | tf_op jit(solution)/shard_map/ppermute | solution.py:510
  271.8 24.6 %collective-permute-start.33 = (bf16[1024,256]{1,0:T(8,128)(2,1)}, bf16[1024,256]{1,0:T(8,128)(2,1)S(1)}, u32[]{:S(2)}, u32[]{:S(2)}) collective-permute-start(bf16[1024,256]{1,0:T(8,128)(2,1)} %slice.33), channel_id=1, source_target_pairs={{2,0},{4,2},{6,4},{7,6},{5,7},{3,5},{1,3},{0,1},{10,8},{12,10},{14... | collective-permute-start | bytes 1572872 | tf_op jit(solution)/shard_map/ppermute | solution.py:510
  273.3 22.0 %collective-permute-start.31 = (bf16[1024,256]{1,0:T(8,128)(2,1)S(1)}, bf16[1024,256]{1,0:T(8,128)(2,1)}, u32[]{:S(2)}, u32[]{:S(2)}) collective-permute-start(bf16[1024,256]{1,0:T(8,128)(2,1)S(1)} %slice.32), channel_id=1, source_target_pairs={{0,2},{2,4},{4,6},{6,7},{7,5},{5,3},{3,1},{1,0},{8,10},{10,12},{12... | collective-permute-start | bytes 1572872 | tf_op jit(solution)/shard_map/ppermute | solution.py:510
  291.9 33.2 %collective-permute-start.38 = (bf16[1024,1024]{1,0:T(8,128)(2,1)}, bf16[1024,1024]{1,0:T(8,128)(2,1)S(1)}, u32[]{:S(2)}, u32[]{:S(2)}) collective-permute-start(bf16[1024,1024]{1,0:T(8,128)(2,1)} %flip.13.refs_1_), channel_id=1, source_target_pairs={{0,16},{1,17},{10,26},{11,27},{20,4},{21,5},{30,14},{31,15}} | collective-permute-start | bytes 6291464 | tf_op jit(solution)/shard_map/ppermute | solution.py:532
  295.2 46.9 %collective-permute-start.37 = (bf16[1024,1024]{1,0:T(8,128)(2,1)}, bf16[1024,1024]{1,0:T(8,128)(2,1)S(1)}, u32[]{:S(2)}, u32[]{:S(2)}) collective-permute-start(bf16[1024,1024]{1,0:T(8,128)(2,1)} %flip.13.refs_1_), channel_id=1, source_target_pairs={{0,8},{8,0},{16,24},{24,16},{1,9},{9,1},{17,25},{25,17},{2,10},{10... | collective-permute-start | bytes 6291464 | tf_op jit(solution)/shard_map/ppermute | solution.py:526
  (50 other events, 537.2 us)

commit v9 on v6

--- a/solution.py
+++ b/solution.py
@@ -513,9 +513,9 @@
         cut = below.shape[0] // 2
         return [jnp.concatenate(go_round(below[:cut], above[cut:]), axis=0)]
 
-    def column(slots, before=(), behind=()):
+    def column(slots, before=(), behind=(), flipped=None):
         slots = [after(slots[0], *before)] + slots[1:] if before else slots
-        copies = [flip(slots, my_part, parts, unit)]
+        copies = [flip(slots, my_part, parts, unit) if flipped is None else flipped]
         for relation in range(1, rows):
             source = relation & (relation - 1)
             hop = relation ^ source
@@ -559,17 +559,20 @@
     lefts = as_lefts(one)
     wide = CHUNKS[0][1] // 2
     first = contract(None, [lefts], rights, unit, 0, wide, 0, 1, 0)
-    second = contract(first, [lefts], rights, unit, 0, wide, 1, 1, 1)
-    copies = [column(sum(two[:2], []), two[2])]
     two.append(go_round(*[after(block, first) for block in two[2]]))
     for t in range(4, half):
         two.append(go_round(*two[t - 1]))
-    copies.append(column(sum(two[2:half], []), two[half - 1]))
-    two.append(last_round(*[after(block, second, copies[0][0]) for block in two[half - 1]]))
+    copies = [column(sum(two[:2], []), two[2] + [first])]
+    lefts = [after(lefts[0], copies[0][0])] + lefts[1:]
+    second = contract(first, [lefts], rights, unit, 0, wide, 1, 1, 1)
+    two.append(last_round(*[after(block, second) for block in two[half - 1]]))
     share = CHUNKS[0][1]
+    flipped = flip(two[half], my_part, parts, unit)
     both = [lefts, as_lefts(two)]
+    both[1][0] = after(both[1][0], flipped)
     result = contract(second, both[1:], rights, unit, share, share, 0, 1, 0)
-    copies.append(column(two[half], (), (result,)))
+    copies.append(column(sum(two[2:half], []), two[half - 1] + [second], (result,)))
+    copies.append(column(two[half], (), (result,), flipped))
     rights = [settle(which, some, pairs) for some in copies]
     result = contract(result, both, rights, unit, 0, share, 0, 1, 1)
     return result.reshape(2, parts * block, block)

time: 394 us -> 376 us (0.954)
  waiting for transfers between devices: 112 us -> 94.3 us
    ppermute x8, waiting for transfers between devices: 29.4 us -> 16.4 us  [go_round(): lax.ppermute(above, 'col', ring_down)]
    ppermute x8, waiting for transfers between devices: 39.2 us -> 30.7 us  [go_round(): lax.ppermute(below, 'col', ring_up)]
  transfers between devices with their start and end apart: 43 -> 43, of which waited for: 19 -> 19; matrix products, arithmetic and copies ran while one was open for 0% -> 0% of each run, Pallas kernels for 30% -> 31%
where the time goes in v9:
time: 376 us; the launch traced here: 375 us
  Pallas kernels  218 us (58%)
  waiting for transfers between devices  94.3 us (25%)
  starting transfers between devices  47.6 us (13%)
  local copies, waits for them, and re-layouts  10.2 us (3%)
  other arithmetic  4.23 us (1%)
    pallas_call x4, Pallas kernels, contract(): pl.pallas_call(lambda *refs: contract_kernel(slot_count, shares, len(righ...  95.5 us
    pallas_call x1, Pallas kernels, transform(): pl.pallas_call(lambda *refs: transform_kernel(pairs, load_steps, step_row...  51 us
    ppermute x8, waiting for transfers between devices, go_round(): lax.ppermute(below, 'col', ring_up)  30.7 us
    pallas_call x7, Pallas kernels, flip(): pl.pallas_call(lambda *refs: flip_kernel(slot_count, *refs), grid_spec=pl...  26.2 us
    ppermute x6, waiting for transfers between devices, across_rows(): lax.ppermute(parcels[s], 'row', [(r, r ^ s) for r in range(rows)])  24.7 us
    pallas_call x7, Pallas kernels, settle(): pl.pallas_call(lambda *refs: settle_kernel(pairs, row_count, *refs), grid...  24.5 us
    ppermute x7, starting transfers between devices, column(): copies.append(lax.ppermute(held, ('row', 'col'), perm))  24.4 us
    ppermute x7, waiting for transfers between devices, column(): copies.append(lax.ppermute(held, ('row', 'col'), perm))  19.1 us
  transfers between devices with their start and end apart: 43, of which 19 were waited for; matrix products, arithmetic and copies ran while one was open for 0% of the time, Pallas kernels for 31%

profile of v9, /device:TPU:0, one launch (start us, length us, event | category | flops | bytes accessed | tf_op | source)
XLA Modules:
  0.0 374.9 jit_solution(1478425167236167328)
XLA Ops:
  6.4 51.0 %transform.1 = (bf16[1024,128]{1,0:T(8,128)(2,1)}, bf16[1024,128]{1,0:T(8,128)(2,1)}, bf16[1024,128]{1,0:T(8,128)(2,1)}, bf16[1024,128]{1,0:T(8,128)(2,1)}, f32[32768,128]{1,0:T(8,128)}) custom-call(s32[8192]{0:T(1024)} %bitcast.65, s32[1]{0:T(128)} %bitcast.refs_1_.refs_0_, bf16[64,256]{1,0:T(8,128)(2,1)} %fusion.16.refs_2_, ...), custom_call_target="tpu_custom_call" | custom-call | flops 9663676416 | bytes 40000000 | tf_op jit(solution)/shard_map/transform/pallas_call | solution.py:233
  60.5 7.3 %collective-permute-done.1.refs_3_ = bf16[1024,128]{1,0:T(8,128)(2,1)S(1)} collective-permute-done((bf16[1024,128]{1,0:T(8,128)(2,1)}, bf16[1024,128]{1,0:T(8,128)(2,1)S(1)}, u32[]{:S(2)}, u32[]{:S(2)}) %collective-permute-start.1) | collective-permute-done | bytes 262176 | tf_op jit(solution)/shard_map/ppermute | solution.py:505
  67.8 5.1 %collective-permute-done.2.refs_4_ = bf16[1024,128]{1,0:T(8,128)(2,1)S(1)} collective-permute-done((bf16[1024,128]{1,0:T(8,128)(2,1)}, bf16[1024,128]{1,0:T(8,128)(2,1)S(1)}, u32[]{:S(2)}, u32[]{:S(2)}) %collective-permute-start.2) | collective-permute-done | bytes 262176 | tf_op jit(solution)/shard_map/ppermute | solution.py:505
  79.0 15.6 %select.45 = (bf16[1024,128]{1,0:T(8,128)(2,1)}, bf16[1024,128]{1,0:T(8,128)(2,1)}, bf16[1024,128]{1,0:T(8,128)(2,1)}, bf16[1024,128]{1,0:T(8,128)(2,1)}) custom-call(s32[8192]{0:T(1024)} %bitcast.62, s32[1]{0:T(128)} %bitcast.refs_1_.refs_0_, f32[32768,128]{1,0:T(8,128)} %get-tuple-element.45.refs_2_), custom_call_target="tpu_custom_call" | custom-call | bytes 50000000 | tf_op jit(solution)/shard_map/select/pallas_call | solution.py:113
  94.6 7.1 %collective-permute-done.3.refs_2_ = bf16[2048,256]{1,0:T(8,128)(2,1)S(1)} collective-permute-done((bf16[2048,256]{1,0:T(8,128)(2,1)}, bf16[2048,256]{1,0:T(8,128)(2,1)S(1)}, u32[]{:S(2)}, u32[]{:S(2)}) %collective-permute-start.3) | collective-permute-done | bytes 1048608 | tf_op jit(solution)/shard_map/ppermute | solution.py:510
  105.6 7.4 %collective-permute-done.6.refs_3_ = bf16[1024,128]{1,0:T(8,128)(2,1)S(1)} collective-permute-done((bf16[1024,128]{1,0:T(8,128)(2,1)}, bf16[1024,128]{1,0:T(8,128)(2,1)S(1)}, u32[]{:S(2)}, u32[]{:S(2)}) %collective-permute-start.6) | collective-permute-done | bytes 262176 | tf_op jit(solution)/shard_map/ppermute | solution.py:505
  113.1 4.8 %collective-permute-done.7.refs_4_ = bf16[1024,128]{1,0:T(8,128)(2,1)S(1)} collective-permute-done((bf16[1024,128]{1,0:T(8,128)(2,1)}, bf16[1024,128]{1,0:T(8,128)(2,1)S(1)}, u32[]{:S(2)}, u32[]{:S(2)}) %collective-permute-start.7) | collective-permute-done | bytes 262176 | tf_op jit(solution)/shard_map/ppermute | solution.py:505
  128.4 4.8 %collective-permute-start.16 = (bf16[768,1024]{1,0:T(8,128)(2,1)}, bf16[768,1024]{1,0:T(8,128)(2,1)}, u32[]{:S(2)}, u32[]{:S(2)}) collective-permute-start(bf16[768,1024]{1,0:T(8,128)(2,1)} %flip.7.refs_1_), channel_id=1, source_target_pairs={{0,16},{1,17},{10,26},{11,27},{20,4},{21,5},{30,14},{31,15}} | collective-permute-start | bytes 4718600 | tf_op jit(solution)/shard_map/ppermute | solution.py:532
  136.8 14.3 %collective-permute-done.9.refs_1_ = bf16[2048,256]{1,0:T(8,128)(2,1)S(1)} collective-permute-done((bf16[2048,256]{1,0:T(8,128)(2,1)}, bf16[2048,256]{1,0:T(8,128)(2,1)S(1)}, u32[]{:S(2)}, u32[]{:S(2)}) %collective-permute-start.9) | collective-permute-done | bytes 1048608 | tf_op jit(solution)/shard_map/ppermute | solution.py:510
  153.3 4.6 %collective-permute-start.19 = (bf16[512,1024]{1,0:T(8,128)(2,1)S(1)}, bf16[512,1024]{1,0:T(8,128)(2,1)}, u32[]{:S(2)}, u32[]{:S(2)}) collective-permute-start(bf16[512,1024]{1,0:T(8,128)(2,1)S(1)} %copy-done.12), channel_id=1, source_target_pairs={{0,16},{1,17},{10,26},{11,27},{20,4},{21,5},{30,14},{31,15}} | collective-permute-start | bytes 3145736 | tf_op jit(solution)/shard_map/ppermute | solution.py:532
  175.9 10.3 %collective-permute-done.28.refs_3_ = bf16[256,1024]{1,0:T(8,128)(2,1)} collective-permute-done((bf16[256,1024]{1,0:T(8,128)(2,1)}, bf16[256,1024]{1,0:T(8,128)(2,1)}, u32[]{:S(2)}, u32[]{:S(2)}) %collective-permute-start.28) | collective-permute-done | bytes 524320 | tf_op jit(solution)/shard_map/ppermute | solution.py:532
  186.7 9.3 %collective-permute-done.22.refs_3_ = bf16[2048,256]{1,0:T(8,128)(2,1)S(1)} collective-permute-done((bf16[2048,256]{1,0:T(8,128)(2,1)S(1)}, bf16[2048,256]{1,0:T(8,128)(2,1)S(1)}, u32[]{:S(2)}, u32[]{:S(2)}) %collective-permute-start.22) | collective-permute-done | bytes 1048608 | tf_op jit(solution)/shard_map/ppermute | solution.py:510
  201.7 4.2 %settle.7.refs_8_ = bf16[2,768,1024]{2,1,0:T(8,128)(2,1)} custom-call(s32[1]{0:T(128)} %bitcast.8.refs_0_, bf16[768,1024]{1,0:T(8,128)(2,1)} %flip.7.refs_1_, bf16[768,1024]{1,0:T(8,128)(2,1)} %collective-permute-done.15.refs_2_, bf16[768,1024]{1,0:T(8,128)(2,1)} %collective-permute-done.16.refs_3_, bf16[768,1024]{1,0:T(8,128)(2,1)} %collective-permute-done.17.refs_4_), custom_call_target="tpu_custom_call" | custom-call | bytes 6291456 | tf_op jit(solution)/shard_map/settle/pallas_call | solution.py:374
  213.5 13.7 %contract.4.refs_12_ = f32[2,2,2048,2048]{3,2,1,0:T(8,128)} custom-call(bf16[2,1024,256]{2,1,0:T(8,128)(2,1)} %bitcast.32, bf16[2,1024,256]{2,1,0:T(8,128)(2,1)} %bitcast.44, bf16[2,1024,256]{2,1,0:T(8,128)(2,1)} %bitcast.47, bf16[2,1024,256]{2,1,0:T(8,128)(2,1)} %bitcast.11.refs_3_, bf16[2,1024,256]{2,1,0:T(8,128)(2,1)} %bitcast.12.refs_4_, ...), custom_call_target="tpu_custom_call" | custom-call | flops 17179869184 | bytes 8388608 | tf_op jit(solution)/shard_map/contract/pallas_call | solution.py:434
  227.2 5.0 %collective-permute-done.23.refs_2_ = bf16[2048,256]{1,0:T(8,128)(2,1)} collective-permute-done((bf16[2048,256]{1,0:T(8,128)(2,1)S(1)}, bf16[2048,256]{1,0:T(8,128)(2,1)}, u32[]{:S(2)}, u32[]{:S(2)}) %collective-permute-start.23) | collective-permute-done | bytes 1048608 | tf_op jit(solution)/shard_map/ppermute | solution.py:510
  238.1 13.7 %contract.5.refs_12_ = f32[2,2,2048,2048]{3,2,1,0:T(8,128)} custom-call(bf16[2,1024,256]{2,1,0:T(8,128)(2,1)} %bitcast.33, bf16[2,1024,256]{2,1,0:T(8,128)(2,1)} %bitcast.45, bf16[2,1024,256]{2,1,0:T(8,128)(2,1)} %bitcast.48, bf16[2,1024,256]{2,1,0:T(8,128)(2,1)} %bitcast.11.refs_3_, ...), custom_call_target="tpu_custom_call", output_to_operand_aliasing={{}: (12, {})} | custom-call | flops 17179869184 | bytes 8388608 | tf_op jit(solution)/shard_map/contract/pallas_call | solution.py:434
  251.9 4.6 %collective-permute-done.30.refs_3_ = bf16[2048,256]{1,0:T(8,128)(2,1)S(1)} collective-permute-done((bf16[2048,256]{1,0:T(8,128)(2,1)}, bf16[2048,256]{1,0:T(8,128)(2,1)S(1)}, u32[]{:S(2)}, u32[]{:S(2)}) %collective-permute-start.30) | collective-permute-done | bytes 1048608 | tf_op jit(solution)/shard_map/ppermute | solution.py:510
  263.0 4.3 %flip.13.refs_1_ = bf16[1024,1024]{1,0:T(8,128)(2,1)} custom-call(s32[1]{0:T(128)} %bitcast.7.refs_0_, bf16[2048,256]{1,0:T(8,128)(2,1)} %collective-permute-done.21.refs_1_, bf16[2048,256]{1,0:T(8,128)(2,1)} %collective-permute-done.23.refs_2_, bf16[2048,256]{1,0:T(8,128)(2,1)} %copy-done.6, bf16[2048,256]{1,0:T(8,128)(2,1)} %copy-done.7), custom_call_target="tpu_custom_call" | custom-call | bytes 8388608 | tf_op jit(solution)/shard_map/flip/pallas_call | solution.py:331
  275.7 24.3 %contract.6.refs_19_ = f32[2,2,2048,2048]{3,2,1,0:T(8,128)} custom-call(bf16[2,1024,256]{2,1,0:T(8,128)(2,1)} %bitcast.50, bf16[2,1024,256]{2,1,0:T(8,128)(2,1)} %bitcast.60, bf16[2,1024,256]{2,1,0:T(8,128)(2,1)} %bitcast.58, bf16[2,1024,256]{2,1,0:T(8,128)(2,1)} %bitcast.19.refs_3_.refs_11_, ...), custom_call_target="tpu_custom_call", output_to_operand_aliasing={{}: (12, {})} | custom-call | flops 34359738368 | bytes 16777216 | tf_op jit(solution)/shard_map/contract/pallas_call | solution.py:434
  302.4 4.3 %collective-permute-start.41 = (bf16[256,1024]{1,0:T(8,128)(2,1)}, bf16[256,1024]{1,0:T(8,128)(2,1)S(1)}, u32[]{:S(2)}, u32[]{:S(2)}) collective-permute-start(bf16[256,1024]{1,0:T(8,128)(2,1)} %flip.12.refs_1_), channel_id=1, source_target_pairs={{0,16},{1,17},{10,26},{11,27},{20,4},{21,5},{30,14},{31,15}} | collective-permute-start | bytes 1572872 | tf_op jit(solution)/shard_map/ppermute | solution.py:532
  307.3 6.4 %collective-permute-done.41.refs_3_ = bf16[256,1024]{1,0:T(8,128)(2,1)S(1)} collective-permute-done((bf16[256,1024]{1,0:T(8,128)(2,1)}, bf16[256,1024]{1,0:T(8,128)(2,1)S(1)}, u32[]{:S(2)}, u32[]{:S(2)}) %collective-permute-start.41) | collective-permute-done | bytes 524320 | tf_op jit(solution)/shard_map/ppermute | solution.py:532
  320.7 4.2 %settle.11.refs_16_ = bf16[2,768,1024]{2,1,0:T(8,128)(2,1)} custom-call(s32[1]{0:T(128)} %bitcast.8.refs_0_, bf16[768,1024]{1,0:T(8,128)(2,1)} %flip.11.refs_1_, bf16[768,1024]{1,0:T(8,128)(2,1)} %collective-permute-done.34.refs_2_, bf16[768,1024]{1,0:T(8,128)(2,1)} %collective-permute-done.35.refs_3_, bf16[768,1024]{1,0:T(8,128)(2,1)} %collective-permute-done.36.refs_4_), custom_call_target="tpu_custom_call" | custom-call | bytes 6291456 | tf_op jit(solution)/shard_map/settle/pallas_call | solution.py:374
  326.2 4.8 %settle.12.refs_17_ = bf16[2,1024,1024]{2,1,0:T(8,128)(2,1)} custom-call(s32[1]{0:T(128)} %bitcast.8.refs_0_, bf16[1024,1024]{1,0:T(8,128)(2,1)} %flip.13.refs_1_, bf16[1024,1024]{1,0:T(8,128)(2,1)} %collective-permute-done.37.refs_2_, bf16[1024,1024]{1,0:T(8,128)(2,1)} %copy-done.13, bf16[1024,1024]{1,0:T(8,128)(2,1)} %copy-done.14), custom_call_target="tpu_custom_call" | custom-call | bytes 8388608 | tf_op jit(solution)/shard_map/settle/pallas_call | solution.py:374
  331.0 43.8 %contract.7 = f32[2,2,2048,2048]{3,2,1,0:T(8,128)} custom-call(bf16[2,1024,256]{2,1,0:T(8,128)(2,1)} %bitcast.34, bf16[2,1024,256]{2,1,0:T(8,128)(2,1)} %bitcast.46, bf16[2,1024,256]{2,1,0:T(8,128)(2,1)} %bitcast.49, bf16[2,1024,256]{2,1,0:T(8,128)(2,1)} %bitcast.11.refs_3_, bf16[2,1024,256]{2,1,0:T(8,128)(2,1)} %bitcast.12.refs_4_, ...), custom_call_target="tpu_custom_call", output_to_operand_aliasing={{}: (19, {})} | custom-call | flops 68719476736 | bytes 33554432 | tf_op jit(solution)/shard_map/contract/pallas_call | solution.py:434
  (157 shorter events, 99.6 us)
Async XLA Ops:
  76.3 25.4 %collective-permute-start.3 = (bf16[2048,256]{1,0:T(8,128)(2,1)}, bf16[2048,256]{1,0:T(8,128)(2,1)S(1)}, u32[]{:S(2)}, u32[]{:S(2)}) collective-permute-start(bf16[2048,256]{1,0:T(8,128)(2,1)} %assemble.2.refs_1_), channel_id=1, source_target_pairs={{0,2},{2,4},{4,6},{6,7},{7,5},{5,3},{3,1},{1,0},{8,10},{10,12},{12... | collective-permute-start | bytes 3145736 | tf_op jit(solution)/shard_map/ppermute | solution.py:510
  78.0 25.6 %collective-permute-start.4 = (bf16[2048,256]{1,0:T(8,128)(2,1)}, bf16[2048,256]{1,0:T(8,128)(2,1)S(1)}, u32[]{:S(2)}, u32[]{:S(2)}) collective-permute-start(bf16[2048,256]{1,0:T(8,128)(2,1)} %assemble.2.refs_1_), channel_id=1, source_target_pairs={{2,0},{4,2},{6,4},{7,6},{5,7},{3,5},{1,3},{0,1},{10,8},{12,10},{14... | collective-permute-start | bytes 3145736 | tf_op jit(solution)/shard_map/ppermute | solution.py:510
  101.7 24.6 %collective-permute-start.8 = (bf16[2048,256]{1,0:T(8,128)(2,1)S(1)}, bf16[2048,256]{1,0:T(8,128)(2,1)}, u32[]{:S(2)}, u32[]{:S(2)}) collective-permute-start(bf16[2048,256]{1,0:T(8,128)(2,1)S(1)} %collective-permute-done.3.refs_2_), channel_id=1, source_target_pairs={{0,2},{2,4},{4,6},{6,7},{7,5},{5,3},{3,1},{1,0},{8,10},{10,12},{12... | collective-permute-start | bytes 3145736 | tf_op jit(solution)/shard_map/ppermute | solution.py:510
  103.6 24.6 %collective-permute-start.10 = (bf16[2048,256]{1,0:T(8,128)(2,1)S(1)}, bf16[2048,256]{1,0:T(8,128)(2,1)}, u32[]{:S(2)}, u32[]{:S(2)}) collective-permute-start(bf16[2048,256]{1,0:T(8,128)(2,1)S(1)} %collective-permute-done.4.refs_3_), channel_id=1, source_target_pairs={{2,0},{4,2},{6,4},{7,6},{5,7},{3,5},{1,3},{0,1},{10,8},{12,10},{14... | collective-permute-start | bytes 3145736 | tf_op jit(solution)/shard_map/ppermute | solution.py:510
  126.4 24.7 %collective-permute-start.9 = (bf16[2048,256]{1,0:T(8,128)(2,1)}, bf16[2048,256]{1,0:T(8,128)(2,1)S(1)}, u32[]{:S(2)}, u32[]{:S(2)}) collective-permute-start(bf16[2048,256]{1,0:T(8,128)(2,1)} %collective-permute-done.8.refs_1_), channel_id=1, source_target_pairs={{0,2},{2,4},{4,6},{6,7},{7,5},{5,3},{3,1},{1,0},{8,10},{10,12},{12... | collective-permute-start | bytes 3145736 | tf_op jit(solution)/shard_map/ppermute | solution.py:510
  128.2 24.8 %collective-permute-start.12 = (bf16[2048,256]{1,0:T(8,128)(2,1)}, bf16[2048,256]{1,0:T(8,128)(2,1)S(1)}, u32[]{:S(2)}, u32[]{:S(2)}) collective-permute-start(bf16[2048,256]{1,0:T(8,128)(2,1)} %collective-permute-done.10.refs_2_), channel_id=1, source_target_pairs={{2,0},{4,2},{6,4},{7,6},{5,7},{3,5},{1,3},{0,1},{10,8},{12,10},{14... | collective-permute-start | bytes 3145736 | tf_op jit(solution)/shard_map/ppermute | solution.py:510
  128.4 45.5 %collective-permute-start.16 = (bf16[768,1024]{1,0:T(8,128)(2,1)}, bf16[768,1024]{1,0:T(8,128)(2,1)}, u32[]{:S(2)}, u32[]{:S(2)}) collective-permute-start(bf16[768,1024]{1,0:T(8,128)(2,1)} %flip.7.refs_1_), channel_id=1, source_target_pairs={{0,16},{1,17},{10,26},{11,27},{20,4},{21,5},{30,14},{31,15}} | collective-permute-start | bytes 4718600 | tf_op jit(solution)/shard_map/ppermute | solution.py:532
  133.1 42.2 %collective-permute-start.15 = (bf16[768,1024]{1,0:T(8,128)(2,1)}, bf16[768,1024]{1,0:T(8,128)(2,1)}, u32[]{:S(2)}, u32[]{:S(2)}) collective-permute-start(bf16[768,1024]{1,0:T(8,128)(2,1)} %flip.7.refs_1_), channel_id=1, source_target_pairs={{0,8},{8,0},{16,24},{24,16},{1,9},{9,1},{17,25},{25,17},{2,10},{10... | collective-permute-start | bytes 4718600 | tf_op jit(solution)/shard_map/ppermute | solution.py:526
  153.1 14.3 %collective-permute-start.13 = (bf16[1024,256]{1,0:T(8,128)(2,1)S(1)}, bf16[1024,256]{1,0:T(8,128)(2,1)S(1)}, u32[]{:S(2)}, u32[]{:S(2)}) collective-permute-start(bf16[1024,256]{1,0:T(8,128)(2,1)S(1)} %slice.31), channel_id=1, source_target_pairs={{2,0},{4,2},{6,4},{7,6},{5,7},{3,5},{1,3},{0,1},{10,8},{12,10},{14... | collective-permute-start | bytes 1572872 | tf_op jit(solution)/shard_map/ppermute | solution.py:510
  153.3 22.6 %collective-permute-start.19 = (bf16[512,1024]{1,0:T(8,128)(2,1)S(1)}, bf16[512,1024]{1,0:T(8,128)(2,1)}, u32[]{:S(2)}, u32[]{:S(2)}) collective-permute-start(bf16[512,1024]{1,0:T(8,128)(2,1)S(1)} %copy-done.12), channel_id=1, source_target_pairs={{0,16},{1,17},{10,26},{11,27},{20,4},{21,5},{30,14},{31,15}} | collective-permute-start | bytes 3145736 | tf_op jit(solution)/shard_map/ppermute | solution.py:532
  163.5 22.6 %collective-permute-start.25 = (bf16[512,1024]{1,0:T(8,128)(2,1)}, bf16[512,1024]{1,0:T(8,128)(2,1)S(1)}, u32[]{:S(2)}, u32[]{:S(2)}) collective-permute-start(bf16[512,1024]{1,0:T(8,128)(2,1)} %flip.9.refs_1_), channel_id=1, source_target_pairs={{0,16},{1,17},{10,26},{11,27},{20,4},{21,5},{30,14},{31,15}} | collective-permute-start | bytes 3145736 | tf_op jit(solution)/shard_map/ppermute | solution.py:532
  171.7 14.4 %collective-permute-start.28 = (bf16[256,1024]{1,0:T(8,128)(2,1)}, bf16[256,1024]{1,0:T(8,128)(2,1)}, u32[]{:S(2)}, u32[]{:S(2)}) collective-permute-start(bf16[256,1024]{1,0:T(8,128)(2,1)} %flip.10.refs_1_), channel_id=1, source_target_pairs={{0,16},{1,17},{10,26},{11,27},{20,4},{21,5},{30,14},{31,15}} | collective-permute-start | bytes 1572872 | tf_op jit(solution)/shard_map/ppermute | solution.py:532
  173.9 22.1 %collective-permute-start.22 = (bf16[2048,256]{1,0:T(8,128)(2,1)S(1)}, bf16[2048,256]{1,0:T(8,128)(2,1)S(1)}, u32[]{:S(2)}, u32[]{:S(2)}) collective-permute-start(bf16[2048,256]{1,0:T(8,128)(2,1)S(1)} %copy-done.5), channel_id=1, source_target_pairs={{2,0},{4,2},{6,4},{7,6},{5,7},{3,5},{1,3},{0,1},{10,8},{12,10},{14... | collective-permute-start | bytes 3145736 | tf_op jit(solution)/shard_map/ppermute | solution.py:510
  175.4 21.8 %collective-permute-start.14 = (bf16[2048,256]{1,0:T(8,128)(2,1)S(1)}, bf16[2048,256]{1,0:T(8,128)(2,1)S(1)}, u32[]{:S(2)}, u32[]{:S(2)}) collective-permute-start(bf16[2048,256]{1,0:T(8,128)(2,1)S(1)} %copy-done.5), channel_id=1, source_target_pairs={{0,2},{2,4},{4,6},{6,7},{7,5},{5,3},{3,1},{1,0},{8,10},{10,12},{12... | collective-permute-start | bytes 3145736 | tf_op jit(solution)/shard_map/ppermute | solution.py:510
  175.9 25.8 %collective-permute-start.17 = (bf16[768,1024]{1,0:T(8,128)(2,1)}, bf16[768,1024]{1,0:T(8,128)(2,1)}, u32[]{:S(2)}, u32[]{:S(2)}) collective-permute-start(bf16[768,1024]{1,0:T(8,128)(2,1)} %collective-permute-done.16.refs_3_), channel_id=1, source_target_pairs={{0,8},{8,0},{16,24},{24,16},{1,9},{9,1},{17,25},{25,17},{2,10},{10... | collective-permute-start | bytes 4718600 | tf_op jit(solution)/shard_map/ppermute | solution.py:526
  196.0 14.6 %collective-permute-start.24 = (bf16[512,1024]{1,0:T(8,128)(2,1)}, bf16[512,1024]{1,0:T(8,128)(2,1)}, u32[]{:S(2)}, u32[]{:S(2)}) collective-permute-start(bf16[512,1024]{1,0:T(8,128)(2,1)} %flip.9.refs_1_), channel_id=1, source_target_pairs={{0,8},{8,0},{16,24},{24,16},{1,9},{9,1},{17,25},{25,17},{2,10},{10... | collective-permute-start | bytes 3145736 | tf_op jit(solution)/shard_map/ppermute | solution.py:526
  205.9 26.3 %collective-permute-start.21 = (bf16[2048,256]{1,0:T(8,128)(2,1)S(1)}, bf16[2048,256]{1,0:T(8,128)(2,1)}, u32[]{:S(2)}, u32[]{:S(2)}) collective-permute-start(bf16[2048,256]{1,0:T(8,128)(2,1)S(1)} %collective-permute-done.14.refs_2_), channel_id=1, source_target_pairs={{0,2},{2,4},{4,6},{6,7},{7,5},{5,3},{3,1},{1,0},{8,10},{10,12},{12... | collective-permute-start | bytes 3145736 | tf_op jit(solution)/shard_map/ppermute | solution.py:510
  207.1 25.1 %collective-permute-start.23 = (bf16[2048,256]{1,0:T(8,128)(2,1)S(1)}, bf16[2048,256]{1,0:T(8,128)(2,1)}, u32[]{:S(2)}, u32[]{:S(2)}) collective-permute-start(bf16[2048,256]{1,0:T(8,128)(2,1)S(1)} %collective-permute-done.22.refs_3_), channel_id=1, source_target_pairs={{2,0},{4,2},{6,4},{7,6},{5,7},{3,5},{1,3},{0,1},{10,8},{12,10},{14... | collective-permute-start | bytes 3145736 | tf_op jit(solution)/shard_map/ppermute | solution.py:510
  232.2 24.3 %collective-permute-start.30 = (bf16[2048,256]{1,0:T(8,128)(2,1)}, bf16[2048,256]{1,0:T(8,128)(2,1)S(1)}, u32[]{:S(2)}, u32[]{:S(2)}) collective-permute-start(bf16[2048,256]{1,0:T(8,128)(2,1)} %collective-permute-done.21.refs_1_), channel_id=1, source_target_pairs={{0,2},{2,4},{4,6},{6,7},{7,5},{5,3},{3,1},{1,0},{8,10},{10,12},{12... | collective-permute-start | bytes 3145736 | tf_op jit(solution)/shard_map/ppermute | solution.py:510
  233.5 24.7 %collective-permute-start.32 = (bf16[2048,256]{1,0:T(8,128)(2,1)}, bf16[2048,256]{1,0:T(8,128)(2,1)S(1)}, u32[]{:S(2)}, u32[]{:S(2)}) collective-permute-start(bf16[2048,256]{1,0:T(8,128)(2,1)} %collective-permute-done.23.refs_2_), channel_id=1, source_target_pairs={{2,0},{4,2},{6,4},{7,6},{5,7},{3,5},{1,3},{0,1},{10,8},{12,10},{14... | collective-permute-start | bytes 3145736 | tf_op jit(solution)/shard_map/ppermute | solution.py:510
  259.5 47.2 %collective-permute-start.35 = (bf16[768,1024]{1,0:T(8,128)(2,1)S(1)}, bf16[768,1024]{1,0:T(8,128)(2,1)}, u32[]{:S(2)}, u32[]{:S(2)}) collective-permute-start(bf16[768,1024]{1,0:T(8,128)(2,1)S(1)} %copy-done.9), channel_id=1, source_target_pairs={{0,16},{1,17},{10,26},{11,27},{20,4},{21,5},{30,14},{31,15}} | collective-permute-start | bytes 4718600 | tf_op jit(solution)/shard_map/ppermute | solution.py:532
  267.3 35.1 %collective-permute-start.38 = (bf16[1024,1024]{1,0:T(8,128)(2,1)}, bf16[1024,1024]{1,0:T(8,128)(2,1)S(1)}, u32[]{:S(2)}, u32[]{:S(2)}) collective-permute-start(bf16[1024,1024]{1,0:T(8,128)(2,1)} %flip.13.refs_1_), channel_id=1, source_target_pairs={{0,16},{1,17},{10,26},{11,27},{20,4},{21,5},{30,14},{31,15}} | collective-permute-start | bytes 6291464 | tf_op jit(solution)/shard_map/ppermute | solution.py:532
  268.7 56.1 %collective-permute-start.37 = (bf16[1024,1024]{1,0:T(8,128)(2,1)}, bf16[1024,1024]{1,0:T(8,128)(2,1)}, u32[]{:S(2)}, u32[]{:S(2)}) collective-permute-start(bf16[1024,1024]{1,0:T(8,128)(2,1)} %flip.13.refs_1_), channel_id=1, source_target_pairs={{0,8},{8,0},{16,24},{24,16},{1,9},{9,1},{17,25},{25,17},{2,10},{10... | collective-permute-start | bytes 6291464 | tf_op jit(solution)/shard_map/ppermute | solution.py:526
  302.4 22.5 %collective-permute-start.39 = (bf16[1024,1024]{1,0:T(8,128)(2,1)S(1)}, bf16[1024,1024]{1,0:T(8,128)(2,1)S(1)}, u32[]{:S(2)}, u32[]{:S(2)}) collective-permute-start(bf16[1024,1024]{1,0:T(8,128)(2,1)S(1)} %collective-permute-done.38.refs_3_), channel_id=1, source_target_pairs={{0,8},{8,0},{16,24},{24,16},{1,9},{9,1},{17,25},{25,17},{2,10},{10... | collective-permute-start | bytes 6291464 | tf_op jit(solution)/shard_map/ppermute | solution.py:526
  (44 other events, 382.4 us)

commit v10 on v9

--- a/solution.py
+++ b/solution.py
@@ -572,8 +572,9 @@
     both[1][0] = after(both[1][0], flipped)
     result = contract(second, both[1:], rights, unit, share, share, 0, 1, 0)
     copies.append(column(sum(two[2:half], []), two[half - 1] + [second], (result,)))
-    copies.append(column(two[half], (), (result,), flipped))
     rights = [settle(which, some, pairs) for some in copies]
+    copies.append(column(two[half], (), (result, *rights), flipped))
+    rights.append(settle(which, copies[-1], pairs))
     result = contract(result, both, rights, unit, 0, share, 0, 1, 1)
     return result.reshape(2, parts * block, block)
 

time: 376 us -> 374 us (level)
  waiting for transfers between devices: 94.3 us -> 89.1 us
    ppermute x7, waiting for transfers between devices: 19.1 us -> 12.8 us  [column(): copies.append(lax.ppermute(held, ('row', 'col'), perm))]
    unnamed x54 -> x56, local copies, waits for them, and re-layouts: 7.68 us -> 8.99 us
  transfers between devices with their start and end apart: 43 -> 43, of which waited for: 19 -> 18; matrix products, arithmetic and copies ran while one was open for 0% -> 0% of each run, Pallas kernels for 31% -> 32%
where the time goes in v10:
time: 374 us; the launch traced here: 372 us
  Pallas kernels  218 us (58%)
  waiting for transfers between devices  89.1 us (24%)
  starting transfers between devices  48.8 us (13%)
  local copies, waits for them, and re-layouts  11.5 us (3%)
  other arithmetic  4.22 us (1%)
    pallas_call x4, Pallas kernels, contract(): pl.pallas_call(lambda *refs: contract_kernel(slot_count, shares, len(righ...  95.5 us
    pallas_call x1, Pallas kernels, transform(): pl.pallas_call(lambda *refs: transform_kernel(pairs, load_steps, step_row...  51 us
    ppermute x8, waiting for transfers between devices, go_round(): lax.ppermute(below, 'col', ring_up)  30.5 us
    pallas_call x7, Pallas kernels, flip(): pl.pallas_call(lambda *refs: flip_kernel(slot_count, *refs), grid_spec=pl...  26.2 us
    ppermute x7, starting transfers between devices, column(): copies.append(lax.ppermute(held, ('row', 'col'), perm))  25.3 us
    pallas_call x7, Pallas kernels, settle(): pl.pallas_call(lambda *refs: settle_kernel(pairs, row_count, *refs), grid...  24.7 us
    ppermute x6, waiting for transfers between devices, across_rows(): lax.ppermute(parcels[s], 'row', [(r, r ^ s) for r in range(rows)])  24.7 us
    ppermute x8, waiting for transfers between devices, go_round(): lax.ppermute(above, 'col', ring_down)  16.3 us
  transfers between devices with their start and end apart: 43, of which 18 were waited for; matrix products, arithmetic and copies ran while one was open for 0% of the time, Pallas kernels for 32%

profile of v10, /device:TPU:0, one launch (start us, length us, event | category | flops | bytes accessed | tf_op | source)
XLA Modules:
  0.0 372.4 jit_solution(2198984231375029058)
XLA Ops:
  6.3 51.0 %transform.1 = (bf16[1024,128]{1,0:T(8,128)(2,1)}, bf16[1024,128]{1,0:T(8,128)(2,1)}, bf16[1024,128]{1,0:T(8,128)(2,1)}, bf16[1024,128]{1,0:T(8,128)(2,1)}, f32[32768,128]{1,0:T(8,128)}) custom-call(s32[8192]{0:T(1024)} %bitcast.65, s32[1]{0:T(128)} %bitcast.refs_1_.refs_0_, bf16[64,256]{1,0:T(8,128)(2,1)} %fusion.16.refs_2_, ...), custom_call_target="tpu_custom_call" | custom-call | flops 9663676416 | bytes 40000000 | tf_op jit(solution)/shard_map/transform/pallas_call | solution.py:233
  60.5 7.3 %collective-permute-done.1.refs_3_ = bf16[1024,128]{1,0:T(8,128)(2,1)S(1)} collective-permute-done((bf16[1024,128]{1,0:T(8,128)(2,1)}, bf16[1024,128]{1,0:T(8,128)(2,1)S(1)}, u32[]{:S(2)}, u32[]{:S(2)}) %collective-permute-start.1) | collective-permute-done | bytes 262176 | tf_op jit(solution)/shard_map/ppermute | solution.py:505
  67.8 5.1 %collective-permute-done.2.refs_4_ = bf16[1024,128]{1,0:T(8,128)(2,1)S(1)} collective-permute-done((bf16[1024,128]{1,0:T(8,128)(2,1)}, bf16[1024,128]{1,0:T(8,128)(2,1)S(1)}, u32[]{:S(2)}, u32[]{:S(2)}) %collective-permute-start.2) | collective-permute-done | bytes 262176 | tf_op jit(solution)/shard_map/ppermute | solution.py:505
  78.9 15.6 %select.45 = (bf16[1024,128]{1,0:T(8,128)(2,1)}, bf16[1024,128]{1,0:T(8,128)(2,1)}, bf16[1024,128]{1,0:T(8,128)(2,1)}, bf16[1024,128]{1,0:T(8,128)(2,1)}) custom-call(s32[8192]{0:T(1024)} %bitcast.62, s32[1]{0:T(128)} %bitcast.refs_1_.refs_0_, f32[32768,128]{1,0:T(8,128)} %get-tuple-element.45.refs_2_), custom_call_target="tpu_custom_call" | custom-call | bytes 50000000 | tf_op jit(solution)/shard_map/select/pallas_call | solution.py:113
  94.6 7.1 %collective-permute-done.3.refs_2_ = bf16[2048,256]{1,0:T(8,128)(2,1)S(1)} collective-permute-done((bf16[2048,256]{1,0:T(8,128)(2,1)}, bf16[2048,256]{1,0:T(8,128)(2,1)S(1)}, u32[]{:S(2)}, u32[]{:S(2)}) %collective-permute-start.3) | collective-permute-done | bytes 1048608 | tf_op jit(solution)/shard_map/ppermute | solution.py:510
  105.6 7.4 %collective-permute-done.6.refs_3_ = bf16[1024,128]{1,0:T(8,128)(2,1)S(1)} collective-permute-done((bf16[1024,128]{1,0:T(8,128)(2,1)}, bf16[1024,128]{1,0:T(8,128)(2,1)S(1)}, u32[]{:S(2)}, u32[]{:S(2)}) %collective-permute-start.6) | collective-permute-done | bytes 262176 | tf_op jit(solution)/shard_map/ppermute | solution.py:505
  113.1 4.8 %collective-permute-done.7.refs_4_ = bf16[1024,128]{1,0:T(8,128)(2,1)S(1)} collective-permute-done((bf16[1024,128]{1,0:T(8,128)(2,1)}, bf16[1024,128]{1,0:T(8,128)(2,1)S(1)}, u32[]{:S(2)}, u32[]{:S(2)}) %collective-permute-start.7) | collective-permute-done | bytes 262176 | tf_op jit(solution)/shard_map/ppermute | solution.py:505
  128.4 4.8 %collective-permute-start.16 = (bf16[768,1024]{1,0:T(8,128)(2,1)}, bf16[768,1024]{1,0:T(8,128)(2,1)}, u32[]{:S(2)}, u32[]{:S(2)}) collective-permute-start(bf16[768,1024]{1,0:T(8,128)(2,1)} %flip.7.refs_1_), channel_id=1, source_target_pairs={{0,16},{1,17},{10,26},{11,27},{20,4},{21,5},{30,14},{31,15}} | collective-permute-start | bytes 4718600 | tf_op jit(solution)/shard_map/ppermute | solution.py:532
  136.9 14.1 %collective-permute-done.9.refs_1_ = bf16[2048,256]{1,0:T(8,128)(2,1)S(1)} collective-permute-done((bf16[2048,256]{1,0:T(8,128)(2,1)}, bf16[2048,256]{1,0:T(8,128)(2,1)S(1)}, u32[]{:S(2)}, u32[]{:S(2)}) %collective-permute-start.9) | collective-permute-done | bytes 1048608 | tf_op jit(solution)/shard_map/ppermute | solution.py:510
  153.3 4.6 %collective-permute-start.19 = (bf16[512,1024]{1,0:T(8,128)(2,1)S(1)}, bf16[512,1024]{1,0:T(8,128)(2,1)}, u32[]{:S(2)}, u32[]{:S(2)}) collective-permute-start(bf16[512,1024]{1,0:T(8,128)(2,1)S(1)} %copy-done.12), channel_id=1, source_target_pairs={{0,16},{1,17},{10,26},{11,27},{20,4},{21,5},{30,14},{31,15}} | collective-permute-start | bytes 3145736 | tf_op jit(solution)/shard_map/ppermute | solution.py:532
  175.8 10.3 %collective-permute-done.28.refs_3_ = bf16[256,1024]{1,0:T(8,128)(2,1)} collective-permute-done((bf16[256,1024]{1,0:T(8,128)(2,1)}, bf16[256,1024]{1,0:T(8,128)(2,1)}, u32[]{:S(2)}, u32[]{:S(2)}) %collective-permute-start.28) | collective-permute-done | bytes 524320 | tf_op jit(solution)/shard_map/ppermute | solution.py:532
  186.7 9.3 %collective-permute-done.22.refs_3_ = bf16[2048,256]{1,0:T(8,128)(2,1)S(1)} collective-permute-done((bf16[2048,256]{1,0:T(8,128)(2,1)S(1)}, bf16[2048,256]{1,0:T(8,128)(2,1)S(1)}, u32[]{:S(2)}, u32[]{:S(2)}) %collective-permute-start.22) | collective-permute-done | bytes 1048608 | tf_op jit(solution)/shard_map/ppermute | solution.py:510
  201.7 4.2 %settle.7.refs_8_ = bf16[2,768,1024]{2,1,0:T(8,128)(2,1)} custom-call(s32[1]{0:T(128)} %bitcast.8.refs_0_, bf16[768,1024]{1,0:T(8,128)(2,1)} %flip.7.refs_1_, bf16[768,1024]{1,0:T(8,128)(2,1)} %collective-permute-done.15.refs_2_, bf16[768,1024]{1,0:T(8,128)(2,1)} %collective-permute-done.16.refs_3_, bf16[768,1024]{1,0:T(8,128)(2,1)} %collective-permute-done.17.refs_4_), custom_call_target="tpu_custom_call" | custom-call | bytes 6291456 | tf_op jit(solution)/shard_map/settle/pallas_call | solution.py:374
  213.6 13.7 %contract.4.refs_12_ = f32[2,2,2048,2048]{3,2,1,0:T(8,128)} custom-call(bf16[2,1024,256]{2,1,0:T(8,128)(2,1)} %bitcast.32, bf16[2,1024,256]{2,1,0:T(8,128)(2,1)} %bitcast.44, bf16[2,1024,256]{2,1,0:T(8,128)(2,1)} %bitcast.47, bf16[2,1024,256]{2,1,0:T(8,128)(2,1)} %bitcast.11.refs_3_, bf16[2,1024,256]{2,1,0:T(8,128)(2,1)} %bitcast.12.refs_4_, ...), custom_call_target="tpu_custom_call" | custom-call | flops 17179869184 | bytes 8388608 | tf_op jit(solution)/shard_map/contract/pallas_call | solution.py:434
  227.3 4.8 %collective-permute-done.23.refs_2_ = bf16[2048,256]{1,0:T(8,128)(2,1)} collective-permute-done((bf16[2048,256]{1,0:T(8,128)(2,1)S(1)}, bf16[2048,256]{1,0:T(8,128)(2,1)}, u32[]{:S(2)}, u32[]{:S(2)}) %collective-permute-start.23) | collective-permute-done | bytes 1048608 | tf_op jit(solution)/shard_map/ppermute | solution.py:510
  234.1 4.0 %flip.11.refs_1_ = bf16[768,1024]{1,0:T(8,128)(2,1)} custom-call(s32[1]{0:T(128)} %bitcast.7.refs_0_, bf16[2048,256]{1,0:T(8,128)(2,1)} %assemble.3.refs_1_, bf16[2048,256]{1,0:T(8,128)(2,1)} %copy-done.11, bf16[2048,256]{1,0:T(8,128)(2,1)} %copy-done.10), custom_call_target="tpu_custom_call" | custom-call | bytes 6291456 | tf_op jit(solution)/shard_map/flip/pallas_call | solution.py:331
  238.1 13.7 %contract.5.refs_12_ = f32[2,2,2048,2048]{3,2,1,0:T(8,128)} custom-call(bf16[2,1024,256]{2,1,0:T(8,128)(2,1)} %bitcast.33, bf16[2,1024,256]{2,1,0:T(8,128)(2,1)} %bitcast.45, bf16[2,1024,256]{2,1,0:T(8,128)(2,1)} %bitcast.48, bf16[2,1024,256]{2,1,0:T(8,128)(2,1)} %bitcast.11.refs_3_, ...), custom_call_target="tpu_custom_call", output_to_operand_aliasing={{}: (12, {})} | custom-call | flops 17179869184 | bytes 8388608 | tf_op jit(solution)/shard_map/contract/pallas_call | solution.py:434
  251.9 4.6 %collective-permute-done.30.refs_3_ = bf16[2048,256]{1,0:T(8,128)(2,1)S(1)} collective-permute-done((bf16[2048,256]{1,0:T(8,128)(2,1)}, bf16[2048,256]{1,0:T(8,128)(2,1)S(1)}, u32[]{:S(2)}, u32[]{:S(2)}) %collective-permute-start.30) | collective-permute-done | bytes 1048608 | tf_op jit(solution)/shard_map/ppermute | solution.py:510
  263.0 4.3 %flip.13.refs_1_ = bf16[1024,1024]{1,0:T(8,128)(2,1)} custom-call(s32[1]{0:T(128)} %bitcast.7.refs_0_, bf16[2048,256]{1,0:T(8,128)(2,1)} %collective-permute-done.21.refs_1_, bf16[2048,256]{1,0:T(8,128)(2,1)} %collective-permute-done.23.refs_2_, bf16[2048,256]{1,0:T(8,128)(2,1)} %copy-done.6, bf16[2048,256]{1,0:T(8,128)(2,1)} %copy-done.7), custom_call_target="tpu_custom_call" | custom-call | bytes 8388608 | tf_op jit(solution)/shard_map/flip/pallas_call | solution.py:331
  275.6 24.3 %contract.6.refs_19_ = f32[2,2,2048,2048]{3,2,1,0:T(8,128)} custom-call(bf16[2,1024,256]{2,1,0:T(8,128)(2,1)} %bitcast.50, bf16[2,1024,256]{2,1,0:T(8,128)(2,1)} %bitcast.60, bf16[2,1024,256]{2,1,0:T(8,128)(2,1)} %bitcast.58, bf16[2,1024,256]{2,1,0:T(8,128)(2,1)} %bitcast.19.refs_3_.refs_11_, ...), custom_call_target="tpu_custom_call", output_to_operand_aliasing={{}: (12, {})} | custom-call | flops 34359738368 | bytes 16777216 | tf_op jit(solution)/shard_map/contract/pallas_call | solution.py:434
  302.8 5.1 %collective-permute-start.41 = (bf16[256,1024]{1,0:T(8,128)(2,1)}, bf16[256,1024]{1,0:T(8,128)(2,1)}, u32[]{:S(2)}, u32[]{:S(2)}) collective-permute-start(bf16[256,1024]{1,0:T(8,128)(2,1)} %flip.12.refs_1_), channel_id=1, source_target_pairs={{0,16},{1,17},{10,26},{11,27},{20,4},{21,5},{30,14},{31,15}} | collective-permute-start | bytes 1572872 | tf_op jit(solution)/shard_map/ppermute | solution.py:532
  312.3 4.2 %settle.11.refs_16_ = bf16[2,768,1024]{2,1,0:T(8,128)(2,1)} custom-call(s32[1]{0:T(128)} %bitcast.8.refs_0_, bf16[768,1024]{1,0:T(8,128)(2,1)} %flip.11.refs_1_, bf16[768,1024]{1,0:T(8,128)(2,1)} %copy-done.15, bf16[768,1024]{1,0:T(8,128)(2,1)} %collective-permute-done.35.refs_3_, bf16[768,1024]{1,0:T(8,128)(2,1)} %collective-permute-done.36.refs_4_), custom_call_target="tpu_custom_call" | custom-call | bytes 6291456 | tf_op jit(solution)/shard_map/settle/pallas_call | solution.py:374
  317.8 4.8 %settle.12.refs_17_ = bf16[2,1024,1024]{2,1,0:T(8,128)(2,1)} custom-call(s32[1]{0:T(128)} %bitcast.8.refs_0_, bf16[1024,1024]{1,0:T(8,128)(2,1)} %flip.13.refs_1_, bf16[1024,1024]{1,0:T(8,128)(2,1)} %collective-permute-done.37.refs_2_, bf16[1024,1024]{1,0:T(8,128)(2,1)} %copy-done.13, bf16[1024,1024]{1,0:T(8,128)(2,1)} %copy-done.14), custom_call_target="tpu_custom_call" | custom-call | bytes 8388608 | tf_op jit(solution)/shard_map/settle/pallas_call | solution.py:374
  328.4 43.8 %contract.7 = f32[2,2,2048,2048]{3,2,1,0:T(8,128)} custom-call(bf16[2,1024,256]{2,1,0:T(8,128)(2,1)} %bitcast.34, bf16[2,1024,256]{2,1,0:T(8,128)(2,1)} %bitcast.46, bf16[2,1024,256]{2,1,0:T(8,128)(2,1)} %bitcast.49, bf16[2,1024,256]{2,1,0:T(8,128)(2,1)} %bitcast.11.refs_3_, bf16[2,1024,256]{2,1,0:T(8,128)(2,1)} %bitcast.12.refs_4_, ...), custom_call_target="tpu_custom_call", output_to_operand_aliasing={{}: (19, {})} | custom-call | flops 68719476736 | bytes 33554432 | tf_op jit(solution)/shard_map/contract/pallas_call | solution.py:434
  (159 shorter events, 98.9 us)
Async XLA Ops:
  76.3 25.4 %collective-permute-start.3 = (bf16[2048,256]{1,0:T(8,128)(2,1)}, bf16[2048,256]{1,0:T(8,128)(2,1)S(1)}, u32[]{:S(2)}, u32[]{:S(2)}) collective-permute-start(bf16[2048,256]{1,0:T(8,128)(2,1)} %assemble.2.refs_1_), channel_id=1, source_target_pairs={{0,2},{2,4},{4,6},{6,7},{7,5},{5,3},{3,1},{1,0},{8,10},{10,12},{12... | collective-permute-start | bytes 3145736 | tf_op jit(solution)/shard_map/ppermute | solution.py:510
  78.0 25.6 %collective-permute-start.4 = (bf16[2048,256]{1,0:T(8,128)(2,1)}, bf16[2048,256]{1,0:T(8,128)(2,1)S(1)}, u32[]{:S(2)}, u32[]{:S(2)}) collective-permute-start(bf16[2048,256]{1,0:T(8,128)(2,1)} %assemble.2.refs_1_), channel_id=1, source_target_pairs={{2,0},{4,2},{6,4},{7,6},{5,7},{3,5},{1,3},{0,1},{10,8},{12,10},{14... | collective-permute-start | bytes 3145736 | tf_op jit(solution)/shard_map/ppermute | solution.py:510
  101.7 24.6 %collective-permute-start.8 = (bf16[2048,256]{1,0:T(8,128)(2,1)S(1)}, bf16[2048,256]{1,0:T(8,128)(2,1)}, u32[]{:S(2)}, u32[]{:S(2)}) collective-permute-start(bf16[2048,256]{1,0:T(8,128)(2,1)S(1)} %collective-permute-done.3.refs_2_), channel_id=1, source_target_pairs={{0,2},{2,4},{4,6},{6,7},{7,5},{5,3},{3,1},{1,0},{8,10},{10,12},{12... | collective-permute-start | bytes 3145736 | tf_op jit(solution)/shard_map/ppermute | solution.py:510
  103.5 24.6 %collective-permute-start.10 = (bf16[2048,256]{1,0:T(8,128)(2,1)S(1)}, bf16[2048,256]{1,0:T(8,128)(2,1)}, u32[]{:S(2)}, u32[]{:S(2)}) collective-permute-start(bf16[2048,256]{1,0:T(8,128)(2,1)S(1)} %collective-permute-done.4.refs_3_), channel_id=1, source_target_pairs={{2,0},{4,2},{6,4},{7,6},{5,7},{3,5},{1,3},{0,1},{10,8},{12,10},{14... | collective-permute-start | bytes 3145736 | tf_op jit(solution)/shard_map/ppermute | solution.py:510
  126.3 24.7 %collective-permute-start.9 = (bf16[2048,256]{1,0:T(8,128)(2,1)}, bf16[2048,256]{1,0:T(8,128)(2,1)S(1)}, u32[]{:S(2)}, u32[]{:S(2)}) collective-permute-start(bf16[2048,256]{1,0:T(8,128)(2,1)} %collective-permute-done.8.refs_1_), channel_id=1, source_target_pairs={{0,2},{2,4},{4,6},{6,7},{7,5},{5,3},{3,1},{1,0},{8,10},{10,12},{12... | collective-permute-start | bytes 3145736 | tf_op jit(solution)/shard_map/ppermute | solution.py:510
  128.2 24.8 %collective-permute-start.12 = (bf16[2048,256]{1,0:T(8,128)(2,1)}, bf16[2048,256]{1,0:T(8,128)(2,1)S(1)}, u32[]{:S(2)}, u32[]{:S(2)}) collective-permute-start(bf16[2048,256]{1,0:T(8,128)(2,1)} %collective-permute-done.10.refs_2_), channel_id=1, source_target_pairs={{2,0},{4,2},{6,4},{7,6},{5,7},{3,5},{1,3},{0,1},{10,8},{12,10},{14... | collective-permute-start | bytes 3145736 | tf_op jit(solution)/shard_map/ppermute | solution.py:510
  128.4 45.4 %collective-permute-start.16 = (bf16[768,1024]{1,0:T(8,128)(2,1)}, bf16[768,1024]{1,0:T(8,128)(2,1)}, u32[]{:S(2)}, u32[]{:S(2)}) collective-permute-start(bf16[768,1024]{1,0:T(8,128)(2,1)} %flip.7.refs_1_), channel_id=1, source_target_pairs={{0,16},{1,17},{10,26},{11,27},{20,4},{21,5},{30,14},{31,15}} | collective-permute-start | bytes 4718600 | tf_op jit(solution)/shard_map/ppermute | solution.py:532
  133.2 42.1 %collective-permute-start.15 = (bf16[768,1024]{1,0:T(8,128)(2,1)}, bf16[768,1024]{1,0:T(8,128)(2,1)}, u32[]{:S(2)}, u32[]{:S(2)}) collective-permute-start(bf16[768,1024]{1,0:T(8,128)(2,1)} %flip.7.refs_1_), channel_id=1, source_target_pairs={{0,8},{8,0},{16,24},{24,16},{1,9},{9,1},{17,25},{25,17},{2,10},{10... | collective-permute-start | bytes 4718600 | tf_op jit(solution)/shard_map/ppermute | solution.py:526
  153.1 14.3 %collective-permute-start.13 = (bf16[1024,256]{1,0:T(8,128)(2,1)S(1)}, bf16[1024,256]{1,0:T(8,128)(2,1)S(1)}, u32[]{:S(2)}, u32[]{:S(2)}) collective-permute-start(bf16[1024,256]{1,0:T(8,128)(2,1)S(1)} %slice.31), channel_id=1, source_target_pairs={{2,0},{4,2},{6,4},{7,6},{5,7},{3,5},{1,3},{0,1},{10,8},{12,10},{14... | collective-permute-start | bytes 1572872 | tf_op jit(solution)/shard_map/ppermute | solution.py:510
  153.3 22.5 %collective-permute-start.19 = (bf16[512,1024]{1,0:T(8,128)(2,1)S(1)}, bf16[512,1024]{1,0:T(8,128)(2,1)}, u32[]{:S(2)}, u32[]{:S(2)}) collective-permute-start(bf16[512,1024]{1,0:T(8,128)(2,1)S(1)} %copy-done.12), channel_id=1, source_target_pairs={{0,16},{1,17},{10,26},{11,27},{20,4},{21,5},{30,14},{31,15}} | collective-permute-start | bytes 3145736 | tf_op jit(solution)/shard_map/ppermute | solution.py:532
  163.6 22.6 %collective-permute-start.25 = (bf16[512,1024]{1,0:T(8,128)(2,1)}, bf16[512,1024]{1,0:T(8,128)(2,1)S(1)}, u32[]{:S(2)}, u32[]{:S(2)}) collective-permute-start(bf16[512,1024]{1,0:T(8,128)(2,1)} %flip.9.refs_1_), channel_id=1, source_target_pairs={{0,16},{1,17},{10,26},{11,27},{20,4},{21,5},{30,14},{31,15}} | collective-permute-start | bytes 3145736 | tf_op jit(solution)/shard_map/ppermute | solution.py:532
  171.7 14.5 %collective-permute-start.28 = (bf16[256,1024]{1,0:T(8,128)(2,1)}, bf16[256,1024]{1,0:T(8,128)(2,1)}, u32[]{:S(2)}, u32[]{:S(2)}) collective-permute-start(bf16[256,1024]{1,0:T(8,128)(2,1)} %flip.10.refs_1_), channel_id=1, source_target_pairs={{0,16},{1,17},{10,26},{11,27},{20,4},{21,5},{30,14},{31,15}} | collective-permute-start | bytes 1572872 | tf_op jit(solution)/shard_map/ppermute | solution.py:532
  173.8 22.1 %collective-permute-start.22 = (bf16[2048,256]{1,0:T(8,128)(2,1)S(1)}, bf16[2048,256]{1,0:T(8,128)(2,1)S(1)}, u32[]{:S(2)}, u32[]{:S(2)}) collective-permute-start(bf16[2048,256]{1,0:T(8,128)(2,1)S(1)} %copy-done.5), channel_id=1, source_target_pairs={{2,0},{4,2},{6,4},{7,6},{5,7},{3,5},{1,3},{0,1},{10,8},{12,10},{14... | collective-permute-start | bytes 3145736 | tf_op jit(solution)/shard_map/ppermute | solution.py:510
  175.3 21.9 %collective-permute-start.14 = (bf16[2048,256]{1,0:T(8,128)(2,1)S(1)}, bf16[2048,256]{1,0:T(8,128)(2,1)S(1)}, u32[]{:S(2)}, u32[]{:S(2)}) collective-permute-start(bf16[2048,256]{1,0:T(8,128)(2,1)S(1)} %copy-done.5), channel_id=1, source_target_pairs={{0,2},{2,4},{4,6},{6,7},{7,5},{5,3},{3,1},{1,0},{8,10},{10,12},{12... | collective-permute-start | bytes 3145736 | tf_op jit(solution)/shard_map/ppermute | solution.py:510
  175.8 25.9 %collective-permute-start.17 = (bf16[768,1024]{1,0:T(8,128)(2,1)}, bf16[768,1024]{1,0:T(8,128)(2,1)}, u32[]{:S(2)}, u32[]{:S(2)}) collective-permute-start(bf16[768,1024]{1,0:T(8,128)(2,1)} %collective-permute-done.16.refs_3_), channel_id=1, source_target_pairs={{0,8},{8,0},{16,24},{24,16},{1,9},{9,1},{17,25},{25,17},{2,10},{10... | collective-permute-start | bytes 4718600 | tf_op jit(solution)/shard_map/ppermute | solution.py:526
  195.9 14.6 %collective-permute-start.24 = (bf16[512,1024]{1,0:T(8,128)(2,1)}, bf16[512,1024]{1,0:T(8,128)(2,1)}, u32[]{:S(2)}, u32[]{:S(2)}) collective-permute-start(bf16[512,1024]{1,0:T(8,128)(2,1)} %flip.9.refs_1_), channel_id=1, source_target_pairs={{0,8},{8,0},{16,24},{24,16},{1,9},{9,1},{17,25},{25,17},{2,10},{10... | collective-permute-start | bytes 3145736 | tf_op jit(solution)/shard_map/ppermute | solution.py:526
  205.9 26.2 %collective-permute-start.21 = (bf16[2048,256]{1,0:T(8,128)(2,1)S(1)}, bf16[2048,256]{1,0:T(8,128)(2,1)}, u32[]{:S(2)}, u32[]{:S(2)}) collective-permute-start(bf16[2048,256]{1,0:T(8,128)(2,1)S(1)} %collective-permute-done.14.refs_2_), channel_id=1, source_target_pairs={{0,2},{2,4},{4,6},{6,7},{7,5},{5,3},{3,1},{1,0},{8,10},{10,12},{12... | collective-permute-start | bytes 3145736 | tf_op jit(solution)/shard_map/ppermute | solution.py:510
  207.0 25.1 %collective-permute-start.23 = (bf16[2048,256]{1,0:T(8,128)(2,1)S(1)}, bf16[2048,256]{1,0:T(8,128)(2,1)}, u32[]{:S(2)}, u32[]{:S(2)}) collective-permute-start(bf16[2048,256]{1,0:T(8,128)(2,1)S(1)} %collective-permute-done.22.refs_3_), channel_id=1, source_target_pairs={{2,0},{4,2},{6,4},{7,6},{5,7},{3,5},{1,3},{0,1},{10,8},{12,10},{14... | collective-permute-start | bytes 3145736 | tf_op jit(solution)/shard_map/ppermute | solution.py:510
  232.1 24.4 %collective-permute-start.30 = (bf16[2048,256]{1,0:T(8,128)(2,1)}, bf16[2048,256]{1,0:T(8,128)(2,1)S(1)}, u32[]{:S(2)}, u32[]{:S(2)}) collective-permute-start(bf16[2048,256]{1,0:T(8,128)(2,1)} %collective-permute-done.21.refs_1_), channel_id=1, source_target_pairs={{0,2},{2,4},{4,6},{6,7},{7,5},{5,3},{3,1},{1,0},{8,10},{10,12},{12... | collective-permute-start | bytes 3145736 | tf_op jit(solution)/shard_map/ppermute | solution.py:510
  233.5 24.7 %collective-permute-start.32 = (bf16[2048,256]{1,0:T(8,128)(2,1)}, bf16[2048,256]{1,0:T(8,128)(2,1)S(1)}, u32[]{:S(2)}, u32[]{:S(2)}) collective-permute-start(bf16[2048,256]{1,0:T(8,128)(2,1)} %collective-permute-done.23.refs_2_), channel_id=1, source_target_pairs={{2,0},{4,2},{6,4},{7,6},{5,7},{3,5},{1,3},{0,1},{10,8},{12,10},{14... | collective-permute-start | bytes 3145736 | tf_op jit(solution)/shard_map/ppermute | solution.py:510
  259.5 43.3 %collective-permute-start.35 = (bf16[768,1024]{1,0:T(8,128)(2,1)S(1)}, bf16[768,1024]{1,0:T(8,128)(2,1)}, u32[]{:S(2)}, u32[]{:S(2)}) collective-permute-start(bf16[768,1024]{1,0:T(8,128)(2,1)S(1)} %copy-done.9), channel_id=1, source_target_pairs={{0,16},{1,17},{10,26},{11,27},{20,4},{21,5},{30,14},{31,15}} | collective-permute-start | bytes 4718600 | tf_op jit(solution)/shard_map/ppermute | solution.py:532
  267.3 35.1 %collective-permute-start.38 = (bf16[1024,1024]{1,0:T(8,128)(2,1)}, bf16[1024,1024]{1,0:T(8,128)(2,1)S(1)}, u32[]{:S(2)}, u32[]{:S(2)}) collective-permute-start(bf16[1024,1024]{1,0:T(8,128)(2,1)} %flip.13.refs_1_), channel_id=1, source_target_pairs={{0,16},{1,17},{10,26},{11,27},{20,4},{21,5},{30,14},{31,15}} | collective-permute-start | bytes 6291464 | tf_op jit(solution)/shard_map/ppermute | solution.py:532
  268.7 47.8 %collective-permute-start.37 = (bf16[1024,1024]{1,0:T(8,128)(2,1)}, bf16[1024,1024]{1,0:T(8,128)(2,1)}, u32[]{:S(2)}, u32[]{:S(2)}) collective-permute-start(bf16[1024,1024]{1,0:T(8,128)(2,1)} %flip.13.refs_1_), channel_id=1, source_target_pairs={{0,8},{8,0},{16,24},{24,16},{1,9},{9,1},{17,25},{25,17},{2,10},{10... | collective-permute-start | bytes 6291464 | tf_op jit(solution)/shard_map/ppermute | solution.py:526
  302.8 19.8 %collective-permute-start.41 = (bf16[256,1024]{1,0:T(8,128)(2,1)}, bf16[256,1024]{1,0:T(8,128)(2,1)}, u32[]{:S(2)}, u32[]{:S(2)}) collective-permute-start(bf16[256,1024]{1,0:T(8,128)(2,1)} %flip.12.refs_1_), channel_id=1, source_target_pairs={{0,16},{1,17},{10,26},{11,27},{20,4},{21,5},{30,14},{31,15}} | collective-permute-start | bytes 1572872 | tf_op jit(solution)/shard_map/ppermute | solution.py:532
  (45 other events, 376.5 us)
